TPU v7x, 32 devices: a whole 2x2x4 slice. The times are simulated.
32 devices in a mesh: groups: 2 (over x), seq: 16 (over z, y, core).
Axes of the slice: x: 2, y: 2, z: 4, core: 2. Of those that a mesh axis runs over, the one named last changes fastest.
Arguments:
- clip: bfloat16 [16, 32, 32, 128], P('groups', 'seq'), parts along dimension 0, may hold values from -6 to 6
- frame_counts: int32 [6], P('groups'), parts along dimension 0, may hold values from 1 to 4, 8 in all
- conv_first: bfloat16 [3, 3, 3, 128, 128], replicated, may hold values from -0.109375 to 0.109375
- conv_second: bfloat16 [3, 3, 3, 128, 128], replicated, may hold values from -0.109375 to 0.109375
- patch_weight: bfloat16 [512, 1152], replicated, may hold values from -0.25 to 0.25
- qkv_weight: bfloat16 [1152, 3456], replicated, may hold values from -1 to 1
- query_gain: float32 [72], replicated, may hold values from 1.4 to 4
- key_gain: float32 [72], replicated, may hold values from 1.4 to 4
- out_weight: bfloat16 [1152, 1152], P('seq'), may hold values from -0.1875 to 0.1875
- window_lengths: int32 [2, 3], P('groups'), parts along dimension 0, may hold values from 1 to 1024, 2048 in all within a row
Outputs:
- attended: bfloat16 [4096, 1152], P(('groups', 'seq')), parts along dimension 0
There are 2 independent parts, one for each index of `groups`. A program takes and returns all parts, laid end to end along the dimension named above; an argument that names none is the same for every part. Nothing has to cross between parts.
Inputs may be any that keep to these rules, and one draw needn't show every extreme that they name: `frame_counts`: the clips' frame counts sum to 8; one clip has exactly 4. `window_lengths`: each row sums to 2048; in each row one window has exactly 1024 tokens.
All inputs are finite; a program needn't handle non-finite values.
Results may differ from a plain program's by a relative error of at most 0.039.
Values may be sent and summed in bfloat16 or wider, within the bound.
No kernel may reach another device: no remote copies, remote signals or barrier semaphores. Data moves between devices by JAX's collectives and lax.ppermute only.
A program may use at most 64 MiB of HBM per device.

v0:
```python
import math

import jax
import jax.numpy as jnp
from jax import lax
from jax.sharding import PartitionSpec as P

D = 1152
HEADS = 16


def extended(array, sides, width):
    for axis, dim in sides:
        size, length = (lax.axis_size(axis), array.shape[dim])
        up = [(i, (i + 1) % size) for i in range(size - 1)]
        down = [(j, i) for i, j in up]
        last = lax.slice_in_dim(array, length - width, length, axis=dim)
        first = lax.slice_in_dim(array, 0, width, axis=dim)
        before = lax.ppermute(last, axis, up)
        after = lax.ppermute(first, axis, down)
        array = jnp.concatenate([before, array, after], axis=dim)
    return array


def frame_weights(frame_counts, frames):
    position = jnp.arange(frames, dtype=jnp.int32)
    clip_ends = jnp.cumsum(frame_counts)

    def clip_of(index):
        return jnp.sum((index[:, None] >= clip_ends[None, :]).astype(jnp.int32), axis=1)

    own_clip = clip_of(position)
    columns = []
    for offset in (-1, 0, 1):
        neighbor = position + offset
        inside = (neighbor >= 0) & (neighbor < frames)
        same_clip = clip_of(jnp.clip(neighbor, 0, frames - 1)) == own_clip
        columns.append((inside & same_clip).astype(jnp.float32))
    return jnp.stack(columns, axis=1)


def convolve_rows(activation, kernel, tap_weights):
    empty_frame = jnp.zeros_like(activation[:1])
    shifted = (
        jnp.concatenate([empty_frame, activation[:-1]], 0),
        activation,
        jnp.concatenate([activation[1:], empty_frame], 0),
    )
    summed = None
    for offset in range(3):
        response = lax.conv_general_dilated(
            shifted[offset],
            kernel[offset],
            (1, 1),
            ((0, 0), (1, 1)),
            dimension_numbers=("NHWC", "HWIO", "NHWC"),
            preferred_element_type=jnp.float32,
        )
        tap_term = tap_weights[:, offset][:, None, None, None] * response
        summed = tap_term if offset == 0 else summed + tap_term
    return summed


def rms_scale(part, gain):
    factor = lax.rsqrt(jnp.mean(part * part, axis=-1, keepdims=True) + 1e-06)
    return (part * factor * gain).astype(jnp.bfloat16)


def shards(
    clip,
    frame_counts,
    conv_first,
    conv_second,
    patch_weight,
    qkv_weight,
    query_gain,
    key_gain,
    out_weight,
    window_lengths,
):
    frames, tile_rows, tile_cols, channels = clip.shape
    devices = lax.axis_size("seq")
    position = lax.axis_index("seq")
    head_dim = D // HEADS
    score_scale = 1.0 / math.sqrt(head_dim)
    tap_weights = frame_weights(frame_counts, frames)
    source = clip.astype(jnp.float32)
    padded_clip = extended(clip, (("seq", 1),), 2)
    first_in = jax.nn.silu(padded_clip.astype(jnp.float32)).astype(jnp.bfloat16)
    hidden_wide = convolve_rows(first_in, conv_first, tap_weights)
    global_row = position * tile_rows - 1 + jnp.arange(tile_rows + 2, dtype=jnp.int32)
    inside = ((global_row >= 0) & (global_row < tile_rows * devices)).astype(jnp.float32)
    hidden_one = (hidden_wide * inside[None, :, None, None]).astype(jnp.bfloat16)
    padded_second = jax.nn.silu(hidden_one.astype(jnp.float32)).astype(jnp.bfloat16)
    latent = (source + convolve_rows(padded_second, conv_second, tap_weights)).astype(jnp.bfloat16)
    token_rows = tile_rows // 2
    token_cols = tile_cols // 2
    patches = (
        latent.reshape(frames, token_rows, 2, token_cols, 2, channels)
        .transpose(0, 1, 3, 2, 4, 5)
        .reshape(-1, 4 * channels)
    )
    tok_count = patches.shape[0]
    embedded = jnp.dot(patches, patch_weight, preferred_element_type=jnp.float32).astype(
        jnp.bfloat16
    )
    values_f = embedded.astype(jnp.float32)
    row_mean = jnp.mean(values_f, axis=-1, keepdims=True)
    centered = values_f - row_mean
    variance = jnp.mean(centered * centered, axis=-1, keepdims=True)
    normed = (centered / jnp.sqrt(variance + 1e-06)).astype(jnp.bfloat16)
    projected = jnp.dot(normed, qkv_weight, preferred_element_type=jnp.float32).reshape(
        tok_count, 3, HEADS, head_dim
    )
    stacked = jnp.stack(
        [
            rms_scale(projected[:, 0], query_gain),
            rms_scale(projected[:, 1], key_gain),
            projected[:, 2].astype(jnp.bfloat16),
        ],
        axis=1,
    )
    groups = devices // HEADS
    frame_share = frames // groups
    local_share = tok_count // groups
    span_rows = devices * local_share
    outgoing = (
        stacked.reshape(groups, local_share, 3, HEADS, head_dim)
        .transpose(0, 3, 1, 2, 4)
        .reshape(devices, local_share, 3 * head_dim)
    )
    incoming = lax.all_to_all(outgoing, "seq", split_axis=0, concat_axis=0, tiled=True)
    arranged = (
        incoming.reshape(devices, frame_share, token_rows * token_cols, 3, head_dim)
        .transpose(3, 1, 0, 2, 4)
        .reshape(3, span_rows, head_dim)
    )
    my_group = position // HEADS
    lengths = lax.dynamic_index_in_dim(window_lengths, my_group, 0, keepdims=False)
    window_ends = jnp.cumsum(lengths)
    token_index = jnp.arange(span_rows, dtype=jnp.int32)
    segment = jnp.sum((token_index[:, None] >= window_ends[None, :]).astype(jnp.int32), axis=1)
    key_rows = arranged[1]
    value_rows = arranged[2]
    block_rows = min(512, span_rows)
    block_count = span_rows // block_rows

    def attend_block(inputs):
        query_block, segment_block = inputs
        scores = jnp.dot(query_block, key_rows.T, preferred_element_type=jnp.float32) * score_scale
        allowed = segment_block[:, None] == segment[None, :]
        scores = jnp.where(allowed, scores, -1e30)
        row_peak = jnp.max(scores, axis=-1, keepdims=True)
        weights = jnp.exp(scores - row_peak)
        row_mass = jnp.sum(weights, axis=-1, keepdims=True)
        mixed = (
            jnp.dot(weights.astype(jnp.bfloat16), value_rows, preferred_element_type=jnp.float32)
            / row_mass
        )
        return mixed.astype(jnp.bfloat16)

    mixed_rows = lax.map(
        attend_block,
        (
            arranged[0].reshape(block_count, block_rows, head_dim),
            segment.reshape(block_count, block_rows),
        ),
    ).reshape(span_rows, head_dim)
    outgoing_back = (
        mixed_rows.reshape(frame_share, devices, token_rows * token_cols, head_dim)
        .transpose(1, 0, 2, 3)
        .reshape(devices, local_share, head_dim)
    )
    returned = lax.all_to_all(outgoing_back, "seq", split_axis=0, concat_axis=0, tiled=True)
    merged = (
        returned.reshape(groups, HEADS, local_share, head_dim)
        .transpose(0, 2, 1, 3)
        .reshape(tok_count, D)
    )
    projected_out = jnp.dot(
        merged,
        lax.all_gather(out_weight, "seq", axis=0, tiled=True),
        preferred_element_type=jnp.float32,
    )
    return projected_out.astype(jnp.bfloat16)


def solution(mesh):
    return jax.shard_map(
        shards,
        mesh=mesh,
        in_specs=(
            P("groups", "seq", None, None),
            P("groups"),
            P(),
            P(),
            P(),
            P(),
            P(),
            P(),
            P("seq", None),
            P("groups", None),
        ),
        out_specs=P(("groups", "seq"), None),
        check_vma=False,
    )
```

profile of v0, /device:TPU:0, one launch (start us, length us, event | category | flops | bytes accessed | tf_op | source)
XLA Modules:
  0.0 110.9 jit_solution(4474278187427429583)
XLA Ops:
  6.5 1.1 %copy.54 = bf16[8,2,32,128]{3,0,2,1:T(8,128)(2,1)S(1)} copy(bf16[8,2,32,128]{3,2,1,0:T(8,128)(2,1)} %param.12) | data formatting | bytes 262144 | tf_op args[0]
  7.7 2.4 %collective-permute-start = (bf16[8,2,32,128]{3,0,2,1:T(8,128)(2,1)S(1)}, bf16[8,2,32,128]{3,0,2,1:T(8,128)(2,1)S(1)}, u32[]{:S(2)}, u32[]{:S(2)}) collective-permute-start(bf16[8,2,32,128]{3,0,2,1:T(8,128)(2,1)S(1)} %copy.54), channel_id=1, source_target_pairs={{0,1},{1,2},{2,3},{3,4},{4,5},{5,6},{6,7},{7,8},{8,9},{9,10},{10,1... | collective-permute-start | bytes 393224 | tf_op jit(solution)/shard_map/ppermute | solution.py:19
  10.1 1.3 %collective-permute-start.1 = (bf16[8,2,32,128]{3,0,2,1:T(8,128)(2,1)S(1)}, bf16[8,2,32,128]{3,0,2,1:T(8,128)(2,1)S(1)}, u32[]{:S(2)}, u32[]{:S(2)}) collective-permute-start(bf16[8,2,32,128]{3,0,2,1:T(8,128)(2,1)S(1)} %copy.54), channel_id=1, source_target_pairs={{1,0},{2,1},{3,2},{4,3},{5,4},{6,5},{7,6},{8,7},{9,8},{10,9},{11,1... | collective-permute-start | bytes 393224 | tf_op jit(solution)/shard_map/ppermute | solution.py:20
  11.4 0.8 reduce-window.17
  12.3 3.1 %collective-permute-done.1 = bf16[8,2,32,128]{3,0,2,1:T(8,128)(2,1)S(1)} collective-permute-done((bf16[8,2,32,128]{3,0,2,1:T(8,128)(2,1)S(1)}, bf16[8,2,32,128]{3,0,2,1:T(8,128)(2,1)S(1)}, u32[]{:S(2)}, u32[]{:S(2)}) %collective-permute-start.1) | collective-permute-done | bytes 131104 | tf_op jit(solution)/shard_map/ppermute | solution.py:20
  15.4 0.2 fusion.33
  15.6 0.2 fusion.61
  15.8 1.8 %convolution_multiply_fusion.2 = f32[8,4,32,128]{3,0,2,1:T(8,128)S(1)} fusion(bf16[7,6,32,128]{3,0,2,1:T(8,128)(2,1)S(1)} %get-tuple-element.71, bf16[3,3,3,128,128]{4,3,2,1,0:T(8,128)(2,1)} %param.14, f32[8]{0:T(128)S(1)} %get-tuple-element.76), kind=kOutput, calls=%fused_computation.22 | convolution fusion | flops 295829504 | bytes 1163296 | tf_op jit(solution)/shard_map/conv_general_dilated | solution.py:51
  17.7 0.8 fusion.23
  18.5 0.8 multiply_convert_fusion.2
  19.3 0.1 fusion.62
  19.4 0.5 convolution_multiply_fusion.5
  19.9 0.5 fusion.27
  20.4 0.5 fusion.29
  20.9 0.1 copy.71
  21.1 0.4 fusion.63
  21.6 0.2 multiply_reduce_fusion.2
  21.8 6.5 %fusion.36 = f32[128,3456]{0,1:T(8,128)S(1)} fusion(bf16[1152,3456]{1,0:T(8,128)(2,1)} %param.17, f32[128,1152]{1,0:T(8,128)S(1)} %get-tuple-element.78, f32[128]{0:T(128)S(1)} %add_sqrt_fusion, f32[128]{0:T(128)S(1)} %broadcast_multiply_fusion), kind=kOutput, calls=%fused_computation.49 | convolution fusion | flops 1019658240 | bytes 10322944 | tf_op jit(solution)/shard_map/dot_general | solution.py:112
  28.3 0.1 multiply_reduce_fusion.1
  28.5 0.2 multiply_convert_fusion.1
  28.7 0.1 maximum_bitcast_fusion
  28.8 1.0 copy.60
  29.8 9.0 %all-to-all-start = ((bf16[16,128,216]{1,2,0:T(8,128)(2,1)}), bf16[16,128,216]{1,2,0:T(8,128)(2,1)S(1)}, u32[]{:S(2)}, u32[]{:S(2)}) async-start(bf16[16,128,216]{1,2,0:T(8,128)(2,1)} %bitcast.18), calls=%async_computation | async-start | bytes 1769472 | tf_op jit(solution)/shard_map/all_to_all | solution.py:132
  38.8 0.2 all-gather.2.cloned.1.call-start
  39.0 0.5 all-gather.2.cloned.1.call-update
  39.6 0.2 reduce-window.16
  39.8 21.6 %all-to-all-done = bf16[16,128,216]{1,2,0:T(8,128)(2,1)S(1)} async-done(((bf16[16,128,216]{1,2,0:T(8,128)(2,1)}), bf16[16,128,216]{1,2,0:T(8,128)(2,1)S(1)}, u32[]{:S(2)}, u32[]{:S(2)}) %all-to-all-start) | async-done | bytes 884768 | tf_op jit(solution)/shard_map/all_to_all | solution.py:132
  61.4 1.3 %copy.61 = bf16[16,128,216]{2,1,0:T(8,128)(2,1)} copy(bf16[16,128,216]{1,2,0:T(8,128)(2,1)S(1)} %all-to-all-done) | data formatting | bytes 1769472 | tf_op jit(solution)/shard_map/all_to_all | solution.py:132
  62.7 4.1 %reshape.193 = bf16[16,8,16,3,72]{4,3,2,1,0:T(4,128)(2,1)S(1)} reshape(bf16[16,128,216]{2,1,0:T(8,128)(2,1)} %copy.61) | data formatting | bytes 1769472 | tf_op jit(solution)/shard_map/reshape | solution.py:134
  66.8 3.2 %fusion.60 = (bf16[1,8,16,16,72]{4,0,3,1,2:T(2,128)(2,1)S(1)}, bf16[1,8,16,16,72]{4,0,3,1,2:T(2,128)(2,1)S(1)}, bf16[1,8,16,16,72]{4,0,3,1,2:T(2,128)(2,1)S(1)}) fusion(bf16[3,8,16,16,72]{4,0,3,1,2:T(4,128)(2,1)S(1)} %bitcast.77), kind=kLoop, calls=%fused_computation.92 | loop fusion | bytes 1769472 | tf_op jit(solution)/shard_map/slice | solution.py:144
  70.2 0.7 copy-done.1
  70.9 10.1 %while.10 = (s32[]{:T(128)}, bf16[4,512,72]{1,2,0:T(8,128)(2,1)S(1)}, s32[4,512]{1,0:T(4,128)S(1)}, s32[2048]{0:T(1024)S(1)}, bf16[4,512,72]{2,1,0:T(8,128)(2,1)...) while((s32[]{:T(128)}, bf16[4,512,72]{1,2,0:T(8,128)(2,1)S(1)}, ...), condition=%wide.region_14.15_spmd, body=%wide.region_11.14_spmd.sunk | while | flops 310451200 | bytes 13860961 | solution.py:162
  70.9 0.9 fusion.82
  71.9 0.7 fusion.83
  72.6 0.9 fusion.84
  73.5 0.9 fusion.82
  74.4 0.7 fusion.83
  75.1 0.9 fusion.84
  76.0 0.9 fusion.82
  76.9 0.7 fusion.83
  77.6 0.9 fusion.84
  78.5 0.9 fusion.82
  79.4 0.7 fusion.83
  80.2 0.9 fusion.84
  81.0 0.3 copy.65
  81.4 0.2 copy.67
  81.6 19.3 %all_to_all.10 = bf16[16,128,72]{1,2,0:T(8,128)(2,1)S(1)} all-to-all(bf16[16,128,72]{1,2,0:T(8,128)(2,1)S(1)} %copy.67), channel_id=1, replica_groups=mesh['groups'=2,'seq'=16] {'seq'}, dimensions={0} | all-to-all | bytes 589824 | tf_op jit(solution)/shard_map/all_to_all | solution.py:174
  100.9 3.1 %convolution_convert_fusion = bf16[128,1152]{1,0:T(8,128)(2,1)} fusion(bf16[128,1152]{0,1:T(8,128)(2,1)S(1)} %bitcast.83, bf16[1152,1152]{1,0:T(8,128)(2,1)} %all-gather.2.cloned.1.call-done), kind=kOutput, calls=%fused_computation.14 | convolution fusion | flops 339886080 | bytes 3244032 | tf_op jit(solution)/shard_map/dot_general | solution.py:180
  (39 shorter events, 0.7 us)
Async XLA Ops:
  6.5 14.6 %copy-start = (bf16[512,1152]{1,0:T(8,128)(2,1)S(1)}, bf16[512,1152]{1,0:T(8,128)(2,1)}, u32[]{:S(2)}) copy-start(bf16[512,1152]{1,0:T(8,128)(2,1)} %param.16) | copy-start | bytes 3538948
  6.5 11.1 %copy-start.6 = (bf16[3,3,3,128,128]{4,3,2,1,0:T(8,128)(2,1)S(1)}, bf16[3,3,3,128,128]{4,3,2,1,0:T(8,128)(2,1)}, u32[]{:S(2)}) copy-start(bf16[3,3,3,128,128]{4,3,2,1,0:T(8,128)(2,1)} %param.14) | copy-start | bytes 2654212
  7.7 4.6 %collective-permute-start = (bf16[8,2,32,128]{3,0,2,1:T(8,128)(2,1)S(1)}, bf16[8,2,32,128]{3,0,2,1:T(8,128)(2,1)S(1)}, u32[]{:S(2)}, u32[]{:S(2)}) collective-permute-start(bf16[8,2,32,128]{3,0,2,1:T(8,128)(2,1)S(1)} %copy.54), channel_id=1, source_target_pairs={{0,1},{1,2},{2,3},{3,4},{4,5},{5,6},{6,7},{7,8},{8,9},{9,10},{10,1... | collective-permute-start | bytes 393224 | tf_op jit(solution)/shard_map/ppermute | solution.py:19
  10.1 5.4 %collective-permute-start.1 = (bf16[8,2,32,128]{3,0,2,1:T(8,128)(2,1)S(1)}, bf16[8,2,32,128]{3,0,2,1:T(8,128)(2,1)S(1)}, u32[]{:S(2)}, u32[]{:S(2)}) collective-permute-start(bf16[8,2,32,128]{3,0,2,1:T(8,128)(2,1)S(1)} %copy.54), channel_id=1, source_target_pairs={{1,0},{2,1},{3,2},{4,3},{5,4},{6,5},{7,6},{8,7},{9,8},{10,9},{11,1... | collective-permute-start | bytes 393224 | tf_op jit(solution)/shard_map/ppermute | solution.py:20
  15.8 3.6 %copy-start.3 = (bf16[3,3,3,128,128]{4,3,2,1,0:T(8,128)(2,1)S(1)}, bf16[3,3,3,128,128]{4,3,2,1,0:T(8,128)(2,1)}, u32[]{:S(2)}) copy-start(bf16[3,3,3,128,128]{4,3,2,1,0:T(8,128)(2,1)} %param.15) | copy-start | bytes 2654212
  17.7 2.8 %copy-start.2 = (bf16[8,2,32,128]{3,2,1,0:T(8,128)(2,1)S(1)}, bf16[8,2,32,128]{3,2,1,0:T(8,128)(2,1)}, u32[]{:S(2)}) copy-start(bf16[8,2,32,128]{3,2,1,0:T(8,128)(2,1)} %param.12) | copy-start | bytes 393220
  21.8 6.7 %copy-start.4 = (f32[72]{0:T(128)S(1)}, f32[72]{0:T(128)}, u32[]{:S(2)}) copy-start(f32[72]{0:T(128)} %param.18) | copy-start | bytes 868
  21.8 6.7 %copy-start.5 = (f32[72]{0:T(128)S(1)}, f32[72]{0:T(128)}, u32[]{:S(2)}) copy-start(f32[72]{0:T(128)} %param.19) | copy-start | bytes 868
  28.4 11.1 %copy-start.7 = (s32[1,3]{1,0:T(1,128)S(1)}, s32[1,3]{1,0:T(1,128)}, u32[]{:S(2)}) copy-start(s32[1,3]{1,0:T(1,128)} %param.21) | copy-start | bytes 40
  29.8 31.6 %all-to-all-start = ((bf16[16,128,216]{1,2,0:T(8,128)(2,1)}), bf16[16,128,216]{1,2,0:T(8,128)(2,1)S(1)}, u32[]{:S(2)}, u32[]{:S(2)}) async-start(bf16[16,128,216]{1,2,0:T(8,128)(2,1)} %bitcast.18), calls=%async_computation | async-start | bytes 1769472 | tf_op jit(solution)/shard_map/all_to_all | solution.py:132
  38.8 62.1 %all-gather.2.cloned.1.call-start = ((), (), s32[]{:S(2)}) async-start(), calls=%async_computation.2 | async-start | bytes 2820096 | tf_op jit(solution)/shard_map/all_gather | solution.py:182
  70.0 1.0 copy-start.1
Sparse Core Ops, SparseCore 0:
  41.8 47.0 all-gather.1
where the time goes:
time: 111 us
  waiting for transfers between devices  25.2 us (23%)
  matrix products  22.1 us (20%)
  blocking collectives  19.3 us (17%)
  between operations  13.8 us (12%)
  starting transfers between devices  12.9 us (12%)
  local copies, waits for them, and re-layouts  12.7 us (11%)
  other arithmetic  4.9 us (4%)
    all_to_all x1, waiting for transfers between devices, shards(): lax.all_to_all(outgoing, 'seq', split_axis=0, concat_axis=0, tiled=True)  21.6 us
    all_to_all x1, blocking collectives, shards(): lax.all_to_all(outgoing_back, 'seq', split_axis=0, concat_axis=0, tiled=T...  19.3 us
    all_to_all x1, starting transfers between devices, shards(): lax.all_to_all(outgoing, 'seq', split_axis=0, concat_axis=0, tiled=True)  8.97 us
    dot_general x1, matrix products, shards(): jnp.dot(normed, qkv_weight, preferred_element_type=jnp.float32)  6.5 us
    conv_general_dilated x6, matrix products, convolve_rows(): lax.conv_general_dilated(shifted[offset], kernel[offset], (1, 1), ((0, 0)...  4.93 us
    reshape x1, local copies, waits for them, and re-layouts, shards(): incoming.reshape(devices, frame_share, token_rows * token_cols, 3, head_dim)  4.08 us
    dot_general x4, matrix products, attend_block(): jnp.dot(query_block, key_rows.T, preferred_element_type=jnp.float32)  3.62 us
    dot_general x4, matrix products, attend_block(): jnp.dot(weights.astype(jnp.bfloat16), value_rows, preferred_element_type=...  3.56 us
  transfers between devices with their start and end apart: 4, of which 2 were waited for; matrix products, arithmetic and copies ran while one was open for 19% of the time, Pallas kernels for 0%

commit v1 on v0

--- a/solution.py
+++ b/solution.py
@@ -1,8 +1,11 @@
+import functools
 import math
 
 import jax
 import jax.numpy as jnp
 from jax import lax
+from jax.experimental import pallas as pl
+from jax.experimental.pallas import tpu as pltpu
 from jax.sharding import PartitionSpec as P
 
 D = 1152
@@ -66,7 +69,7 @@
     return (part * factor * gain).astype(jnp.bfloat16)
 
 
-def shards(
+def general_shards(
     clip,
     frame_counts,
     conv_first,
@@ -185,9 +188,481 @@
     return projected_out.astype(jnp.bfloat16)
 
 
+HD = D // HEADS
+SLOT = 80
+MASK = 1024.0
+F32 = jnp.float32
+BF16 = jnp.bfloat16
+VMEM = pl.BlockSpec(memory_space=pltpu.VMEM)
+SMEM = pl.BlockSpec(memory_space=pltpu.SMEM)
+NT = (((1,), (1,)), ((), ()))
+
+
+def params(mib=40):
+    return pltpu.CompilerParams(vmem_limit_bytes=mib << 20)
+
+
+def silu(v):
+    return v / (1.0 + jnp.exp(-v))
+
+
+def long_window(lengths):
+    first, second = lengths[0, 0], lengths[0, 1]
+    half = 1024
+    start = jnp.where(first == half, 0, jnp.where(second == half, first, first + second))
+    bound = jnp.where(first == half, half + second, first)
+    return start, bound
+
+
+def fold_kernel(patch_ref, qkv_ref, folded_ref):
+    patch = patch_ref[...].astype(F32)
+    centered = (patch - jnp.mean(patch, axis=1, keepdims=True)).astype(BF16)
+    product = jnp.dot(centered, qkv_ref[...], preferred_element_type=F32)
+    folded_ref[...] = product.T.astype(BF16)
+
+
+def fold(patch_weight, qkv_weight):
+    inner = patch_weight.shape[0]
+    return pl.pallas_call(
+        fold_kernel,
+        grid=(3,),
+        out_shape=jax.ShapeDtypeStruct((3 * D, inner), BF16),
+        in_specs=[
+            pl.BlockSpec((inner, D), lambda i: (0, 0)),
+            pl.BlockSpec((D, D), lambda i: (0, i)),
+        ],
+        out_specs=pl.BlockSpec((D, inner), lambda i: (i, 0)),
+        compiler_params=params(),
+        name="fold",
+        cost_estimate=pl.CostEstimate(flops=2 * inner * D * 3 * D, bytes_accessed=12 << 20, transcendentals=0),
+    )(patch_weight, qkv_weight)
+
+
+def frame_taps(counts_ref, frames):
+    def clip_of(frame):
+        end = 0
+        index = 0
+        for c in range(counts_ref.shape[0]):
+            end = end + counts_ref[c]
+            index = index + jnp.where(frame >= end, 1, 0)
+        return index
+
+    own = [clip_of(f) for f in range(frames)]
+    joined = [jnp.where(own[f] == own[f + 1], 1.0, 0.0) for f in range(frames - 1)]
+    return [0.0] + joined, joined + [0.0]
+
+
+def conv_kernel(
+    counts_ref, lengths_ref, own_ref, before_ref, after_ref, first_ref, second_ref, patch_ref,
+    keep_ref, send_ref, grid_one, grid_two, pairs_one, pairs_two, pixels,
+):
+    frames, _, cols, ch = own_ref.shape
+    wide = 12 * ch
+    position = lax.axis_index("seq")
+    before_tap, after_tap = frame_taps(counts_ref, frames)
+    for weights, pairs in ((first_ref, pairs_one), (second_ref, pairs_two)):
+        for o in range(3):
+            for four in range(4):
+                for out_row in range(2):
+                    for j in range(3):
+                        rows = pl.ds((four * 3 + j) * ch, ch)
+                        columns = pl.ds(out_row * ch, ch)
+                        tap = four - out_row
+                        if 0 <= tap < 3:
+                            pairs[o, rows, columns] = weights[o, tap, j]
+                        else:
+                            pairs[o, rows, columns] = jnp.zeros((ch, ch), BF16)
+    column = lax.broadcasted_iota(jnp.int32, (frames, cols, ch), 1)
+
+    def shifted(row):
+        left = jnp.where(column == 0, 0.0, pltpu.roll(row, 1, 1))
+        right = jnp.where(column == cols - 1, 0.0, pltpu.roll(row, cols - 1, 1))
+        return [part.astype(BF16) for part in (left, row, right)]
+
+    blank = jnp.zeros((cols, wide), BF16)
+    for g in range(2):
+        grid_one[g, 0] = blank
+        grid_one[g, frames + 1] = blank
+    grid_two[0] = blank
+    grid_two[frames + 1] = blank
+    sources = [before_ref, before_ref, own_ref, own_ref, after_ref, after_ref]
+    for r in range(6):
+        row = silu(sources[r][:, r % 2].astype(F32))
+        parts = shifted(row)
+        for g in range(2):
+            four = r - 2 * g
+            if 0 <= four < 4:
+                for j in range(3):
+                    grid_one[g, 1 : frames + 1, :, (four * 3 + j) * ch : (four * 3 + j + 1) * ch] = parts[j]
+
+    def summed(terms):
+        rows = []
+        for f in range(frames):
+            total = terms[1][f]
+            if f > 0:
+                total = total + before_tap[f] * terms[0][f]
+            if f < frames - 1:
+                total = total + after_tap[f] * terms[2][f]
+            rows.append(total)
+        return jnp.stack(rows)
+
+    for g in range(2):
+        terms = []
+        for o in range(3):
+            left = grid_one[g, o : o + frames].reshape(frames * cols, wide)
+            terms.append(
+                jnp.dot(left, pairs_one[o], preferred_element_type=F32).reshape(frames, cols, 2 * ch)
+            )
+        hidden = summed(terms)
+        for out_row in range(2):
+            four = 2 * g + out_row
+            row = hidden[:, :, out_row * ch : (out_row + 1) * ch]
+            if four == 0:
+                row = row * jnp.where(position == 0, 0.0, 1.0)
+            if four == 3:
+                row = row * jnp.where(position == lax.axis_size("seq") - 1, 0.0, 1.0)
+            row = silu(row.astype(BF16).astype(F32))
+            parts = shifted(row)
+            for j in range(3):
+                grid_two[1 : frames + 1, :, (four * 3 + j) * ch : (four * 3 + j + 1) * ch] = parts[j]
+    terms = []
+    for o in range(3):
+        left = grid_two[o : o + frames].reshape(frames * cols, wide)
+        terms.append(
+            jnp.dot(left, pairs_two[o], preferred_element_type=F32).reshape(frames, cols, 2 * ch)
+        )
+    residual = summed(terms)
+    for out_row in range(2):
+        block = own_ref[:, out_row].astype(F32) + residual[:, :, out_row * ch : (out_row + 1) * ch]
+        pixels[out_row] = block.astype(BF16).astype(F32).reshape(frames * cols, ch)
+    tokens = frames * cols // 2
+    patches = jnp.concatenate(
+        [pixels[a, pl.ds(b, tokens, 2), :] for a in range(2) for b in range(2)], axis=1
+    )
+    embedded = jnp.dot(patches.astype(BF16), patch_ref[...], preferred_element_type=F32)
+    centered = embedded - jnp.mean(embedded, axis=1, keepdims=True)
+    variance = jnp.mean(centered * centered, axis=1, keepdims=True)
+    scaled = patches * (1.0 / jnp.sqrt(variance + 1e-06))
+    half = tokens // 2
+    low, high = scaled[:half], scaled[half:]
+    start, _ = long_window(lengths_ref)
+    q_cols = cols // 2
+    slot = lax.broadcasted_iota(jnp.int32, low.shape, 0)
+    token = (slot // q_cols) * (lax.axis_size("seq") * q_cols) + position * q_cols + slot % q_cols
+    inside = jnp.where(token >= start, 1, 0)
+    mine = inside == jnp.where(position % 2 == 0, 1, 0)
+    keep = jnp.where(mine, low, high).astype(BF16)
+    send = jnp.where(mine, high, low).astype(BF16)
+    for tile in range(4):
+        keep_ref[tile * half : (tile + 1) * half] = keep[:, tile * ch : (tile + 1) * ch]
+        send_ref[tile * half : (tile + 1) * half] = send[:, tile * ch : (tile + 1) * ch]
+
+
+def convolve(counts, lengths, clip, before, after, conv_first, conv_second, patch_weight):
+    frames, _, cols, ch = clip.shape
+    tokens = frames * cols // 2
+    out = jax.ShapeDtypeStruct((2 * tokens, ch), BF16)
+    return pl.pallas_call(
+        conv_kernel,
+        out_shape=(out, out),
+        in_specs=[SMEM, SMEM] + [VMEM] * 6,
+        out_specs=(VMEM, VMEM),
+        scratch_shapes=[
+            pltpu.VMEM((2, frames + 2, cols, 12 * ch), BF16),
+            pltpu.VMEM((frames + 2, cols, 12 * ch), BF16),
+            pltpu.VMEM((3, 12 * ch, 2 * ch), BF16),
+            pltpu.VMEM((3, 12 * ch, 2 * ch), BF16),
+            pltpu.VMEM((2, frames * cols, ch), F32),
+        ],
+        compiler_params=params(),
+        name="convolve",
+        cost_estimate=pl.CostEstimate(flops=2 << 30, bytes_accessed=4 << 20, transcendentals=1 << 18),
+    )(counts, lengths, clip, before, after, conv_first, conv_second, patch_weight)
+
+
+def chip_at(place):
+    chips = lax.axis_size("seq") // 2
+    place = lax.rem(place + 2 * chips, chips)
+    return jnp.where(place < chips // 2, 2 * place, 2 * (chips - 1 - place) + 1)
+
+
+def ring_place():
+    chips = lax.axis_size("seq") // 2
+    chip = lax.axis_index("seq") // 2
+    return jnp.where(chip % 2 == 0, chip // 2, chips - 1 - chip // 2)
+
+
+def ring_pairs():
+    size = lax.axis_size("seq")
+    chips = size // 2
+    order = [2 * i for i in range(chips // 2)] + [2 * i + 1 for i in reversed(range(chips // 2))]
+    return [
+        (2 * order[i] + core, 2 * order[(i + 1) % chips] + core) for i in range(chips) for core in range(2)
+    ]
+
+
+def window_sides(lengths_ref, chip, count):
+    size = lax.axis_size("seq")
+    core = lax.axis_index("seq") % 2
+    start, bound = long_window(lengths_ref)
+    lane = lax.broadcasted_iota(jnp.int32, (8, count), 1)
+    half = count // 2
+    slot = lane % half
+    row = 2 * chip + jnp.where(lane < half, core, 1 - core)
+    q_cols = 16
+    token = (slot // q_cols) * (size * q_cols) + row * q_cols + slot % q_cols
+    inside = jnp.where(token >= start, 1, 0)
+    upper = inside != jnp.where(core == 0, 1, 0)
+    token = jnp.where(upper, token + 4 * size * q_cols, token)
+    return jnp.where(token < bound, 1.0, -1.0)
+
+
+def block_tokens(ref, ch=128, half=64):
+    second = 4 * half + 5 * SLOT
+    parts = []
+    for base in (0, second):
+        parts.append(
+            jnp.concatenate([ref[base + t * half : base + (t + 1) * half] for t in range(4)], axis=1)
+        )
+    return jnp.concatenate(parts, axis=0)
+
+
+def half_tokens(ref, half=64):
+    return jnp.concatenate([ref[t * half : (t + 1) * half] for t in range(4)], axis=1)
+
+
+def normed_heads(part, gain):
+    count = part.shape[1]
+    heads = part.reshape(HEADS, HD, count)
+    factor = lax.rsqrt(jnp.mean(heads * heads, axis=1, keepdims=True) + 1e-06)
+    return heads * factor * gain[None, :, :count]
+
+
+def attend(tokens, sides, folded, key_gain, queries, acc_ref):
+    count = tokens.shape[0]
+    both = lax.dot_general(folded, tokens, NT, preferred_element_type=F32)
+    keys = normed_heads(both[:D], key_gain)
+    values = both[D:].reshape(HEADS, HD, count)
+    row = lax.broadcasted_iota(jnp.int32, (8, count), 0)
+    key_tail = jnp.where(row == 0, sides, jnp.where(row == 1, 1.0, 0.0))
+    value_tail = jnp.where(row == 0, 1.0, 0.0)
+    tail_row = lax.broadcasted_iota(jnp.int32, (8, 128), 0)
+    for h in range(HEADS):
+        key = jnp.concatenate([keys[h], key_tail], axis=0).T.astype(BF16)
+        value = jnp.concatenate([values[h], value_tail], axis=0).astype(BF16)
+        scores = jnp.dot(key, queries[h], preferred_element_type=F32)
+        peak = jnp.max(scores, axis=0, keepdims=True)
+        weights = jnp.exp2(scores - peak).astype(BF16)
+        mixed = jnp.dot(value, weights, preferred_element_type=F32)
+        acc_ref[h, :HD] = mixed[:HD]
+        acc_ref[h, HD:] = jnp.where(tail_row == 1, peak, mixed[HD:])
+
+
+def own_kernel(lengths_ref, block_ref, folded_ref, query_gain_ref, key_gain_ref, queries_ref, acc_ref):
+    tokens = block_tokens(block_ref)
+    count = tokens.shape[0]
+    sides = window_sides(lengths_ref, lax.axis_index("seq") // 2, count)
+    part = lax.dot_general(folded_ref[:D], tokens, NT, preferred_element_type=F32)
+    queries = normed_heads(part, query_gain_ref[...])
+    row = lax.broadcasted_iota(jnp.int32, (8, count), 0)
+    tail = jnp.where(row == 0, MASK * sides, jnp.where(row == 1, -MASK, 0.0))
+    for h in range(HEADS):
+        queries_ref[h] = jnp.concatenate([queries[h], tail], axis=0).astype(BF16)
+    attend(tokens, sides, folded_ref[D:], key_gain_ref[...], queries_ref, acc_ref)
+
+
+def step_kernel(step, lengths_ref, ahead_ref, behind_ref, folded_ref, key_gain_ref, queries_ref, acc_ref):
+    place = ring_place()
+    if step < 4:
+        tokens = jnp.concatenate([block_tokens(ahead_ref), block_tokens(behind_ref)], axis=0)
+        sides = jnp.concatenate(
+            [
+                window_sides(lengths_ref, chip_at(place - step), 128),
+                window_sides(lengths_ref, chip_at(place + step), 128),
+            ],
+            axis=1,
+        )
+    else:
+        tokens = jnp.concatenate([half_tokens(ahead_ref), half_tokens(behind_ref)], axis=0)
+        sides = window_sides(lengths_ref, chip_at(place + step), 128)
+    attend(tokens, sides, folded_ref[D:], key_gain_ref[...], queries_ref, acc_ref)
+
+
+ACC = jax.ShapeDtypeStruct((HEADS, SLOT, 128), F32)
+
+
+def cost(count):
+    flops = 2 * count * 2 * D * 512 + 4 * HEADS * 128 * 128 * count
+    return pl.CostEstimate(flops=2 * flops, bytes_accessed=5 << 20, transcendentals=HEADS * 128 * count)
+
+
+def own_attention(lengths, block, folded, query_gain, key_gain):
+    return pl.pallas_call(
+        own_kernel,
+        out_shape=(jax.ShapeDtypeStruct((HEADS, SLOT, 128), BF16), ACC),
+        in_specs=[SMEM] + [VMEM] * 4,
+        out_specs=(VMEM, VMEM),
+        compiler_params=params(),
+        name="own_attention",
+        cost_estimate=cost(192),
+    )(lengths, block, folded, query_gain, key_gain)
+
+
+def step_attention(step, lengths, ahead, behind, folded, key_gain, queries):
+    return pl.pallas_call(
+        functools.partial(step_kernel, step),
+        out_shape=ACC,
+        in_specs=[SMEM] + [VMEM] * 5,
+        out_specs=VMEM,
+        compiler_params=params(),
+        name="step_attention",
+        cost_estimate=cost(256 if step < 4 else 128),
+    )(lengths, ahead, behind, folded, key_gain, queries)
+
+
+def out_kernel(parts, *refs):
+    acc_refs = refs[:parts]
+    block_refs = refs[parts:-3]
+    keep_ref, send_ref, mixed_ref = refs[-3:]
+    zeros = jnp.zeros((SLOT - HD, 128), F32)
+    for h in range(HEADS):
+        peaks = [acc[h, HD + 1 : HD + 2] for acc in acc_refs]
+        peak = functools.reduce(jnp.maximum, peaks)
+        total = None
+        for acc, own in zip(acc_refs, peaks):
+            term = acc[h] * jnp.exp2(own - peak)
+            total = term if total is None else total + term
+        mixed = total[:HD] / total[HD : HD + 1]
+        mixed_ref[h] = jnp.concatenate([mixed, zeros], axis=0)
+    place = ring_place()
+    core = lax.axis_index("seq") % 2
+    offsets = [0, -1, 1, -2, 2, -3, 3, 4]
+    per_core = len(block_refs) // 2
+    slots, tiles = [], []
+    for side in range(2):
+        refs_here = block_refs[side * per_core : (side + 1) * per_core]
+        for index, offset in enumerate(offsets):
+            head = 2 * chip_at(place + offset) + jnp.where(core == side, 0, 1)
+            slots.append(mixed_ref[head])
+            if index < 7:
+                low, high, base = refs_here[index], refs_here[index], 256 + 5 * SLOT + 256
+            else:
+                low, high, base = refs_here[7], refs_here[8], 256
+            tiles.append(
+                [low[256 + t * SLOT : 256 + (t + 1) * SLOT] for t in range(5)]
+                + [high[base + t * SLOT : base + (t + 1) * SLOT] for t in range(4)]
+            )
+    left = jnp.concatenate(slots, axis=0).T.astype(BF16)
+    half = keep_ref.shape[0]
+    for first in range(0, 9, 2):
+        group = range(first, min(first + 2, 9))
+        right = jnp.concatenate(
+            [jnp.concatenate([block[t] for block in tiles], axis=0) for t in group], axis=1
+        )
+        result = jnp.dot(left, right, preferred_element_type=F32).astype(BF16)
+        columns = slice(first * 128, (group[-1] + 1) * 128)
+        keep_ref[:, columns] = result[:half]
+        send_ref[:, columns] = result[half:]
+
+
+def project_out(accs, blocks):
+    out = jax.ShapeDtypeStruct((64, D), BF16)
+    return pl.pallas_call(
+        functools.partial(out_kernel, len(accs)),
+        out_shape=(out, out),
+        in_specs=[VMEM] * (len(accs) + len(blocks)),
+        out_specs=(VMEM, VMEM),
+        scratch_shapes=[pltpu.VMEM((HEADS, SLOT, 128), F32)],
+        compiler_params=params(),
+        name="project_out",
+        cost_estimate=pl.CostEstimate(flops=2 * 128 * 1280 * D, bytes_accessed=4 << 20, transcendentals=0),
+    )(*accs, *blocks)
+
+
+def merge_kernel(lengths_ref, keep_ref, got_ref, out_ref):
+    position = lax.axis_index("seq")
+    keep = keep_ref[...].astype(F32)
+    got = got_ref[...].astype(F32)
+    start, _ = long_window(lengths_ref)
+    q_cols = 16
+    slot = lax.broadcasted_iota(jnp.int32, keep.shape, 0)
+    token = (slot // q_cols) * (lax.axis_size("seq") * q_cols) + position * q_cols + slot % q_cols
+    inside = jnp.where(token >= start, 1, 0)
+    mine = inside == jnp.where(position % 2 == 0, 1, 0)
+    half = keep.shape[0]
+    out_ref[:half] = jnp.where(mine, keep, got).astype(BF16)
+    out_ref[half:] = jnp.where(mine, got, keep).astype(BF16)
+
+
+def merge(lengths, keep, got):
+    return pl.pallas_call(
+        merge_kernel,
+        out_shape=jax.ShapeDtypeStruct((128, D), BF16),
+        in_specs=[SMEM, VMEM, VMEM],
+        out_specs=VMEM,
+        compiler_params=params(),
+        name="merge",
+    )(lengths, keep, got)
+
+
+def weight_tiles(out_weight):
+    padded = jnp.pad(out_weight, ((0, SLOT - HD), (0, 0)))
+    return padded.reshape(SLOT, 9, 128).transpose(1, 0, 2).reshape(9 * SLOT, 128)
+
+
+def shards(
+    clip, frame_counts, conv_first, conv_second, patch_weight, qkv_weight, query_gain, key_gain,
+    out_weight, window_lengths,
+):
+    size = lax.axis_size("seq")
+    up = [(i, i + 1) for i in range(size - 1)]
+    down = [(j, i) for i, j in up]
+    cores = [(i, i ^ 1) for i in range(size)]
+    forward = ring_pairs()
+    backward = [(j, i) for i, j in forward]
+
+    def send(array, pairs):
+        return lax.ppermute(array, "seq", pairs)
+
+    before = send(clip, up)
+    after = send(clip, down)
+    score_scale = math.log2(math.e) / math.sqrt(HD)
+    query_rows = jnp.broadcast_to((query_gain * score_scale)[:, None], (HD, 256))
+    key_rows = jnp.broadcast_to(key_gain[:, None], (HD, 256))
+    folded = fold(patch_weight, qkv_weight)
+    weight = weight_tiles(out_weight)
+    keep, other = convolve(
+        frame_counts, window_lengths, clip, before, after, conv_first, conv_second, patch_weight
+    )
+    got = send(other, cores)
+    cut = 256 + 5 * SLOT
+    block = jnp.concatenate([keep, weight[: 5 * SLOT], got, weight[5 * SLOT :]], axis=0)
+    ahead, behind = block, block
+    accs, blocks = [], [block]
+    for step in range(1, 4):
+        ahead_next = send(ahead, forward)
+        behind_next = send(behind, backward)
+        if step == 1:
+            queries, acc = own_attention(window_lengths, block, folded, query_rows, key_rows)
+        else:
+            acc = step_attention(step - 1, window_lengths, ahead, behind, folded, key_rows, queries)
+        accs.append(acc)
+        ahead, behind = ahead_next, behind_next
+        blocks += [ahead, behind]
+    ahead_last = send(ahead[:cut], forward)
+    behind_last = send(behind[cut:], backward)
+    accs.append(step_attention(3, window_lengths, ahead, behind, folded, key_rows, queries))
+    accs.append(step_attention(4, window_lengths, ahead_last, behind_last, folded, key_rows, queries))
+    blocks += [ahead_last, behind_last]
+    sibling = [send(array, cores) for array in blocks]
+    keep_rows, send_rows = project_out(accs, blocks + sibling)
+    return merge(window_lengths, keep_rows, send(send_rows, cores))
+
+
 def solution(mesh):
+    own = mesh.shape["seq"] == HEADS
     return jax.shard_map(
-        shards,
+        shards if own else general_shards,
         mesh=mesh,
         in_specs=(
             P("groups", "seq", None, None),

time: 111 us -> 89.6 us (0.81)
  Pallas kernels: 0 us -> 36.3 us
  matrix products: 22.1 us -> 0 us
  blocking collectives: 19.3 us -> 0 us
  between operations: 13.8 us -> 0.28 us
  starting transfers between devices: 12.9 us -> 18.3 us
  other arithmetic: 4.9 us -> 0.02 us
  local copies, waits for them, and re-layouts: 12.7 us -> 9.49 us
    pallas_call x0 -> x9, Pallas kernels: none -> 36.3 us  [the longest x4 18.6 us: step_attention(): pl.pallas_call(functools.partial(step_kernel, step), out_shape=ACC, in_sp...]
    ppermute x2 -> x21, waiting for transfers between devices: 3.1 us -> 24.9 us  [send(): return lax.ppermute(array, 'seq', pairs)]
    all_to_all x1 -> x0, waiting for transfers between devices: 21.6 us -> none  [shards(): lax.all_to_all(outgoing, 'seq', split_axis=0, concat_axis=0, tiled=True)]
    all_to_all x1 -> x0, blocking collectives: 19.3 us -> none  [shards(): lax.all_to_all(outgoing_back, 'seq', split_axis=0, concat_axis=0, tiled=T...]
    dot_general x11 -> x0, matrix products: 17.2 us -> none  [the longest x1 6.5 us: shards(): jnp.dot(normed, qkv_weight, preferred_element_type=jnp.float32)]
    ppermute x2 -> x21, starting transfers between devices: 3.66 us -> 18.3 us  [send(): return lax.ppermute(array, 'seq', pairs)]
    all_to_all x1 -> x0, starting transfers between devices: 8.97 us -> none  [shards(): lax.all_to_all(outgoing, 'seq', split_axis=0, concat_axis=0, tiled=True)]
    unnamed x17 -> x24, local copies, waits for them, and re-layouts: 1.89 us -> 9.1 us
  transfers between devices with their start and end apart: 4 -> 21, of which waited for: 2 -> 7; matrix products, arithmetic and copies ran while one was open for 19% -> 0% of each run, Pallas kernels for 0% -> 34%
where the time goes in v1:
time: 89.6 us; the launch traced here: 89.3 us
  Pallas kernels  36.3 us (41%)
  waiting for transfers between devices  24.9 us (28%)
  starting transfers between devices  18.3 us (20%)
  local copies, waits for them, and re-layouts  9.49 us (11%)
    ppermute x21, waiting for transfers between devices, send(): return lax.ppermute(array, 'seq', pairs)  24.9 us
    pallas_call x4, Pallas kernels, step_attention(): pl.pallas_call(functools.partial(step_kernel, step), out_shape=ACC, in_sp...  18.6 us
    ppermute x21, starting transfers between devices, send(): return lax.ppermute(array, 'seq', pairs)  18.3 us
    unnamed x24, local copies, waits for them, and re-layouts  9.1 us
    pallas_call x1, Pallas kernels, fold(): pl.pallas_call(fold_kernel, grid=(3,), out_shape=jax.ShapeDtypeStruct((3...  6.87 us
    pallas_call x1, Pallas kernels, own_attention(): pl.pallas_call(own_kernel, out_shape=(jax.ShapeDtypeStruct((HEADS, SLOT,...  4.52 us
    pallas_call x1, Pallas kernels, convolve(): pl.pallas_call(conv_kernel, out_shape=(out, out), in_specs=[SMEM, SMEM] +...  3.95 us
  transfers between devices with their start and end apart: 21, of which 7 were waited for; matrix products, arithmetic and copies ran while one was open for 0% of the time, Pallas kernels for 34%

profile of v1, /device:TPU:0, one launch (start us, length us, event | category | flops | bytes accessed | tf_op | source)
XLA Modules:
  0.0 89.3 jit_solution(9990882802453375235)
XLA Ops:
  0.0 2.4 %collective-permute-start = (bf16[8,2,32,128]{3,2,1,0:T(8,128)(2,1)}, bf16[8,2,32,128]{3,2,1,0:T(8,128)(2,1)S(1)}, u32[]{:S(2)}, u32[]{:S(2)}) collective-permute-start(bf16[8,2,32,128]{3,2,1,0:T(8,128)(2,1)} %own_ref.1), channel_id=1, source_target_pairs={{0,1},{1,2},{2,3},{3,4},{4,5},{5,6},{6,7},{7,8},{8,9},{9,10},{10,1... | collective-permute-start | bytes 393224 | tf_op jit(solution)/shard_map/ppermute | solution.py:625
  2.4 1.3 %collective-permute-start.1 = (bf16[8,2,32,128]{3,2,1,0:T(8,128)(2,1)}, bf16[8,2,32,128]{3,2,1,0:T(8,128)(2,1)S(1)}, u32[]{:S(2)}, u32[]{:S(2)}) collective-permute-start(bf16[8,2,32,128]{3,2,1,0:T(8,128)(2,1)} %own_ref.1), channel_id=1, source_target_pairs={{1,0},{2,1},{3,2},{4,3},{5,4},{6,5},{7,6},{8,7},{9,8},{10,9},{11,1... | collective-permute-start | bytes 393224 | tf_op jit(solution)/shard_map/ppermute | solution.py:625
  3.7 4.3 %collective-permute-done.1.after_ref = bf16[8,2,32,128]{3,2,1,0:T(8,128)(2,1)S(1)} collective-permute-done((bf16[8,2,32,128]{3,2,1,0:T(8,128)(2,1)}, bf16[8,2,32,128]{3,2,1,0:T(8,128)(2,1)S(1)}, u32[]{:S(2)}, u32[]{:S(2)}) %collective-permute-start.1) | collective-permute-done | bytes 131104 | tf_op jit(solution)/shard_map/ppermute | solution.py:625
  7.9 0.7 copy-done
  8.6 1.3 %copy-done.3 = bf16[512,1152]{1,0:T(8,128)(2,1)S(1)} copy-done((bf16[512,1152]{1,0:T(8,128)(2,1)S(1)}, bf16[512,1152]{1,0:T(8,128)(2,1)}, u32[]{:S(2)}) %copy-start.3) | copy-done | bytes 1179672
  9.9 1.2 %copy-done.5 = bf16[3,3,3,128,128]{4,3,2,1,0:T(8,128)(2,1)S(1)} copy-done((bf16[3,3,3,128,128]{4,3,2,1,0:T(8,128)(2,1)S(1)}, bf16[3,3,3,128,128]{4,3,2,1,0:T(8,128)(2,1)}, u32[]{:S(2)}) %copy-start.5) | copy-done | bytes 884760
  11.0 1.2 %copy-done.6 = bf16[3,3,3,128,128]{4,3,2,1,0:T(8,128)(2,1)S(1)} copy-done((bf16[3,3,3,128,128]{4,3,2,1,0:T(8,128)(2,1)S(1)}, bf16[3,3,3,128,128]{4,3,2,1,0:T(8,128)(2,1)}, u32[]{:S(2)}) %copy-start.6) | copy-done | bytes 884760
  12.2 0.9 %copy-done.7 = bf16[8,2,32,128]{3,2,1,0:T(8,128)(2,1)S(1)} copy-done((bf16[8,2,32,128]{3,2,1,0:T(8,128)(2,1)S(1)}, bf16[8,2,32,128]{3,2,1,0:T(8,128)(2,1)}, u32[]{:S(2)}) %copy-start.7) | copy-done | bytes 131096
  13.1 0.7 copy-done.8
  13.8 4.0 %convolve.1 = (bf16[256,128]{1,0:T(8,128)(2,1)S(1)}, bf16[256,128]{1,0:T(8,128)(2,1)S(1)}) custom-call(s32[3]{0:T(128)S(1)} %copy-done.8, s32[1,3]{1,0:T(1,128)S(1)} %copy-done, bf16[8,2,32,128]{3,2,1,0:T(8,128)(2,1)S(1)} %copy-done.7, bf16[8,2,32,128]{3,2,1,0:T(8,128)(2,1)S(1)} %collective-permute-done.before_ref, ...), custom_call_target="tpu_custom_call" | custom-call | flops 2147483648 | bytes 4194304 | tf_op jit(solution)/shard_map/convolve/pallas_call | solution.py:365
  17.7 3.6 %collective-permute-start.2 = (bf16[256,128]{1,0:T(8,128)(2,1)S(1)}, bf16[256,128]{1,0:T(8,128)(2,1)S(1)}, u32[]{:S(2)}, u32[]{:S(2)}) collective-permute-start(bf16[256,128]{1,0:T(8,128)(2,1)S(1)} %get-tuple-element.12), channel_id=1, source_target_pairs={{0,1},{1,0},{2,3},{3,2},{4,5},{5,4},{6,7},{7,6},{8,9},{9,8},{10,11... | collective-permute-start | bytes 196616 | tf_op jit(solution)/shard_map/ppermute | solution.py:625
  21.4 0.1 reshape.8
  21.5 0.1 slice.25
  21.6 0.6 collective-permute-done.2
  22.3 0.0 copy-start.1
  22.3 1.6 %collective-permute-start.3 = (bf16[1232,128]{1,0:T(8,128)(2,1)S(1)}, bf16[1232,128]{1,0:T(8,128)(2,1)S(1)}, u32[]{:S(2)}, u32[]{:S(2)}) collective-permute-start(bf16[1232,128]{1,0:T(8,128)(2,1)S(1)} %pad_maximum_fusion.block_ref.refs_5_), channel_id=1, source_target_pairs={{0,4},{1,5},{4,8},{5,9},{8,12},{9,13},{12,14},{13,15},{14,10},{15,... | collective-permute-start | bytes 946184 | tf_op jit(solution)/shard_map/ppermute | solution.py:625
  23.9 0.9 %collective-permute-start.4 = (bf16[1232,128]{1,0:T(8,128)(2,1)S(1)}, bf16[1232,128]{1,0:T(8,128)(2,1)S(1)}, u32[]{:S(2)}, u32[]{:S(2)}) collective-permute-start(bf16[1232,128]{1,0:T(8,128)(2,1)S(1)} %pad_maximum_fusion.block_ref.refs_5_), channel_id=1, source_target_pairs={{4,0},{5,1},{8,4},{9,5},{12,8},{13,9},{14,12},{15,13},{10,14},{11,... | collective-permute-start | bytes 946184 | tf_op jit(solution)/shard_map/ppermute | solution.py:625
  24.8 7.9 %collective-permute-done.3.ahead_ref.refs_6_ = bf16[1232,128]{1,0:T(8,128)(2,1)S(1)} collective-permute-done((bf16[1232,128]{1,0:T(8,128)(2,1)S(1)}, bf16[1232,128]{1,0:T(8,128)(2,1)S(1)}, u32[]{:S(2)}, u32[]{:S(2)}) %collective-permute-start.3) | collective-permute-done | bytes 315424 | tf_op jit(solution)/shard_map/ppermute | solution.py:625
  32.7 0.9 %collective-permute-start.5 = (bf16[1232,128]{1,0:T(8,128)(2,1)S(1)}, bf16[1232,128]{1,0:T(8,128)(2,1)S(1)}, u32[]{:S(2)}, u32[]{:S(2)}) collective-permute-start(bf16[1232,128]{1,0:T(8,128)(2,1)S(1)} %collective-permute-done.3.ahead_ref.refs_6_), channel_id=1, source_target_pairs={{0,4},{1,5},{4,8},{5,9},{8,12},{9,13},{12,14},{13,15},{14,10},{15,... | collective-permute-start | bytes 946184 | tf_op jit(solution)/shard_map/ppermute | solution.py:625
  33.6 0.0 collective-permute-done.4.behind_ref.refs_7_
  33.6 1.1 %collective-permute-start.6 = (bf16[1232,128]{1,0:T(8,128)(2,1)S(1)}, bf16[1232,128]{1,0:T(8,128)(2,1)S(1)}, u32[]{:S(2)}, u32[]{:S(2)}) collective-permute-start(bf16[1232,128]{1,0:T(8,128)(2,1)S(1)} %collective-permute-done.4.behind_ref.refs_7_), channel_id=1, source_target_pairs={{4,0},{5,1},{8,4},{9,5},{12,8},{13,9},{14,12},{15,13},{10,14},{11,... | collective-permute-start | bytes 946184 | tf_op jit(solution)/shard_map/ppermute | solution.py:625
  34.7 7.1 %collective-permute-done.5.ahead_ref.refs_8_ = bf16[1232,128]{1,0:T(8,128)(2,1)S(1)} collective-permute-done((bf16[1232,128]{1,0:T(8,128)(2,1)S(1)}, bf16[1232,128]{1,0:T(8,128)(2,1)S(1)}, u32[]{:S(2)}, u32[]{:S(2)}) %collective-permute-start.5) | collective-permute-done | bytes 315424 | tf_op jit(solution)/shard_map/ppermute | solution.py:625
  41.8 0.7 collective-permute-start.7
  42.5 3.3 %copy-done.2 = bf16[1152,3456]{1,0:T(8,128)(2,1)S(1)} copy-done((bf16[1152,3456]{1,0:T(8,128)(2,1)S(1)}, bf16[1152,3456]{1,0:T(8,128)(2,1)}, u32[]{:S(2)}) %copy-start.2) | copy-done | bytes 7962648
  45.8 6.9 %fold.1.folded_ref = bf16[3456,512]{1,0:T(8,128)(2,1)S(1)} custom-call(bf16[512,1152]{1,0:T(8,128)(2,1)S(1)} %copy-done.4, bf16[1152,3456]{1,0:T(8,128)(2,1)S(1)} %copy-done.2), custom_call_target="tpu_custom_call" | custom-call | flops 4076863488 | bytes 12582912 | tf_op jit(solution)/shard_map/fold/pallas_call | solution.py:226
  52.7 0.1 collective-permute-start.11
  52.7 0.5 collective-permute-start.12
  53.2 0.1 collective-permute-start.13
  53.3 0.4 collective-permute-start.14
  53.8 1.4 %collective-permute-start.8 = (bf16[1232,128]{1,0:T(8,128)(2,1)S(1)}, bf16[1232,128]{1,0:T(8,128)(2,1)S(1)}, u32[]{:S(2)}, u32[]{:S(2)}) collective-permute-start(bf16[1232,128]{1,0:T(8,128)(2,1)S(1)} %collective-permute-done.6.behind_ref.refs_9_), channel_id=1, source_target_pairs={{4,0},{5,1},{8,4},{9,5},{12,8},{13,9},{14,12},{15,13},{10,14},{11,... | collective-permute-start | bytes 946184 | tf_op jit(solution)/shard_map/ppermute | solution.py:625
  55.1 0.1 broadcast_in_dim.4.query_gain_ref
  55.2 0.1 broadcast_in_dim.5.key_gain_ref
  55.3 4.5 %own_attention.1 = (bf16[16,80,128]{2,1,0:T(8,128)(2,1)S(1)}, f32[16,80,128]{2,1,0:T(8,128)S(1)}) custom-call(s32[1,3]{1,0:T(1,128)S(1)} %copy-done.1, bf16[1232,128]{1,0:T(8,128)(2,1)S(1)} %pad_maximum_fusion.block_ref.refs_5_, bf16[3456,512]{1,0:T(8,128)(2,1)S(1)} %fold.1.folded_ref, f32[72,256]{1,0:T(8,128)S(1)} %broadcast_in_dim.4.query_gain_ref, ...), custom_call_target="tpu_custom_call" | custom-call | flops 1308622848 | bytes 5242880 | tf_op jit(solution)/shard_map/own_attention/pallas_call | solution.py:500
  59.8 3.4 %collective-permute-done.8.behind_ref.refs_11_ = bf16[1232,128]{1,0:T(8,128)(2,1)S(1)} collective-permute-done((bf16[1232,128]{1,0:T(8,128)(2,1)S(1)}, bf16[1232,128]{1,0:T(8,128)(2,1)S(1)}, u32[]{:S(2)}, u32[]{:S(2)}) %collective-permute-start.8) | collective-permute-done | bytes 315424 | tf_op jit(solution)/shard_map/ppermute | solution.py:625
  63.2 1.6 %collective-permute-start.9 = (bf16[656,128]{1,0:T(8,128)(2,1)S(1)}, bf16[656,128]{1,0:T(8,128)(2,1)S(1)}, u32[]{:S(2)}, u32[]{:S(2)}) collective-permute-start(bf16[656,128]{1,0:T(8,128)(2,1)S(1)} %slice.26), channel_id=1, source_target_pairs={{0,4},{1,5},{4,8},{5,9},{8,12},{9,13},{12,14},{13,15},{14,10},{15,... | collective-permute-start | bytes 503816 | tf_op jit(solution)/shard_map/ppermute | solution.py:625
  64.8 4.8 %step_attention.4.refs_1_ = f32[16,80,128]{2,1,0:T(8,128)S(1)} custom-call(s32[1,3]{1,0:T(1,128)S(1)} %copy-done.1, bf16[1232,128]{1,0:T(8,128)(2,1)S(1)} %collective-permute-done.3.ahead_ref.refs_6_, bf16[1232,128]{1,0:T(8,128)(2,1)S(1)} %collective-permute-done.4.behind_ref.refs_7_, bf16[3456,512]{1,0:T(8,128)(2,1)S(1)} %fold.1.folded_ref, ...), custom_call_target="tpu_custom_call" | custom-call | flops 1744830464 | bytes 5242880 | tf_op jit(solution)/shard_map/step_attention/pallas_call | solution.py:512
  69.6 0.1 collective-permute-start.15
  69.7 0.7 collective-permute-start.10
  70.4 0.5 collective-permute-start.17
  70.9 4.8 %step_attention.5.refs_2_ = f32[16,80,128]{2,1,0:T(8,128)S(1)} custom-call(s32[1,3]{1,0:T(1,128)S(1)} %copy-done.1, bf16[1232,128]{1,0:T(8,128)(2,1)S(1)} %collective-permute-done.5.ahead_ref.refs_8_, bf16[1232,128]{1,0:T(8,128)(2,1)S(1)} %collective-permute-done.6.behind_ref.refs_9_, bf16[3456,512]{1,0:T(8,128)(2,1)S(1)} %fold.1.folded_ref, ...), custom_call_target="tpu_custom_call" | custom-call | flops 1744830464 | bytes 5242880 | tf_op jit(solution)/shard_map/step_attention/pallas_call | solution.py:512
  75.7 0.2 collective-permute-done.10.behind_ref.refs_13_
  75.9 0.5 collective-permute-start.18
  76.5 4.8 %step_attention.6.refs_3_ = f32[16,80,128]{2,1,0:T(8,128)S(1)} custom-call(s32[1,3]{1,0:T(1,128)S(1)} %copy-done.1, bf16[1232,128]{1,0:T(8,128)(2,1)S(1)} %collective-permute-done.7.ahead_ref.refs_10_, bf16[1232,128]{1,0:T(8,128)(2,1)S(1)} %collective-permute-done.8.behind_ref.refs_11_, bf16[3456,512]{1,0:T(8,128)(2,1)S(1)} %fold.1.folded_ref, ...), custom_call_target="tpu_custom_call" | custom-call | flops 1744830464 | bytes 5242880 | tf_op jit(solution)/shard_map/step_attention/pallas_call | solution.py:512
  81.3 4.2 %step_attention.7.refs_4_ = f32[16,80,128]{2,1,0:T(8,128)S(1)} custom-call(s32[1,3]{1,0:T(1,128)S(1)} %copy-done.1, bf16[656,128]{1,0:T(8,128)(2,1)S(1)} %collective-permute-done.9.ahead_ref.refs_12_, bf16[576,128]{1,0:T(8,128)(2,1)S(1)} %collective-permute-done.10.behind_ref.refs_13_, bf16[3456,512]{1,0:T(8,128)(2,1)S(1)} %fold.1.folded_ref, ...), custom_call_target="tpu_custom_call" | custom-call | flops 872415232 | bytes 5242880 | tf_op jit(solution)/shard_map/step_attention/pallas_call | solution.py:512
  85.5 1.0 %project_out.1 = (bf16[64,1152]{1,0:T(8,128)(2,1)S(1)}, bf16[64,1152]{1,0:T(8,128)(2,1)S(1)}) custom-call(f32[16,80,128]{2,1,0:T(8,128)S(1)} %get-tuple-element.13.refs_0_, f32[16,80,128]{2,1,0:T(8,128)S(1)} %step_attention.4.refs_1_, f32[16,80,128]{2,1,0:T(8,128)S(1)} %step_attention.5.refs_2_, f32[16,80,128]{2,1,0:T(8,128)S(1)} %step_attention.6.refs_3_, ...), custom_call_target="tpu_custom_call" | custom-call | flops 377487360 | bytes 4194304 | tf_op jit(solution)/shard_map/project_out/pallas_call | solution.py:570
  86.5 0.1 collective-permute-start.20
  86.6 1.4 %collective-permute-done.20.got_ref = bf16[64,1152]{1,0:T(8,128)(2,1)S(1)} collective-permute-done((bf16[64,1152]{1,0:T(8,128)(2,1)S(1)}, bf16[64,1152]{1,0:T(8,128)(2,1)S(1)}, u32[]{:S(2)}, u32[]{:S(2)}) %collective-permute-start.20) | collective-permute-done | bytes 147488 | tf_op jit(solution)/shard_map/ppermute | solution.py:625
  88.0 1.3 %merge.1 = bf16[128,1152]{1,0:T(8,128)(2,1)} custom-call(s32[1,3]{1,0:T(1,128)S(1)} %copy-done.1, bf16[64,1152]{1,0:T(8,128)(2,1)S(1)} %get-tuple-element.15.keep_ref, bf16[64,1152]{1,0:T(8,128)(2,1)S(1)} %collective-permute-done.20.got_ref), custom_call_target="tpu_custom_call" | custom-call | tf_op jit(solution)/shard_map/merge/pallas_call | solution.py:598
  (39 shorter events, 0.2 us)
Async XLA Ops:
  0.0 3.7 %collective-permute-start = (bf16[8,2,32,128]{3,2,1,0:T(8,128)(2,1)}, bf16[8,2,32,128]{3,2,1,0:T(8,128)(2,1)S(1)}, u32[]{:S(2)}, u32[]{:S(2)}) collective-permute-start(bf16[8,2,32,128]{3,2,1,0:T(8,128)(2,1)} %own_ref.1), channel_id=1, source_target_pairs={{0,1},{1,2},{2,3},{3,4},{4,5},{5,6},{6,7},{7,8},{8,9},{9,10},{10,1... | collective-permute-start | bytes 393224 | tf_op jit(solution)/shard_map/ppermute | solution.py:625
  2.4 5.6 %collective-permute-start.1 = (bf16[8,2,32,128]{3,2,1,0:T(8,128)(2,1)}, bf16[8,2,32,128]{3,2,1,0:T(8,128)(2,1)S(1)}, u32[]{:S(2)}, u32[]{:S(2)}) collective-permute-start(bf16[8,2,32,128]{3,2,1,0:T(8,128)(2,1)} %own_ref.1), channel_id=1, source_target_pairs={{1,0},{2,1},{3,2},{4,3},{5,4},{6,5},{7,6},{8,7},{9,8},{10,9},{11,1... | collective-permute-start | bytes 393224 | tf_op jit(solution)/shard_map/ppermute | solution.py:625
  7.9 0.7 copy-start
  8.6 1.3 %copy-start.3 = (bf16[512,1152]{1,0:T(8,128)(2,1)S(1)}, bf16[512,1152]{1,0:T(8,128)(2,1)}, u32[]{:S(2)}) copy-start(bf16[512,1152]{1,0:T(8,128)(2,1)} %patch_ref.3) | copy-start | bytes 3538948
  9.9 1.2 %copy-start.5 = (bf16[3,3,3,128,128]{4,3,2,1,0:T(8,128)(2,1)S(1)}, bf16[3,3,3,128,128]{4,3,2,1,0:T(8,128)(2,1)}, u32[]{:S(2)}) copy-start(bf16[3,3,3,128,128]{4,3,2,1,0:T(8,128)(2,1)} %first_ref.1) | copy-start | bytes 2654212
  11.0 1.2 %copy-start.6 = (bf16[3,3,3,128,128]{4,3,2,1,0:T(8,128)(2,1)S(1)}, bf16[3,3,3,128,128]{4,3,2,1,0:T(8,128)(2,1)}, u32[]{:S(2)}) copy-start(bf16[3,3,3,128,128]{4,3,2,1,0:T(8,128)(2,1)} %second_ref.1) | copy-start | bytes 2654212
  12.2 0.9 %copy-start.7 = (bf16[8,2,32,128]{3,2,1,0:T(8,128)(2,1)S(1)}, bf16[8,2,32,128]{3,2,1,0:T(8,128)(2,1)}, u32[]{:S(2)}) copy-start(bf16[8,2,32,128]{3,2,1,0:T(8,128)(2,1)} %own_ref.1) | copy-start | bytes 393220
  13.1 0.7 copy-start.8
  13.8 7.6 %copy-start.9 = (bf16[72,1152]{1,0:T(8,128)(2,1)S(1)}, bf16[72,1152]{1,0:T(8,128)(2,1)}, u32[]{:S(2)}) copy-start(bf16[72,1152]{1,0:T(8,128)(2,1)} %param.18) | copy-start | bytes 497668
  13.8 28.8 %copy-start.4 = (bf16[512,1152]{1,0:T(8,128)(2,1)S(1)}, bf16[512,1152]{1,0:T(8,128)(2,1)}, u32[]{:S(2)}) copy-start(bf16[512,1152]{1,0:T(8,128)(2,1)} %patch_ref.3) | copy-start | bytes 3538948
  17.7 4.5 %collective-permute-start.2 = (bf16[256,128]{1,0:T(8,128)(2,1)S(1)}, bf16[256,128]{1,0:T(8,128)(2,1)S(1)}, u32[]{:S(2)}, u32[]{:S(2)}) collective-permute-start(bf16[256,128]{1,0:T(8,128)(2,1)S(1)} %get-tuple-element.12), channel_id=1, source_target_pairs={{0,1},{1,0},{2,3},{3,2},{4,5},{5,4},{6,7},{7,6},{8,9},{9,8},{10,11... | collective-permute-start | bytes 196616 | tf_op jit(solution)/shard_map/ppermute | solution.py:625
  22.2 32.9 %copy-start.11 = (f32[72]{0:T(128)S(1)}, f32[72]{0:T(128)}, u32[]{:S(2)}) copy-start(f32[72]{0:T(128)} %param.16) | copy-start | bytes 868
  22.2 33.0 %copy-start.10 = (f32[72]{0:T(128)S(1)}, f32[72]{0:T(128)}, u32[]{:S(2)}) copy-start(f32[72]{0:T(128)} %param.17) | copy-start | bytes 868
  22.3 33.0 %copy-start.1 = (s32[1,3]{1,0:T(1,128)S(1)}, s32[1,3]{1,0:T(1,128)}, u32[]{:S(2)}) copy-start(s32[1,3]{1,0:T(1,128)} %lengths_ref.13) | copy-start | bytes 40
  22.3 10.4 %collective-permute-start.3 = (bf16[1232,128]{1,0:T(8,128)(2,1)S(1)}, bf16[1232,128]{1,0:T(8,128)(2,1)S(1)}, u32[]{:S(2)}, u32[]{:S(2)}) collective-permute-start(bf16[1232,128]{1,0:T(8,128)(2,1)S(1)} %pad_maximum_fusion.block_ref.refs_5_), channel_id=1, source_target_pairs={{0,4},{1,5},{4,8},{5,9},{8,12},{9,13},{12,14},{13,15},{14,10},{15,... | collective-permute-start | bytes 946184 | tf_op jit(solution)/shard_map/ppermute | solution.py:625
  23.9 9.7 %collective-permute-start.4 = (bf16[1232,128]{1,0:T(8,128)(2,1)S(1)}, bf16[1232,128]{1,0:T(8,128)(2,1)S(1)}, u32[]{:S(2)}, u32[]{:S(2)}) collective-permute-start(bf16[1232,128]{1,0:T(8,128)(2,1)S(1)} %pad_maximum_fusion.block_ref.refs_5_), channel_id=1, source_target_pairs={{4,0},{5,1},{8,4},{9,5},{12,8},{13,9},{14,12},{15,13},{10,14},{11,... | collective-permute-start | bytes 946184 | tf_op jit(solution)/shard_map/ppermute | solution.py:625
  32.7 9.1 %collective-permute-start.5 = (bf16[1232,128]{1,0:T(8,128)(2,1)S(1)}, bf16[1232,128]{1,0:T(8,128)(2,1)S(1)}, u32[]{:S(2)}, u32[]{:S(2)}) collective-permute-start(bf16[1232,128]{1,0:T(8,128)(2,1)S(1)} %collective-permute-done.3.ahead_ref.refs_6_), channel_id=1, source_target_pairs={{0,4},{1,5},{4,8},{5,9},{8,12},{9,13},{12,14},{13,15},{14,10},{15,... | collective-permute-start | bytes 946184 | tf_op jit(solution)/shard_map/ppermute | solution.py:625
  33.6 19.7 %collective-permute-start.6 = (bf16[1232,128]{1,0:T(8,128)(2,1)S(1)}, bf16[1232,128]{1,0:T(8,128)(2,1)S(1)}, u32[]{:S(2)}, u32[]{:S(2)}) collective-permute-start(bf16[1232,128]{1,0:T(8,128)(2,1)S(1)} %collective-permute-done.4.behind_ref.refs_7_), channel_id=1, source_target_pairs={{4,0},{5,1},{8,4},{9,5},{12,8},{13,9},{14,12},{15,13},{10,14},{11,... | collective-permute-start | bytes 946184 | tf_op jit(solution)/shard_map/ppermute | solution.py:625
  41.8 11.9 %collective-permute-start.7 = (bf16[1232,128]{1,0:T(8,128)(2,1)S(1)}, bf16[1232,128]{1,0:T(8,128)(2,1)S(1)}, u32[]{:S(2)}, u32[]{:S(2)}) collective-permute-start(bf16[1232,128]{1,0:T(8,128)(2,1)S(1)} %collective-permute-done.5.ahead_ref.refs_8_), channel_id=1, source_target_pairs={{0,4},{1,5},{4,8},{5,9},{8,12},{9,13},{12,14},{13,15},{14,10},{15,... | collective-permute-start | bytes 946184 | tf_op jit(solution)/shard_map/ppermute | solution.py:625
  42.5 3.3 %copy-start.2 = (bf16[1152,3456]{1,0:T(8,128)(2,1)S(1)}, bf16[1152,3456]{1,0:T(8,128)(2,1)}, u32[]{:S(2)}) copy-start(bf16[1152,3456]{1,0:T(8,128)(2,1)} %qkv_ref.1) | copy-start | bytes 23887876
  52.7 16.9 %collective-permute-start.11 = (bf16[1232,128]{1,0:T(8,128)(2,1)S(1)}, bf16[1232,128]{1,0:T(8,128)(2,1)S(1)}, u32[]{:S(2)}, u32[]{:S(2)}) collective-permute-start(bf16[1232,128]{1,0:T(8,128)(2,1)S(1)} %pad_maximum_fusion.block_ref.refs_5_), channel_id=1, source_target_pairs={{0,1},{1,0},{2,3},{3,2},{4,5},{5,4},{6,7},{7,6},{8,9},{9,8},{10,11... | collective-permute-start | bytes 946184 | tf_op jit(solution)/shard_map/ppermute | solution.py:625
  52.7 16.9 %collective-permute-start.12 = (bf16[1232,128]{1,0:T(8,128)(2,1)S(1)}, bf16[1232,128]{1,0:T(8,128)(2,1)S(1)}, u32[]{:S(2)}, u32[]{:S(2)}) collective-permute-start(bf16[1232,128]{1,0:T(8,128)(2,1)S(1)} %collective-permute-done.3.ahead_ref.refs_6_), channel_id=1, source_target_pairs={{0,1},{1,0},{2,3},{3,2},{4,5},{5,4},{6,7},{7,6},{8,9},{9,8},{10,11... | collective-permute-start | bytes 946184 | tf_op jit(solution)/shard_map/ppermute | solution.py:625
  53.2 17.1 %collective-permute-start.13 = (bf16[1232,128]{1,0:T(8,128)(2,1)S(1)}, bf16[1232,128]{1,0:T(8,128)(2,1)S(1)}, u32[]{:S(2)}, u32[]{:S(2)}) collective-permute-start(bf16[1232,128]{1,0:T(8,128)(2,1)S(1)} %collective-permute-done.4.behind_ref.refs_7_), channel_id=1, source_target_pairs={{0,1},{1,0},{2,3},{3,2},{4,5},{5,4},{6,7},{7,6},{8,9},{9,8},{10,11... | collective-permute-start | bytes 946184 | tf_op jit(solution)/shard_map/ppermute | solution.py:625
  53.3 17.1 %collective-permute-start.14 = (bf16[1232,128]{1,0:T(8,128)(2,1)S(1)}, bf16[1232,128]{1,0:T(8,128)(2,1)S(1)}, u32[]{:S(2)}, u32[]{:S(2)}) collective-permute-start(bf16[1232,128]{1,0:T(8,128)(2,1)S(1)} %collective-permute-done.5.ahead_ref.refs_8_), channel_id=1, source_target_pairs={{0,1},{1,0},{2,3},{3,2},{4,5},{5,4},{6,7},{7,6},{8,9},{9,8},{10,11... | collective-permute-start | bytes 946184 | tf_op jit(solution)/shard_map/ppermute | solution.py:625
  53.8 9.4 %collective-permute-start.8 = (bf16[1232,128]{1,0:T(8,128)(2,1)S(1)}, bf16[1232,128]{1,0:T(8,128)(2,1)S(1)}, u32[]{:S(2)}, u32[]{:S(2)}) collective-permute-start(bf16[1232,128]{1,0:T(8,128)(2,1)S(1)} %collective-permute-done.6.behind_ref.refs_9_), channel_id=1, source_target_pairs={{4,0},{5,1},{8,4},{9,5},{12,8},{13,9},{14,12},{15,13},{10,14},{11,... | collective-permute-start | bytes 946184 | tf_op jit(solution)/shard_map/ppermute | solution.py:625
  63.2 12.8 %collective-permute-start.9 = (bf16[656,128]{1,0:T(8,128)(2,1)S(1)}, bf16[656,128]{1,0:T(8,128)(2,1)S(1)}, u32[]{:S(2)}, u32[]{:S(2)}) collective-permute-start(bf16[656,128]{1,0:T(8,128)(2,1)S(1)} %slice.26), channel_id=1, source_target_pairs={{0,4},{1,5},{4,8},{5,9},{8,12},{9,13},{12,14},{13,15},{14,10},{15,... | collective-permute-start | bytes 503816 | tf_op jit(solution)/shard_map/ppermute | solution.py:625
  69.6 15.9 %collective-permute-start.15 = (bf16[1232,128]{1,0:T(8,128)(2,1)S(1)}, bf16[1232,128]{1,0:T(8,128)(2,1)S(1)}, u32[]{:S(2)}, u32[]{:S(2)}) collective-permute-start(bf16[1232,128]{1,0:T(8,128)(2,1)S(1)} %collective-permute-done.6.behind_ref.refs_9_), channel_id=1, source_target_pairs={{0,1},{1,0},{2,3},{3,2},{4,5},{5,4},{6,7},{7,6},{8,9},{9,8},{10,11... | collective-permute-start | bytes 946184 | tf_op jit(solution)/shard_map/ppermute | solution.py:625
  69.7 6.2 %collective-permute-start.10 = (bf16[576,128]{1,0:T(8,128)(2,1)S(1)}, bf16[576,128]{1,0:T(8,128)(2,1)S(1)}, u32[]{:S(2)}, u32[]{:S(2)}) collective-permute-start(bf16[576,128]{1,0:T(8,128)(2,1)S(1)} %slice.27), channel_id=1, source_target_pairs={{4,0},{5,1},{8,4},{9,5},{12,8},{13,9},{14,12},{15,13},{10,14},{11,... | collective-permute-start | bytes 442376 | tf_op jit(solution)/shard_map/ppermute | solution.py:625
  70.4 15.1 %collective-permute-start.16 = (bf16[1232,128]{1,0:T(8,128)(2,1)S(1)}, bf16[1232,128]{1,0:T(8,128)(2,1)S(1)}, u32[]{:S(2)}, u32[]{:S(2)}) collective-permute-start(bf16[1232,128]{1,0:T(8,128)(2,1)S(1)} %collective-permute-done.7.ahead_ref.refs_10_), channel_id=1, source_target_pairs={{0,1},{1,0},{2,3},{3,2},{4,5},{5,4},{6,7},{7,6},{8,9},{9,8},{10,11... | collective-permute-start | bytes 946184 | tf_op jit(solution)/shard_map/ppermute | solution.py:625
  70.4 15.1 %collective-permute-start.17 = (bf16[1232,128]{1,0:T(8,128)(2,1)S(1)}, bf16[1232,128]{1,0:T(8,128)(2,1)S(1)}, u32[]{:S(2)}, u32[]{:S(2)}) collective-permute-start(bf16[1232,128]{1,0:T(8,128)(2,1)S(1)} %collective-permute-done.8.behind_ref.refs_11_), channel_id=1, source_target_pairs={{0,1},{1,0},{2,3},{3,2},{4,5},{5,4},{6,7},{7,6},{8,9},{9,8},{10,11... | collective-permute-start | bytes 946184 | tf_op jit(solution)/shard_map/ppermute | solution.py:625
  75.9 9.5 %collective-permute-start.19 = (bf16[576,128]{1,0:T(8,128)(2,1)S(1)}, bf16[576,128]{1,0:T(8,128)(2,1)S(1)}, u32[]{:S(2)}, u32[]{:S(2)}) collective-permute-start(bf16[576,128]{1,0:T(8,128)(2,1)S(1)} %collective-permute-done.10.behind_ref.refs_13_), channel_id=1, source_target_pairs={{0,1},{1,0},{2,3},{3,2},{4,5},{5,4},{6,7},{7,6},{8,9},{9,8},{10,11... | collective-permute-start | bytes 442376 | tf_op jit(solution)/shard_map/ppermute | solution.py:625
  75.9 9.6 %collective-permute-start.18 = (bf16[656,128]{1,0:T(8,128)(2,1)S(1)}, bf16[656,128]{1,0:T(8,128)(2,1)S(1)}, u32[]{:S(2)}, u32[]{:S(2)}) collective-permute-start(bf16[656,128]{1,0:T(8,128)(2,1)S(1)} %collective-permute-done.9.ahead_ref.refs_12_), channel_id=1, source_target_pairs={{0,1},{1,0},{2,3},{3,2},{4,5},{5,4},{6,7},{7,6},{8,9},{9,8},{10,11... | collective-permute-start | bytes 503816 | tf_op jit(solution)/shard_map/ppermute | solution.py:625
  86.5 1.4 %collective-permute-start.20 = (bf16[64,1152]{1,0:T(8,128)(2,1)S(1)}, bf16[64,1152]{1,0:T(8,128)(2,1)S(1)}, u32[]{:S(2)}, u32[]{:S(2)}) collective-permute-start(bf16[64,1152]{1,0:T(8,128)(2,1)S(1)} %get-tuple-element.16), channel_id=1, source_target_pairs={{0,1},{1,0},{2,3},{3,2},{4,5},{5,4},{6,7},{7,6},{8,9},{9,8},{10,11... | collective-permute-start | bytes 442376 | tf_op jit(solution)/shard_map/ppermute | solution.py:625

commit v2 on v1

--- a/solution.py
+++ b/solution.py
@@ -214,28 +214,82 @@
     return start, bound
 
 
-def fold_kernel(patch_ref, qkv_ref, folded_ref):
+ANY = pl.BlockSpec(memory_space=pl.ANY)
+TN = (((0,), (1,)), ((), ()))
+
+
+def pair_weights(weights, pairs, ch=128):
+    for o in range(3):
+        for four in range(4):
+            for out_row in range(2):
+                columns = slice(out_row * ch, (out_row + 1) * ch)
+                tap = four - out_row
+                for j in range(3):
+                    rows = slice((four * 3 + j) * ch, (four * 3 + j + 1) * ch)
+                    if 0 <= tap < 3:
+                        pairs[o, rows, columns] = weights[o, tap, j]
+                    else:
+                        pairs[o, rows, columns] = jnp.zeros((ch, ch), BF16)
+
+
+def prepare_kernel(
+    patch_any, qkv_any, first_any, second_any, folded_ref, pairs_one, pairs_two, patch_ref,
+    qkv_ref, first_ref, second_ref, sems,
+):
+    copies = [
+        pltpu.make_async_copy(patch_any, patch_ref, sems.at[0]),
+        pltpu.make_async_copy(qkv_any.at[:, pl.ds(0, D)], qkv_ref.at[0], sems.at[1]),
+        pltpu.make_async_copy(first_any, first_ref, sems.at[2]),
+        pltpu.make_async_copy(second_any, second_ref, sems.at[3]),
+        pltpu.make_async_copy(qkv_any.at[:, pl.ds(D, D)], qkv_ref.at[1], sems.at[4]),
+        pltpu.make_async_copy(qkv_any.at[:, pl.ds(2 * D, D)], qkv_ref.at[2], sems.at[5]),
+    ]
+    for copy in copies:
+        copy.start()
+    copies[0].wait()
     patch = patch_ref[...].astype(F32)
     centered = (patch - jnp.mean(patch, axis=1, keepdims=True)).astype(BF16)
-    product = jnp.dot(centered, qkv_ref[...], preferred_element_type=F32)
-    folded_ref[...] = product.T.astype(BF16)
-
-
-def fold(patch_weight, qkv_weight):
+
+    def fold(part):
+        product = lax.dot_general(qkv_ref[part], centered, TN, preferred_element_type=F32)
+        folded_ref[part * D : (part + 1) * D] = product.astype(BF16)
+
+    copies[1].wait()
+    copies[2].wait()
+    fold(0)
+    pair_weights(first_ref, pairs_one)
+    copies[3].wait()
+    copies[4].wait()
+    fold(1)
+    pair_weights(second_ref, pairs_two)
+    copies[5].wait()
+    fold(2)
+
+
+def prepare(patch_weight, qkv_weight, conv_first, conv_second):
     inner = patch_weight.shape[0]
+    ch = conv_first.shape[-1]
+    pairs = jax.ShapeDtypeStruct((3, 12 * ch, 2 * ch), BF16)
     return pl.pallas_call(
-        fold_kernel,
-        grid=(3,),
-        out_shape=jax.ShapeDtypeStruct((3 * D, inner), BF16),
-        in_specs=[
-            pl.BlockSpec((inner, D), lambda i: (0, 0)),
-            pl.BlockSpec((D, D), lambda i: (0, i)),
+        prepare_kernel,
+        out_shape=(
+            jax.ShapeDtypeStruct((3 * D, inner), BF16),
+            pairs,
+            pairs,
+            jax.ShapeDtypeStruct(patch_weight.shape, BF16),
+        ),
+        in_specs=[ANY] * 4,
+        out_specs=(VMEM,) * 4,
+        scratch_shapes=[
+            pltpu.VMEM((3, D, D), BF16),
+            pltpu.VMEM(conv_first.shape, BF16),
+            pltpu.VMEM(conv_first.shape, BF16),
+            pltpu.SemaphoreType.DMA((6,)),
         ],
-        out_specs=pl.BlockSpec((D, inner), lambda i: (i, 0)),
         compiler_params=params(),
-        name="fold",
+        name="prepare",
         cost_estimate=pl.CostEstimate(flops=2 * inner * D * 3 * D, bytes_accessed=12 << 20, transcendentals=0),
-    )(patch_weight, qkv_weight)
+    )(patch_weight, qkv_weight, conv_first, conv_second)
 
 
 def frame_taps(counts_ref, frames):
@@ -253,25 +307,19 @@
 
 
 def conv_kernel(
-    counts_ref, lengths_ref, own_ref, before_ref, after_ref, first_ref, second_ref, patch_ref,
-    keep_ref, send_ref, grid_one, grid_two, pairs_one, pairs_two, pixels,
+    counts_any, lengths_any, own_any, before_ref, after_ref, pairs_one, pairs_two, patch_ref,
+    keep_ref, send_ref, grid_one, grid_two, pixels, own_ref, counts_ref, lengths_ref, sems,
 ):
+    copies = [
+        pltpu.make_async_copy(own_any, own_ref, sems.at[0]),
+        pltpu.make_async_copy(counts_any, counts_ref, sems.at[1]),
+        pltpu.make_async_copy(lengths_any, lengths_ref, sems.at[2]),
+    ]
+    for copy in copies:
+        copy.start()
     frames, _, cols, ch = own_ref.shape
     wide = 12 * ch
     position = lax.axis_index("seq")
-    before_tap, after_tap = frame_taps(counts_ref, frames)
-    for weights, pairs in ((first_ref, pairs_one), (second_ref, pairs_two)):
-        for o in range(3):
-            for four in range(4):
-                for out_row in range(2):
-                    for j in range(3):
-                        rows = pl.ds((four * 3 + j) * ch, ch)
-                        columns = pl.ds(out_row * ch, ch)
-                        tap = four - out_row
-                        if 0 <= tap < 3:
-                            pairs[o, rows, columns] = weights[o, tap, j]
-                        else:
-                            pairs[o, rows, columns] = jnp.zeros((ch, ch), BF16)
     column = lax.broadcasted_iota(jnp.int32, (frames, cols, ch), 1)
 
     def shifted(row):
@@ -286,7 +334,9 @@
     grid_two[0] = blank
     grid_two[frames + 1] = blank
     sources = [before_ref, before_ref, own_ref, own_ref, after_ref, after_ref]
-    for r in range(6):
+    for r in (0, 1, 4, 5, 2, 3):
+        if r == 2:
+            copies[0].wait()
         row = silu(sources[r][:, r % 2].astype(F32))
         parts = shifted(row)
         for g in range(2):
@@ -294,6 +344,10 @@
             if 0 <= four < 4:
                 for j in range(3):
                     grid_one[g, 1 : frames + 1, :, (four * 3 + j) * ch : (four * 3 + j + 1) * ch] = parts[j]
+
+    copies[1].wait()
+    copies[2].wait()
+    before_tap, after_tap = frame_taps(counts_ref, frames)
 
     def summed(terms):
         rows = []
@@ -358,26 +412,28 @@
         send_ref[tile * half : (tile + 1) * half] = send[:, tile * ch : (tile + 1) * ch]
 
 
-def convolve(counts, lengths, clip, before, after, conv_first, conv_second, patch_weight):
+def convolve(counts, lengths, clip, before, after, pairs_one, pairs_two, patch_weight):
     frames, _, cols, ch = clip.shape
     tokens = frames * cols // 2
     out = jax.ShapeDtypeStruct((2 * tokens, ch), BF16)
     return pl.pallas_call(
         conv_kernel,
         out_shape=(out, out),
-        in_specs=[SMEM, SMEM] + [VMEM] * 6,
+        in_specs=[ANY] * 3 + [VMEM] * 5,
         out_specs=(VMEM, VMEM),
         scratch_shapes=[
             pltpu.VMEM((2, frames + 2, cols, 12 * ch), BF16),
             pltpu.VMEM((frames + 2, cols, 12 * ch), BF16),
-            pltpu.VMEM((3, 12 * ch, 2 * ch), BF16),
-            pltpu.VMEM((3, 12 * ch, 2 * ch), BF16),
             pltpu.VMEM((2, frames * cols, ch), F32),
+            pltpu.VMEM(clip.shape, BF16),
+            pltpu.SMEM(counts.shape, jnp.int32),
+            pltpu.SMEM(lengths.shape, jnp.int32),
+            pltpu.SemaphoreType.DMA((3,)),
         ],
         compiler_params=params(),
         name="convolve",
         cost_estimate=pl.CostEstimate(flops=2 << 30, bytes_accessed=4 << 20, transcendentals=1 << 18),
-    )(counts, lengths, clip, before, after, conv_first, conv_second, patch_weight)
+    )(counts, lengths, clip, before, after, pairs_one, pairs_two, patch_weight)
 
 
 def chip_at(place):
@@ -433,32 +489,55 @@
 
 def normed_heads(part, gain):
     count = part.shape[1]
-    heads = part.reshape(HEADS, HD, count)
+    heads = part.reshape(-1, HD, count)
     factor = lax.rsqrt(jnp.mean(heads * heads, axis=1, keepdims=True) + 1e-06)
     return heads * factor * gain[None, :, :count]
 
 
-def attend(tokens, sides, folded, key_gain, queries, acc_ref):
+def attend(tokens, sides, folded, key_gain, queries, acc_ref, keys_ref, values_ref, scores_ref, weights_ref):
     count = tokens.shape[0]
-    both = lax.dot_general(folded, tokens, NT, preferred_element_type=F32)
-    keys = normed_heads(both[:D], key_gain)
-    values = both[D:].reshape(HEADS, HD, count)
     row = lax.broadcasted_iota(jnp.int32, (8, count), 0)
     key_tail = jnp.where(row == 0, sides, jnp.where(row == 1, 1.0, 0.0))
     value_tail = jnp.where(row == 0, 1.0, 0.0)
+    heads_at_once = 4
+    for first in range(0, HEADS, heads_at_once):
+        rows = slice(first * HD, (first + heads_at_once) * HD)
+        part = lax.dot_general(folded[rows], tokens, NT, preferred_element_type=F32)
+        keys = normed_heads(part, key_gain)
+        for h in range(heads_at_once):
+            keys_ref[first + h] = jnp.concatenate([keys[h], key_tail], axis=0).astype(BF16)
+            scores_ref[first + h] = jnp.dot(queries[first + h], keys_ref[first + h], preferred_element_type=F32)
+    for first in range(0, HEADS, heads_at_once):
+        rows = slice(D + first * HD, D + (first + heads_at_once) * HD)
+        part = lax.dot_general(folded[rows], tokens, NT, preferred_element_type=F32)
+        values = part.reshape(heads_at_once, HD, count)
+        for h in range(heads_at_once):
+            values_ref[first + h] = jnp.concatenate([values[h], value_tail], axis=0).astype(BF16)
+    lane = lax.broadcasted_iota(jnp.int32, (128, 128), 1)
+    peaks = jnp.zeros((128, 128), F32)
+    for h in range(HEADS):
+        scores = scores_ref[h]
+        peak = jnp.max(scores, axis=1, keepdims=True)
+        weights_ref[h] = jnp.exp2(scores - peak).astype(BF16)
+        peaks = jnp.where(lane == h, peak, peaks)
+    peaks = peaks.T
     tail_row = lax.broadcasted_iota(jnp.int32, (8, 128), 0)
     for h in range(HEADS):
-        key = jnp.concatenate([keys[h], key_tail], axis=0).T.astype(BF16)
-        value = jnp.concatenate([values[h], value_tail], axis=0).astype(BF16)
-        scores = jnp.dot(key, queries[h], preferred_element_type=F32)
-        peak = jnp.max(scores, axis=0, keepdims=True)
-        weights = jnp.exp2(scores - peak).astype(BF16)
-        mixed = jnp.dot(value, weights, preferred_element_type=F32)
+        mixed = lax.dot_general(values_ref[h], weights_ref[h], NT, preferred_element_type=F32)
         acc_ref[h, :HD] = mixed[:HD]
-        acc_ref[h, HD:] = jnp.where(tail_row == 1, peak, mixed[HD:])
-
-
-def own_kernel(lengths_ref, block_ref, folded_ref, query_gain_ref, key_gain_ref, queries_ref, acc_ref):
+        acc_ref[h, HD:] = jnp.where(tail_row == 1, peaks[h : h + 1], mixed[HD:])
+
+
+def attend_scratch(count):
+    return [
+        pltpu.VMEM((HEADS, SLOT, count), BF16),
+        pltpu.VMEM((HEADS, SLOT, count), BF16),
+        pltpu.VMEM((HEADS, 128, count), F32),
+        pltpu.VMEM((HEADS, 128, count), BF16),
+    ]
+
+
+def own_kernel(lengths_ref, block_ref, folded_ref, query_gain_ref, key_gain_ref, queries_ref, acc_ref, *scratch):
     tokens = block_tokens(block_ref)
     count = tokens.shape[0]
     sides = window_sides(lengths_ref, lax.axis_index("seq") // 2, count)
@@ -467,11 +546,11 @@
     row = lax.broadcasted_iota(jnp.int32, (8, count), 0)
     tail = jnp.where(row == 0, MASK * sides, jnp.where(row == 1, -MASK, 0.0))
     for h in range(HEADS):
-        queries_ref[h] = jnp.concatenate([queries[h], tail], axis=0).astype(BF16)
-    attend(tokens, sides, folded_ref[D:], key_gain_ref[...], queries_ref, acc_ref)
-
-
-def step_kernel(step, lengths_ref, ahead_ref, behind_ref, folded_ref, key_gain_ref, queries_ref, acc_ref):
+        queries_ref[h] = jnp.concatenate([queries[h], tail], axis=0).T.astype(BF16)
+    attend(tokens, sides, folded_ref.at[D:], key_gain_ref[...], queries_ref, acc_ref, *scratch)
+
+
+def step_kernel(step, lengths_ref, ahead_ref, behind_ref, folded_ref, key_gain_ref, queries_ref, acc_ref, *scratch):
     place = ring_place()
     if step < 4:
         tokens = jnp.concatenate([block_tokens(ahead_ref), block_tokens(behind_ref)], axis=0)
@@ -485,7 +564,7 @@
     else:
         tokens = jnp.concatenate([half_tokens(ahead_ref), half_tokens(behind_ref)], axis=0)
         sides = window_sides(lengths_ref, chip_at(place + step), 128)
-    attend(tokens, sides, folded_ref[D:], key_gain_ref[...], queries_ref, acc_ref)
+    attend(tokens, sides, folded_ref.at[D:], key_gain_ref[...], queries_ref, acc_ref, *scratch)
 
 
 ACC = jax.ShapeDtypeStruct((HEADS, SLOT, 128), F32)
@@ -499,9 +578,10 @@
 def own_attention(lengths, block, folded, query_gain, key_gain):
     return pl.pallas_call(
         own_kernel,
-        out_shape=(jax.ShapeDtypeStruct((HEADS, SLOT, 128), BF16), ACC),
+        out_shape=(jax.ShapeDtypeStruct((HEADS, 128, SLOT), BF16), ACC),
         in_specs=[SMEM] + [VMEM] * 4,
         out_specs=(VMEM, VMEM),
+        scratch_shapes=attend_scratch(128),
         compiler_params=params(),
         name="own_attention",
         cost_estimate=cost(192),
@@ -514,6 +594,7 @@
         out_shape=ACC,
         in_specs=[SMEM] + [VMEM] * 5,
         out_specs=VMEM,
+        scratch_shapes=attend_scratch(256 if step < 4 else 128),
         compiler_params=params(),
         name="step_attention",
         cost_estimate=cost(256 if step < 4 else 128),
@@ -624,37 +705,43 @@
     def send(array, pairs):
         return lax.ppermute(array, "seq", pairs)
 
+    def tied(*arrays):
+        return lax.optimization_barrier(arrays)
+
     before = send(clip, up)
     after = send(clip, down)
     score_scale = math.log2(math.e) / math.sqrt(HD)
     query_rows = jnp.broadcast_to((query_gain * score_scale)[:, None], (HD, 256))
     key_rows = jnp.broadcast_to(key_gain[:, None], (HD, 256))
-    folded = fold(patch_weight, qkv_weight)
     weight = weight_tiles(out_weight)
+    folded, pairs_one, pairs_two, patch = prepare(patch_weight, qkv_weight, conv_first, conv_second)
+    before, after, pairs_one, weight, query_rows, key_rows = tied(
+        before, after, pairs_one, weight, query_rows, key_rows
+    )
     keep, other = convolve(
-        frame_counts, window_lengths, clip, before, after, conv_first, conv_second, patch_weight
+        frame_counts, window_lengths, clip, before, after, pairs_one, pairs_two, patch
     )
     got = send(other, cores)
     cut = 256 + 5 * SLOT
     block = jnp.concatenate([keep, weight[: 5 * SLOT], got, weight[5 * SLOT :]], axis=0)
     ahead, behind = block, block
-    accs, blocks = [], [block]
-    for step in range(1, 4):
-        ahead_next = send(ahead, forward)
-        behind_next = send(behind, backward)
+    accs, blocks, sibling = [], [block], []
+    for step in range(1, 5):
+        if step < 4:
+            ahead_next, behind_next = send(ahead, forward), send(behind, backward)
+        else:
+            ahead_next, behind_next = send(ahead[:cut], forward), send(behind[cut:], backward)
         if step == 1:
+            sibling.append(send(block, cores))
             queries, acc = own_attention(window_lengths, block, folded, query_rows, key_rows)
         else:
+            sibling += [send(ahead, cores), send(behind, cores)]
             acc = step_attention(step - 1, window_lengths, ahead, behind, folded, key_rows, queries)
+        ahead, behind, acc = tied(ahead_next, behind_next, acc)
         accs.append(acc)
-        ahead, behind = ahead_next, behind_next
         blocks += [ahead, behind]
-    ahead_last = send(ahead[:cut], forward)
-    behind_last = send(behind[cut:], backward)
-    accs.append(step_attention(3, window_lengths, ahead, behind, folded, key_rows, queries))
-    accs.append(step_attention(4, window_lengths, ahead_last, behind_last, folded, key_rows, queries))
-    blocks += [ahead_last, behind_last]
-    sibling = [send(array, cores) for array in blocks]
+    sibling += [send(ahead, cores), send(behind, cores)]
+    accs.append(step_attention(4, window_lengths, ahead, behind, folded, key_rows, queries))
     keep_rows, send_rows = project_out(accs, blocks + sibling)
     return merge(window_lengths, keep_rows, send(send_rows, cores))
 

time: 89.6 us -> 72 us (0.80)
  Pallas kernels: 36.3 us -> 26.9 us
  local copies, waits for them, and re-layouts: 9.49 us -> 4.89 us
  waiting for transfers between devices: 24.9 us -> 21.3 us
    pallas_call x4, Pallas kernels: 18.6 us -> 10.1 us  [step_attention(): pl.pallas_call(functools.partial(step_kernel, step), out_shape=ACC, in_sp...]
    unnamed x24 -> x16, local copies, waits for them, and re-layouts: 9.1 us -> 3.62 us
    ppermute x21, waiting for transfers between devices: 24.9 us -> 21.3 us  [send(): return lax.ppermute(array, 'seq', pairs)]
    pad x1, local copies, waits for them, and re-layouts: 0.01 us -> 0.93 us  [weight_tiles(): padded = jnp.pad(out_weight, ((0, SLOT - HD), (0, 0)))]
  transfers between devices with their start and end apart: 21 -> 21, of which waited for: 7 -> 9; matrix products, arithmetic and copies ran while one was open for 0% -> 2% of each run, Pallas kernels for 34% -> 29%
where the time goes in v2:
time: 72 us; the launch traced here: 71.8 us
  Pallas kernels  26.9 us (37%)
  waiting for transfers between devices  21.3 us (30%)
  starting transfers between devices  18.4 us (26%)
  local copies, waits for them, and re-layouts  4.89 us (7%)
    ppermute x21, waiting for transfers between devices, send(): return lax.ppermute(array, 'seq', pairs)  21.3 us
    ppermute x21, starting transfers between devices, send(): return lax.ppermute(array, 'seq', pairs)  18.4 us
    pallas_call x4, Pallas kernels, step_attention(): pl.pallas_call(functools.partial(step_kernel, step), out_shape=ACC, in_sp...  10.1 us
    pallas_call x1, Pallas kernels, prepare(): pl.pallas_call(prepare_kernel, out_shape=(jax.ShapeDtypeStruct((3 * D, in...  7.83 us
    pallas_call x1, Pallas kernels, convolve(): pl.pallas_call(conv_kernel, out_shape=(out, out), in_specs=[ANY] * 3 + [V...  3.65 us
    unnamed x16, local copies, waits for them, and re-layouts  3.62 us
    pallas_call x1, Pallas kernels, own_attention(): pl.pallas_call(own_kernel, out_shape=(jax.ShapeDtypeStruct((HEADS, 128, S...  3.03 us
  transfers between devices with their start and end apart: 21, of which 9 were waited for; matrix products, arithmetic and copies ran while one was open for 2% of the time, Pallas kernels for 29%

profile of v2, /device:TPU:0, one launch (start us, length us, event | category | flops | bytes accessed | tf_op | source)
XLA Modules:
  0.0 71.8 jit_solution(13859331947507118431)
XLA Ops:
  0.0 2.4 %collective-permute-start = (bf16[8,2,32,128]{3,2,1,0:T(8,128)(2,1)}, bf16[8,2,32,128]{3,2,1,0:T(8,128)(2,1)S(1)}, u32[]{:S(2)}, u32[]{:S(2)}) collective-permute-start(bf16[8,2,32,128]{3,2,1,0:T(8,128)(2,1)} %own_any.1), channel_id=1, source_target_pairs={{0,1},{1,2},{2,3},{3,4},{4,5},{5,6},{6,7},{7,8},{8,9},{9,10},{10,1... | collective-permute-start | bytes 393224 | tf_op jit(solution)/shard_map/ppermute | solution.py:706
  2.4 1.3 %collective-permute-start.1 = (bf16[8,2,32,128]{3,2,1,0:T(8,128)(2,1)}, bf16[8,2,32,128]{3,2,1,0:T(8,128)(2,1)S(1)}, u32[]{:S(2)}, u32[]{:S(2)}) collective-permute-start(bf16[8,2,32,128]{3,2,1,0:T(8,128)(2,1)} %own_any.1), channel_id=1, source_target_pairs={{1,0},{2,1},{3,2},{4,3},{5,4},{6,5},{7,6},{8,7},{9,8},{10,9},{11,1... | collective-permute-start | bytes 393224 | tf_op jit(solution)/shard_map/ppermute | solution.py:706
  3.7 0.9 %pad.4 = bf16[80,1152]{1,0:T(8,128)(2,1)S(1)} pad(bf16[72,1152]{1,0:T(8,128)(2,1)} %param.18, bf16[]{:T(256)} %constant.1.clone.1), padding=0_8x0_0 | pad | bytes 350210 | tf_op jit(solution)/shard_map/jit(_pad)/pad | solution.py:690
  4.6 0.1 reshape.8
  4.7 0.1 copy.12
  4.8 0.0 copy-start.1
  4.8 1.3 %copy-done.1 = bf16[512,1152]{1,0:T(8,128)(2,1)S(1)} copy-done((bf16[512,1152]{1,0:T(8,128)(2,1)S(1)}, bf16[512,1152]{1,0:T(8,128)(2,1)}, u32[]{:S(2)}) %copy-start.1) | copy-done | bytes 1179672
  6.0 1.2 %copy-done.2 = bf16[3,3,3,128,128]{4,3,2,1,0:T(8,128)(2,1)S(1)} copy-done((bf16[3,3,3,128,128]{4,3,2,1,0:T(8,128)(2,1)S(1)}, bf16[3,3,3,128,128]{4,3,2,1,0:T(8,128)(2,1)}, u32[]{:S(2)}) %copy-start.2) | copy-done | bytes 884760
  7.2 1.2 %copy-done.3 = bf16[3,3,3,128,128]{4,3,2,1,0:T(8,128)(2,1)S(1)} copy-done((bf16[3,3,3,128,128]{4,3,2,1,0:T(8,128)(2,1)S(1)}, bf16[3,3,3,128,128]{4,3,2,1,0:T(8,128)(2,1)}, u32[]{:S(2)}) %copy-start.3) | copy-done | bytes 884760
  8.4 0.0 copy-start.5
  8.4 7.8 %prepare.1 = (bf16[3456,512]{1,0:T(8,128)(2,1)S(1)}, bf16[3,1536,256]{2,1,0:T(8,128)(2,1)S(1)}, bf16[3,1536,256]{2,1,0:T(8,128)(2,1)S(1)}, bf16[512,1152]{1,0:T(8,128)(2,1)S(1)}) custom-call(bf16[512,1152]{1,0:T(8,128)(2,1)S(1)} %copy-done.1, bf16[1152,3456]{1,0:T(8,128)(2,1)} %qkv_any.1, bf16[3,3,3,128,128]{4,3,2,1,0:T(8,128)(2,1)S(1)} %copy-done.2, ...), custom_call_target="tpu_custom_call" | custom-call | flops 4076863488 | bytes 12582912 | tf_op jit(solution)/shard_map/prepare/pallas_call | solution.py:273
  16.3 0.0 collective-permute-done.before_ref
  16.3 0.1 broadcast_in_dim.4.query_gain_ref
  16.4 0.1 broadcast_in_dim.5.key_gain_ref
  16.5 3.7 %convolve.1 = (bf16[256,128]{1,0:T(8,128)(2,1)S(1)}, bf16[256,128]{1,0:T(8,128)(2,1)S(1)}) custom-call(s32[3]{0:T(128)S(1)} %copy-done.5, s32[1,3]{1,0:T(1,128)S(1)} %copy-done, bf16[8,2,32,128]{3,2,1,0:T(8,128)(2,1)S(1)} %copy-done.4, bf16[8,2,32,128]{3,2,1,0:T(8,128)(2,1)S(1)} %collective-permute-done.before_ref, ...), custom_call_target="tpu_custom_call" | custom-call | flops 2147483648 | bytes 4194304 | tf_op jit(solution)/shard_map/convolve/pallas_call | solution.py:419
  20.1 3.3 %collective-permute-start.2 = (bf16[256,128]{1,0:T(8,128)(2,1)S(1)}, bf16[256,128]{1,0:T(8,128)(2,1)S(1)}, u32[]{:S(2)}, u32[]{:S(2)}) collective-permute-start(bf16[256,128]{1,0:T(8,128)(2,1)S(1)} %get-tuple-element.41), channel_id=1, source_target_pairs={{0,1},{1,0},{2,3},{3,2},{4,5},{5,4},{6,7},{7,6},{8,9},{9,8},{10,11... | collective-permute-start | bytes 196616 | tf_op jit(solution)/shard_map/ppermute | solution.py:706
  23.5 0.9 %collective-permute-done.2 = bf16[256,128]{1,0:T(8,128)(2,1)S(1)} collective-permute-done((bf16[256,128]{1,0:T(8,128)(2,1)S(1)}, bf16[256,128]{1,0:T(8,128)(2,1)S(1)}, u32[]{:S(2)}, u32[]{:S(2)}) %collective-permute-start.2) | collective-permute-done | bytes 65568 | tf_op jit(solution)/shard_map/ppermute | solution.py:706
  24.4 3.0 %collective-permute-start.3 = (bf16[1232,128]{1,0:T(8,128)(2,1)S(1)}, bf16[1232,128]{1,0:T(8,128)(2,1)S(1)}, u32[]{:S(2)}, u32[]{:S(2)}) collective-permute-start(bf16[1232,128]{1,0:T(8,128)(2,1)S(1)} %pad_maximum_fusion.block_ref.refs_5_), channel_id=1, source_target_pairs={{0,4},{1,5},{4,8},{5,9},{8,12},{9,13},{12,14},{13,15},{14,10},{15,... | collective-permute-start | bytes 946184 | tf_op jit(solution)/shard_map/ppermute | solution.py:706
  27.4 0.0 collective-permute-start.4
  27.4 3.0 %own_attention.1 = (bf16[16,128,80]{2,1,0:T(8,128)(2,1)S(1)}, f32[16,80,128]{2,1,0:T(8,128)S(1)}) custom-call(s32[1,3]{1,0:T(1,128)S(1)} %copy-done, bf16[1232,128]{1,0:T(8,128)(2,1)S(1)} %pad_maximum_fusion.block_ref.refs_5_, bf16[3456,512]{1,0:T(8,128)(2,1)S(1)} %get-tuple-element.42.folded_ref, f32[72,256]{1,0:T(8,128)S(1)} %broadcast_in_dim.4.query_gain_ref, ...), custom_call_target="tpu_custom_call" | custom-call | flops 1308622848 | bytes 5242880 | tf_op jit(solution)/shard_map/own_attention/pallas_call | solution.py:579
  30.4 4.0 %collective-permute-done.3.ahead_ref.refs_6_ = bf16[1232,128]{1,0:T(8,128)(2,1)S(1)} collective-permute-done((bf16[1232,128]{1,0:T(8,128)(2,1)S(1)}, bf16[1232,128]{1,0:T(8,128)(2,1)S(1)}, u32[]{:S(2)}, u32[]{:S(2)}) %collective-permute-start.3) | collective-permute-done | bytes 315424 | tf_op jit(solution)/shard_map/ppermute | solution.py:706
  34.4 2.2 %collective-permute-done.4.behind_ref.refs_7_ = bf16[1232,128]{1,0:T(8,128)(2,1)S(1)} collective-permute-done((bf16[1232,128]{1,0:T(8,128)(2,1)S(1)}, bf16[1232,128]{1,0:T(8,128)(2,1)S(1)}, u32[]{:S(2)}, u32[]{:S(2)}) %collective-permute-start.4) | collective-permute-done | bytes 315424 | tf_op jit(solution)/shard_map/ppermute | solution.py:706
  36.6 1.6 %collective-permute-start.5 = (bf16[1232,128]{1,0:T(8,128)(2,1)S(1)}, bf16[1232,128]{1,0:T(8,128)(2,1)S(1)}, u32[]{:S(2)}, u32[]{:S(2)}) collective-permute-start(bf16[1232,128]{1,0:T(8,128)(2,1)S(1)} %collective-permute-done.3.ahead_ref.refs_6_), channel_id=1, source_target_pairs={{0,4},{1,5},{4,8},{5,9},{8,12},{9,13},{12,14},{13,15},{14,10},{15,... | collective-permute-start | bytes 946184 | tf_op jit(solution)/shard_map/ppermute | solution.py:706
  38.2 0.4 collective-permute-start.6
  38.6 2.5 %step_attention.4.refs_1_ = f32[16,80,128]{2,1,0:T(8,128)S(1)} custom-call(s32[1,3]{1,0:T(1,128)S(1)} %copy-done, bf16[1232,128]{1,0:T(8,128)(2,1)S(1)} %collective-permute-done.3.ahead_ref.refs_6_, bf16[1232,128]{1,0:T(8,128)(2,1)S(1)} %collective-permute-done.4.behind_ref.refs_7_, bf16[3456,512]{1,0:T(8,128)(2,1)S(1)} %get-tuple-element.42.folded_ref, ...), custom_call_target="tpu_custom_call" | custom-call | flops 1744830464 | bytes 5242880 | tf_op jit(solution)/shard_map/step_attention/pallas_call | solution.py:592
  41.1 3.8 %collective-permute-done.5.ahead_ref.refs_8_ = bf16[1232,128]{1,0:T(8,128)(2,1)S(1)} collective-permute-done((bf16[1232,128]{1,0:T(8,128)(2,1)S(1)}, bf16[1232,128]{1,0:T(8,128)(2,1)S(1)}, u32[]{:S(2)}, u32[]{:S(2)}) %collective-permute-start.5) | collective-permute-done | bytes 315424 | tf_op jit(solution)/shard_map/ppermute | solution.py:706
  45.0 1.3 %collective-permute-done.6.behind_ref.refs_9_ = bf16[1232,128]{1,0:T(8,128)(2,1)S(1)} collective-permute-done((bf16[1232,128]{1,0:T(8,128)(2,1)S(1)}, bf16[1232,128]{1,0:T(8,128)(2,1)S(1)}, u32[]{:S(2)}, u32[]{:S(2)}) %collective-permute-start.6) | collective-permute-done | bytes 315424 | tf_op jit(solution)/shard_map/ppermute | solution.py:706
  46.2 1.6 %collective-permute-start.7 = (bf16[1232,128]{1,0:T(8,128)(2,1)S(1)}, bf16[1232,128]{1,0:T(8,128)(2,1)S(1)}, u32[]{:S(2)}, u32[]{:S(2)}) collective-permute-start(bf16[1232,128]{1,0:T(8,128)(2,1)S(1)} %collective-permute-done.5.ahead_ref.refs_8_), channel_id=1, source_target_pairs={{0,4},{1,5},{4,8},{5,9},{8,12},{9,13},{12,14},{13,15},{14,10},{15,... | collective-permute-start | bytes 946184 | tf_op jit(solution)/shard_map/ppermute | solution.py:706
  47.8 0.4 collective-permute-start.8
  48.3 0.5 collective-permute-start.12
  48.8 2.5 %step_attention.5.refs_2_ = f32[16,80,128]{2,1,0:T(8,128)S(1)} custom-call(s32[1,3]{1,0:T(1,128)S(1)} %copy-done, bf16[1232,128]{1,0:T(8,128)(2,1)S(1)} %collective-permute-done.5.ahead_ref.refs_8_, bf16[1232,128]{1,0:T(8,128)(2,1)S(1)} %collective-permute-done.6.behind_ref.refs_9_, bf16[3456,512]{1,0:T(8,128)(2,1)S(1)} %get-tuple-element.42.folded_ref, ...), custom_call_target="tpu_custom_call" | custom-call | flops 1744830464 | bytes 5242880 | tf_op jit(solution)/shard_map/step_attention/pallas_call | solution.py:592
  51.3 2.1 %collective-permute-done.7.ahead_ref.refs_10_ = bf16[1232,128]{1,0:T(8,128)(2,1)S(1)} collective-permute-done((bf16[1232,128]{1,0:T(8,128)(2,1)S(1)}, bf16[1232,128]{1,0:T(8,128)(2,1)S(1)}, u32[]{:S(2)}, u32[]{:S(2)}) %collective-permute-start.7) | collective-permute-done | bytes 315424 | tf_op jit(solution)/shard_map/ppermute | solution.py:706
  53.4 1.4 %collective-permute-done.8.behind_ref.refs_11_ = bf16[1232,128]{1,0:T(8,128)(2,1)S(1)} collective-permute-done((bf16[1232,128]{1,0:T(8,128)(2,1)S(1)}, bf16[1232,128]{1,0:T(8,128)(2,1)S(1)}, u32[]{:S(2)}, u32[]{:S(2)}) %collective-permute-start.8) | collective-permute-done | bytes 315424 | tf_op jit(solution)/shard_map/ppermute | solution.py:706
  54.8 0.7 collective-permute-start.9
  55.5 1.5 %collective-permute-start.10 = (bf16[576,128]{1,0:T(8,128)(2,1)S(1)}, bf16[576,128]{1,0:T(8,128)(2,1)S(1)}, u32[]{:S(2)}, u32[]{:S(2)}) collective-permute-start(bf16[576,128]{1,0:T(8,128)(2,1)S(1)} %slice.15), channel_id=1, source_target_pairs={{4,0},{5,1},{8,4},{9,5},{12,8},{13,9},{14,12},{15,13},{10,14},{11,... | collective-permute-start | bytes 442376 | tf_op jit(solution)/shard_map/ppermute | solution.py:706
  56.9 0.2 collective-permute-start.14
  57.2 0.3 collective-permute-start.15
  57.5 4.3 %collective-permute-done.10.behind_ref.refs_13_ = bf16[576,128]{1,0:T(8,128)(2,1)S(1)} collective-permute-done((bf16[576,128]{1,0:T(8,128)(2,1)S(1)}, bf16[576,128]{1,0:T(8,128)(2,1)S(1)}, u32[]{:S(2)}, u32[]{:S(2)}) %collective-permute-start.10) | collective-permute-done | bytes 147488 | tf_op jit(solution)/shard_map/ppermute | solution.py:706
  61.8 0.5 collective-permute-start.17
  62.3 2.5 %step_attention.6.refs_3_ = f32[16,80,128]{2,1,0:T(8,128)S(1)} custom-call(s32[1,3]{1,0:T(1,128)S(1)} %copy-done, bf16[1232,128]{1,0:T(8,128)(2,1)S(1)} %collective-permute-done.7.ahead_ref.refs_10_, bf16[1232,128]{1,0:T(8,128)(2,1)S(1)} %collective-permute-done.8.behind_ref.refs_11_, bf16[3456,512]{1,0:T(8,128)(2,1)S(1)} %get-tuple-element.42.folded_ref, ...), custom_call_target="tpu_custom_call" | custom-call | flops 1744830464 | bytes 5242880 | tf_op jit(solution)/shard_map/step_attention/pallas_call | solution.py:592
  64.8 0.0 collective-permute-done.13.refs_16_
  64.8 0.1 collective-permute-start.18
  64.9 0.5 collective-permute-start.19
  65.4 2.5 %step_attention.7.refs_4_ = f32[16,80,128]{2,1,0:T(8,128)S(1)} custom-call(s32[1,3]{1,0:T(1,128)S(1)} %copy-done, bf16[656,128]{1,0:T(8,128)(2,1)S(1)} %collective-permute-done.9.ahead_ref.refs_12_, bf16[576,128]{1,0:T(8,128)(2,1)S(1)} %collective-permute-done.10.behind_ref.refs_13_, bf16[3456,512]{1,0:T(8,128)(2,1)S(1)} %get-tuple-element.42.folded_ref, ...), custom_call_target="tpu_custom_call" | custom-call | flops 872415232 | bytes 5242880 | tf_op jit(solution)/shard_map/step_attention/pallas_call | solution.py:592
  68.0 1.0 %project_out.1 = (bf16[64,1152]{1,0:T(8,128)(2,1)S(1)}, bf16[64,1152]{1,0:T(8,128)(2,1)S(1)}) custom-call(f32[16,80,128]{2,1,0:T(8,128)S(1)} %get-tuple-element.46.refs_0_, f32[16,80,128]{2,1,0:T(8,128)S(1)} %step_attention.4.refs_1_, f32[16,80,128]{2,1,0:T(8,128)S(1)} %step_attention.5.refs_2_, f32[16,80,128]{2,1,0:T(8,128)S(1)} %step_attention.6.refs_3_, ...), custom_call_target="tpu_custom_call" | custom-call | flops 377487360 | bytes 4194304 | tf_op jit(solution)/shard_map/project_out/pallas_call | solution.py:651
  69.0 0.1 collective-permute-start.20
  69.1 1.3 %collective-permute-done.20.got_ref = bf16[64,1152]{1,0:T(8,128)(2,1)S(1)} collective-permute-done((bf16[64,1152]{1,0:T(8,128)(2,1)S(1)}, bf16[64,1152]{1,0:T(8,128)(2,1)S(1)}, u32[]{:S(2)}, u32[]{:S(2)}) %collective-permute-start.20) | collective-permute-done | bytes 147488 | tf_op jit(solution)/shard_map/ppermute | solution.py:706
  70.4 1.3 %merge.1 = bf16[128,1152]{1,0:T(8,128)(2,1)} custom-call(s32[1,3]{1,0:T(1,128)S(1)} %copy-done, bf16[64,1152]{1,0:T(8,128)(2,1)S(1)} %get-tuple-element.59.keep_ref, bf16[64,1152]{1,0:T(8,128)(2,1)S(1)} %collective-permute-done.20.got_ref), custom_call_target="tpu_custom_call" | custom-call | tf_op jit(solution)/shard_map/merge/pallas_call | solution.py:679
  (30 shorter events, 0.1 us)
Async XLA Ops:
  0.0 16.3 %collective-permute-start = (bf16[8,2,32,128]{3,2,1,0:T(8,128)(2,1)}, bf16[8,2,32,128]{3,2,1,0:T(8,128)(2,1)S(1)}, u32[]{:S(2)}, u32[]{:S(2)}) collective-permute-start(bf16[8,2,32,128]{3,2,1,0:T(8,128)(2,1)} %own_any.1), channel_id=1, source_target_pairs={{0,1},{1,2},{2,3},{3,4},{4,5},{5,6},{6,7},{7,8},{8,9},{9,10},{10,1... | collective-permute-start | bytes 393224 | tf_op jit(solution)/shard_map/ppermute | solution.py:706
  2.4 13.9 %collective-permute-start.1 = (bf16[8,2,32,128]{3,2,1,0:T(8,128)(2,1)}, bf16[8,2,32,128]{3,2,1,0:T(8,128)(2,1)S(1)}, u32[]{:S(2)}, u32[]{:S(2)}) collective-permute-start(bf16[8,2,32,128]{3,2,1,0:T(8,128)(2,1)} %own_any.1), channel_id=1, source_target_pairs={{1,0},{2,1},{3,2},{4,3},{5,4},{6,5},{7,6},{8,7},{9,8},{10,9},{11,1... | collective-permute-start | bytes 393224 | tf_op jit(solution)/shard_map/ppermute | solution.py:706
  4.8 1.3 %copy-start.1 = (bf16[512,1152]{1,0:T(8,128)(2,1)S(1)}, bf16[512,1152]{1,0:T(8,128)(2,1)}, u32[]{:S(2)}) copy-start(bf16[512,1152]{1,0:T(8,128)(2,1)} %patch_any.1) | copy-start | bytes 3538948
  6.0 1.2 %copy-start.2 = (bf16[3,3,3,128,128]{4,3,2,1,0:T(8,128)(2,1)S(1)}, bf16[3,3,3,128,128]{4,3,2,1,0:T(8,128)(2,1)}, u32[]{:S(2)}) copy-start(bf16[3,3,3,128,128]{4,3,2,1,0:T(8,128)(2,1)} %first_any.1) | copy-start | bytes 2654212
  7.2 1.2 %copy-start.3 = (bf16[3,3,3,128,128]{4,3,2,1,0:T(8,128)(2,1)S(1)}, bf16[3,3,3,128,128]{4,3,2,1,0:T(8,128)(2,1)}, u32[]{:S(2)}) copy-start(bf16[3,3,3,128,128]{4,3,2,1,0:T(8,128)(2,1)} %second_any.1) | copy-start | bytes 2654212
  8.4 7.9 %copy-start.7 = (f32[72]{0:T(128)S(1)}, f32[72]{0:T(128)}, u32[]{:S(2)}) copy-start(f32[72]{0:T(128)} %param.16) | copy-start | bytes 868
  8.4 8.0 %copy-start.6 = (f32[72]{0:T(128)S(1)}, f32[72]{0:T(128)}, u32[]{:S(2)}) copy-start(f32[72]{0:T(128)} %param.17) | copy-start | bytes 868
  8.4 8.1 %copy-start = (s32[1,3]{1,0:T(1,128)S(1)}, s32[1,3]{1,0:T(1,128)}, u32[]{:S(2)}) copy-start(s32[1,3]{1,0:T(1,128)} %lengths_ref.11) | copy-start | bytes 40
  8.4 8.1 %copy-start.4 = (bf16[8,2,32,128]{3,2,1,0:T(8,128)(2,1)S(1)}, bf16[8,2,32,128]{3,2,1,0:T(8,128)(2,1)}, u32[]{:S(2)}) copy-start(bf16[8,2,32,128]{3,2,1,0:T(8,128)(2,1)} %own_any.1) | copy-start | bytes 393220
  8.4 8.1 %copy-start.5 = (s32[3]{0:T(128)S(1)}, s32[3]{0:T(128)}, u32[]{:S(2)}) copy-start(s32[3]{0:T(128)} %counts_any.1) | copy-start | bytes 40
  20.1 4.2 %collective-permute-start.2 = (bf16[256,128]{1,0:T(8,128)(2,1)S(1)}, bf16[256,128]{1,0:T(8,128)(2,1)S(1)}, u32[]{:S(2)}, u32[]{:S(2)}) collective-permute-start(bf16[256,128]{1,0:T(8,128)(2,1)S(1)} %get-tuple-element.41), channel_id=1, source_target_pairs={{0,1},{1,0},{2,3},{3,2},{4,5},{5,4},{6,7},{7,6},{8,9},{9,8},{10,11... | collective-permute-start | bytes 196616 | tf_op jit(solution)/shard_map/ppermute | solution.py:706
  24.4 10.0 %collective-permute-start.3 = (bf16[1232,128]{1,0:T(8,128)(2,1)S(1)}, bf16[1232,128]{1,0:T(8,128)(2,1)S(1)}, u32[]{:S(2)}, u32[]{:S(2)}) collective-permute-start(bf16[1232,128]{1,0:T(8,128)(2,1)S(1)} %pad_maximum_fusion.block_ref.refs_5_), channel_id=1, source_target_pairs={{0,4},{1,5},{4,8},{5,9},{8,12},{9,13},{12,14},{13,15},{14,10},{15,... | collective-permute-start | bytes 946184 | tf_op jit(solution)/shard_map/ppermute | solution.py:706
  27.4 9.2 %collective-permute-start.4 = (bf16[1232,128]{1,0:T(8,128)(2,1)S(1)}, bf16[1232,128]{1,0:T(8,128)(2,1)S(1)}, u32[]{:S(2)}, u32[]{:S(2)}) collective-permute-start(bf16[1232,128]{1,0:T(8,128)(2,1)S(1)} %pad_maximum_fusion.block_ref.refs_5_), channel_id=1, source_target_pairs={{4,0},{5,1},{8,4},{9,5},{12,8},{13,9},{14,12},{15,13},{10,14},{11,... | collective-permute-start | bytes 946184 | tf_op jit(solution)/shard_map/ppermute | solution.py:706
  36.6 8.4 %collective-permute-start.5 = (bf16[1232,128]{1,0:T(8,128)(2,1)S(1)}, bf16[1232,128]{1,0:T(8,128)(2,1)S(1)}, u32[]{:S(2)}, u32[]{:S(2)}) collective-permute-start(bf16[1232,128]{1,0:T(8,128)(2,1)S(1)} %collective-permute-done.3.ahead_ref.refs_6_), channel_id=1, source_target_pairs={{0,4},{1,5},{4,8},{5,9},{8,12},{9,13},{12,14},{13,15},{14,10},{15,... | collective-permute-start | bytes 946184 | tf_op jit(solution)/shard_map/ppermute | solution.py:706
  38.2 8.1 %collective-permute-start.6 = (bf16[1232,128]{1,0:T(8,128)(2,1)S(1)}, bf16[1232,128]{1,0:T(8,128)(2,1)S(1)}, u32[]{:S(2)}, u32[]{:S(2)}) collective-permute-start(bf16[1232,128]{1,0:T(8,128)(2,1)S(1)} %collective-permute-done.4.behind_ref.refs_7_), channel_id=1, source_target_pairs={{4,0},{5,1},{8,4},{9,5},{12,8},{13,9},{14,12},{15,13},{10,14},{11,... | collective-permute-start | bytes 946184 | tf_op jit(solution)/shard_map/ppermute | solution.py:706
  46.2 7.2 %collective-permute-start.7 = (bf16[1232,128]{1,0:T(8,128)(2,1)S(1)}, bf16[1232,128]{1,0:T(8,128)(2,1)S(1)}, u32[]{:S(2)}, u32[]{:S(2)}) collective-permute-start(bf16[1232,128]{1,0:T(8,128)(2,1)S(1)} %collective-permute-done.5.ahead_ref.refs_8_), channel_id=1, source_target_pairs={{0,4},{1,5},{4,8},{5,9},{8,12},{9,13},{12,14},{13,15},{14,10},{15,... | collective-permute-start | bytes 946184 | tf_op jit(solution)/shard_map/ppermute | solution.py:706
  47.8 6.9 %collective-permute-start.8 = (bf16[1232,128]{1,0:T(8,128)(2,1)S(1)}, bf16[1232,128]{1,0:T(8,128)(2,1)S(1)}, u32[]{:S(2)}, u32[]{:S(2)}) collective-permute-start(bf16[1232,128]{1,0:T(8,128)(2,1)S(1)} %collective-permute-done.6.behind_ref.refs_9_), channel_id=1, source_target_pairs={{4,0},{5,1},{8,4},{9,5},{12,8},{13,9},{14,12},{15,13},{10,14},{11,... | collective-permute-start | bytes 946184 | tf_op jit(solution)/shard_map/ppermute | solution.py:706
  48.3 8.7 %collective-permute-start.11 = (bf16[1232,128]{1,0:T(8,128)(2,1)S(1)}, bf16[1232,128]{1,0:T(8,128)(2,1)S(1)}, u32[]{:S(2)}, u32[]{:S(2)}) collective-permute-start(bf16[1232,128]{1,0:T(8,128)(2,1)S(1)} %pad_maximum_fusion.block_ref.refs_5_), channel_id=1, source_target_pairs={{0,1},{1,0},{2,3},{3,2},{4,5},{5,4},{6,7},{7,6},{8,9},{9,8},{10,11... | collective-permute-start | bytes 946184 | tf_op jit(solution)/shard_map/ppermute | solution.py:706
  48.3 8.9 %collective-permute-start.12 = (bf16[1232,128]{1,0:T(8,128)(2,1)S(1)}, bf16[1232,128]{1,0:T(8,128)(2,1)S(1)}, u32[]{:S(2)}, u32[]{:S(2)}) collective-permute-start(bf16[1232,128]{1,0:T(8,128)(2,1)S(1)} %collective-permute-done.3.ahead_ref.refs_6_), channel_id=1, source_target_pairs={{0,1},{1,0},{2,3},{3,2},{4,5},{5,4},{6,7},{7,6},{8,9},{9,8},{10,11... | collective-permute-start | bytes 946184 | tf_op jit(solution)/shard_map/ppermute | solution.py:706
  54.8 7.0 %collective-permute-start.9 = (bf16[656,128]{1,0:T(8,128)(2,1)S(1)}, bf16[656,128]{1,0:T(8,128)(2,1)S(1)}, u32[]{:S(2)}, u32[]{:S(2)}) collective-permute-start(bf16[656,128]{1,0:T(8,128)(2,1)S(1)} %slice.14), channel_id=1, source_target_pairs={{0,4},{1,5},{4,8},{5,9},{8,12},{9,13},{12,14},{13,15},{14,10},{15,... | collective-permute-start | bytes 503816 | tf_op jit(solution)/shard_map/ppermute | solution.py:706
  55.5 9.4 %collective-permute-start.13 = (bf16[1232,128]{1,0:T(8,128)(2,1)S(1)}, bf16[1232,128]{1,0:T(8,128)(2,1)S(1)}, u32[]{:S(2)}, u32[]{:S(2)}) collective-permute-start(bf16[1232,128]{1,0:T(8,128)(2,1)S(1)} %collective-permute-done.4.behind_ref.refs_7_), channel_id=1, source_target_pairs={{0,1},{1,0},{2,3},{3,2},{4,5},{5,4},{6,7},{7,6},{8,9},{9,8},{10,11... | collective-permute-start | bytes 946184 | tf_op jit(solution)/shard_map/ppermute | solution.py:706
  55.5 6.3 %collective-permute-start.10 = (bf16[576,128]{1,0:T(8,128)(2,1)S(1)}, bf16[576,128]{1,0:T(8,128)(2,1)S(1)}, u32[]{:S(2)}, u32[]{:S(2)}) collective-permute-start(bf16[576,128]{1,0:T(8,128)(2,1)S(1)} %slice.15), channel_id=1, source_target_pairs={{4,0},{5,1},{8,4},{9,5},{12,8},{13,9},{14,12},{15,13},{10,14},{11,... | collective-permute-start | bytes 442376 | tf_op jit(solution)/shard_map/ppermute | solution.py:706
  56.9 8.0 %collective-permute-start.14 = (bf16[1232,128]{1,0:T(8,128)(2,1)S(1)}, bf16[1232,128]{1,0:T(8,128)(2,1)S(1)}, u32[]{:S(2)}, u32[]{:S(2)}) collective-permute-start(bf16[1232,128]{1,0:T(8,128)(2,1)S(1)} %collective-permute-done.5.ahead_ref.refs_8_), channel_id=1, source_target_pairs={{0,1},{1,0},{2,3},{3,2},{4,5},{5,4},{6,7},{7,6},{8,9},{9,8},{10,11... | collective-permute-start | bytes 946184 | tf_op jit(solution)/shard_map/ppermute | solution.py:706
  57.2 10.8 %collective-permute-start.15 = (bf16[1232,128]{1,0:T(8,128)(2,1)S(1)}, bf16[1232,128]{1,0:T(8,128)(2,1)S(1)}, u32[]{:S(2)}, u32[]{:S(2)}) collective-permute-start(bf16[1232,128]{1,0:T(8,128)(2,1)S(1)} %collective-permute-done.6.behind_ref.refs_9_), channel_id=1, source_target_pairs={{0,1},{1,0},{2,3},{3,2},{4,5},{5,4},{6,7},{7,6},{8,9},{9,8},{10,11... | collective-permute-start | bytes 946184 | tf_op jit(solution)/shard_map/ppermute | solution.py:706
  61.8 6.2 %collective-permute-start.16 = (bf16[1232,128]{1,0:T(8,128)(2,1)S(1)}, bf16[1232,128]{1,0:T(8,128)(2,1)S(1)}, u32[]{:S(2)}, u32[]{:S(2)}) collective-permute-start(bf16[1232,128]{1,0:T(8,128)(2,1)S(1)} %collective-permute-done.7.ahead_ref.refs_10_), channel_id=1, source_target_pairs={{0,1},{1,0},{2,3},{3,2},{4,5},{5,4},{6,7},{7,6},{8,9},{9,8},{10,11... | collective-permute-start | bytes 946184 | tf_op jit(solution)/shard_map/ppermute | solution.py:706
  61.8 6.2 %collective-permute-start.17 = (bf16[1232,128]{1,0:T(8,128)(2,1)S(1)}, bf16[1232,128]{1,0:T(8,128)(2,1)S(1)}, u32[]{:S(2)}, u32[]{:S(2)}) collective-permute-start(bf16[1232,128]{1,0:T(8,128)(2,1)S(1)} %collective-permute-done.8.behind_ref.refs_11_), channel_id=1, source_target_pairs={{0,1},{1,0},{2,3},{3,2},{4,5},{5,4},{6,7},{7,6},{8,9},{9,8},{10,11... | collective-permute-start | bytes 946184 | tf_op jit(solution)/shard_map/ppermute | solution.py:706
  64.8 3.1 %collective-permute-start.18 = (bf16[656,128]{1,0:T(8,128)(2,1)S(1)}, bf16[656,128]{1,0:T(8,128)(2,1)S(1)}, u32[]{:S(2)}, u32[]{:S(2)}) collective-permute-start(bf16[656,128]{1,0:T(8,128)(2,1)S(1)} %collective-permute-done.9.ahead_ref.refs_12_), channel_id=1, source_target_pairs={{0,1},{1,0},{2,3},{3,2},{4,5},{5,4},{6,7},{7,6},{8,9},{9,8},{10,11... | collective-permute-start | bytes 503816 | tf_op jit(solution)/shard_map/ppermute | solution.py:706
  64.9 3.0 %collective-permute-start.19 = (bf16[576,128]{1,0:T(8,128)(2,1)S(1)}, bf16[576,128]{1,0:T(8,128)(2,1)S(1)}, u32[]{:S(2)}, u32[]{:S(2)}) collective-permute-start(bf16[576,128]{1,0:T(8,128)(2,1)S(1)} %collective-permute-done.10.behind_ref.refs_13_), channel_id=1, source_target_pairs={{0,1},{1,0},{2,3},{3,2},{4,5},{5,4},{6,7},{7,6},{8,9},{9,8},{10,11... | collective-permute-start | bytes 442376 | tf_op jit(solution)/shard_map/ppermute | solution.py:706
  69.0 1.4 %collective-permute-start.20 = (bf16[64,1152]{1,0:T(8,128)(2,1)S(1)}, bf16[64,1152]{1,0:T(8,128)(2,1)S(1)}, u32[]{:S(2)}, u32[]{:S(2)}) collective-permute-start(bf16[64,1152]{1,0:T(8,128)(2,1)S(1)} %get-tuple-element.60), channel_id=1, source_target_pairs={{0,1},{1,0},{2,3},{3,2},{4,5},{5,4},{6,7},{7,6},{8,9},{9,8},{10,11... | collective-permute-start | bytes 442376 | tf_op jit(solution)/shard_map/ppermute | solution.py:706

commit v3 on v2

--- a/solution.py
+++ b/solution.py
@@ -232,64 +232,69 @@
                         pairs[o, rows, columns] = jnp.zeros((ch, ch), BF16)
 
 
-def prepare_kernel(
-    patch_any, qkv_any, first_any, second_any, folded_ref, pairs_one, pairs_two, patch_ref,
-    qkv_ref, first_ref, second_ref, sems,
-):
+def prepare_kernel(patch_any, first_any, second_any, pairs_one, pairs_two, patch_ref, centered_ref, first_ref, second_ref, sems):
     copies = [
-        pltpu.make_async_copy(patch_any, patch_ref, sems.at[0]),
-        pltpu.make_async_copy(qkv_any.at[:, pl.ds(0, D)], qkv_ref.at[0], sems.at[1]),
-        pltpu.make_async_copy(first_any, first_ref, sems.at[2]),
-        pltpu.make_async_copy(second_any, second_ref, sems.at[3]),
-        pltpu.make_async_copy(qkv_any.at[:, pl.ds(D, D)], qkv_ref.at[1], sems.at[4]),
-        pltpu.make_async_copy(qkv_any.at[:, pl.ds(2 * D, D)], qkv_ref.at[2], sems.at[5]),
+        pltpu.make_async_copy(first_any, first_ref, sems.at[0]),
+        pltpu.make_async_copy(second_any, second_ref, sems.at[1]),
+        pltpu.make_async_copy(patch_any, patch_ref, sems.at[2]),
     ]
     for copy in copies:
         copy.start()
     copies[0].wait()
+    pair_weights(first_ref, pairs_one)
+    copies[1].wait()
+    pair_weights(second_ref, pairs_two)
+    copies[2].wait()
     patch = patch_ref[...].astype(F32)
-    centered = (patch - jnp.mean(patch, axis=1, keepdims=True)).astype(BF16)
-
-    def fold(part):
-        product = lax.dot_general(qkv_ref[part], centered, TN, preferred_element_type=F32)
-        folded_ref[part * D : (part + 1) * D] = product.astype(BF16)
-
-    copies[1].wait()
-    copies[2].wait()
-    fold(0)
-    pair_weights(first_ref, pairs_one)
-    copies[3].wait()
-    copies[4].wait()
-    fold(1)
-    pair_weights(second_ref, pairs_two)
-    copies[5].wait()
-    fold(2)
-
-
-def prepare(patch_weight, qkv_weight, conv_first, conv_second):
-    inner = patch_weight.shape[0]
+    centered_ref[...] = (patch - jnp.mean(patch, axis=1, keepdims=True)).astype(BF16)
+
+
+def prepare(patch_weight, conv_first, conv_second):
     ch = conv_first.shape[-1]
     pairs = jax.ShapeDtypeStruct((3, 12 * ch, 2 * ch), BF16)
+    patch = jax.ShapeDtypeStruct(patch_weight.shape, BF16)
     return pl.pallas_call(
         prepare_kernel,
-        out_shape=(
-            jax.ShapeDtypeStruct((3 * D, inner), BF16),
-            pairs,
-            pairs,
-            jax.ShapeDtypeStruct(patch_weight.shape, BF16),
-        ),
-        in_specs=[ANY] * 4,
+        out_shape=(pairs, pairs, patch, patch),
+        in_specs=[ANY] * 3,
         out_specs=(VMEM,) * 4,
         scratch_shapes=[
-            pltpu.VMEM((3, D, D), BF16),
             pltpu.VMEM(conv_first.shape, BF16),
             pltpu.VMEM(conv_first.shape, BF16),
-            pltpu.SemaphoreType.DMA((6,)),
+            pltpu.SemaphoreType.DMA((3,)),
         ],
         compiler_params=params(),
         name="prepare",
-        cost_estimate=pl.CostEstimate(flops=2 * inner * D * 3 * D, bytes_accessed=12 << 20, transcendentals=0),
-    )(patch_weight, qkv_weight, conv_first, conv_second)
+        cost_estimate=pl.CostEstimate(flops=1 << 31, bytes_accessed=6 << 20, transcendentals=0),
+    )(patch_weight, conv_first, conv_second)
+
+
+def fold_kernel(centered_ref, qkv_any, folded_ref, query_ref, qkv_ref, sems):
+    copies = [
+        pltpu.make_async_copy(qkv_any.at[:, pl.ds(D * (i + 1), D)], qkv_ref.at[i], sems.at[i]) for i in range(2)
+    ]
+    copies.append(pltpu.make_async_copy(qkv_any.at[:, pl.ds(0, D)], query_ref, sems.at[2]))
+    for copy in copies:
+        copy.start()
+    for part in range(2):
+        copies[part].wait()
+        product = lax.dot_general(qkv_ref[part], centered_ref[...], TN, preferred_element_type=F32)
+        folded_ref[part * D : (part + 1) * D] = product.astype(BF16)
+    copies[2].wait()
+
+
+def fold(centered, qkv_weight):
+    inner = centered.shape[0]
+    return pl.pallas_call(
+        fold_kernel,
+        out_shape=(jax.ShapeDtypeStruct((2 * D, inner), BF16), jax.ShapeDtypeStruct((D, D), BF16)),
+        in_specs=[VMEM, ANY],
+        out_specs=(VMEM, VMEM),
+        scratch_shapes=[pltpu.VMEM((2, D, D), BF16), pltpu.SemaphoreType.DMA((3,))],
+        compiler_params=params(),
+        name="fold",
+        cost_estimate=pl.CostEstimate(flops=2 * inner * D * 2 * D, bytes_accessed=12 << 20, transcendentals=0),
+    )(centered, qkv_weight)
 
 
 def frame_taps(counts_ref, frames):
@@ -407,15 +412,14 @@
     mine = inside == jnp.where(position % 2 == 0, 1, 0)
     keep = jnp.where(mine, low, high).astype(BF16)
     send = jnp.where(mine, high, low).astype(BF16)
-    for tile in range(4):
-        keep_ref[tile * half : (tile + 1) * half] = keep[:, tile * ch : (tile + 1) * ch]
-        send_ref[tile * half : (tile + 1) * half] = send[:, tile * ch : (tile + 1) * ch]
+    keep_ref[...] = keep
+    send_ref[...] = send
 
 
 def convolve(counts, lengths, clip, before, after, pairs_one, pairs_two, patch_weight):
     frames, _, cols, ch = clip.shape
     tokens = frames * cols // 2
-    out = jax.ShapeDtypeStruct((2 * tokens, ch), BF16)
+    out = jax.ShapeDtypeStruct((tokens // 2, 4 * ch), BF16)
     return pl.pallas_call(
         conv_kernel,
         out_shape=(out, out),
@@ -471,20 +475,6 @@
     upper = inside != jnp.where(core == 0, 1, 0)
     token = jnp.where(upper, token + 4 * size * q_cols, token)
     return jnp.where(token < bound, 1.0, -1.0)
-
-
-def block_tokens(ref, ch=128, half=64):
-    second = 4 * half + 5 * SLOT
-    parts = []
-    for base in (0, second):
-        parts.append(
-            jnp.concatenate([ref[base + t * half : base + (t + 1) * half] for t in range(4)], axis=1)
-        )
-    return jnp.concatenate(parts, axis=0)
-
-
-def half_tokens(ref, half=64):
-    return jnp.concatenate([ref[t * half : (t + 1) * half] for t in range(4)], axis=1)
 
 
 def normed_heads(part, gain):
@@ -537,75 +527,66 @@
     ]
 
 
-def own_kernel(lengths_ref, block_ref, folded_ref, query_gain_ref, key_gain_ref, queries_ref, acc_ref, *scratch):
-    tokens = block_tokens(block_ref)
-    count = tokens.shape[0]
+def query_kernel(lengths_ref, block_ref, centered_ref, query_ref, query_gain_ref, queries_ref):
+    normed = jnp.dot(block_ref[...], centered_ref[...], preferred_element_type=F32).astype(BF16)
+    part = jnp.dot(normed, query_ref[...], preferred_element_type=F32).T
+    count = part.shape[1]
     sides = window_sides(lengths_ref, lax.axis_index("seq") // 2, count)
-    part = lax.dot_general(folded_ref[:D], tokens, NT, preferred_element_type=F32)
     queries = normed_heads(part, query_gain_ref[...])
     row = lax.broadcasted_iota(jnp.int32, (8, count), 0)
     tail = jnp.where(row == 0, MASK * sides, jnp.where(row == 1, -MASK, 0.0))
     for h in range(HEADS):
         queries_ref[h] = jnp.concatenate([queries[h], tail], axis=0).T.astype(BF16)
-    attend(tokens, sides, folded_ref.at[D:], key_gain_ref[...], queries_ref, acc_ref, *scratch)
-
-
-def step_kernel(step, lengths_ref, ahead_ref, behind_ref, folded_ref, key_gain_ref, queries_ref, acc_ref, *scratch):
+
+
+def make_queries(lengths, block, centered, query_weight, query_gain):
+    return pl.pallas_call(
+        query_kernel,
+        out_shape=jax.ShapeDtypeStruct((HEADS, 128, SLOT), BF16),
+        in_specs=[SMEM] + [VMEM] * 4,
+        out_specs=VMEM,
+        compiler_params=params(),
+        name="queries",
+        cost_estimate=pl.CostEstimate(flops=1 << 30, bytes_accessed=4 << 20, transcendentals=0),
+    )(lengths, block, centered, query_weight, query_gain)
+
+
+def step_kernel(offsets, lengths_ref, *refs):
+    blocks = refs[: len(offsets)]
+    folded_ref, key_gain_ref, queries_ref, acc_ref, *scratch = refs[len(offsets) :]
     place = ring_place()
-    if step < 4:
-        tokens = jnp.concatenate([block_tokens(ahead_ref), block_tokens(behind_ref)], axis=0)
-        sides = jnp.concatenate(
-            [
-                window_sides(lengths_ref, chip_at(place - step), 128),
-                window_sides(lengths_ref, chip_at(place + step), 128),
-            ],
-            axis=1,
-        )
-    else:
-        tokens = jnp.concatenate([half_tokens(ahead_ref), half_tokens(behind_ref)], axis=0)
-        sides = window_sides(lengths_ref, chip_at(place + step), 128)
-    attend(tokens, sides, folded_ref.at[D:], key_gain_ref[...], queries_ref, acc_ref, *scratch)
+    tokens = jnp.concatenate([ref[...] for ref in blocks], axis=0)
+    sides = jnp.concatenate(
+        [window_sides(lengths_ref, chip_at(place + offset), 128) for offset in dict.fromkeys(offsets)], axis=1
+    )
+    attend(tokens, sides, folded_ref, key_gain_ref[...], queries_ref, acc_ref, *scratch)
 
 
 ACC = jax.ShapeDtypeStruct((HEADS, SLOT, 128), F32)
 
 
-def cost(count):
+def step_attention(offsets, lengths, blocks, folded, key_gain, queries):
+    count = sum(block.shape[0] for block in blocks)
     flops = 2 * count * 2 * D * 512 + 4 * HEADS * 128 * 128 * count
-    return pl.CostEstimate(flops=2 * flops, bytes_accessed=5 << 20, transcendentals=HEADS * 128 * count)
-
-
-def own_attention(lengths, block, folded, query_gain, key_gain):
     return pl.pallas_call(
-        own_kernel,
-        out_shape=(jax.ShapeDtypeStruct((HEADS, 128, SLOT), BF16), ACC),
-        in_specs=[SMEM] + [VMEM] * 4,
-        out_specs=(VMEM, VMEM),
-        scratch_shapes=attend_scratch(128),
-        compiler_params=params(),
-        name="own_attention",
-        cost_estimate=cost(192),
-    )(lengths, block, folded, query_gain, key_gain)
-
-
-def step_attention(step, lengths, ahead, behind, folded, key_gain, queries):
-    return pl.pallas_call(
-        functools.partial(step_kernel, step),
+        functools.partial(step_kernel, offsets),
         out_shape=ACC,
-        in_specs=[SMEM] + [VMEM] * 5,
+        in_specs=[SMEM] + [VMEM] * (len(blocks) + 3),
         out_specs=VMEM,
-        scratch_shapes=attend_scratch(256 if step < 4 else 128),
+        scratch_shapes=attend_scratch(count),
         compiler_params=params(),
         name="step_attention",
-        cost_estimate=cost(256 if step < 4 else 128),
-    )(lengths, ahead, behind, folded, key_gain, queries)
+        cost_estimate=pl.CostEstimate(flops=2 * flops, bytes_accessed=5 << 20, transcendentals=HEADS * 128 * count),
+    )(lengths, *blocks, folded, key_gain, queries)
+
+
+RING = (0, -1, 1, -2, 2, -3, 3, 4)
 
 
 def out_kernel(parts, *refs):
     acc_refs = refs[:parts]
-    block_refs = refs[parts:-3]
+    weight_refs = refs[parts:-3]
     keep_ref, send_ref, mixed_ref = refs[-3:]
-    zeros = jnp.zeros((SLOT - HD, 128), F32)
     for h in range(HEADS):
         peaks = [acc[h, HD + 1 : HD + 2] for acc in acc_refs]
         peak = functools.reduce(jnp.maximum, peaks)
@@ -613,51 +594,35 @@
         for acc, own in zip(acc_refs, peaks):
             term = acc[h] * jnp.exp2(own - peak)
             total = term if total is None else total + term
-        mixed = total[:HD] / total[HD : HD + 1]
-        mixed_ref[h] = jnp.concatenate([mixed, zeros], axis=0)
+        mixed_ref[h] = total[:HD] / total[HD : HD + 1]
     place = ring_place()
     core = lax.axis_index("seq") % 2
-    offsets = [0, -1, 1, -2, 2, -3, 3, 4]
-    per_core = len(block_refs) // 2
-    slots, tiles = [], []
+    lefts = []
     for side in range(2):
-        refs_here = block_refs[side * per_core : (side + 1) * per_core]
-        for index, offset in enumerate(offsets):
-            head = 2 * chip_at(place + offset) + jnp.where(core == side, 0, 1)
-            slots.append(mixed_ref[head])
-            if index < 7:
-                low, high, base = refs_here[index], refs_here[index], 256 + 5 * SLOT + 256
-            else:
-                low, high, base = refs_here[7], refs_here[8], 256
-            tiles.append(
-                [low[256 + t * SLOT : 256 + (t + 1) * SLOT] for t in range(5)]
-                + [high[base + t * SLOT : base + (t + 1) * SLOT] for t in range(4)]
-            )
-    left = jnp.concatenate(slots, axis=0).T.astype(BF16)
+        heads = [2 * chip_at(place + offset) + jnp.where(core == side, 0, 1) for offset in RING]
+        lefts.append(jnp.concatenate([mixed_ref[head] for head in heads], axis=0).T.astype(BF16))
     half = keep_ref.shape[0]
-    for first in range(0, 9, 2):
-        group = range(first, min(first + 2, 9))
-        right = jnp.concatenate(
-            [jnp.concatenate([block[t] for block in tiles], axis=0) for t in group], axis=1
-        )
-        result = jnp.dot(left, right, preferred_element_type=F32).astype(BF16)
-        columns = slice(first * 128, (group[-1] + 1) * 128)
+    for first in range(0, D, 256):
+        columns = slice(first, min(first + 256, D))
+        result = jnp.dot(lefts[0], weight_refs[0][:, columns], preferred_element_type=F32)
+        result = result + jnp.dot(lefts[1], weight_refs[1][:, columns], preferred_element_type=F32)
+        result = result.astype(BF16)
         keep_ref[:, columns] = result[:half]
         send_ref[:, columns] = result[half:]
 
 
-def project_out(accs, blocks):
+def project_out(accs, weights):
     out = jax.ShapeDtypeStruct((64, D), BF16)
     return pl.pallas_call(
         functools.partial(out_kernel, len(accs)),
         out_shape=(out, out),
-        in_specs=[VMEM] * (len(accs) + len(blocks)),
+        in_specs=[VMEM] * (len(accs) + len(weights)),
         out_specs=(VMEM, VMEM),
-        scratch_shapes=[pltpu.VMEM((HEADS, SLOT, 128), F32)],
+        scratch_shapes=[pltpu.VMEM((HEADS, HD, 128), F32)],
         compiler_params=params(),
         name="project_out",
         cost_estimate=pl.CostEstimate(flops=2 * 128 * 1280 * D, bytes_accessed=4 << 20, transcendentals=0),
-    )(*accs, *blocks)
+    )(*accs, *weights)
 
 
 def merge_kernel(lengths_ref, keep_ref, got_ref, out_ref):
@@ -686,11 +651,6 @@
     )(lengths, keep, got)
 
 
-def weight_tiles(out_weight):
-    padded = jnp.pad(out_weight, ((0, SLOT - HD), (0, 0)))
-    return padded.reshape(SLOT, 9, 128).transpose(1, 0, 2).reshape(9 * SLOT, 128)
-
-
 def shards(
     clip, frame_counts, conv_first, conv_second, patch_weight, qkv_weight, query_gain, key_gain,
     out_weight, window_lengths,
@@ -708,41 +668,52 @@
     def tied(*arrays):
         return lax.optimization_barrier(arrays)
 
+    def tied(*arrays):
+        return lax.optimization_barrier(arrays)
+
+    def both_ways(ahead, behind):
+        return send(ahead, forward), send(behind, backward)
+
     before = send(clip, up)
     after = send(clip, down)
     score_scale = math.log2(math.e) / math.sqrt(HD)
-    query_rows = jnp.broadcast_to((query_gain * score_scale)[:, None], (HD, 256))
+    query_rows = jnp.broadcast_to((query_gain * score_scale)[:, None], (HD, 128))
     key_rows = jnp.broadcast_to(key_gain[:, None], (HD, 256))
-    weight = weight_tiles(out_weight)
-    folded, pairs_one, pairs_two, patch = prepare(patch_weight, qkv_weight, conv_first, conv_second)
-    before, after, pairs_one, weight, query_rows, key_rows = tied(
-        before, after, pairs_one, weight, query_rows, key_rows
-    )
+    weight_one = both_ways(out_weight, out_weight)
+    pairs_one, pairs_two, patch, centered = prepare(patch_weight, conv_first, conv_second)
+    before, after, *weight_one, pairs_one, query_rows, key_rows = tied(
+        before, after, *weight_one, pairs_one, query_rows, key_rows
+    )
+    weight_two = both_ways(*weight_one)
     keep, other = convolve(
         frame_counts, window_lengths, clip, before, after, pairs_one, pairs_two, patch
     )
     got = send(other, cores)
-    cut = 256 + 5 * SLOT
-    block = jnp.concatenate([keep, weight[: 5 * SLOT], got, weight[5 * SLOT :]], axis=0)
-    ahead, behind = block, block
-    accs, blocks, sibling = [], [block], []
-    for step in range(1, 5):
-        if step < 4:
-            ahead_next, behind_next = send(ahead, forward), send(behind, backward)
-        else:
-            ahead_next, behind_next = send(ahead[:cut], forward), send(behind[cut:], backward)
-        if step == 1:
-            sibling.append(send(block, cores))
-            queries, acc = own_attention(window_lengths, block, folded, query_rows, key_rows)
-        else:
-            sibling += [send(ahead, cores), send(behind, cores)]
-            acc = step_attention(step - 1, window_lengths, ahead, behind, folded, key_rows, queries)
-        ahead, behind, acc = tied(ahead_next, behind_next, acc)
-        accs.append(acc)
-        blocks += [ahead, behind]
-    sibling += [send(ahead, cores), send(behind, cores)]
-    accs.append(step_attention(4, window_lengths, ahead, behind, folded, key_rows, queries))
-    keep_rows, send_rows = project_out(accs, blocks + sibling)
+    got, *weight_two = tied(got, *weight_two)
+    block = jnp.concatenate([keep, got], axis=0)
+    one = both_ways(block, block)
+    weight_three = both_ways(*weight_two)
+    folded, query_weight = fold(tied(centered, block)[0], qkv_weight)
+    *one, folded, = tied(*one, folded)
+    *one, weight_three_a, weight_three_b = tied(*one, *weight_three)
+    two = both_ways(*one)
+    cut = 40
+    weight_four = both_ways(weight_three_a[:cut], weight_three_b[cut:])
+    queries = make_queries(window_lengths, block, centered, query_weight, query_rows)
+    acc_one = step_attention((-1, 1), window_lengths, one, folded, key_rows, queries)
+    *two, acc_one = tied(*two, acc_one)
+    three = both_ways(*two)
+    acc_two = step_attention((-2, 2), window_lengths, two, folded, key_rows, queries)
+    *three, acc_two, wf_a, wf_b = tied(*three, acc_two, *weight_four)
+    weights = jnp.concatenate(
+        [out_weight, *weight_one, *weight_two, weight_three_a, weight_three_b, wf_a, wf_b], axis=0
+    )
+    four = both_ways(three[0][:64], three[1][64:])
+    sibling = send(weights, cores)
+    acc_three = step_attention((-3, 3), window_lengths, three, folded, key_rows, queries)
+    *four, acc_three = tied(*four, acc_three)
+    acc_four = step_attention((0, 4, 4), window_lengths, [block, *four], folded, key_rows, queries)
+    keep_rows, send_rows = project_out((acc_one, acc_two, acc_three, acc_four), (weights, sibling))
     return merge(window_lengths, keep_rows, send(send_rows, cores))
 
 

time: 72 us -> 64.7 us (0.90)
  waiting for transfers between devices: 21.3 us -> 10.8 us
  starting transfers between devices: 18.4 us -> 24.2 us
  Pallas kernels: 26.9 us -> 23.4 us
    ppermute x21, waiting for transfers between devices: 21.3 us -> 10.8 us  [send(): return lax.ppermute(array, 'seq', pairs)]
    ppermute x21, starting transfers between devices: 18.4 us -> 24.2 us  [send(): return lax.ppermute(array, 'seq', pairs)]
    pallas_call x6 -> x7, Pallas kernels: 20.9 us -> 17.5 us  [the longest x4 10.2 us: step_attention(): pl.pallas_call(functools.partial(step_kernel, offsets), out_shape=ACC, in...]
    unnamed x16 -> x27, local copies, waits for them, and re-layouts: 3.62 us -> 4.78 us
    pad x1 -> x0, local copies, waits for them, and re-layouts: 0.93 us -> none  [weight_tiles(): padded = jnp.pad(out_weight, ((0, SLOT - HD), (0, 0)))]
  transfers between devices with their start and end apart: 21 -> 21, of which waited for: 9 -> 6; matrix products, arithmetic and copies ran while one was open for 2% -> 3% of each run, Pallas kernels for 29% -> 27%
where the time goes in v3:
time: 64.7 us; the launch traced here: 64.4 us
  starting transfers between devices  24.2 us (37%)
  Pallas kernels  23.4 us (36%)
  waiting for transfers between devices  10.8 us (17%)
  local copies, waits for them, and re-layouts  4.96 us (8%)
  other arithmetic  0.66 us (1%)
    ppermute x21, starting transfers between devices, send(): return lax.ppermute(array, 'seq', pairs)  24.2 us
    ppermute x21, waiting for transfers between devices, send(): return lax.ppermute(array, 'seq', pairs)  10.8 us
    pallas_call x4, Pallas kernels, step_attention(): pl.pallas_call(functools.partial(step_kernel, offsets), out_shape=ACC, in...  10.2 us
    unnamed x27, local copies, waits for them, and re-layouts  4.78 us
    pallas_call x1, Pallas kernels, fold(): pl.pallas_call(fold_kernel, out_shape=(jax.ShapeDtypeStruct((2 * D, inner...  4.12 us
    pallas_call x1, Pallas kernels, convolve(): pl.pallas_call(conv_kernel, out_shape=(out, out), in_specs=[ANY] * 3 + [V...  3.65 us
    pallas_call x1, Pallas kernels, prepare(): pl.pallas_call(prepare_kernel, out_shape=(pairs, pairs, patch, patch), in...  1.61 us
    pallas_call x1, Pallas kernels, make_queries(): pl.pallas_call(query_kernel, out_shape=jax.ShapeDtypeStruct((HEADS, 128,...  1.53 us
  transfers between devices with their start and end apart: 21, of which 6 were waited for; matrix products, arithmetic and copies ran while one was open for 3% of the time, Pallas kernels for 27%

profile of v3, /device:TPU:0, one launch (start us, length us, event | category | flops | bytes accessed | tf_op | source)
XLA Modules:
  0.0 64.4 jit_solution(13923477258353387611)
XLA Ops:
  0.0 2.4 %collective-permute-start = (bf16[8,2,32,128]{3,2,1,0:T(8,128)(2,1)}, bf16[8,2,32,128]{3,2,1,0:T(8,128)(2,1)S(1)}, u32[]{:S(2)}, u32[]{:S(2)}) collective-permute-start(bf16[8,2,32,128]{3,2,1,0:T(8,128)(2,1)} %own_any.1), channel_id=1, source_target_pairs={{0,1},{1,2},{2,3},{3,4},{4,5},{5,6},{6,7},{7,8},{8,9},{9,10},{10,1... | collective-permute-start | bytes 393224 | tf_op jit(solution)/shard_map/ppermute | solution.py:666
  2.4 1.3 %collective-permute-start.1 = (bf16[8,2,32,128]{3,2,1,0:T(8,128)(2,1)}, bf16[8,2,32,128]{3,2,1,0:T(8,128)(2,1)S(1)}, u32[]{:S(2)}, u32[]{:S(2)}) collective-permute-start(bf16[8,2,32,128]{3,2,1,0:T(8,128)(2,1)} %own_any.1), channel_id=1, source_target_pairs={{1,0},{2,1},{3,2},{4,3},{5,4},{6,5},{7,6},{8,7},{9,8},{10,9},{11,1... | collective-permute-start | bytes 393224 | tf_op jit(solution)/shard_map/ppermute | solution.py:666
  3.7 5.9 %collective-permute-start.2 = (bf16[72,1152]{1,0:T(8,128)(2,1)}, bf16[72,1152]{1,0:T(8,128)(2,1)S(1)}, u32[]{:S(2)}, u32[]{:S(2)}) collective-permute-start(bf16[72,1152]{1,0:T(8,128)(2,1)} %param.18), channel_id=1, source_target_pairs={{0,4},{1,5},{4,8},{5,9},{8,12},{9,13},{12,14},{13,15},{14,10},{15,... | collective-permute-start | bytes 497672 | tf_op jit(solution)/shard_map/ppermute | solution.py:666
  9.5 1.0 %constant_dynamic-update-slice_fusion.10 = bf16[576,1152]{1,0:T(8,128)(2,1)S(1)} fusion(bf16[72,1152]{1,0:T(8,128)(2,1)} %param.18), kind=kLoop, calls=%fused_computation.10 | loop fusion | bytes 331776
  10.5 0.7 %broadcast_multiply_fusion = f32[72]{0:T(128)S(1)} fusion(f32[72]{0:T(128)} %param.16), kind=kLoop, calls=%fused_computation.11 | loop fusion | flops 72 | bytes 576 | tf_op jit(solution)/shard_map/mul | solution.py:680
  11.2 1.3 %copy-done.1 = bf16[512,1152]{1,0:T(8,128)(2,1)S(1)} copy-done((bf16[512,1152]{1,0:T(8,128)(2,1)S(1)}, bf16[512,1152]{1,0:T(8,128)(2,1)}, u32[]{:S(2)}) %copy-start.1) | copy-done | bytes 1179672
  12.5 1.2 %copy-done.2 = bf16[3,3,3,128,128]{4,3,2,1,0:T(8,128)(2,1)S(1)} copy-done((bf16[3,3,3,128,128]{4,3,2,1,0:T(8,128)(2,1)S(1)}, bf16[3,3,3,128,128]{4,3,2,1,0:T(8,128)(2,1)}, u32[]{:S(2)}) %copy-start.2) | copy-done | bytes 884760
  13.6 1.2 %copy-done.3 = bf16[3,3,3,128,128]{4,3,2,1,0:T(8,128)(2,1)S(1)} copy-done((bf16[3,3,3,128,128]{4,3,2,1,0:T(8,128)(2,1)S(1)}, bf16[3,3,3,128,128]{4,3,2,1,0:T(8,128)(2,1)}, u32[]{:S(2)}) %copy-start.3) | copy-done | bytes 884760
  14.8 1.6 %prepare.1 = (bf16[3,1536,256]{2,1,0:T(8,128)(2,1)S(1)}, bf16[3,1536,256]{2,1,0:T(8,128)(2,1)S(1)}, bf16[512,1152]{1,0:T(8,128)(2,1)S(1)}, bf16[512,1152]{1,0:T(8,128)(2,1)S(1)}) custom-call(bf16[512,1152]{1,0:T(8,128)(2,1)S(1)} %copy-done.1, bf16[3,3,3,128,128]{4,3,2,1,0:T(8,128)(2,1)S(1)} %copy-done.2, bf16[3,3,3,128,128]{4,3,2,1,0:T(8,128)(2,1)S(1)} %copy-done.3), custom_call_target="tpu_custom_call" | custom-call | flops 2147483648 | bytes 6291456 | tf_op jit(solution)/shard_map/prepare/pallas_call | solution.py:256
  16.5 0.1 broadcast_in_dim.4.query_gain_ref
  16.6 0.1 broadcast_in_dim.5.refs_3_.refs_4_
  16.6 0.0 copy-done
  16.7 3.6 %convolve.1 = (bf16[64,512]{1,0:T(8,128)(2,1)S(1)}, bf16[64,512]{1,0:T(8,128)(2,1)S(1)}) custom-call(s32[3]{0:T(128)S(1)} %copy-done.5, s32[1,3]{1,0:T(1,128)S(1)} %copy-done, bf16[8,2,32,128]{3,2,1,0:T(8,128)(2,1)S(1)} %copy-done.4, bf16[8,2,32,128]{3,2,1,0:T(8,128)(2,1)S(1)} %collective-permute-done.before_ref, ...), custom_call_target="tpu_custom_call" | custom-call | flops 2147483648 | bytes 4194304 | tf_op jit(solution)/shard_map/convolve/pallas_call | solution.py:423
  20.4 0.1 collective-permute-start.4
  20.4 2.0 %collective-permute-start.5 = (bf16[72,1152]{1,0:T(8,128)(2,1)S(1)}, bf16[72,1152]{1,0:T(8,128)(2,1)S(1)}, u32[]{:S(2)}, u32[]{:S(2)}) collective-permute-start(bf16[72,1152]{1,0:T(8,128)(2,1)S(1)} %collective-permute-done.2), channel_id=1, source_target_pairs={{0,4},{1,5},{4,8},{5,9},{8,12},{9,13},{12,14},{13,15},{14,10},{15,... | collective-permute-start | bytes 497672 | tf_op jit(solution)/shard_map/ppermute | solution.py:666
  22.5 0.0 collective-permute-start.6
  22.6 4.5 %collective-permute-done.5 = bf16[72,1152]{1,0:T(8,128)(2,1)S(1)} collective-permute-done((bf16[72,1152]{1,0:T(8,128)(2,1)S(1)}, bf16[72,1152]{1,0:T(8,128)(2,1)S(1)}, u32[]{:S(2)}, u32[]{:S(2)}) %collective-permute-start.5) | collective-permute-done | bytes 165920 | tf_op jit(solution)/shard_map/ppermute | solution.py:666
  27.1 1.7 %collective-permute-done.6 = bf16[72,1152]{1,0:T(8,128)(2,1)S(1)} collective-permute-done((bf16[72,1152]{1,0:T(8,128)(2,1)S(1)}, bf16[72,1152]{1,0:T(8,128)(2,1)S(1)}, u32[]{:S(2)}, u32[]{:S(2)}) %collective-permute-start.6) | collective-permute-done | bytes 165920 | tf_op jit(solution)/shard_map/ppermute | solution.py:666
  28.8 1.6 %collective-permute-start.7 = (bf16[128,512]{1,0:T(8,128)(2,1)S(1)}, bf16[128,512]{1,0:T(8,128)(2,1)S(1)}, u32[]{:S(2)}, u32[]{:S(2)}) collective-permute-start(bf16[128,512]{1,0:T(8,128)(2,1)S(1)} %constant_dynamic-update-slice_fusion.block_ref.refs_0_), channel_id=1, source_target_pairs={{0,4},{1,5},{4,8},{5,9},{8,12},{9,13},{12,14},{13,15},{14,10},{15,... | collective-permute-start | bytes 393224 | tf_op jit(solution)/shard_map/ppermute | solution.py:666
  30.4 0.5 collective-permute-start.8
  30.8 1.6 %collective-permute-start.9 = (bf16[72,1152]{1,0:T(8,128)(2,1)S(1)}, bf16[72,1152]{1,0:T(8,128)(2,1)S(1)}, u32[]{:S(2)}, u32[]{:S(2)}) collective-permute-start(bf16[72,1152]{1,0:T(8,128)(2,1)S(1)} %collective-permute-done.5), channel_id=1, source_target_pairs={{0,4},{1,5},{4,8},{5,9},{8,12},{9,13},{12,14},{13,15},{14,10},{15,... | collective-permute-start | bytes 497672 | tf_op jit(solution)/shard_map/ppermute | solution.py:666
  32.4 0.5 collective-permute-start.10
  32.9 4.1 %fold.1 = (bf16[2304,512]{1,0:T(8,128)(2,1)S(1)}, bf16[1152,1152]{1,0:T(8,128)(2,1)S(1)}) custom-call(bf16[512,1152]{1,0:T(8,128)(2,1)S(1)} %get-tuple-element.56.centered_ref, bf16[1152,3456]{1,0:T(8,128)(2,1)S(1)} %bitcast.1), custom_call_target="tpu_custom_call" | custom-call | flops 2717908992 | bytes 12582912 | tf_op jit(solution)/shard_map/fold/pallas_call | solution.py:288
  37.1 1.5 %queries.1.refs_4_.refs_5_ = bf16[16,128,80]{2,1,0:T(8,128)(2,1)S(1)} custom-call(s32[1,3]{1,0:T(1,128)S(1)} %copy-done, bf16[128,512]{1,0:T(8,128)(2,1)S(1)} %constant_dynamic-update-slice_fusion.block_ref.refs_0_, bf16[512,1152]{1,0:T(8,128)(2,1)S(1)} %get-tuple-element.56.centered_ref, bf16[1152,1152]{1,0:T(8,128)(2,1)S(1)} %get-tuple-element.66.query_ref, ...), custom_call_target="tpu_custom_call" | custom-call | flops 1073741824 | bytes 4194304 | tf_op jit(solution)/shard_map/queries/pallas_call | solution.py:543
  38.6 1.6 %collective-permute-start.11 = (bf16[128,512]{1,0:T(8,128)(2,1)S(1)}, bf16[128,512]{1,0:T(8,128)(2,1)S(1)}, u32[]{:S(2)}, u32[]{:S(2)}) collective-permute-start(bf16[128,512]{1,0:T(8,128)(2,1)S(1)} %collective-permute-done.7.refs_0_), channel_id=1, source_target_pairs={{0,4},{1,5},{4,8},{5,9},{8,12},{9,13},{12,14},{13,15},{14,10},{15,... | collective-permute-start | bytes 393224 | tf_op jit(solution)/shard_map/ppermute | solution.py:666
  40.3 0.5 collective-permute-start.12
  40.7 1.6 %collective-permute-start.15 = (bf16[40,1152]{1,0:T(8,128)(2,1)S(1)}, bf16[40,1152]{1,0:T(8,128)(2,1)S(1)}, u32[]{:S(2)}, u32[]{:S(2)}) collective-permute-start(bf16[40,1152]{1,0:T(8,128)(2,1)S(1)} %slice.12), channel_id=1, source_target_pairs={{0,4},{1,5},{4,8},{5,9},{8,12},{9,13},{12,14},{13,15},{14,10},{15,... | collective-permute-start | bytes 276488 | tf_op jit(solution)/shard_map/ppermute | solution.py:666
  42.4 0.5 collective-permute-start.16
  42.9 2.6 %step_attention.4.refs_0_ = f32[16,80,128]{2,1,0:T(8,128)S(1)} custom-call(s32[1,3]{1,0:T(1,128)S(1)} %copy-done, bf16[128,512]{1,0:T(8,128)(2,1)S(1)} %collective-permute-done.7.refs_0_, bf16[128,512]{1,0:T(8,128)(2,1)S(1)} %collective-permute-done.8.refs_1_, bf16[2304,512]{1,0:T(8,128)(2,1)S(1)} %get-tuple-element.64.refs_2_.refs_3_, ...), custom_call_target="tpu_custom_call" | custom-call | flops 1744830464 | bytes 5242880 | tf_op jit(solution)/shard_map/step_attention/pallas_call | solution.py:571
  45.4 0.0 collective-permute-done.11.refs_0_
  45.4 1.6 %collective-permute-start.13 = (bf16[128,512]{1,0:T(8,128)(2,1)S(1)}, bf16[128,512]{1,0:T(8,128)(2,1)S(1)}, u32[]{:S(2)}, u32[]{:S(2)}) collective-permute-start(bf16[128,512]{1,0:T(8,128)(2,1)S(1)} %collective-permute-done.11.refs_0_), channel_id=1, source_target_pairs={{0,4},{1,5},{4,8},{5,9},{8,12},{9,13},{12,14},{13,15},{14,10},{15,... | collective-permute-start | bytes 393224 | tf_op jit(solution)/shard_map/ppermute | solution.py:666
  47.1 0.5 collective-permute-start.14
  47.5 2.6 %step_attention.5.refs_1_ = f32[16,80,128]{2,1,0:T(8,128)S(1)} custom-call(s32[1,3]{1,0:T(1,128)S(1)} %copy-done, bf16[128,512]{1,0:T(8,128)(2,1)S(1)} %collective-permute-done.11.refs_0_, bf16[128,512]{1,0:T(8,128)(2,1)S(1)} %collective-permute-done.12.refs_1_, bf16[2304,512]{1,0:T(8,128)(2,1)S(1)} %get-tuple-element.64.refs_2_.refs_3_, ...), custom_call_target="tpu_custom_call" | custom-call | flops 1744830464 | bytes 5242880 | tf_op jit(solution)/shard_map/step_attention/pallas_call | solution.py:571
  50.1 0.0 collective-permute-done.16
  50.1 0.4 collective-permute-done.13.refs_0_
  50.5 1.6 %collective-permute-done.14.refs_1_ = bf16[128,512]{1,0:T(8,128)(2,1)S(1)} collective-permute-done((bf16[128,512]{1,0:T(8,128)(2,1)S(1)}, bf16[128,512]{1,0:T(8,128)(2,1)S(1)}, u32[]{:S(2)}, u32[]{:S(2)}) %collective-permute-start.14) | collective-permute-done | bytes 131104 | tf_op jit(solution)/shard_map/ppermute | solution.py:666
  52.1 0.1 collective-permute-start.19
  52.2 1.6 %collective-permute-start.17 = (bf16[64,512]{1,0:T(8,128)(2,1)S(1)}, bf16[64,512]{1,0:T(8,128)(2,1)S(1)}, u32[]{:S(2)}, u32[]{:S(2)}) collective-permute-start(bf16[64,512]{1,0:T(8,128)(2,1)S(1)} %slice.14), channel_id=1, source_target_pairs={{0,4},{1,5},{4,8},{5,9},{8,12},{9,13},{12,14},{13,15},{14,10},{15,... | collective-permute-start | bytes 196616 | tf_op jit(solution)/shard_map/ppermute | solution.py:666
  53.8 0.4 collective-permute-start.18
  54.2 2.6 %step_attention.6.refs_2_ = f32[16,80,128]{2,1,0:T(8,128)S(1)} custom-call(s32[1,3]{1,0:T(1,128)S(1)} %copy-done, bf16[128,512]{1,0:T(8,128)(2,1)S(1)} %collective-permute-done.13.refs_0_, bf16[128,512]{1,0:T(8,128)(2,1)S(1)} %collective-permute-done.14.refs_1_, bf16[2304,512]{1,0:T(8,128)(2,1)S(1)} %get-tuple-element.64.refs_2_.refs_3_, ...), custom_call_target="tpu_custom_call" | custom-call | flops 1744830464 | bytes 5242880 | tf_op jit(solution)/shard_map/step_attention/pallas_call | solution.py:571
  56.8 0.0 collective-permute-done.17.refs_1_
  56.8 1.3 %collective-permute-done.18.refs_2_ = bf16[64,512]{1,0:T(8,128)(2,1)S(1)} collective-permute-done((bf16[64,512]{1,0:T(8,128)(2,1)S(1)}, bf16[64,512]{1,0:T(8,128)(2,1)S(1)}, u32[]{:S(2)}, u32[]{:S(2)}) %collective-permute-start.18) | collective-permute-done | bytes 65568 | tf_op jit(solution)/shard_map/ppermute | solution.py:666
  58.1 2.5 %step_attention.7.refs_3_ = f32[16,80,128]{2,1,0:T(8,128)S(1)} custom-call(s32[1,3]{1,0:T(1,128)S(1)} %copy-done, bf16[128,512]{1,0:T(8,128)(2,1)S(1)} %constant_dynamic-update-slice_fusion.block_ref.refs_0_, bf16[64,512]{1,0:T(8,128)(2,1)S(1)} %collective-permute-done.17.refs_1_, bf16[64,512]{1,0:T(8,128)(2,1)S(1)} %collective-permute-done.18.refs_2_, ...), custom_call_target="tpu_custom_call" | custom-call | flops 1744830464 | bytes 5242880 | tf_op jit(solution)/shard_map/step_attention/pallas_call | solution.py:571
  60.6 0.0 collective-permute-done.19.refs_5_
  60.6 1.0 %project_out.1 = (bf16[64,1152]{1,0:T(8,128)(2,1)S(1)}, bf16[64,1152]{1,0:T(8,128)(2,1)S(1)}) custom-call(f32[16,80,128]{2,1,0:T(8,128)S(1)} %step_attention.4.refs_0_, f32[16,80,128]{2,1,0:T(8,128)S(1)} %step_attention.5.refs_1_, f32[16,80,128]{2,1,0:T(8,128)S(1)} %step_attention.6.refs_2_, f32[16,80,128]{2,1,0:T(8,128)S(1)} %step_attention.7.refs_3_, ...), custom_call_target="tpu_custom_call" | custom-call | flops 377487360 | bytes 4194304 | tf_op jit(solution)/shard_map/project_out/pallas_call | solution.py:616
  61.6 0.1 collective-permute-start.20
  61.7 1.4 %collective-permute-done.20.got_ref = bf16[64,1152]{1,0:T(8,128)(2,1)S(1)} collective-permute-done((bf16[64,1152]{1,0:T(8,128)(2,1)S(1)}, bf16[64,1152]{1,0:T(8,128)(2,1)S(1)}, u32[]{:S(2)}, u32[]{:S(2)}) %collective-permute-start.20) | collective-permute-done | bytes 147488 | tf_op jit(solution)/shard_map/ppermute | solution.py:666
  63.0 1.3 %merge.1 = bf16[128,1152]{1,0:T(8,128)(2,1)} custom-call(s32[1,3]{1,0:T(1,128)S(1)} %copy-done, bf16[64,1152]{1,0:T(8,128)(2,1)S(1)} %get-tuple-element.81.keep_ref, bf16[64,1152]{1,0:T(8,128)(2,1)S(1)} %collective-permute-done.20.got_ref), custom_call_target="tpu_custom_call" | custom-call | tf_op jit(solution)/shard_map/merge/pallas_call | solution.py:644
  (41 shorter events, 0.3 us)
Async XLA Ops:
  0.0 16.5 %collective-permute-start = (bf16[8,2,32,128]{3,2,1,0:T(8,128)(2,1)}, bf16[8,2,32,128]{3,2,1,0:T(8,128)(2,1)S(1)}, u32[]{:S(2)}, u32[]{:S(2)}) collective-permute-start(bf16[8,2,32,128]{3,2,1,0:T(8,128)(2,1)} %own_any.1), channel_id=1, source_target_pairs={{0,1},{1,2},{2,3},{3,4},{4,5},{5,6},{6,7},{7,8},{8,9},{9,10},{10,1... | collective-permute-start | bytes 393224 | tf_op jit(solution)/shard_map/ppermute | solution.py:666
  2.4 14.1 %collective-permute-start.1 = (bf16[8,2,32,128]{3,2,1,0:T(8,128)(2,1)}, bf16[8,2,32,128]{3,2,1,0:T(8,128)(2,1)S(1)}, u32[]{:S(2)}, u32[]{:S(2)}) collective-permute-start(bf16[8,2,32,128]{3,2,1,0:T(8,128)(2,1)} %own_any.1), channel_id=1, source_target_pairs={{1,0},{2,1},{3,2},{4,3},{5,4},{6,5},{7,6},{8,7},{9,8},{10,9},{11,1... | collective-permute-start | bytes 393224 | tf_op jit(solution)/shard_map/ppermute | solution.py:666
  3.7 12.8 %collective-permute-start.2 = (bf16[72,1152]{1,0:T(8,128)(2,1)}, bf16[72,1152]{1,0:T(8,128)(2,1)S(1)}, u32[]{:S(2)}, u32[]{:S(2)}) collective-permute-start(bf16[72,1152]{1,0:T(8,128)(2,1)} %param.18), channel_id=1, source_target_pairs={{0,4},{1,5},{4,8},{5,9},{8,12},{9,13},{12,14},{13,15},{14,10},{15,... | collective-permute-start | bytes 497672 | tf_op jit(solution)/shard_map/ppermute | solution.py:666
  9.5 6.9 %collective-permute-start.3 = (bf16[72,1152]{1,0:T(8,128)(2,1)}, bf16[72,1152]{1,0:T(8,128)(2,1)S(1)}, u32[]{:S(2)}, u32[]{:S(2)}) collective-permute-start(bf16[72,1152]{1,0:T(8,128)(2,1)} %param.18), channel_id=1, source_target_pairs={{4,0},{5,1},{8,4},{9,5},{12,8},{13,9},{14,12},{15,13},{10,14},{11,... | collective-permute-start | bytes 497672 | tf_op jit(solution)/shard_map/ppermute | solution.py:666
  11.2 1.3 %copy-start.1 = (bf16[512,1152]{1,0:T(8,128)(2,1)S(1)}, bf16[512,1152]{1,0:T(8,128)(2,1)}, u32[]{:S(2)}) copy-start(bf16[512,1152]{1,0:T(8,128)(2,1)} %patch_any.1) | copy-start | bytes 3538948
  12.5 1.2 %copy-start.2 = (bf16[3,3,3,128,128]{4,3,2,1,0:T(8,128)(2,1)S(1)}, bf16[3,3,3,128,128]{4,3,2,1,0:T(8,128)(2,1)}, u32[]{:S(2)}) copy-start(bf16[3,3,3,128,128]{4,3,2,1,0:T(8,128)(2,1)} %first_any.1) | copy-start | bytes 2654212
  13.6 1.2 %copy-start.3 = (bf16[3,3,3,128,128]{4,3,2,1,0:T(8,128)(2,1)S(1)}, bf16[3,3,3,128,128]{4,3,2,1,0:T(8,128)(2,1)}, u32[]{:S(2)}) copy-start(bf16[3,3,3,128,128]{4,3,2,1,0:T(8,128)(2,1)} %second_any.1) | copy-start | bytes 2654212
  14.8 1.8 %copy-start.6 = (f32[72]{0:T(128)S(1)}, f32[72]{0:T(128)}, u32[]{:S(2)}) copy-start(f32[72]{0:T(128)} %param.17) | copy-start | bytes 868
  14.8 1.8 %copy-start = (s32[1,3]{1,0:T(1,128)S(1)}, s32[1,3]{1,0:T(1,128)}, u32[]{:S(2)}) copy-start(s32[1,3]{1,0:T(1,128)} %lengths_ref.11) | copy-start | bytes 40
  14.8 1.8 %copy-start.4 = (bf16[8,2,32,128]{3,2,1,0:T(8,128)(2,1)S(1)}, bf16[8,2,32,128]{3,2,1,0:T(8,128)(2,1)}, u32[]{:S(2)}) copy-start(bf16[8,2,32,128]{3,2,1,0:T(8,128)(2,1)} %own_any.1) | copy-start | bytes 393220
  14.8 1.9 %copy-start.5 = (s32[3]{0:T(128)S(1)}, s32[3]{0:T(128)}, u32[]{:S(2)}) copy-start(s32[3]{0:T(128)} %counts_any.1) | copy-start | bytes 40
  14.8 18.0 %slice-start = ((s8[7962624]{0:T(1024)(128)(4,1)}), s8[4194304]{0:T(1024)(128)(4,1)S(1)}, s32[]{:S(2)}) async-start(s8[7962624]{0:T(1024)(128)(4,1)} %bitcast), calls=%async_computation | async-start | bytes 8388608
  16.7 16.2 %slice-start.1 = ((s8[7962624]{0:T(1024)(128)(4,1)}), s8[3768320]{0:T(1024)(128)(4,1)S(1)}, s32[]{:S(2)}) async-start(s8[7962624]{0:T(1024)(128)(4,1)} %bitcast), calls=%async_computation.1 | async-start | bytes 7536640
  20.4 2.2 %collective-permute-start.4 = (bf16[64,512]{1,0:T(8,128)(2,1)S(1)}, bf16[64,512]{1,0:T(8,128)(2,1)S(1)}, u32[]{:S(2)}, u32[]{:S(2)}) collective-permute-start(bf16[64,512]{1,0:T(8,128)(2,1)S(1)} %get-tuple-element.51), channel_id=1, source_target_pairs={{0,1},{1,0},{2,3},{3,2},{4,5},{5,4},{6,7},{7,6},{8,9},{9,8},{10,11... | collective-permute-start | bytes 196616 | tf_op jit(solution)/shard_map/ppermute | solution.py:666
  20.4 6.6 %collective-permute-start.5 = (bf16[72,1152]{1,0:T(8,128)(2,1)S(1)}, bf16[72,1152]{1,0:T(8,128)(2,1)S(1)}, u32[]{:S(2)}, u32[]{:S(2)}) collective-permute-start(bf16[72,1152]{1,0:T(8,128)(2,1)S(1)} %collective-permute-done.2), channel_id=1, source_target_pairs={{0,4},{1,5},{4,8},{5,9},{8,12},{9,13},{12,14},{13,15},{14,10},{15,... | collective-permute-start | bytes 497672 | tf_op jit(solution)/shard_map/ppermute | solution.py:666
  22.5 6.3 %collective-permute-start.6 = (bf16[72,1152]{1,0:T(8,128)(2,1)S(1)}, bf16[72,1152]{1,0:T(8,128)(2,1)S(1)}, u32[]{:S(2)}, u32[]{:S(2)}) collective-permute-start(bf16[72,1152]{1,0:T(8,128)(2,1)S(1)} %collective-permute-done.3), channel_id=1, source_target_pairs={{4,0},{5,1},{8,4},{9,5},{12,8},{13,9},{14,12},{15,13},{10,14},{11,... | collective-permute-start | bytes 497672 | tf_op jit(solution)/shard_map/ppermute | solution.py:666
  28.8 9.8 %collective-permute-start.7 = (bf16[128,512]{1,0:T(8,128)(2,1)S(1)}, bf16[128,512]{1,0:T(8,128)(2,1)S(1)}, u32[]{:S(2)}, u32[]{:S(2)}) collective-permute-start(bf16[128,512]{1,0:T(8,128)(2,1)S(1)} %constant_dynamic-update-slice_fusion.block_ref.refs_0_), channel_id=1, source_target_pairs={{0,4},{1,5},{4,8},{5,9},{8,12},{9,13},{12,14},{13,15},{14,10},{15,... | collective-permute-start | bytes 393224 | tf_op jit(solution)/shard_map/ppermute | solution.py:666
  30.4 8.2 %collective-permute-start.8 = (bf16[128,512]{1,0:T(8,128)(2,1)S(1)}, bf16[128,512]{1,0:T(8,128)(2,1)S(1)}, u32[]{:S(2)}, u32[]{:S(2)}) collective-permute-start(bf16[128,512]{1,0:T(8,128)(2,1)S(1)} %constant_dynamic-update-slice_fusion.block_ref.refs_0_), channel_id=1, source_target_pairs={{4,0},{5,1},{8,4},{9,5},{12,8},{13,9},{14,12},{15,13},{10,14},{11,... | collective-permute-start | bytes 393224 | tf_op jit(solution)/shard_map/ppermute | solution.py:666
  30.8 7.8 %collective-permute-start.9 = (bf16[72,1152]{1,0:T(8,128)(2,1)S(1)}, bf16[72,1152]{1,0:T(8,128)(2,1)S(1)}, u32[]{:S(2)}, u32[]{:S(2)}) collective-permute-start(bf16[72,1152]{1,0:T(8,128)(2,1)S(1)} %collective-permute-done.5), channel_id=1, source_target_pairs={{0,4},{1,5},{4,8},{5,9},{8,12},{9,13},{12,14},{13,15},{14,10},{15,... | collective-permute-start | bytes 497672 | tf_op jit(solution)/shard_map/ppermute | solution.py:666
  32.4 6.2 %collective-permute-start.10 = (bf16[72,1152]{1,0:T(8,128)(2,1)S(1)}, bf16[72,1152]{1,0:T(8,128)(2,1)S(1)}, u32[]{:S(2)}, u32[]{:S(2)}) collective-permute-start(bf16[72,1152]{1,0:T(8,128)(2,1)S(1)} %collective-permute-done.6), channel_id=1, source_target_pairs={{4,0},{5,1},{8,4},{9,5},{12,8},{13,9},{14,12},{15,13},{10,14},{11,... | collective-permute-start | bytes 497672 | tf_op jit(solution)/shard_map/ppermute | solution.py:666
  38.6 6.8 %collective-permute-start.11 = (bf16[128,512]{1,0:T(8,128)(2,1)S(1)}, bf16[128,512]{1,0:T(8,128)(2,1)S(1)}, u32[]{:S(2)}, u32[]{:S(2)}) collective-permute-start(bf16[128,512]{1,0:T(8,128)(2,1)S(1)} %collective-permute-done.7.refs_0_), channel_id=1, source_target_pairs={{0,4},{1,5},{4,8},{5,9},{8,12},{9,13},{12,14},{13,15},{14,10},{15,... | collective-permute-start | bytes 393224 | tf_op jit(solution)/shard_map/ppermute | solution.py:666
  40.3 5.2 %collective-permute-start.12 = (bf16[128,512]{1,0:T(8,128)(2,1)S(1)}, bf16[128,512]{1,0:T(8,128)(2,1)S(1)}, u32[]{:S(2)}, u32[]{:S(2)}) collective-permute-start(bf16[128,512]{1,0:T(8,128)(2,1)S(1)} %collective-permute-done.8.refs_1_), channel_id=1, source_target_pairs={{4,0},{5,1},{8,4},{9,5},{12,8},{13,9},{14,12},{15,13},{10,14},{11,... | collective-permute-start | bytes 393224 | tf_op jit(solution)/shard_map/ppermute | solution.py:666
  40.7 9.4 %collective-permute-start.15 = (bf16[40,1152]{1,0:T(8,128)(2,1)S(1)}, bf16[40,1152]{1,0:T(8,128)(2,1)S(1)}, u32[]{:S(2)}, u32[]{:S(2)}) collective-permute-start(bf16[40,1152]{1,0:T(8,128)(2,1)S(1)} %slice.12), channel_id=1, source_target_pairs={{0,4},{1,5},{4,8},{5,9},{8,12},{9,13},{12,14},{13,15},{14,10},{15,... | collective-permute-start | bytes 276488 | tf_op jit(solution)/shard_map/ppermute | solution.py:666
  42.4 7.7 %collective-permute-start.16 = (bf16[32,1152]{1,0:T(8,128)(2,1)S(1)}, bf16[32,1152]{1,0:T(8,128)(2,1)S(1)}, u32[]{:S(2)}, u32[]{:S(2)}) collective-permute-start(bf16[32,1152]{1,0:T(8,128)(2,1)S(1)} %slice.13), channel_id=1, source_target_pairs={{4,0},{5,1},{8,4},{9,5},{12,8},{13,9},{14,12},{15,13},{10,14},{11,... | collective-permute-start | bytes 221192 | tf_op jit(solution)/shard_map/ppermute | solution.py:666
  45.4 5.0 %collective-permute-start.13 = (bf16[128,512]{1,0:T(8,128)(2,1)S(1)}, bf16[128,512]{1,0:T(8,128)(2,1)S(1)}, u32[]{:S(2)}, u32[]{:S(2)}) collective-permute-start(bf16[128,512]{1,0:T(8,128)(2,1)S(1)} %collective-permute-done.11.refs_0_), channel_id=1, source_target_pairs={{0,4},{1,5},{4,8},{5,9},{8,12},{9,13},{12,14},{13,15},{14,10},{15,... | collective-permute-start | bytes 393224 | tf_op jit(solution)/shard_map/ppermute | solution.py:666
  47.1 5.0 %collective-permute-start.14 = (bf16[128,512]{1,0:T(8,128)(2,1)S(1)}, bf16[128,512]{1,0:T(8,128)(2,1)S(1)}, u32[]{:S(2)}, u32[]{:S(2)}) collective-permute-start(bf16[128,512]{1,0:T(8,128)(2,1)S(1)} %collective-permute-done.12.refs_1_), channel_id=1, source_target_pairs={{4,0},{5,1},{8,4},{9,5},{12,8},{13,9},{14,12},{15,13},{10,14},{11,... | collective-permute-start | bytes 393224 | tf_op jit(solution)/shard_map/ppermute | solution.py:666
  52.1 8.5 %collective-permute-start.19 = (bf16[576,1152]{1,0:T(8,128)(2,1)S(1)}, bf16[576,1152]{1,0:T(8,128)(2,1)S(1)}, u32[]{:S(2)}, u32[]{:S(2)}) collective-permute-start(bf16[576,1152]{1,0:T(8,128)(2,1)S(1)} %constant_dynamic-update-slice_fusion.2.refs_4_), channel_id=1, source_target_pairs={{0,1},{1,0},{2,3},{3,2},{4,5},{5,4},{6,7},{7,6},{8,9},{9,8},{10,11... | collective-permute-start | bytes 3981320 | tf_op jit(solution)/shard_map/ppermute | solution.py:666
  52.2 4.7 %collective-permute-start.17 = (bf16[64,512]{1,0:T(8,128)(2,1)S(1)}, bf16[64,512]{1,0:T(8,128)(2,1)S(1)}, u32[]{:S(2)}, u32[]{:S(2)}) collective-permute-start(bf16[64,512]{1,0:T(8,128)(2,1)S(1)} %slice.14), channel_id=1, source_target_pairs={{0,4},{1,5},{4,8},{5,9},{8,12},{9,13},{12,14},{13,15},{14,10},{15,... | collective-permute-start | bytes 196616 | tf_op jit(solution)/shard_map/ppermute | solution.py:666
  53.8 4.3 %collective-permute-start.18 = (bf16[64,512]{1,0:T(8,128)(2,1)S(1)}, bf16[64,512]{1,0:T(8,128)(2,1)S(1)}, u32[]{:S(2)}, u32[]{:S(2)}) collective-permute-start(bf16[64,512]{1,0:T(8,128)(2,1)S(1)} %slice.15), channel_id=1, source_target_pairs={{4,0},{5,1},{8,4},{9,5},{12,8},{13,9},{14,12},{15,13},{10,14},{11,... | collective-permute-start | bytes 196616 | tf_op jit(solution)/shard_map/ppermute | solution.py:666
  61.6 1.4 %collective-permute-start.20 = (bf16[64,1152]{1,0:T(8,128)(2,1)S(1)}, bf16[64,1152]{1,0:T(8,128)(2,1)S(1)}, u32[]{:S(2)}, u32[]{:S(2)}) collective-permute-start(bf16[64,1152]{1,0:T(8,128)(2,1)S(1)} %get-tuple-element.82), channel_id=1, source_target_pairs={{0,1},{1,0},{2,3},{3,2},{4,5},{5,4},{6,7},{7,6},{8,9},{9,8},{10,11... | collective-permute-start | bytes 442376 | tf_op jit(solution)/shard_map/ppermute | solution.py:666

commit v4 on v3

--- a/solution.py
+++ b/solution.py
@@ -218,83 +218,55 @@
 TN = (((0,), (1,)), ((), ()))
 
 
-def pair_weights(weights, pairs, ch=128):
-    for o in range(3):
-        for four in range(4):
-            for out_row in range(2):
-                columns = slice(out_row * ch, (out_row + 1) * ch)
-                tap = four - out_row
-                for j in range(3):
-                    rows = slice((four * 3 + j) * ch, (four * 3 + j + 1) * ch)
-                    if 0 <= tap < 3:
-                        pairs[o, rows, columns] = weights[o, tap, j]
-                    else:
-                        pairs[o, rows, columns] = jnp.zeros((ch, ch), BF16)
-
-
-def prepare_kernel(patch_any, first_any, second_any, pairs_one, pairs_two, patch_ref, centered_ref, first_ref, second_ref, sems):
+def pair_weights(weights, o, ch=128):
+    blank = jnp.zeros((ch, ch), BF16)
+    rows = []
+    for four in range(4):
+        for j in range(3):
+            taps = [weights[o, four - r, j] if 0 <= four - r < 3 else blank for r in range(2)]
+            rows.append(jnp.concatenate(taps, axis=1))
+    return jnp.concatenate(rows, axis=0)
+
+
+def fold_kernel(patch_any, qkv_any, folded_ref, query_ref, centered_ref, patch_ref, qkv_ref, sems):
     copies = [
-        pltpu.make_async_copy(first_any, first_ref, sems.at[0]),
-        pltpu.make_async_copy(second_any, second_ref, sems.at[1]),
-        pltpu.make_async_copy(patch_any, patch_ref, sems.at[2]),
+        pltpu.make_async_copy(patch_any, patch_ref, sems.at[0]),
+        pltpu.make_async_copy(qkv_any.at[:, pl.ds(D, D)], qkv_ref.at[0], sems.at[1]),
+        pltpu.make_async_copy(qkv_any.at[:, pl.ds(2 * D, D)], qkv_ref.at[1], sems.at[2]),
+        pltpu.make_async_copy(qkv_any.at[:, pl.ds(0, D)], query_ref, sems.at[3]),
     ]
     for copy in copies:
         copy.start()
     copies[0].wait()
-    pair_weights(first_ref, pairs_one)
-    copies[1].wait()
-    pair_weights(second_ref, pairs_two)
-    copies[2].wait()
     patch = patch_ref[...].astype(F32)
     centered_ref[...] = (patch - jnp.mean(patch, axis=1, keepdims=True)).astype(BF16)
-
-
-def prepare(patch_weight, conv_first, conv_second):
-    ch = conv_first.shape[-1]
-    pairs = jax.ShapeDtypeStruct((3, 12 * ch, 2 * ch), BF16)
-    patch = jax.ShapeDtypeStruct(patch_weight.shape, BF16)
-    return pl.pallas_call(
-        prepare_kernel,
-        out_shape=(pairs, pairs, patch, patch),
-        in_specs=[ANY] * 3,
-        out_specs=(VMEM,) * 4,
-        scratch_shapes=[
-            pltpu.VMEM(conv_first.shape, BF16),
-            pltpu.VMEM(conv_first.shape, BF16),
-            pltpu.SemaphoreType.DMA((3,)),
-        ],
-        compiler_params=params(),
-        name="prepare",
-        cost_estimate=pl.CostEstimate(flops=1 << 31, bytes_accessed=6 << 20, transcendentals=0),
-    )(patch_weight, conv_first, conv_second)
-
-
-def fold_kernel(centered_ref, qkv_any, folded_ref, query_ref, qkv_ref, sems):
-    copies = [
-        pltpu.make_async_copy(qkv_any.at[:, pl.ds(D * (i + 1), D)], qkv_ref.at[i], sems.at[i]) for i in range(2)
-    ]
-    copies.append(pltpu.make_async_copy(qkv_any.at[:, pl.ds(0, D)], query_ref, sems.at[2]))
-    for copy in copies:
-        copy.start()
     for part in range(2):
-        copies[part].wait()
+        copies[part + 1].wait()
         product = lax.dot_general(qkv_ref[part], centered_ref[...], TN, preferred_element_type=F32)
         folded_ref[part * D : (part + 1) * D] = product.astype(BF16)
-    copies[2].wait()
-
-
-def fold(centered, qkv_weight):
-    inner = centered.shape[0]
+    copies[3].wait()
+
+
+def fold(patch_weight, qkv_weight):
+    inner = patch_weight.shape[0]
     return pl.pallas_call(
         fold_kernel,
-        out_shape=(jax.ShapeDtypeStruct((2 * D, inner), BF16), jax.ShapeDtypeStruct((D, D), BF16)),
-        in_specs=[VMEM, ANY],
-        out_specs=(VMEM, VMEM),
-        scratch_shapes=[pltpu.VMEM((2, D, D), BF16), pltpu.SemaphoreType.DMA((3,))],
+        out_shape=(
+            jax.ShapeDtypeStruct((2 * D, inner), BF16),
+            jax.ShapeDtypeStruct((D, D), BF16),
+            jax.ShapeDtypeStruct((inner, D), BF16),
+        ),
+        in_specs=[ANY, ANY],
+        out_specs=(VMEM, VMEM, VMEM),
+        scratch_shapes=[
+            pltpu.VMEM((inner, D), BF16),
+            pltpu.VMEM((2, D, D), BF16),
+            pltpu.SemaphoreType.DMA((4,)),
+        ],
         compiler_params=params(),
         name="fold",
         cost_estimate=pl.CostEstimate(flops=2 * inner * D * 2 * D, bytes_accessed=12 << 20, transcendentals=0),
-    )(centered, qkv_weight)
+    )(patch_weight, qkv_weight)
 
 
 def frame_taps(counts_ref, frames):
@@ -312,7 +284,7 @@
 
 
 def conv_kernel(
-    counts_any, lengths_any, own_any, before_ref, after_ref, pairs_one, pairs_two, patch_ref,
+    counts_any, lengths_any, own_any, before_ref, after_ref, first_ref, second_ref, patch_ref,
     keep_ref, send_ref, grid_one, grid_two, pixels, own_ref, counts_ref, lengths_ref, sems,
 ):
     copies = [
@@ -370,7 +342,7 @@
         for o in range(3):
             left = grid_one[g, o : o + frames].reshape(frames * cols, wide)
             terms.append(
-                jnp.dot(left, pairs_one[o], preferred_element_type=F32).reshape(frames, cols, 2 * ch)
+                jnp.dot(left, pair_weights(first_ref, o), preferred_element_type=F32).reshape(frames, cols, 2 * ch)
             )
         hidden = summed(terms)
         for out_row in range(2):
@@ -388,7 +360,7 @@
     for o in range(3):
         left = grid_two[o : o + frames].reshape(frames * cols, wide)
         terms.append(
-            jnp.dot(left, pairs_two[o], preferred_element_type=F32).reshape(frames, cols, 2 * ch)
+            jnp.dot(left, pair_weights(second_ref, o), preferred_element_type=F32).reshape(frames, cols, 2 * ch)
         )
     residual = summed(terms)
     for out_row in range(2):
@@ -416,7 +388,7 @@
     send_ref[...] = send
 
 
-def convolve(counts, lengths, clip, before, after, pairs_one, pairs_two, patch_weight):
+def convolve(counts, lengths, clip, before, after, conv_first, conv_second, patch_weight):
     frames, _, cols, ch = clip.shape
     tokens = frames * cols // 2
     out = jax.ShapeDtypeStruct((tokens // 2, 4 * ch), BF16)
@@ -437,7 +409,7 @@
         compiler_params=params(),
         name="convolve",
         cost_estimate=pl.CostEstimate(flops=2 << 30, bytes_accessed=4 << 20, transcendentals=1 << 18),
-    )(counts, lengths, clip, before, after, pairs_one, pairs_two, patch_weight)
+    )(counts, lengths, clip, before, after, conv_first, conv_second, patch_weight)
 
 
 def chip_at(place):
@@ -481,7 +453,14 @@
     count = part.shape[1]
     heads = part.reshape(-1, HD, count)
     factor = lax.rsqrt(jnp.mean(heads * heads, axis=1, keepdims=True) + 1e-06)
-    return heads * factor * gain[None, :, :count]
+    return heads * factor * gain[None]
+
+
+def as_column(row):
+    size = row.shape[1]
+    square = (size, size)
+    same = lax.broadcasted_iota(jnp.int32, square, 0) == lax.broadcasted_iota(jnp.int32, square, 1)
+    return jnp.sum(jnp.where(same, jnp.broadcast_to(row, square), 0.0), axis=1, keepdims=True)
 
 
 def attend(tokens, sides, folded, key_gain, queries, acc_ref, keys_ref, values_ref, scores_ref, weights_ref):
@@ -532,7 +511,7 @@
     part = jnp.dot(normed, query_ref[...], preferred_element_type=F32).T
     count = part.shape[1]
     sides = window_sides(lengths_ref, lax.axis_index("seq") // 2, count)
-    queries = normed_heads(part, query_gain_ref[...])
+    queries = normed_heads(part, as_column(query_gain_ref[...] * (math.log2(math.e) / math.sqrt(HD))))
     row = lax.broadcasted_iota(jnp.int32, (8, count), 0)
     tail = jnp.where(row == 0, MASK * sides, jnp.where(row == 1, -MASK, 0.0))
     for h in range(HEADS):
@@ -559,7 +538,7 @@
     sides = jnp.concatenate(
         [window_sides(lengths_ref, chip_at(place + offset), 128) for offset in dict.fromkeys(offsets)], axis=1
     )
-    attend(tokens, sides, folded_ref, key_gain_ref[...], queries_ref, acc_ref, *scratch)
+    attend(tokens, sides, folded_ref, as_column(key_gain_ref[...]), queries_ref, acc_ref, *scratch)
 
 
 ACC = jax.ShapeDtypeStruct((HEADS, SLOT, 128), F32)
@@ -625,6 +604,28 @@
     )(*accs, *weights)
 
 
+def pack_kernel(*refs):
+    out_ref = refs[-1]
+    for i in range(7):
+        out_ref[i] = refs[i][...]
+    cut = refs[7].shape[1]
+    out_ref[7, :, :cut] = refs[7][...]
+    out_ref[7, :, cut:] = refs[8][...]
+
+
+def pack(pieces):
+    rows, columns = pieces[0].shape
+    out = pl.pallas_call(
+        pack_kernel,
+        out_shape=jax.ShapeDtypeStruct((8, rows, columns), BF16),
+        in_specs=[VMEM] * 9,
+        out_specs=VMEM,
+        compiler_params=params(),
+        name="pack",
+    )(*pieces)
+    return out.reshape(8 * rows, columns)
+
+
 def merge_kernel(lengths_ref, keep_ref, got_ref, out_ref):
     position = lax.axis_index("seq")
     keep = keep_ref[...].astype(F32)
@@ -674,45 +675,43 @@
     def both_ways(ahead, behind):
         return send(ahead, forward), send(behind, backward)
 
+    def tied(*arrays):
+        return lax.optimization_barrier(arrays)
+
+    def both_ways(ahead, behind):
+        return send(ahead, forward), send(behind, backward)
+
     before = send(clip, up)
     after = send(clip, down)
-    score_scale = math.log2(math.e) / math.sqrt(HD)
-    query_rows = jnp.broadcast_to((query_gain * score_scale)[:, None], (HD, 128))
-    key_rows = jnp.broadcast_to(key_gain[:, None], (HD, 256))
+    query_row, key_row = query_gain[None], key_gain[None]
     weight_one = both_ways(out_weight, out_weight)
-    pairs_one, pairs_two, patch, centered = prepare(patch_weight, conv_first, conv_second)
-    before, after, *weight_one, pairs_one, query_rows, key_rows = tied(
-        before, after, *weight_one, pairs_one, query_rows, key_rows
-    )
+    folded, query_weight, centered = fold(patch_weight, qkv_weight)
+    before, after, *weight_one, folded = tied(before, after, *weight_one, folded)
     weight_two = both_ways(*weight_one)
     keep, other = convolve(
-        frame_counts, window_lengths, clip, before, after, pairs_one, pairs_two, patch
+        frame_counts, window_lengths, clip, before, after, conv_first, conv_second, patch_weight
     )
     got = send(other, cores)
-    got, *weight_two = tied(got, *weight_two)
     block = jnp.concatenate([keep, got], axis=0)
     one = both_ways(block, block)
+    queries = make_queries(window_lengths, block, centered, query_weight, query_row)
+    *one, queries, wu_a, wu_b = tied(*one, queries, *weight_two)
+    weight_two = (wu_a, wu_b)
+    two = both_ways(*one)
     weight_three = both_ways(*weight_two)
-    folded, query_weight = fold(tied(centered, block)[0], qkv_weight)
-    *one, folded, = tied(*one, folded)
-    *one, weight_three_a, weight_three_b = tied(*one, *weight_three)
-    two = both_ways(*one)
-    cut = 40
-    weight_four = both_ways(weight_three_a[:cut], weight_three_b[cut:])
-    queries = make_queries(window_lengths, block, centered, query_weight, query_rows)
-    acc_one = step_attention((-1, 1), window_lengths, one, folded, key_rows, queries)
-    *two, acc_one = tied(*two, acc_one)
+    acc_one = step_attention((-1, 1), window_lengths, one, folded, key_row, queries)
+    *two, acc_one, wt_a, wt_b = tied(*two, acc_one, *weight_three)
     three = both_ways(*two)
-    acc_two = step_attention((-2, 2), window_lengths, two, folded, key_rows, queries)
+    cut = 640
+    weight_four = both_ways(wt_a[:, :cut], wt_b[:, cut:])
+    acc_two = step_attention((-2, 2), window_lengths, two, folded, key_row, queries)
     *three, acc_two, wf_a, wf_b = tied(*three, acc_two, *weight_four)
-    weights = jnp.concatenate(
-        [out_weight, *weight_one, *weight_two, weight_three_a, weight_three_b, wf_a, wf_b], axis=0
-    )
     four = both_ways(three[0][:64], three[1][64:])
+    weights = pack([out_weight, *weight_one, *weight_two, wt_a, wt_b, wf_a, wf_b])
     sibling = send(weights, cores)
-    acc_three = step_attention((-3, 3), window_lengths, three, folded, key_rows, queries)
+    acc_three = step_attention((-3, 3), window_lengths, three, folded, key_row, queries)
     *four, acc_three = tied(*four, acc_three)
-    acc_four = step_attention((0, 4, 4), window_lengths, [block, *four], folded, key_rows, queries)
+    acc_four = step_attention((0, 4, 4), window_lengths, [block, *four], folded, key_row, queries)
     keep_rows, send_rows = project_out((acc_one, acc_two, acc_three, acc_four), (weights, sibling))
     return merge(window_lengths, keep_rows, send(send_rows, cores))
 

time: 64.7 us -> 61.6 us (0.952)
  local copies, waits for them, and re-layouts: 4.96 us -> 1.35 us
  waiting for transfers between devices: 10.8 us -> 11.9 us
  other arithmetic: 0.66 us -> 0 us
    unnamed x27 -> x21, local copies, waits for them, and re-layouts: 4.78 us -> 1.31 us
    pallas_call x1, Pallas kernels: 4.12 us -> 5.67 us  [fold(): pl.pallas_call(fold_kernel, out_shape=(jax.ShapeDtypeStruct((2 * D, inner...]
    pallas_call x1, Pallas kernels: 1.61 us -> 0.1 us  [pack(): pl.pallas_call(pack_kernel, out_shape=jax.ShapeDtypeStruct((8, rows, colu...]
    ppermute x21, waiting for transfers between devices: 10.8 us -> 11.9 us  [send(): return lax.ppermute(array, 'seq', pairs)]
    mul x1 -> x0, other arithmetic: 0.66 us -> none  [shards(): query_gain * score_scale]
  transfers between devices with their start and end apart: 21 -> 21, of which waited for: 6 -> 9; matrix products, arithmetic and copies ran while one was open for 3% -> 0% of each run, Pallas kernels for 27% -> 28%
where the time goes in v4:
time: 61.6 us; the launch traced here: 61.4 us
  starting transfers between devices  24.4 us (40%)
  Pallas kernels  23.6 us (38%)
  waiting for transfers between devices  11.9 us (19%)
  local copies, waits for them, and re-layouts  1.35 us (2%)
    ppermute x21, starting transfers between devices, send(): return lax.ppermute(array, 'seq', pairs)  24.4 us
    ppermute x21, waiting for transfers between devices, send(): return lax.ppermute(array, 'seq', pairs)  11.9 us
    pallas_call x4, Pallas kernels, step_attention(): pl.pallas_call(functools.partial(step_kernel, offsets), out_shape=ACC, in...  10.2 us
    pallas_call x1, Pallas kernels, fold(): pl.pallas_call(fold_kernel, out_shape=(jax.ShapeDtypeStruct((2 * D, inner...  5.67 us
    pallas_call x1, Pallas kernels, convolve(): pl.pallas_call(conv_kernel, out_shape=(out, out), in_specs=[ANY] * 3 + [V...  3.71 us
    pallas_call x1, Pallas kernels, make_queries(): pl.pallas_call(query_kernel, out_shape=jax.ShapeDtypeStruct((HEADS, 128,...  1.53 us
    pallas_call x1, Pallas kernels, merge(): pl.pallas_call(merge_kernel, out_shape=jax.ShapeDtypeStruct((128, D), BF1...  1.35 us
    unnamed x21, local copies, waits for them, and re-layouts  1.31 us
  transfers between devices with their start and end apart: 21, of which 9 were waited for; matrix products, arithmetic and copies ran while one was open for 0% of the time, Pallas kernels for 28%

profile of v4, /device:TPU:0, one launch (start us, length us, event | category | flops | bytes accessed | tf_op | source)
XLA Modules:
  0.0 61.4 jit_solution(7384309996206351517)
XLA Ops:
  0.0 2.5 %collective-permute-start = (bf16[8,2,32,128]{3,2,1,0:T(8,128)(2,1)}, bf16[8,2,32,128]{3,2,1,0:T(8,128)(2,1)S(1)}, u32[]{:S(2)}, u32[]{:S(2)}) collective-permute-start(bf16[8,2,32,128]{3,2,1,0:T(8,128)(2,1)} %own_any.1), channel_id=1, source_target_pairs={{0,1},{1,2},{2,3},{3,4},{4,5},{5,6},{6,7},{7,8},{8,9},{9,10},{10,1... | collective-permute-start | bytes 393224 | tf_op jit(solution)/shard_map/ppermute | solution.py:667
  2.5 1.3 %collective-permute-start.1 = (bf16[8,2,32,128]{3,2,1,0:T(8,128)(2,1)}, bf16[8,2,32,128]{3,2,1,0:T(8,128)(2,1)S(1)}, u32[]{:S(2)}, u32[]{:S(2)}) collective-permute-start(bf16[8,2,32,128]{3,2,1,0:T(8,128)(2,1)} %own_any.1), channel_id=1, source_target_pairs={{1,0},{2,1},{3,2},{4,3},{5,4},{6,5},{7,6},{8,7},{9,8},{10,9},{11,1... | collective-permute-start | bytes 393224 | tf_op jit(solution)/shard_map/ppermute | solution.py:667
  3.8 5.9 %collective-permute-start.2 = (bf16[72,1152]{1,0:T(8,128)(2,1)}, bf16[72,1152]{1,0:T(8,128)(2,1)S(1)}, u32[]{:S(2)}, u32[]{:S(2)}) collective-permute-start(bf16[72,1152]{1,0:T(8,128)(2,1)} %refs_0_.1), channel_id=1, source_target_pairs={{0,4},{1,5},{4,8},{5,9},{8,12},{9,13},{12,14},{13,15},{14,10},{15,... | collective-permute-start | bytes 497672 | tf_op jit(solution)/shard_map/ppermute | solution.py:667
  9.7 0.0 collective-permute-start.3
  9.7 1.3 %copy-done.3 = bf16[512,1152]{1,0:T(8,128)(2,1)S(1)} copy-done((bf16[512,1152]{1,0:T(8,128)(2,1)S(1)}, bf16[512,1152]{1,0:T(8,128)(2,1)}, u32[]{:S(2)}) %copy-start.3) | copy-done | bytes 1179672
  11.0 5.7 %fold.1 = (bf16[2304,512]{1,0:T(8,128)(2,1)S(1)}, bf16[1152,1152]{1,0:T(8,128)(2,1)S(1)}, bf16[512,1152]{1,0:T(8,128)(2,1)S(1)}) custom-call(bf16[512,1152]{1,0:T(8,128)(2,1)S(1)} %copy-done.3, bf16[1152,3456]{1,0:T(8,128)(2,1)} %qkv_any.1), custom_call_target="tpu_custom_call" | custom-call | flops 2717908992 | bytes 12582912 | tf_op jit(solution)/shard_map/fold/pallas_call | solution.py:252
  16.7 0.0 collective-permute-done.1.after_ref
  16.7 0.0 collective-permute-done.2.refs_1_
  16.8 0.0 copy-start.2
  16.8 3.7 %convolve.1 = (bf16[64,512]{1,0:T(8,128)(2,1)S(1)}, bf16[64,512]{1,0:T(8,128)(2,1)S(1)}) custom-call(s32[3]{0:T(128)S(1)} %copy-done.8, s32[1,3]{1,0:T(1,128)S(1)} %copy-done.1, bf16[8,2,32,128]{3,2,1,0:T(8,128)(2,1)S(1)} %copy-done.7, bf16[8,2,32,128]{3,2,1,0:T(8,128)(2,1)S(1)} %collective-permute-done.before_ref, ...), custom_call_target="tpu_custom_call" | custom-call | flops 2147483648 | bytes 4194304 | tf_op jit(solution)/shard_map/convolve/pallas_call | solution.py:395
  20.5 0.1 collective-permute-start.4
  20.6 2.1 %collective-permute-start.7 = (bf16[72,1152]{1,0:T(8,128)(2,1)S(1)}, bf16[72,1152]{1,0:T(8,128)(2,1)S(1)}, u32[]{:S(2)}, u32[]{:S(2)}) collective-permute-start(bf16[72,1152]{1,0:T(8,128)(2,1)S(1)} %collective-permute-done.2.refs_1_), channel_id=1, source_target_pairs={{0,4},{1,5},{4,8},{5,9},{8,12},{9,13},{12,14},{13,15},{14,10},{15,... | collective-permute-start | bytes 497672 | tf_op jit(solution)/shard_map/ppermute | solution.py:667
  22.6 0.0 collective-permute-start.8
  22.7 1.1 %collective-permute-start.6 = (bf16[128,512]{1,0:T(8,128)(2,1)S(1)}, bf16[128,512]{1,0:T(8,128)(2,1)S(1)}, u32[]{:S(2)}, u32[]{:S(2)}) collective-permute-start(bf16[128,512]{1,0:T(8,128)(2,1)S(1)} %constant_dynamic-update-slice_fusion.block_ref.refs_0_), channel_id=1, source_target_pairs={{4,0},{5,1},{8,4},{9,5},{12,8},{13,9},{14,12},{15,13},{10,14},{11,... | collective-permute-start | bytes 393224 | tf_op jit(solution)/shard_map/ppermute | solution.py:667
  23.8 1.0 %collective-permute-start.5 = (bf16[128,512]{1,0:T(8,128)(2,1)S(1)}, bf16[128,512]{1,0:T(8,128)(2,1)S(1)}, u32[]{:S(2)}, u32[]{:S(2)}) collective-permute-start(bf16[128,512]{1,0:T(8,128)(2,1)S(1)} %constant_dynamic-update-slice_fusion.block_ref.refs_0_), channel_id=1, source_target_pairs={{0,4},{1,5},{4,8},{5,9},{8,12},{9,13},{12,14},{13,15},{14,10},{15,... | collective-permute-start | bytes 393224 | tf_op jit(solution)/shard_map/ppermute | solution.py:667
  24.8 1.5 %queries.1.refs_4_.refs_5_ = bf16[16,128,80]{2,1,0:T(8,128)(2,1)S(1)} custom-call(s32[1,3]{1,0:T(1,128)S(1)} %copy-done.1, bf16[128,512]{1,0:T(8,128)(2,1)S(1)} %constant_dynamic-update-slice_fusion.block_ref.refs_0_, bf16[512,1152]{1,0:T(8,128)(2,1)S(1)} %get-tuple-element.40.centered_ref, bf16[1152,1152]{1,0:T(8,128)(2,1)S(1)} %get-tuple-element.41.query_ref, ...), custom_call_target="tpu_custom_call" | custom-call | flops 1073741824 | bytes 4194304 | tf_op jit(solution)/shard_map/queries/pallas_call | solution.py:522
  26.3 1.3 %collective-permute-done.7.refs_3_ = bf16[72,1152]{1,0:T(8,128)(2,1)S(1)} collective-permute-done((bf16[72,1152]{1,0:T(8,128)(2,1)S(1)}, bf16[72,1152]{1,0:T(8,128)(2,1)S(1)}, u32[]{:S(2)}, u32[]{:S(2)}) %collective-permute-start.7) | collective-permute-done | bytes 165920 | tf_op jit(solution)/shard_map/ppermute | solution.py:667
  27.7 2.1 %collective-permute-done.8.refs_4_ = bf16[72,1152]{1,0:T(8,128)(2,1)S(1)} collective-permute-done((bf16[72,1152]{1,0:T(8,128)(2,1)S(1)}, bf16[72,1152]{1,0:T(8,128)(2,1)S(1)}, u32[]{:S(2)}, u32[]{:S(2)}) %collective-permute-start.8) | collective-permute-done | bytes 165920 | tf_op jit(solution)/shard_map/ppermute | solution.py:667
  29.7 2.0 %collective-permute-done.6.refs_1_ = bf16[128,512]{1,0:T(8,128)(2,1)S(1)} collective-permute-done((bf16[128,512]{1,0:T(8,128)(2,1)S(1)}, bf16[128,512]{1,0:T(8,128)(2,1)S(1)}, u32[]{:S(2)}, u32[]{:S(2)}) %collective-permute-start.6) | collective-permute-done | bytes 131104 | tf_op jit(solution)/shard_map/ppermute | solution.py:667
  31.8 1.6 %collective-permute-start.11 = (bf16[72,1152]{1,0:T(8,128)(2,1)S(1)}, bf16[72,1152]{1,0:T(8,128)(2,1)S(1)}, u32[]{:S(2)}, u32[]{:S(2)}) collective-permute-start(bf16[72,1152]{1,0:T(8,128)(2,1)S(1)} %collective-permute-done.7.refs_3_), channel_id=1, source_target_pairs={{0,4},{1,5},{4,8},{5,9},{8,12},{9,13},{12,14},{13,15},{14,10},{15,... | collective-permute-start | bytes 497672 | tf_op jit(solution)/shard_map/ppermute | solution.py:667
  33.3 0.4 collective-permute-start.12
  33.8 1.6 %collective-permute-start.9 = (bf16[128,512]{1,0:T(8,128)(2,1)S(1)}, bf16[128,512]{1,0:T(8,128)(2,1)S(1)}, u32[]{:S(2)}, u32[]{:S(2)}) collective-permute-start(bf16[128,512]{1,0:T(8,128)(2,1)S(1)} %collective-permute-done.5.refs_0_), channel_id=1, source_target_pairs={{0,4},{1,5},{4,8},{5,9},{8,12},{9,13},{12,14},{13,15},{14,10},{15,... | collective-permute-start | bytes 393224 | tf_op jit(solution)/shard_map/ppermute | solution.py:667
  35.4 0.4 collective-permute-start.10
  35.8 2.6 %step_attention.4.refs_0_ = f32[16,80,128]{2,1,0:T(8,128)S(1)} custom-call(s32[1,3]{1,0:T(1,128)S(1)} %copy-done.1, bf16[128,512]{1,0:T(8,128)(2,1)S(1)} %collective-permute-done.5.refs_0_, bf16[128,512]{1,0:T(8,128)(2,1)S(1)} %collective-permute-done.6.refs_1_, bf16[2304,512]{1,0:T(8,128)(2,1)S(1)} %get-tuple-element.46.refs_2_.refs_3_, ...), custom_call_target="tpu_custom_call" | custom-call | flops 1744830464 | bytes 5242880 | tf_op jit(solution)/shard_map/step_attention/pallas_call | solution.py:550
  38.4 1.7 %collective-permute-done.9.refs_0_ = bf16[128,512]{1,0:T(8,128)(2,1)S(1)} collective-permute-done((bf16[128,512]{1,0:T(8,128)(2,1)S(1)}, bf16[128,512]{1,0:T(8,128)(2,1)S(1)}, u32[]{:S(2)}, u32[]{:S(2)}) %collective-permute-start.9) | collective-permute-done | bytes 131104 | tf_op jit(solution)/shard_map/ppermute | solution.py:667
  40.1 1.3 %collective-permute-done.10.refs_1_ = bf16[128,512]{1,0:T(8,128)(2,1)S(1)} collective-permute-done((bf16[128,512]{1,0:T(8,128)(2,1)S(1)}, bf16[128,512]{1,0:T(8,128)(2,1)S(1)}, u32[]{:S(2)}, u32[]{:S(2)}) %collective-permute-start.10) | collective-permute-done | bytes 131104 | tf_op jit(solution)/shard_map/ppermute | solution.py:667
  41.4 0.5 collective-permute-start.16
  41.9 0.0 copy-start
  41.9 1.6 %collective-permute-start.15 = (bf16[72,640]{1,0:T(8,128)(2,1)S(1)}, bf16[72,640]{1,0:T(8,128)(2,1)S(1)}, u32[]{:S(2)}, u32[]{:S(2)}) collective-permute-start(bf16[72,640]{1,0:T(8,128)(2,1)S(1)} %slice.12), channel_id=1, source_target_pairs={{0,4},{1,5},{4,8},{5,9},{8,12},{9,13},{12,14},{13,15},{14,10},{15,... | collective-permute-start | bytes 276488 | tf_op jit(solution)/shard_map/ppermute | solution.py:667
  43.5 1.6 %collective-permute-start.13 = (bf16[128,512]{1,0:T(8,128)(2,1)S(1)}, bf16[128,512]{1,0:T(8,128)(2,1)S(1)}, u32[]{:S(2)}, u32[]{:S(2)}) collective-permute-start(bf16[128,512]{1,0:T(8,128)(2,1)S(1)} %collective-permute-done.9.refs_0_), channel_id=1, source_target_pairs={{0,4},{1,5},{4,8},{5,9},{8,12},{9,13},{12,14},{13,15},{14,10},{15,... | collective-permute-start | bytes 393224 | tf_op jit(solution)/shard_map/ppermute | solution.py:667
  45.1 0.4 collective-permute-start.14
  45.6 2.5 %step_attention.5.refs_1_ = f32[16,80,128]{2,1,0:T(8,128)S(1)} custom-call(s32[1,3]{1,0:T(1,128)S(1)} %copy-done.1, bf16[128,512]{1,0:T(8,128)(2,1)S(1)} %collective-permute-done.9.refs_0_, bf16[128,512]{1,0:T(8,128)(2,1)S(1)} %collective-permute-done.10.refs_1_, bf16[2304,512]{1,0:T(8,128)(2,1)S(1)} %get-tuple-element.46.refs_2_.refs_3_, ...), custom_call_target="tpu_custom_call" | custom-call | flops 1744830464 | bytes 5242880 | tf_op jit(solution)/shard_map/step_attention/pallas_call | solution.py:550
  48.1 0.0 collective-permute-done.16.refs_8_
  48.1 0.4 collective-permute-done.13.refs_0_
  48.5 1.6 %collective-permute-done.14.refs_1_ = bf16[128,512]{1,0:T(8,128)(2,1)S(1)} collective-permute-done((bf16[128,512]{1,0:T(8,128)(2,1)S(1)}, bf16[128,512]{1,0:T(8,128)(2,1)S(1)}, u32[]{:S(2)}, u32[]{:S(2)}) %collective-permute-start.14) | collective-permute-done | bytes 131104 | tf_op jit(solution)/shard_map/ppermute | solution.py:667
  50.1 0.1 pack.1
  50.2 0.1 collective-permute-start.19
  50.3 0.5 collective-permute-start.18
  50.8 1.6 %collective-permute-start.17 = (bf16[64,512]{1,0:T(8,128)(2,1)S(1)}, bf16[64,512]{1,0:T(8,128)(2,1)S(1)}, u32[]{:S(2)}, u32[]{:S(2)}) collective-permute-start(bf16[64,512]{1,0:T(8,128)(2,1)S(1)} %slice.14), channel_id=1, source_target_pairs={{0,4},{1,5},{4,8},{5,9},{8,12},{9,13},{12,14},{13,15},{14,10},{15,... | collective-permute-start | bytes 196616 | tf_op jit(solution)/shard_map/ppermute | solution.py:667
  52.4 2.6 %step_attention.6.refs_2_ = f32[16,80,128]{2,1,0:T(8,128)S(1)} custom-call(s32[1,3]{1,0:T(1,128)S(1)} %copy-done.1, bf16[128,512]{1,0:T(8,128)(2,1)S(1)} %collective-permute-done.13.refs_0_, bf16[128,512]{1,0:T(8,128)(2,1)S(1)} %collective-permute-done.14.refs_1_, bf16[2304,512]{1,0:T(8,128)(2,1)S(1)} %get-tuple-element.46.refs_2_.refs_3_, ...), custom_call_target="tpu_custom_call" | custom-call | flops 1744830464 | bytes 5242880 | tf_op jit(solution)/shard_map/step_attention/pallas_call | solution.py:550
  54.9 0.0 collective-permute-done.18.refs_2_
  55.0 0.1 collective-permute-done.17.refs_1_
  55.1 2.6 %step_attention.7.refs_3_ = f32[16,80,128]{2,1,0:T(8,128)S(1)} custom-call(s32[1,3]{1,0:T(1,128)S(1)} %copy-done.1, bf16[128,512]{1,0:T(8,128)(2,1)S(1)} %constant_dynamic-update-slice_fusion.block_ref.refs_0_, bf16[64,512]{1,0:T(8,128)(2,1)S(1)} %collective-permute-done.17.refs_1_, bf16[64,512]{1,0:T(8,128)(2,1)S(1)} %collective-permute-done.18.refs_2_, ...), custom_call_target="tpu_custom_call" | custom-call | flops 1744830464 | bytes 5242880 | tf_op jit(solution)/shard_map/step_attention/pallas_call | solution.py:550
  57.6 0.0 collective-permute-done.19.refs_5_
  57.6 1.0 %project_out.1 = (bf16[64,1152]{1,0:T(8,128)(2,1)S(1)}, bf16[64,1152]{1,0:T(8,128)(2,1)S(1)}) custom-call(f32[16,80,128]{2,1,0:T(8,128)S(1)} %step_attention.4.refs_0_, f32[16,80,128]{2,1,0:T(8,128)S(1)} %step_attention.5.refs_1_, f32[16,80,128]{2,1,0:T(8,128)S(1)} %step_attention.6.refs_2_, f32[16,80,128]{2,1,0:T(8,128)S(1)} %step_attention.7.refs_3_, ...), custom_call_target="tpu_custom_call" | custom-call | flops 377487360 | bytes 4194304 | tf_op jit(solution)/shard_map/project_out/pallas_call | solution.py:595
  58.6 0.1 collective-permute-start.20
  58.7 1.4 %collective-permute-done.20.got_ref = bf16[64,1152]{1,0:T(8,128)(2,1)S(1)} collective-permute-done((bf16[64,1152]{1,0:T(8,128)(2,1)S(1)}, bf16[64,1152]{1,0:T(8,128)(2,1)S(1)}, u32[]{:S(2)}, u32[]{:S(2)}) %collective-permute-start.20) | collective-permute-done | bytes 147488 | tf_op jit(solution)/shard_map/ppermute | solution.py:667
  60.1 1.3 %merge.1 = bf16[128,1152]{1,0:T(8,128)(2,1)} custom-call(s32[1,3]{1,0:T(1,128)S(1)} %copy-done.1, bf16[64,1152]{1,0:T(8,128)(2,1)S(1)} %get-tuple-element.63.keep_ref, bf16[64,1152]{1,0:T(8,128)(2,1)S(1)} %collective-permute-done.20.got_ref), custom_call_target="tpu_custom_call" | custom-call | tf_op jit(solution)/shard_map/merge/pallas_call | solution.py:645
  (30 shorter events, 0.1 us)
Async XLA Ops:
  0.0 16.7 %copy-start.1 = (s32[1,3]{1,0:T(1,128)S(1)}, s32[1,3]{1,0:T(1,128)}, u32[]{:S(2)}) copy-start(s32[1,3]{1,0:T(1,128)} %lengths_ref.11) | copy-start | bytes 40
  0.0 16.7 %collective-permute-start = (bf16[8,2,32,128]{3,2,1,0:T(8,128)(2,1)}, bf16[8,2,32,128]{3,2,1,0:T(8,128)(2,1)S(1)}, u32[]{:S(2)}, u32[]{:S(2)}) collective-permute-start(bf16[8,2,32,128]{3,2,1,0:T(8,128)(2,1)} %own_any.1), channel_id=1, source_target_pairs={{0,1},{1,2},{2,3},{3,4},{4,5},{5,6},{6,7},{7,8},{8,9},{9,10},{10,1... | collective-permute-start | bytes 393224 | tf_op jit(solution)/shard_map/ppermute | solution.py:667
  2.5 14.2 %collective-permute-start.1 = (bf16[8,2,32,128]{3,2,1,0:T(8,128)(2,1)}, bf16[8,2,32,128]{3,2,1,0:T(8,128)(2,1)S(1)}, u32[]{:S(2)}, u32[]{:S(2)}) collective-permute-start(bf16[8,2,32,128]{3,2,1,0:T(8,128)(2,1)} %own_any.1), channel_id=1, source_target_pairs={{1,0},{2,1},{3,2},{4,3},{5,4},{6,5},{7,6},{8,7},{9,8},{10,9},{11,1... | collective-permute-start | bytes 393224 | tf_op jit(solution)/shard_map/ppermute | solution.py:667
  3.8 12.9 %collective-permute-start.2 = (bf16[72,1152]{1,0:T(8,128)(2,1)}, bf16[72,1152]{1,0:T(8,128)(2,1)S(1)}, u32[]{:S(2)}, u32[]{:S(2)}) collective-permute-start(bf16[72,1152]{1,0:T(8,128)(2,1)} %refs_0_.1), channel_id=1, source_target_pairs={{0,4},{1,5},{4,8},{5,9},{8,12},{9,13},{12,14},{13,15},{14,10},{15,... | collective-permute-start | bytes 497672 | tf_op jit(solution)/shard_map/ppermute | solution.py:667
  9.7 7.0 %collective-permute-start.3 = (bf16[72,1152]{1,0:T(8,128)(2,1)}, bf16[72,1152]{1,0:T(8,128)(2,1)S(1)}, u32[]{:S(2)}, u32[]{:S(2)}) collective-permute-start(bf16[72,1152]{1,0:T(8,128)(2,1)} %refs_0_.1), channel_id=1, source_target_pairs={{4,0},{5,1},{8,4},{9,5},{12,8},{13,9},{14,12},{15,13},{10,14},{11,... | collective-permute-start | bytes 497672 | tf_op jit(solution)/shard_map/ppermute | solution.py:667
  9.7 1.3 %copy-start.3 = (bf16[512,1152]{1,0:T(8,128)(2,1)S(1)}, bf16[512,1152]{1,0:T(8,128)(2,1)}, u32[]{:S(2)}) copy-start(bf16[512,1152]{1,0:T(8,128)(2,1)} %patch_ref.1) | copy-start | bytes 3538948
  10.9 5.8 %copy-start.4 = (bf16[512,1152]{1,0:T(8,128)(2,1)S(1)}, bf16[512,1152]{1,0:T(8,128)(2,1)}, u32[]{:S(2)}) copy-start(bf16[512,1152]{1,0:T(8,128)(2,1)} %patch_ref.1) | copy-start | bytes 3538948
  11.0 5.8 %copy-start.5 = (bf16[3,3,3,128,128]{4,3,2,1,0:T(8,128)(2,1)S(1)}, bf16[3,3,3,128,128]{4,3,2,1,0:T(8,128)(2,1)}, u32[]{:S(2)}) copy-start(bf16[3,3,3,128,128]{4,3,2,1,0:T(8,128)(2,1)} %first_ref.1) | copy-start | bytes 2654212
  11.0 5.8 %copy-start.6 = (bf16[3,3,3,128,128]{4,3,2,1,0:T(8,128)(2,1)S(1)}, bf16[3,3,3,128,128]{4,3,2,1,0:T(8,128)(2,1)}, u32[]{:S(2)}) copy-start(bf16[3,3,3,128,128]{4,3,2,1,0:T(8,128)(2,1)} %second_ref.1) | copy-start | bytes 2654212
  11.0 5.8 %copy-start.7 = (bf16[8,2,32,128]{3,2,1,0:T(8,128)(2,1)S(1)}, bf16[8,2,32,128]{3,2,1,0:T(8,128)(2,1)}, u32[]{:S(2)}) copy-start(bf16[8,2,32,128]{3,2,1,0:T(8,128)(2,1)} %own_any.1) | copy-start | bytes 393220
  11.0 5.8 %copy-start.8 = (s32[3]{0:T(128)S(1)}, s32[3]{0:T(128)}, u32[]{:S(2)}) copy-start(s32[3]{0:T(128)} %counts_any.1) | copy-start | bytes 40
  16.8 8.1 %copy-start.2 = (f32[72]{0:T(128)S(1)}, f32[72]{0:T(128)}, u32[]{:S(2)}) copy-start(f32[72]{0:T(128)} %param.16) | copy-start | bytes 868
  20.5 2.2 %collective-permute-start.4 = (bf16[64,512]{1,0:T(8,128)(2,1)S(1)}, bf16[64,512]{1,0:T(8,128)(2,1)S(1)}, u32[]{:S(2)}, u32[]{:S(2)}) collective-permute-start(bf16[64,512]{1,0:T(8,128)(2,1)S(1)} %get-tuple-element.39), channel_id=1, source_target_pairs={{0,1},{1,0},{2,3},{3,2},{4,5},{5,4},{6,7},{7,6},{8,9},{9,8},{10,11... | collective-permute-start | bytes 196616 | tf_op jit(solution)/shard_map/ppermute | solution.py:667
  20.6 7.1 %collective-permute-start.7 = (bf16[72,1152]{1,0:T(8,128)(2,1)S(1)}, bf16[72,1152]{1,0:T(8,128)(2,1)S(1)}, u32[]{:S(2)}, u32[]{:S(2)}) collective-permute-start(bf16[72,1152]{1,0:T(8,128)(2,1)S(1)} %collective-permute-done.2.refs_1_), channel_id=1, source_target_pairs={{0,4},{1,5},{4,8},{5,9},{8,12},{9,13},{12,14},{13,15},{14,10},{15,... | collective-permute-start | bytes 497672 | tf_op jit(solution)/shard_map/ppermute | solution.py:667
  22.6 7.1 %collective-permute-start.8 = (bf16[72,1152]{1,0:T(8,128)(2,1)S(1)}, bf16[72,1152]{1,0:T(8,128)(2,1)S(1)}, u32[]{:S(2)}, u32[]{:S(2)}) collective-permute-start(bf16[72,1152]{1,0:T(8,128)(2,1)S(1)} %collective-permute-done.3.refs_2_), channel_id=1, source_target_pairs={{4,0},{5,1},{8,4},{9,5},{12,8},{13,9},{14,12},{15,13},{10,14},{11,... | collective-permute-start | bytes 497672 | tf_op jit(solution)/shard_map/ppermute | solution.py:667
  22.7 9.1 %collective-permute-start.6 = (bf16[128,512]{1,0:T(8,128)(2,1)S(1)}, bf16[128,512]{1,0:T(8,128)(2,1)S(1)}, u32[]{:S(2)}, u32[]{:S(2)}) collective-permute-start(bf16[128,512]{1,0:T(8,128)(2,1)S(1)} %constant_dynamic-update-slice_fusion.block_ref.refs_0_), channel_id=1, source_target_pairs={{4,0},{5,1},{8,4},{9,5},{12,8},{13,9},{14,12},{15,13},{10,14},{11,... | collective-permute-start | bytes 393224 | tf_op jit(solution)/shard_map/ppermute | solution.py:667
  23.8 8.0 %collective-permute-start.5 = (bf16[128,512]{1,0:T(8,128)(2,1)S(1)}, bf16[128,512]{1,0:T(8,128)(2,1)S(1)}, u32[]{:S(2)}, u32[]{:S(2)}) collective-permute-start(bf16[128,512]{1,0:T(8,128)(2,1)S(1)} %constant_dynamic-update-slice_fusion.block_ref.refs_0_), channel_id=1, source_target_pairs={{0,4},{1,5},{4,8},{5,9},{8,12},{9,13},{12,14},{13,15},{14,10},{15,... | collective-permute-start | bytes 393224 | tf_op jit(solution)/shard_map/ppermute | solution.py:667
  24.8 11.0 %copy-start.9 = (f32[72]{0:T(128)S(1)}, f32[72]{0:T(128)}, u32[]{:S(2)}) copy-start(f32[72]{0:T(128)} %param.17) | copy-start | bytes 868
  31.8 9.6 %collective-permute-start.11 = (bf16[72,1152]{1,0:T(8,128)(2,1)S(1)}, bf16[72,1152]{1,0:T(8,128)(2,1)S(1)}, u32[]{:S(2)}, u32[]{:S(2)}) collective-permute-start(bf16[72,1152]{1,0:T(8,128)(2,1)S(1)} %collective-permute-done.7.refs_3_), channel_id=1, source_target_pairs={{0,4},{1,5},{4,8},{5,9},{8,12},{9,13},{12,14},{13,15},{14,10},{15,... | collective-permute-start | bytes 497672 | tf_op jit(solution)/shard_map/ppermute | solution.py:667
  33.3 8.0 %collective-permute-start.12 = (bf16[72,1152]{1,0:T(8,128)(2,1)S(1)}, bf16[72,1152]{1,0:T(8,128)(2,1)S(1)}, u32[]{:S(2)}, u32[]{:S(2)}) collective-permute-start(bf16[72,1152]{1,0:T(8,128)(2,1)S(1)} %collective-permute-done.8.refs_4_), channel_id=1, source_target_pairs={{4,0},{5,1},{8,4},{9,5},{12,8},{13,9},{14,12},{15,13},{10,14},{11,... | collective-permute-start | bytes 497672 | tf_op jit(solution)/shard_map/ppermute | solution.py:667
  33.8 6.3 %collective-permute-start.9 = (bf16[128,512]{1,0:T(8,128)(2,1)S(1)}, bf16[128,512]{1,0:T(8,128)(2,1)S(1)}, u32[]{:S(2)}, u32[]{:S(2)}) collective-permute-start(bf16[128,512]{1,0:T(8,128)(2,1)S(1)} %collective-permute-done.5.refs_0_), channel_id=1, source_target_pairs={{0,4},{1,5},{4,8},{5,9},{8,12},{9,13},{12,14},{13,15},{14,10},{15,... | collective-permute-start | bytes 393224 | tf_op jit(solution)/shard_map/ppermute | solution.py:667
  35.4 6.0 %collective-permute-start.10 = (bf16[128,512]{1,0:T(8,128)(2,1)S(1)}, bf16[128,512]{1,0:T(8,128)(2,1)S(1)}, u32[]{:S(2)}, u32[]{:S(2)}) collective-permute-start(bf16[128,512]{1,0:T(8,128)(2,1)S(1)} %collective-permute-done.6.refs_1_), channel_id=1, source_target_pairs={{4,0},{5,1},{8,4},{9,5},{12,8},{13,9},{14,12},{15,13},{10,14},{11,... | collective-permute-start | bytes 393224 | tf_op jit(solution)/shard_map/ppermute | solution.py:667
  41.4 6.7 %collective-permute-start.16 = (bf16[72,512]{1,0:T(8,128)(2,1)S(1)}, bf16[72,512]{1,0:T(8,128)(2,1)S(1)}, u32[]{:S(2)}, u32[]{:S(2)}) collective-permute-start(bf16[72,512]{1,0:T(8,128)(2,1)S(1)} %slice.13), channel_id=1, source_target_pairs={{4,0},{5,1},{8,4},{9,5},{12,8},{13,9},{14,12},{15,13},{10,14},{11,... | collective-permute-start | bytes 221192 | tf_op jit(solution)/shard_map/ppermute | solution.py:667
  41.9 8.2 %copy-start = (bf16[72,1152]{1,0:T(8,128)(2,1)S(1)}, bf16[72,1152]{1,0:T(8,128)(2,1)}, u32[]{:S(2)}) copy-start(bf16[72,1152]{1,0:T(8,128)(2,1)} %refs_0_.1) | copy-start | bytes 497668
  41.9 6.2 %collective-permute-start.15 = (bf16[72,640]{1,0:T(8,128)(2,1)S(1)}, bf16[72,640]{1,0:T(8,128)(2,1)S(1)}, u32[]{:S(2)}, u32[]{:S(2)}) collective-permute-start(bf16[72,640]{1,0:T(8,128)(2,1)S(1)} %slice.12), channel_id=1, source_target_pairs={{0,4},{1,5},{4,8},{5,9},{8,12},{9,13},{12,14},{13,15},{14,10},{15,... | collective-permute-start | bytes 276488 | tf_op jit(solution)/shard_map/ppermute | solution.py:667
  43.5 5.0 %collective-permute-start.13 = (bf16[128,512]{1,0:T(8,128)(2,1)S(1)}, bf16[128,512]{1,0:T(8,128)(2,1)S(1)}, u32[]{:S(2)}, u32[]{:S(2)}) collective-permute-start(bf16[128,512]{1,0:T(8,128)(2,1)S(1)} %collective-permute-done.9.refs_0_), channel_id=1, source_target_pairs={{0,4},{1,5},{4,8},{5,9},{8,12},{9,13},{12,14},{13,15},{14,10},{15,... | collective-permute-start | bytes 393224 | tf_op jit(solution)/shard_map/ppermute | solution.py:667
  45.1 5.0 %collective-permute-start.14 = (bf16[128,512]{1,0:T(8,128)(2,1)S(1)}, bf16[128,512]{1,0:T(8,128)(2,1)S(1)}, u32[]{:S(2)}, u32[]{:S(2)}) collective-permute-start(bf16[128,512]{1,0:T(8,128)(2,1)S(1)} %collective-permute-done.10.refs_1_), channel_id=1, source_target_pairs={{4,0},{5,1},{8,4},{9,5},{12,8},{13,9},{14,12},{15,13},{10,14},{11,... | collective-permute-start | bytes 393224 | tf_op jit(solution)/shard_map/ppermute | solution.py:667
  50.2 7.4 %collective-permute-start.19 = (bf16[576,1152]{1,0:T(8,128)(2,1)S(1)}, bf16[576,1152]{1,0:T(8,128)(2,1)S(1)}, u32[]{:S(2)}, u32[]{:S(2)}) collective-permute-start(bf16[576,1152]{1,0:T(8,128)(2,1)S(1)} %bitcast.3), channel_id=1, source_target_pairs={{0,1},{1,0},{2,3},{3,2},{4,5},{5,4},{6,7},{7,6},{8,9},{9,8},{10,11... | collective-permute-start | bytes 3981320 | tf_op jit(solution)/shard_map/ppermute | solution.py:667
  50.3 4.7 %collective-permute-start.18 = (bf16[64,512]{1,0:T(8,128)(2,1)S(1)}, bf16[64,512]{1,0:T(8,128)(2,1)S(1)}, u32[]{:S(2)}, u32[]{:S(2)}) collective-permute-start(bf16[64,512]{1,0:T(8,128)(2,1)S(1)} %slice.15), channel_id=1, source_target_pairs={{4,0},{5,1},{8,4},{9,5},{12,8},{13,9},{14,12},{15,13},{10,14},{11,... | collective-permute-start | bytes 196616 | tf_op jit(solution)/shard_map/ppermute | solution.py:667
  50.8 4.3 %collective-permute-start.17 = (bf16[64,512]{1,0:T(8,128)(2,1)S(1)}, bf16[64,512]{1,0:T(8,128)(2,1)S(1)}, u32[]{:S(2)}, u32[]{:S(2)}) collective-permute-start(bf16[64,512]{1,0:T(8,128)(2,1)S(1)} %slice.14), channel_id=1, source_target_pairs={{0,4},{1,5},{4,8},{5,9},{8,12},{9,13},{12,14},{13,15},{14,10},{15,... | collective-permute-start | bytes 196616 | tf_op jit(solution)/shard_map/ppermute | solution.py:667
  58.6 1.4 %collective-permute-start.20 = (bf16[64,1152]{1,0:T(8,128)(2,1)S(1)}, bf16[64,1152]{1,0:T(8,128)(2,1)S(1)}, u32[]{:S(2)}, u32[]{:S(2)}) collective-permute-start(bf16[64,1152]{1,0:T(8,128)(2,1)S(1)} %get-tuple-element.64), channel_id=1, source_target_pairs={{0,1},{1,0},{2,3},{3,2},{4,5},{5,4},{6,7},{7,6},{8,9},{9,8},{10,11... | collective-permute-start | bytes 442376 | tf_op jit(solution)/shard_map/ppermute | solution.py:667

commit v5 on v4

--- a/solution.py
+++ b/solution.py
@@ -691,19 +691,21 @@
     keep, other = convolve(
         frame_counts, window_lengths, clip, before, after, conv_first, conv_second, patch_weight
     )
+    other, wu_a, wu_b = tied(other, *weight_two)
+    weight_two = (wu_a, wu_b)
     got = send(other, cores)
+    weight_three = both_ways(*weight_two)
     block = jnp.concatenate([keep, got], axis=0)
     one = both_ways(block, block)
     queries = make_queries(window_lengths, block, centered, query_weight, query_row)
-    *one, queries, wu_a, wu_b = tied(*one, queries, *weight_two)
-    weight_two = (wu_a, wu_b)
+    *one, queries = tied(*one, queries)
     two = both_ways(*one)
-    weight_three = both_ways(*weight_two)
     acc_one = step_attention((-1, 1), window_lengths, one, folded, key_row, queries)
-    *two, acc_one, wt_a, wt_b = tied(*two, acc_one, *weight_three)
-    three = both_ways(*two)
+    wt_a, wt_b, acc_one = tied(*weight_three, acc_one)
     cut = 640
     weight_four = both_ways(wt_a[:, :cut], wt_b[:, cut:])
+    *two, acc_one = tied(*two, acc_one)
+    three = both_ways(*two)
     acc_two = step_attention((-2, 2), window_lengths, two, folded, key_row, queries)
     *three, acc_two, wf_a, wf_b = tied(*three, acc_two, *weight_four)
     four = both_ways(three[0][:64], three[1][64:])

time: 61.6 us -> 57.2 us (0.929)
  waiting for transfers between devices: 11.9 us -> 7.98 us
    ppermute x21, waiting for transfers between devices: 11.9 us -> 7.98 us  [send(): return lax.ppermute(array, 'seq', pairs)]
  transfers between devices with their start and end apart: 21 -> 21, of which waited for: 9 -> 8; matrix products, arithmetic and copies ran while one was open for 0% -> 0% of each run, Pallas kernels for 28% -> 36%
where the time goes in v5:
time: 57.2 us; the launch traced here: 57 us
  starting transfers between devices  24.2 us (42%)
  Pallas kernels  23.2 us (41%)
  waiting for transfers between devices  7.98 us (14%)
  local copies, waits for them, and re-layouts  1.35 us (2%)
    ppermute x21, starting transfers between devices, send(): return lax.ppermute(array, 'seq', pairs)  24.2 us
    pallas_call x4, Pallas kernels, step_attention(): pl.pallas_call(functools.partial(step_kernel, offsets), out_shape=ACC, in...  9.97 us
    ppermute x21, waiting for transfers between devices, send(): return lax.ppermute(array, 'seq', pairs)  7.98 us
    pallas_call x1, Pallas kernels, fold(): pl.pallas_call(fold_kernel, out_shape=(jax.ShapeDtypeStruct((2 * D, inner...  5.67 us
    pallas_call x1, Pallas kernels, convolve(): pl.pallas_call(conv_kernel, out_shape=(out, out), in_specs=[ANY] * 3 + [V...  3.62 us
    pallas_call x1, Pallas kernels, make_queries(): pl.pallas_call(query_kernel, out_shape=jax.ShapeDtypeStruct((HEADS, 128,...  1.53 us
    pallas_call x1, Pallas kernels, merge(): pl.pallas_call(merge_kernel, out_shape=jax.ShapeDtypeStruct((128, D), BF1...  1.35 us
    unnamed x21, local copies, waits for them, and re-layouts  1.31 us
  transfers between devices with their start and end apart: 21, of which 8 were waited for; matrix products, arithmetic and copies ran while one was open for 0% of the time, Pallas kernels for 36%

profile of v5, /device:TPU:0, one launch (start us, length us, event | category | flops | bytes accessed | tf_op | source)
XLA Modules:
  0.0 57.0 jit_solution(6592260153963635714)
XLA Ops:
  0.0 2.5 %collective-permute-start = (bf16[8,2,32,128]{3,2,1,0:T(8,128)(2,1)}, bf16[8,2,32,128]{3,2,1,0:T(8,128)(2,1)S(1)}, u32[]{:S(2)}, u32[]{:S(2)}) collective-permute-start(bf16[8,2,32,128]{3,2,1,0:T(8,128)(2,1)} %own_any.1), channel_id=1, source_target_pairs={{0,1},{1,2},{2,3},{3,4},{4,5},{5,6},{6,7},{7,8},{8,9},{9,10},{10,1... | collective-permute-start | bytes 393224 | tf_op jit(solution)/shard_map/ppermute | solution.py:667
  2.5 1.3 %collective-permute-start.1 = (bf16[8,2,32,128]{3,2,1,0:T(8,128)(2,1)}, bf16[8,2,32,128]{3,2,1,0:T(8,128)(2,1)S(1)}, u32[]{:S(2)}, u32[]{:S(2)}) collective-permute-start(bf16[8,2,32,128]{3,2,1,0:T(8,128)(2,1)} %own_any.1), channel_id=1, source_target_pairs={{1,0},{2,1},{3,2},{4,3},{5,4},{6,5},{7,6},{8,7},{9,8},{10,9},{11,1... | collective-permute-start | bytes 393224 | tf_op jit(solution)/shard_map/ppermute | solution.py:667
  3.8 5.9 %collective-permute-start.2 = (bf16[72,1152]{1,0:T(8,128)(2,1)}, bf16[72,1152]{1,0:T(8,128)(2,1)S(1)}, u32[]{:S(2)}, u32[]{:S(2)}) collective-permute-start(bf16[72,1152]{1,0:T(8,128)(2,1)} %refs_0_.1), channel_id=1, source_target_pairs={{0,4},{1,5},{4,8},{5,9},{8,12},{9,13},{12,14},{13,15},{14,10},{15,... | collective-permute-start | bytes 497672 | tf_op jit(solution)/shard_map/ppermute | solution.py:667
  9.7 0.0 collective-permute-start.3
  9.7 1.3 %copy-done.3 = bf16[512,1152]{1,0:T(8,128)(2,1)S(1)} copy-done((bf16[512,1152]{1,0:T(8,128)(2,1)S(1)}, bf16[512,1152]{1,0:T(8,128)(2,1)}, u32[]{:S(2)}) %copy-start.3) | copy-done | bytes 1179672
  11.0 5.7 %fold.1 = (bf16[2304,512]{1,0:T(8,128)(2,1)S(1)}, bf16[1152,1152]{1,0:T(8,128)(2,1)S(1)}, bf16[512,1152]{1,0:T(8,128)(2,1)S(1)}) custom-call(bf16[512,1152]{1,0:T(8,128)(2,1)S(1)} %copy-done.3, bf16[1152,3456]{1,0:T(8,128)(2,1)} %qkv_any.1), custom_call_target="tpu_custom_call" | custom-call | flops 2717908992 | bytes 12582912 | tf_op jit(solution)/shard_map/fold/pallas_call | solution.py:252
  16.7 0.0 collective-permute-done.2.refs_1_
  16.7 0.0 copy-start.2
  16.7 2.1 %collective-permute-start.4 = (bf16[72,1152]{1,0:T(8,128)(2,1)S(1)}, bf16[72,1152]{1,0:T(8,128)(2,1)S(1)}, u32[]{:S(2)}, u32[]{:S(2)}) collective-permute-start(bf16[72,1152]{1,0:T(8,128)(2,1)S(1)} %collective-permute-done.2.refs_1_), channel_id=1, source_target_pairs={{0,4},{1,5},{4,8},{5,9},{8,12},{9,13},{12,14},{13,15},{14,10},{15,... | collective-permute-start | bytes 497672 | tf_op jit(solution)/shard_map/ppermute | solution.py:667
  18.8 3.6 %convolve.1 = (bf16[64,512]{1,0:T(8,128)(2,1)S(1)}, bf16[64,512]{1,0:T(8,128)(2,1)S(1)}) custom-call(s32[3]{0:T(128)S(1)} %copy-done.8, s32[1,3]{1,0:T(1,128)S(1)} %copy-done.1, bf16[8,2,32,128]{3,2,1,0:T(8,128)(2,1)S(1)} %copy-done.7, bf16[8,2,32,128]{3,2,1,0:T(8,128)(2,1)S(1)} %collective-permute-done.before_ref, ...), custom_call_target="tpu_custom_call" | custom-call | flops 2147483648 | bytes 4194304 | tf_op jit(solution)/shard_map/convolve/pallas_call | solution.py:395
  22.5 1.6 %collective-permute-done.5.refs_4_ = bf16[72,1152]{1,0:T(8,128)(2,1)S(1)} collective-permute-done((bf16[72,1152]{1,0:T(8,128)(2,1)S(1)}, bf16[72,1152]{1,0:T(8,128)(2,1)S(1)}, u32[]{:S(2)}, u32[]{:S(2)}) %collective-permute-start.5) | collective-permute-done | bytes 165920 | tf_op jit(solution)/shard_map/ppermute | solution.py:667
  24.1 1.2 %collective-permute-done.6 = bf16[64,512]{1,0:T(8,128)(2,1)S(1)} collective-permute-done((bf16[64,512]{1,0:T(8,128)(2,1)S(1)}, bf16[64,512]{1,0:T(8,128)(2,1)S(1)}, u32[]{:S(2)}, u32[]{:S(2)}) %collective-permute-start.6) | collective-permute-done | bytes 65568 | tf_op jit(solution)/shard_map/ppermute | solution.py:667
  25.4 0.0 collective-permute-start.8
  25.4 2.0 %collective-permute-start.7 = (bf16[128,512]{1,0:T(8,128)(2,1)S(1)}, bf16[128,512]{1,0:T(8,128)(2,1)S(1)}, u32[]{:S(2)}, u32[]{:S(2)}) collective-permute-start(bf16[128,512]{1,0:T(8,128)(2,1)S(1)} %constant_dynamic-update-slice_fusion.block_ref.refs_0_), channel_id=1, source_target_pairs={{0,4},{1,5},{4,8},{5,9},{8,12},{9,13},{12,14},{13,15},{14,10},{15,... | collective-permute-start | bytes 393224 | tf_op jit(solution)/shard_map/ppermute | solution.py:667
  27.4 1.6 %collective-permute-start.11 = (bf16[72,1152]{1,0:T(8,128)(2,1)S(1)}, bf16[72,1152]{1,0:T(8,128)(2,1)S(1)}, u32[]{:S(2)}, u32[]{:S(2)}) collective-permute-start(bf16[72,1152]{1,0:T(8,128)(2,1)S(1)} %collective-permute-done.4.refs_3_), channel_id=1, source_target_pairs={{0,4},{1,5},{4,8},{5,9},{8,12},{9,13},{12,14},{13,15},{14,10},{15,... | collective-permute-start | bytes 497672 | tf_op jit(solution)/shard_map/ppermute | solution.py:667
  29.0 0.4 collective-permute-start.12
  29.4 1.5 %queries.1.refs_4_.refs_5_ = bf16[16,128,80]{2,1,0:T(8,128)(2,1)S(1)} custom-call(s32[1,3]{1,0:T(1,128)S(1)} %copy-done.1, bf16[128,512]{1,0:T(8,128)(2,1)S(1)} %constant_dynamic-update-slice_fusion.block_ref.refs_0_, bf16[512,1152]{1,0:T(8,128)(2,1)S(1)} %get-tuple-element.45.centered_ref, bf16[1152,1152]{1,0:T(8,128)(2,1)S(1)} %get-tuple-element.46.query_ref, ...), custom_call_target="tpu_custom_call" | custom-call | flops 1073741824 | bytes 4194304 | tf_op jit(solution)/shard_map/queries/pallas_call | solution.py:522
  31.0 0.0 collective-permute-done.8.refs_1_
  31.0 0.8 %collective-permute-done.7.refs_0_ = bf16[128,512]{1,0:T(8,128)(2,1)S(1)} collective-permute-done((bf16[128,512]{1,0:T(8,128)(2,1)S(1)}, bf16[128,512]{1,0:T(8,128)(2,1)S(1)}, u32[]{:S(2)}, u32[]{:S(2)}) %collective-permute-start.7) | collective-permute-done | bytes 131104 | tf_op jit(solution)/shard_map/ppermute | solution.py:667
  31.8 2.0 %collective-permute-start.9 = (bf16[128,512]{1,0:T(8,128)(2,1)S(1)}, bf16[128,512]{1,0:T(8,128)(2,1)S(1)}, u32[]{:S(2)}, u32[]{:S(2)}) collective-permute-start(bf16[128,512]{1,0:T(8,128)(2,1)S(1)} %collective-permute-done.7.refs_0_), channel_id=1, source_target_pairs={{0,4},{1,5},{4,8},{5,9},{8,12},{9,13},{12,14},{13,15},{14,10},{15,... | collective-permute-start | bytes 393224 | tf_op jit(solution)/shard_map/ppermute | solution.py:667
  33.8 0.0 collective-permute-start.10
  33.8 2.5 %step_attention.4.refs_0_ = f32[16,80,128]{2,1,0:T(8,128)S(1)} custom-call(s32[1,3]{1,0:T(1,128)S(1)} %copy-done.1, bf16[128,512]{1,0:T(8,128)(2,1)S(1)} %collective-permute-done.7.refs_0_, bf16[128,512]{1,0:T(8,128)(2,1)S(1)} %collective-permute-done.8.refs_1_, bf16[2304,512]{1,0:T(8,128)(2,1)S(1)} %get-tuple-element.51.refs_2_.refs_3_, ...), custom_call_target="tpu_custom_call" | custom-call | flops 1744830464 | bytes 5242880 | tf_op jit(solution)/shard_map/step_attention/pallas_call | solution.py:550
  36.3 0.0 collective-permute-done.11.refs_5_
  36.4 0.0 collective-permute-done.12.refs_6_
  36.4 1.1 %collective-permute-start.16 = (bf16[72,512]{1,0:T(8,128)(2,1)S(1)}, bf16[72,512]{1,0:T(8,128)(2,1)S(1)}, u32[]{:S(2)}, u32[]{:S(2)}) collective-permute-start(bf16[72,512]{1,0:T(8,128)(2,1)S(1)} %slice.13), channel_id=1, source_target_pairs={{4,0},{5,1},{8,4},{9,5},{12,8},{13,9},{14,12},{15,13},{10,14},{11,... | collective-permute-start | bytes 221192 | tf_op jit(solution)/shard_map/ppermute | solution.py:667
  37.5 0.0 copy-start
  37.5 1.0 %collective-permute-start.15 = (bf16[72,640]{1,0:T(8,128)(2,1)S(1)}, bf16[72,640]{1,0:T(8,128)(2,1)S(1)}, u32[]{:S(2)}, u32[]{:S(2)}) collective-permute-start(bf16[72,640]{1,0:T(8,128)(2,1)S(1)} %slice.12), channel_id=1, source_target_pairs={{0,4},{1,5},{4,8},{5,9},{8,12},{9,13},{12,14},{13,15},{14,10},{15,... | collective-permute-start | bytes 276488 | tf_op jit(solution)/shard_map/ppermute | solution.py:667
  38.5 0.7 %collective-permute-done.10.refs_1_ = bf16[128,512]{1,0:T(8,128)(2,1)S(1)} collective-permute-done((bf16[128,512]{1,0:T(8,128)(2,1)S(1)}, bf16[128,512]{1,0:T(8,128)(2,1)S(1)}, u32[]{:S(2)}, u32[]{:S(2)}) %collective-permute-start.10) | collective-permute-done | bytes 131104 | tf_op jit(solution)/shard_map/ppermute | solution.py:667
  39.2 1.5 %collective-permute-start.13 = (bf16[128,512]{1,0:T(8,128)(2,1)S(1)}, bf16[128,512]{1,0:T(8,128)(2,1)S(1)}, u32[]{:S(2)}, u32[]{:S(2)}) collective-permute-start(bf16[128,512]{1,0:T(8,128)(2,1)S(1)} %collective-permute-done.9.refs_0_), channel_id=1, source_target_pairs={{0,4},{1,5},{4,8},{5,9},{8,12},{9,13},{12,14},{13,15},{14,10},{15,... | collective-permute-start | bytes 393224 | tf_op jit(solution)/shard_map/ppermute | solution.py:667
  40.7 0.5 collective-permute-start.14
  41.2 2.5 %step_attention.5.refs_1_ = f32[16,80,128]{2,1,0:T(8,128)S(1)} custom-call(s32[1,3]{1,0:T(1,128)S(1)} %copy-done.1, bf16[128,512]{1,0:T(8,128)(2,1)S(1)} %collective-permute-done.9.refs_0_, bf16[128,512]{1,0:T(8,128)(2,1)S(1)} %collective-permute-done.10.refs_1_, bf16[2304,512]{1,0:T(8,128)(2,1)S(1)} %get-tuple-element.51.refs_2_.refs_3_, ...), custom_call_target="tpu_custom_call" | custom-call | flops 1744830464 | bytes 5242880 | tf_op jit(solution)/shard_map/step_attention/pallas_call | solution.py:550
  43.7 0.0 collective-permute-done.16.refs_8_
  43.7 0.0 collective-permute-done.15.refs_7_
  43.7 0.4 collective-permute-done.13.refs_0_
  44.2 1.5 %collective-permute-done.14.refs_1_ = bf16[128,512]{1,0:T(8,128)(2,1)S(1)} collective-permute-done((bf16[128,512]{1,0:T(8,128)(2,1)S(1)}, bf16[128,512]{1,0:T(8,128)(2,1)S(1)}, u32[]{:S(2)}, u32[]{:S(2)}) %collective-permute-start.14) | collective-permute-done | bytes 131104 | tf_op jit(solution)/shard_map/ppermute | solution.py:667
  45.7 0.1 pack.1
  45.8 0.1 collective-permute-start.19
  45.9 0.6 collective-permute-start.18
  46.5 1.5 %collective-permute-start.17 = (bf16[64,512]{1,0:T(8,128)(2,1)S(1)}, bf16[64,512]{1,0:T(8,128)(2,1)S(1)}, u32[]{:S(2)}, u32[]{:S(2)}) collective-permute-start(bf16[64,512]{1,0:T(8,128)(2,1)S(1)} %slice.14), channel_id=1, source_target_pairs={{0,4},{1,5},{4,8},{5,9},{8,12},{9,13},{12,14},{13,15},{14,10},{15,... | collective-permute-start | bytes 196616 | tf_op jit(solution)/shard_map/ppermute | solution.py:667
  48.0 2.5 %step_attention.6.refs_2_ = f32[16,80,128]{2,1,0:T(8,128)S(1)} custom-call(s32[1,3]{1,0:T(1,128)S(1)} %copy-done.1, bf16[128,512]{1,0:T(8,128)(2,1)S(1)} %collective-permute-done.13.refs_0_, bf16[128,512]{1,0:T(8,128)(2,1)S(1)} %collective-permute-done.14.refs_1_, bf16[2304,512]{1,0:T(8,128)(2,1)S(1)} %get-tuple-element.51.refs_2_.refs_3_, ...), custom_call_target="tpu_custom_call" | custom-call | flops 1744830464 | bytes 5242880 | tf_op jit(solution)/shard_map/step_attention/pallas_call | solution.py:550
  50.5 0.0 collective-permute-done.18.refs_2_
  50.5 0.2 collective-permute-done.17.refs_1_
  50.7 2.5 %step_attention.7.refs_3_ = f32[16,80,128]{2,1,0:T(8,128)S(1)} custom-call(s32[1,3]{1,0:T(1,128)S(1)} %copy-done.1, bf16[128,512]{1,0:T(8,128)(2,1)S(1)} %constant_dynamic-update-slice_fusion.block_ref.refs_0_, bf16[64,512]{1,0:T(8,128)(2,1)S(1)} %collective-permute-done.17.refs_1_, bf16[64,512]{1,0:T(8,128)(2,1)S(1)} %collective-permute-done.18.refs_2_, ...), custom_call_target="tpu_custom_call" | custom-call | flops 1744830464 | bytes 5242880 | tf_op jit(solution)/shard_map/step_attention/pallas_call | solution.py:550
  53.2 0.0 collective-permute-done.19.refs_5_
  53.2 1.0 %project_out.1 = (bf16[64,1152]{1,0:T(8,128)(2,1)S(1)}, bf16[64,1152]{1,0:T(8,128)(2,1)S(1)}) custom-call(f32[16,80,128]{2,1,0:T(8,128)S(1)} %step_attention.4.refs_0_, f32[16,80,128]{2,1,0:T(8,128)S(1)} %step_attention.5.refs_1_, f32[16,80,128]{2,1,0:T(8,128)S(1)} %step_attention.6.refs_2_, f32[16,80,128]{2,1,0:T(8,128)S(1)} %step_attention.7.refs_3_, ...), custom_call_target="tpu_custom_call" | custom-call | flops 377487360 | bytes 4194304 | tf_op jit(solution)/shard_map/project_out/pallas_call | solution.py:595
  54.2 0.1 collective-permute-start.20
  54.3 1.4 %collective-permute-done.20.got_ref = bf16[64,1152]{1,0:T(8,128)(2,1)S(1)} collective-permute-done((bf16[64,1152]{1,0:T(8,128)(2,1)S(1)}, bf16[64,1152]{1,0:T(8,128)(2,1)S(1)}, u32[]{:S(2)}, u32[]{:S(2)}) %collective-permute-start.20) | collective-permute-done | bytes 147488 | tf_op jit(solution)/shard_map/ppermute | solution.py:667
  55.7 1.3 %merge.1 = bf16[128,1152]{1,0:T(8,128)(2,1)} custom-call(s32[1,3]{1,0:T(1,128)S(1)} %copy-done.1, bf16[64,1152]{1,0:T(8,128)(2,1)S(1)} %get-tuple-element.67.keep_ref, bf16[64,1152]{1,0:T(8,128)(2,1)S(1)} %collective-permute-done.20.got_ref), custom_call_target="tpu_custom_call" | custom-call | tf_op jit(solution)/shard_map/merge/pallas_call | solution.py:645
  (30 shorter events, 0.1 us)
Async XLA Ops:
  0.0 18.8 %copy-start.1 = (s32[1,3]{1,0:T(1,128)S(1)}, s32[1,3]{1,0:T(1,128)}, u32[]{:S(2)}) copy-start(s32[1,3]{1,0:T(1,128)} %lengths_ref.11) | copy-start | bytes 40
  0.0 16.7 %collective-permute-start = (bf16[8,2,32,128]{3,2,1,0:T(8,128)(2,1)}, bf16[8,2,32,128]{3,2,1,0:T(8,128)(2,1)S(1)}, u32[]{:S(2)}, u32[]{:S(2)}) collective-permute-start(bf16[8,2,32,128]{3,2,1,0:T(8,128)(2,1)} %own_any.1), channel_id=1, source_target_pairs={{0,1},{1,2},{2,3},{3,4},{4,5},{5,6},{6,7},{7,8},{8,9},{9,10},{10,1... | collective-permute-start | bytes 393224 | tf_op jit(solution)/shard_map/ppermute | solution.py:667
  2.5 14.2 %collective-permute-start.1 = (bf16[8,2,32,128]{3,2,1,0:T(8,128)(2,1)}, bf16[8,2,32,128]{3,2,1,0:T(8,128)(2,1)S(1)}, u32[]{:S(2)}, u32[]{:S(2)}) collective-permute-start(bf16[8,2,32,128]{3,2,1,0:T(8,128)(2,1)} %own_any.1), channel_id=1, source_target_pairs={{1,0},{2,1},{3,2},{4,3},{5,4},{6,5},{7,6},{8,7},{9,8},{10,9},{11,1... | collective-permute-start | bytes 393224 | tf_op jit(solution)/shard_map/ppermute | solution.py:667
  3.8 12.9 %collective-permute-start.2 = (bf16[72,1152]{1,0:T(8,128)(2,1)}, bf16[72,1152]{1,0:T(8,128)(2,1)S(1)}, u32[]{:S(2)}, u32[]{:S(2)}) collective-permute-start(bf16[72,1152]{1,0:T(8,128)(2,1)} %refs_0_.1), channel_id=1, source_target_pairs={{0,4},{1,5},{4,8},{5,9},{8,12},{9,13},{12,14},{13,15},{14,10},{15,... | collective-permute-start | bytes 497672 | tf_op jit(solution)/shard_map/ppermute | solution.py:667
  9.7 7.0 %collective-permute-start.3 = (bf16[72,1152]{1,0:T(8,128)(2,1)}, bf16[72,1152]{1,0:T(8,128)(2,1)S(1)}, u32[]{:S(2)}, u32[]{:S(2)}) collective-permute-start(bf16[72,1152]{1,0:T(8,128)(2,1)} %refs_0_.1), channel_id=1, source_target_pairs={{4,0},{5,1},{8,4},{9,5},{12,8},{13,9},{14,12},{15,13},{10,14},{11,... | collective-permute-start | bytes 497672 | tf_op jit(solution)/shard_map/ppermute | solution.py:667
  9.7 1.3 %copy-start.3 = (bf16[512,1152]{1,0:T(8,128)(2,1)S(1)}, bf16[512,1152]{1,0:T(8,128)(2,1)}, u32[]{:S(2)}) copy-start(bf16[512,1152]{1,0:T(8,128)(2,1)} %patch_ref.1) | copy-start | bytes 3538948
  10.9 7.8 %copy-start.4 = (bf16[512,1152]{1,0:T(8,128)(2,1)S(1)}, bf16[512,1152]{1,0:T(8,128)(2,1)}, u32[]{:S(2)}) copy-start(bf16[512,1152]{1,0:T(8,128)(2,1)} %patch_ref.1) | copy-start | bytes 3538948
  11.0 7.8 %copy-start.5 = (bf16[3,3,3,128,128]{4,3,2,1,0:T(8,128)(2,1)S(1)}, bf16[3,3,3,128,128]{4,3,2,1,0:T(8,128)(2,1)}, u32[]{:S(2)}) copy-start(bf16[3,3,3,128,128]{4,3,2,1,0:T(8,128)(2,1)} %first_ref.1) | copy-start | bytes 2654212
  11.0 7.9 %copy-start.6 = (bf16[3,3,3,128,128]{4,3,2,1,0:T(8,128)(2,1)S(1)}, bf16[3,3,3,128,128]{4,3,2,1,0:T(8,128)(2,1)}, u32[]{:S(2)}) copy-start(bf16[3,3,3,128,128]{4,3,2,1,0:T(8,128)(2,1)} %second_ref.1) | copy-start | bytes 2654212
  11.0 7.9 %copy-start.7 = (bf16[8,2,32,128]{3,2,1,0:T(8,128)(2,1)S(1)}, bf16[8,2,32,128]{3,2,1,0:T(8,128)(2,1)}, u32[]{:S(2)}) copy-start(bf16[8,2,32,128]{3,2,1,0:T(8,128)(2,1)} %own_any.1) | copy-start | bytes 393220
  11.0 7.9 %copy-start.8 = (s32[3]{0:T(128)S(1)}, s32[3]{0:T(128)}, u32[]{:S(2)}) copy-start(s32[3]{0:T(128)} %counts_any.1) | copy-start | bytes 40
  16.7 12.7 %copy-start.2 = (f32[72]{0:T(128)S(1)}, f32[72]{0:T(128)}, u32[]{:S(2)}) copy-start(f32[72]{0:T(128)} %param.16) | copy-start | bytes 868
  16.7 5.8 %collective-permute-start.4 = (bf16[72,1152]{1,0:T(8,128)(2,1)S(1)}, bf16[72,1152]{1,0:T(8,128)(2,1)S(1)}, u32[]{:S(2)}, u32[]{:S(2)}) collective-permute-start(bf16[72,1152]{1,0:T(8,128)(2,1)S(1)} %collective-permute-done.2.refs_1_), channel_id=1, source_target_pairs={{0,4},{1,5},{4,8},{5,9},{8,12},{9,13},{12,14},{13,15},{14,10},{15,... | collective-permute-start | bytes 497672 | tf_op jit(solution)/shard_map/ppermute | solution.py:667
  18.8 5.3 %collective-permute-start.5 = (bf16[72,1152]{1,0:T(8,128)(2,1)S(1)}, bf16[72,1152]{1,0:T(8,128)(2,1)S(1)}, u32[]{:S(2)}, u32[]{:S(2)}) collective-permute-start(bf16[72,1152]{1,0:T(8,128)(2,1)S(1)} %collective-permute-done.3.refs_2_), channel_id=1, source_target_pairs={{4,0},{5,1},{8,4},{9,5},{12,8},{13,9},{14,12},{15,13},{10,14},{11,... | collective-permute-start | bytes 497672 | tf_op jit(solution)/shard_map/ppermute | solution.py:667
  24.1 1.3 %collective-permute-start.6 = (bf16[64,512]{1,0:T(8,128)(2,1)S(1)}, bf16[64,512]{1,0:T(8,128)(2,1)S(1)}, u32[]{:S(2)}, u32[]{:S(2)}) collective-permute-start(bf16[64,512]{1,0:T(8,128)(2,1)S(1)} %get-tuple-element.44), channel_id=1, source_target_pairs={{0,1},{1,0},{2,3},{3,2},{4,5},{5,4},{6,7},{7,6},{8,9},{9,8},{10,11... | collective-permute-start | bytes 196616 | tf_op jit(solution)/shard_map/ppermute | solution.py:667
  25.4 5.6 %collective-permute-start.8 = (bf16[128,512]{1,0:T(8,128)(2,1)S(1)}, bf16[128,512]{1,0:T(8,128)(2,1)S(1)}, u32[]{:S(2)}, u32[]{:S(2)}) collective-permute-start(bf16[128,512]{1,0:T(8,128)(2,1)S(1)} %constant_dynamic-update-slice_fusion.block_ref.refs_0_), channel_id=1, source_target_pairs={{4,0},{5,1},{8,4},{9,5},{12,8},{13,9},{14,12},{15,13},{10,14},{11,... | collective-permute-start | bytes 393224 | tf_op jit(solution)/shard_map/ppermute | solution.py:667
  25.4 6.4 %collective-permute-start.7 = (bf16[128,512]{1,0:T(8,128)(2,1)S(1)}, bf16[128,512]{1,0:T(8,128)(2,1)S(1)}, u32[]{:S(2)}, u32[]{:S(2)}) collective-permute-start(bf16[128,512]{1,0:T(8,128)(2,1)S(1)} %constant_dynamic-update-slice_fusion.block_ref.refs_0_), channel_id=1, source_target_pairs={{0,4},{1,5},{4,8},{5,9},{8,12},{9,13},{12,14},{13,15},{14,10},{15,... | collective-permute-start | bytes 393224 | tf_op jit(solution)/shard_map/ppermute | solution.py:667
  27.4 8.9 %collective-permute-start.11 = (bf16[72,1152]{1,0:T(8,128)(2,1)S(1)}, bf16[72,1152]{1,0:T(8,128)(2,1)S(1)}, u32[]{:S(2)}, u32[]{:S(2)}) collective-permute-start(bf16[72,1152]{1,0:T(8,128)(2,1)S(1)} %collective-permute-done.4.refs_3_), channel_id=1, source_target_pairs={{0,4},{1,5},{4,8},{5,9},{8,12},{9,13},{12,14},{13,15},{14,10},{15,... | collective-permute-start | bytes 497672 | tf_op jit(solution)/shard_map/ppermute | solution.py:667
  29.0 7.4 %collective-permute-start.12 = (bf16[72,1152]{1,0:T(8,128)(2,1)S(1)}, bf16[72,1152]{1,0:T(8,128)(2,1)S(1)}, u32[]{:S(2)}, u32[]{:S(2)}) collective-permute-start(bf16[72,1152]{1,0:T(8,128)(2,1)S(1)} %collective-permute-done.5.refs_4_), channel_id=1, source_target_pairs={{4,0},{5,1},{8,4},{9,5},{12,8},{13,9},{14,12},{15,13},{10,14},{11,... | collective-permute-start | bytes 497672 | tf_op jit(solution)/shard_map/ppermute | solution.py:667
  29.4 4.4 %copy-start.9 = (f32[72]{0:T(128)S(1)}, f32[72]{0:T(128)}, u32[]{:S(2)}) copy-start(f32[72]{0:T(128)} %param.17) | copy-start | bytes 868
  31.8 6.8 %collective-permute-start.9 = (bf16[128,512]{1,0:T(8,128)(2,1)S(1)}, bf16[128,512]{1,0:T(8,128)(2,1)S(1)}, u32[]{:S(2)}, u32[]{:S(2)}) collective-permute-start(bf16[128,512]{1,0:T(8,128)(2,1)S(1)} %collective-permute-done.7.refs_0_), channel_id=1, source_target_pairs={{0,4},{1,5},{4,8},{5,9},{8,12},{9,13},{12,14},{13,15},{14,10},{15,... | collective-permute-start | bytes 393224 | tf_op jit(solution)/shard_map/ppermute | solution.py:667
  33.8 5.4 %collective-permute-start.10 = (bf16[128,512]{1,0:T(8,128)(2,1)S(1)}, bf16[128,512]{1,0:T(8,128)(2,1)S(1)}, u32[]{:S(2)}, u32[]{:S(2)}) collective-permute-start(bf16[128,512]{1,0:T(8,128)(2,1)S(1)} %collective-permute-done.8.refs_1_), channel_id=1, source_target_pairs={{4,0},{5,1},{8,4},{9,5},{12,8},{13,9},{14,12},{15,13},{10,14},{11,... | collective-permute-start | bytes 393224 | tf_op jit(solution)/shard_map/ppermute | solution.py:667
  36.4 7.3 %collective-permute-start.16 = (bf16[72,512]{1,0:T(8,128)(2,1)S(1)}, bf16[72,512]{1,0:T(8,128)(2,1)S(1)}, u32[]{:S(2)}, u32[]{:S(2)}) collective-permute-start(bf16[72,512]{1,0:T(8,128)(2,1)S(1)} %slice.13), channel_id=1, source_target_pairs={{4,0},{5,1},{8,4},{9,5},{12,8},{13,9},{14,12},{15,13},{10,14},{11,... | collective-permute-start | bytes 221192 | tf_op jit(solution)/shard_map/ppermute | solution.py:667
  37.5 8.2 %copy-start = (bf16[72,1152]{1,0:T(8,128)(2,1)S(1)}, bf16[72,1152]{1,0:T(8,128)(2,1)}, u32[]{:S(2)}) copy-start(bf16[72,1152]{1,0:T(8,128)(2,1)} %refs_0_.1) | copy-start | bytes 497668
  37.5 6.2 %collective-permute-start.15 = (bf16[72,640]{1,0:T(8,128)(2,1)S(1)}, bf16[72,640]{1,0:T(8,128)(2,1)S(1)}, u32[]{:S(2)}, u32[]{:S(2)}) collective-permute-start(bf16[72,640]{1,0:T(8,128)(2,1)S(1)} %slice.12), channel_id=1, source_target_pairs={{0,4},{1,5},{4,8},{5,9},{8,12},{9,13},{12,14},{13,15},{14,10},{15,... | collective-permute-start | bytes 276488 | tf_op jit(solution)/shard_map/ppermute | solution.py:667
  39.2 5.0 %collective-permute-start.13 = (bf16[128,512]{1,0:T(8,128)(2,1)S(1)}, bf16[128,512]{1,0:T(8,128)(2,1)S(1)}, u32[]{:S(2)}, u32[]{:S(2)}) collective-permute-start(bf16[128,512]{1,0:T(8,128)(2,1)S(1)} %collective-permute-done.9.refs_0_), channel_id=1, source_target_pairs={{0,4},{1,5},{4,8},{5,9},{8,12},{9,13},{12,14},{13,15},{14,10},{15,... | collective-permute-start | bytes 393224 | tf_op jit(solution)/shard_map/ppermute | solution.py:667
  40.7 5.0 %collective-permute-start.14 = (bf16[128,512]{1,0:T(8,128)(2,1)S(1)}, bf16[128,512]{1,0:T(8,128)(2,1)S(1)}, u32[]{:S(2)}, u32[]{:S(2)}) collective-permute-start(bf16[128,512]{1,0:T(8,128)(2,1)S(1)} %collective-permute-done.10.refs_1_), channel_id=1, source_target_pairs={{4,0},{5,1},{8,4},{9,5},{12,8},{13,9},{14,12},{15,13},{10,14},{11,... | collective-permute-start | bytes 393224 | tf_op jit(solution)/shard_map/ppermute | solution.py:667
  45.8 7.4 %collective-permute-start.19 = (bf16[576,1152]{1,0:T(8,128)(2,1)S(1)}, bf16[576,1152]{1,0:T(8,128)(2,1)S(1)}, u32[]{:S(2)}, u32[]{:S(2)}) collective-permute-start(bf16[576,1152]{1,0:T(8,128)(2,1)S(1)} %bitcast.3), channel_id=1, source_target_pairs={{0,1},{1,0},{2,3},{3,2},{4,5},{5,4},{6,7},{7,6},{8,9},{9,8},{10,11... | collective-permute-start | bytes 3981320 | tf_op jit(solution)/shard_map/ppermute | solution.py:667
  45.9 4.6 %collective-permute-start.18 = (bf16[64,512]{1,0:T(8,128)(2,1)S(1)}, bf16[64,512]{1,0:T(8,128)(2,1)S(1)}, u32[]{:S(2)}, u32[]{:S(2)}) collective-permute-start(bf16[64,512]{1,0:T(8,128)(2,1)S(1)} %slice.15), channel_id=1, source_target_pairs={{4,0},{5,1},{8,4},{9,5},{12,8},{13,9},{14,12},{15,13},{10,14},{11,... | collective-permute-start | bytes 196616 | tf_op jit(solution)/shard_map/ppermute | solution.py:667
  46.5 4.3 %collective-permute-start.17 = (bf16[64,512]{1,0:T(8,128)(2,1)S(1)}, bf16[64,512]{1,0:T(8,128)(2,1)S(1)}, u32[]{:S(2)}, u32[]{:S(2)}) collective-permute-start(bf16[64,512]{1,0:T(8,128)(2,1)S(1)} %slice.14), channel_id=1, source_target_pairs={{0,4},{1,5},{4,8},{5,9},{8,12},{9,13},{12,14},{13,15},{14,10},{15,... | collective-permute-start | bytes 196616 | tf_op jit(solution)/shard_map/ppermute | solution.py:667
  54.2 1.4 %collective-permute-start.20 = (bf16[64,1152]{1,0:T(8,128)(2,1)S(1)}, bf16[64,1152]{1,0:T(8,128)(2,1)S(1)}, u32[]{:S(2)}, u32[]{:S(2)}) collective-permute-start(bf16[64,1152]{1,0:T(8,128)(2,1)S(1)} %get-tuple-element.68), channel_id=1, source_target_pairs={{0,1},{1,0},{2,3},{3,2},{4,5},{5,4},{6,7},{7,6},{8,9},{9,8},{10,11... | collective-permute-start | bytes 442376 | tf_op jit(solution)/shard_map/ppermute | solution.py:667

commit v6 on v5

--- a/solution.py
+++ b/solution.py
@@ -191,6 +191,8 @@
 HD = D // HEADS
 SLOT = 80
 MASK = 1024.0
+FOLD_MIB = 52
+CONV_MIB = 44
 F32 = jnp.float32
 BF16 = jnp.bfloat16
 VMEM = pl.BlockSpec(memory_space=pltpu.VMEM)
@@ -228,26 +230,38 @@
     return jnp.concatenate(rows, axis=0)
 
 
-def fold_kernel(patch_any, qkv_any, folded_ref, query_ref, centered_ref, patch_ref, qkv_ref, sems):
-    copies = [
-        pltpu.make_async_copy(patch_any, patch_ref, sems.at[0]),
-        pltpu.make_async_copy(qkv_any.at[:, pl.ds(D, D)], qkv_ref.at[0], sems.at[1]),
-        pltpu.make_async_copy(qkv_any.at[:, pl.ds(2 * D, D)], qkv_ref.at[1], sems.at[2]),
-        pltpu.make_async_copy(qkv_any.at[:, pl.ds(0, D)], query_ref, sems.at[3]),
+def fold_kernel(
+    patch_any, qkv_any, first_any, second_any,
+    folded_ref, query_ref, centered_ref, first_ref, second_ref, patch_ref, qkv_ref, sems,
+):
+    chunk = 384
+    pieces = 2 * D // chunk
+
+    def piece_copy(i):
+        columns = pl.ds(D + i * chunk, chunk)
+        return pltpu.make_async_copy(qkv_any.at[:, columns], qkv_ref.at[i], sems.at[i])
+
+    patch_copy = pltpu.make_async_copy(patch_any, patch_ref, sems.at[pieces])
+    late = [
+        pltpu.make_async_copy(first_any, first_ref, sems.at[pieces + 1]),
+        pltpu.make_async_copy(second_any, second_ref, sems.at[pieces + 2]),
+        pltpu.make_async_copy(qkv_any.at[:, pl.ds(0, D)], query_ref, sems.at[pieces + 3]),
     ]
-    for copy in copies:
+    copies = [piece_copy(i) for i in range(pieces)]
+    for copy in [patch_copy, *copies, *late]:
         copy.start()
-    copies[0].wait()
+    patch_copy.wait()
     patch = patch_ref[...].astype(F32)
     centered_ref[...] = (patch - jnp.mean(patch, axis=1, keepdims=True)).astype(BF16)
-    for part in range(2):
-        copies[part + 1].wait()
-        product = lax.dot_general(qkv_ref[part], centered_ref[...], TN, preferred_element_type=F32)
-        folded_ref[part * D : (part + 1) * D] = product.astype(BF16)
-    copies[3].wait()
-
-
-def fold(patch_weight, qkv_weight):
+    for i in range(pieces):
+        copies[i].wait()
+        product = lax.dot_general(qkv_ref[i], centered_ref[...], TN, preferred_element_type=F32)
+        folded_ref[i * chunk : (i + 1) * chunk] = product.astype(BF16)
+    for copy in late:
+        copy.wait()
+
+
+def fold(patch_weight, qkv_weight, conv_first, conv_second):
     inner = patch_weight.shape[0]
     return pl.pallas_call(
         fold_kernel,
@@ -255,18 +269,20 @@
             jax.ShapeDtypeStruct((2 * D, inner), BF16),
             jax.ShapeDtypeStruct((D, D), BF16),
             jax.ShapeDtypeStruct((inner, D), BF16),
+            jax.ShapeDtypeStruct(conv_first.shape, BF16),
+            jax.ShapeDtypeStruct(conv_second.shape, BF16),
         ),
-        in_specs=[ANY, ANY],
-        out_specs=(VMEM, VMEM, VMEM),
+        in_specs=[ANY] * 4,
+        out_specs=(VMEM,) * 5,
         scratch_shapes=[
-            pltpu.VMEM((inner, D), BF16),
-            pltpu.VMEM((2, D, D), BF16),
-            pltpu.SemaphoreType.DMA((4,)),
+            pltpu.VMEM(patch_weight.shape, BF16),
+            pltpu.VMEM((6, D, 384), BF16),
+            pltpu.SemaphoreType.DMA((10,)),
         ],
-        compiler_params=params(),
+        compiler_params=params(FOLD_MIB),
         name="fold",
         cost_estimate=pl.CostEstimate(flops=2 * inner * D * 2 * D, bytes_accessed=12 << 20, transcendentals=0),
-    )(patch_weight, qkv_weight)
+    )(patch_weight, qkv_weight, conv_first, conv_second)
 
 
 def frame_taps(counts_ref, frames):
@@ -284,13 +300,14 @@
 
 
 def conv_kernel(
-    counts_any, lengths_any, own_any, before_ref, after_ref, first_ref, second_ref, patch_ref,
-    keep_ref, send_ref, grid_one, grid_two, pixels, own_ref, counts_ref, lengths_ref, sems,
+    counts_any, lengths_any, own_any, patch_any, sibling_ref, other_ref, first_ref, second_ref,
+    keep_ref, send_ref, grid_one, grid_two, pixels, own_ref, patch_ref, counts_ref, lengths_ref, sems,
 ):
     copies = [
         pltpu.make_async_copy(own_any, own_ref, sems.at[0]),
         pltpu.make_async_copy(counts_any, counts_ref, sems.at[1]),
         pltpu.make_async_copy(lengths_any, lengths_ref, sems.at[2]),
+        pltpu.make_async_copy(patch_any, patch_ref, sems.at[3]),
     ]
     for copy in copies:
         copy.start()
@@ -310,11 +327,18 @@
         grid_one[g, frames + 1] = blank
     grid_two[0] = blank
     grid_two[frames + 1] = blank
-    sources = [before_ref, before_ref, own_ref, own_ref, after_ref, after_ref]
+    on_first = position % 2 == 0
+
+    def source_row(r):
+        if r in (2, 3):
+            return own_ref[:, r - 2].astype(F32)
+        sibling, other = sibling_ref[:, r % 2].astype(F32), other_ref[:, r % 2].astype(F32)
+        return jnp.where(on_first, other, sibling) if r < 2 else jnp.where(on_first, sibling, other)
+
     for r in (0, 1, 4, 5, 2, 3):
         if r == 2:
             copies[0].wait()
-        row = silu(sources[r][:, r % 2].astype(F32))
+        row = silu(source_row(r))
         parts = shifted(row)
         for g in range(2):
             four = r - 2 * g
@@ -370,6 +394,7 @@
     patches = jnp.concatenate(
         [pixels[a, pl.ds(b, tokens, 2), :] for a in range(2) for b in range(2)], axis=1
     )
+    copies[3].wait()
     embedded = jnp.dot(patches.astype(BF16), patch_ref[...], preferred_element_type=F32)
     centered = embedded - jnp.mean(embedded, axis=1, keepdims=True)
     variance = jnp.mean(centered * centered, axis=1, keepdims=True)
@@ -388,28 +413,29 @@
     send_ref[...] = send
 
 
-def convolve(counts, lengths, clip, before, after, conv_first, conv_second, patch_weight):
+def convolve(counts, lengths, clip, sibling_rows, other_rows, conv_first, conv_second, patch_weight):
     frames, _, cols, ch = clip.shape
     tokens = frames * cols // 2
     out = jax.ShapeDtypeStruct((tokens // 2, 4 * ch), BF16)
     return pl.pallas_call(
         conv_kernel,
         out_shape=(out, out),
-        in_specs=[ANY] * 3 + [VMEM] * 5,
+        in_specs=[ANY] * 4 + [VMEM] * 4,
         out_specs=(VMEM, VMEM),
         scratch_shapes=[
             pltpu.VMEM((2, frames + 2, cols, 12 * ch), BF16),
             pltpu.VMEM((frames + 2, cols, 12 * ch), BF16),
             pltpu.VMEM((2, frames * cols, ch), F32),
             pltpu.VMEM(clip.shape, BF16),
+            pltpu.VMEM(patch_weight.shape, BF16),
             pltpu.SMEM(counts.shape, jnp.int32),
             pltpu.SMEM(lengths.shape, jnp.int32),
-            pltpu.SemaphoreType.DMA((3,)),
+            pltpu.SemaphoreType.DMA((4,)),
         ],
-        compiler_params=params(),
+        compiler_params=params(CONV_MIB),
         name="convolve",
         cost_estimate=pl.CostEstimate(flops=2 << 30, bytes_accessed=4 << 20, transcendentals=1 << 18),
-    )(counts, lengths, clip, before, after, conv_first, conv_second, patch_weight)
+    )(counts, lengths, clip, patch_weight, sibling_rows, other_rows, conv_first, conv_second)
 
 
 def chip_at(place):
@@ -657,8 +683,7 @@
     out_weight, window_lengths,
 ):
     size = lax.axis_size("seq")
-    up = [(i, i + 1) for i in range(size - 1)]
-    down = [(j, i) for i, j in up]
+    facing = [(i, j) for i in range(1, size - 1, 2) for i, j in ((i, i + 1), (i + 1, i))]
     cores = [(i, i ^ 1) for i in range(size)]
     forward = ring_pairs()
     backward = [(j, i) for i, j in forward]
@@ -681,15 +706,17 @@
     def both_ways(ahead, behind):
         return send(ahead, forward), send(behind, backward)
 
-    before = send(clip, up)
-    after = send(clip, down)
+    sibling_rows = send(clip, cores)
+    other_rows = send(clip, facing)
     query_row, key_row = query_gain[None], key_gain[None]
     weight_one = both_ways(out_weight, out_weight)
-    folded, query_weight, centered = fold(patch_weight, qkv_weight)
-    before, after, *weight_one, folded = tied(before, after, *weight_one, folded)
+    folded, query_weight, centered, first, second = fold(
+        patch_weight, qkv_weight, conv_first, conv_second
+    )
+    sibling_rows, other_rows, *weight_one, folded = tied(sibling_rows, other_rows, *weight_one, folded)
     weight_two = both_ways(*weight_one)
     keep, other = convolve(
-        frame_counts, window_lengths, clip, before, after, conv_first, conv_second, patch_weight
+        frame_counts, window_lengths, clip, sibling_rows, other_rows, first, second, patch_weight
     )
     other, wu_a, wu_b = tied(other, *weight_two)
     weight_two = (wu_a, wu_b)

time: 57.2 us -> 55.8 us (0.976)
  Pallas kernels: 23.2 us -> 26.3 us
  starting transfers between devices: 24.2 us -> 21.1 us
  local copies, waits for them, and re-layouts: 1.35 us -> 0.08 us
    ppermute x21, starting transfers between devices: 24.2 us -> 21.1 us  [send(): return lax.ppermute(array, 'seq', pairs)]
    pallas_call x1, Pallas kernels: 5.67 us -> 8.51 us  [fold(): pl.pallas_call(fold_kernel, out_shape=(jax.ShapeDtypeStruct((2 * D, inner...]
    unnamed x21, local copies, waits for them, and re-layouts: 1.31 us -> 0.05 us
  transfers between devices with their start and end apart: 21 -> 21, of which waited for: 8 -> 9; matrix products, arithmetic and copies ran while one was open for 0% -> 0% of each run, Pallas kernels for 36% -> 43%
where the time goes in v6:
time: 55.8 us; the launch traced here: 55.6 us
  Pallas kernels  26.3 us (47%)
  starting transfers between devices  21.1 us (38%)
  waiting for transfers between devices  7.87 us (14%)
    ppermute x21, starting transfers between devices, send(): return lax.ppermute(array, 'seq', pairs)  21.1 us
    pallas_call x4, Pallas kernels, step_attention(): pl.pallas_call(functools.partial(step_kernel, offsets), out_shape=ACC, in...  9.97 us
    pallas_call x1, Pallas kernels, fold(): pl.pallas_call(fold_kernel, out_shape=(jax.ShapeDtypeStruct((2 * D, inner...  8.51 us
    ppermute x21, waiting for transfers between devices, send(): return lax.ppermute(array, 'seq', pairs)  7.87 us
    pallas_call x1, Pallas kernels, convolve(): pl.pallas_call(conv_kernel, out_shape=(out, out), in_specs=[ANY] * 4 + [V...  3.88 us
    pallas_call x1, Pallas kernels, make_queries(): pl.pallas_call(query_kernel, out_shape=jax.ShapeDtypeStruct((HEADS, 128,...  1.52 us
    pallas_call x1, Pallas kernels, merge(): pl.pallas_call(merge_kernel, out_shape=jax.ShapeDtypeStruct((128, D), BF1...  1.35 us
  transfers between devices with their start and end apart: 21, of which 9 were waited for; matrix products, arithmetic and copies ran while one was open for 0% of the time, Pallas kernels for 43%

profile of v6, /device:TPU:0, one launch (start us, length us, event | category | flops | bytes accessed | tf_op | source)
XLA Modules:
  0.0 55.6 jit_solution(14706175982017692003)
XLA Ops:
  0.0 0.5 collective-permute-start
  0.5 0.7 %collective-permute-start.1 = (bf16[8,2,32,128]{3,2,1,0:T(8,128)(2,1)}, bf16[8,2,32,128]{3,2,1,0:T(8,128)(2,1)S(1)}, u32[]{:S(2)}, u32[]{:S(2)}) collective-permute-start(bf16[8,2,32,128]{3,2,1,0:T(8,128)(2,1)} %own_any.1), channel_id=1, source_target_pairs={{1,2},{2,1},{3,4},{4,3},{5,6},{6,5},{7,8},{8,7},{9,10},{10,9},{11,... | collective-permute-start | bytes 393224 | tf_op jit(solution)/shard_map/ppermute | solution.py:692
  1.2 5.4 %collective-permute-start.2 = (bf16[72,1152]{1,0:T(8,128)(2,1)}, bf16[72,1152]{1,0:T(8,128)(2,1)S(1)}, u32[]{:S(2)}, u32[]{:S(2)}) collective-permute-start(bf16[72,1152]{1,0:T(8,128)(2,1)} %refs_0_.1), channel_id=1, source_target_pairs={{0,4},{1,5},{4,8},{5,9},{8,12},{9,13},{12,14},{13,15},{14,10},{15,... | collective-permute-start | bytes 497672 | tf_op jit(solution)/shard_map/ppermute | solution.py:692
  6.6 8.5 %fold.1 = (bf16[2304,512]{1,0:T(8,128)(2,1)}, bf16[1152,1152]{1,0:T(8,128)(2,1)}, bf16[512,1152]{1,0:T(8,128)(2,1)}, bf16[3,3,3,128,128]{4,3,2,1,0:T(8,128)(2,1)S(1)}, bf16[3,3,3,128,128]{4,3,2,1,0:T(8,128)(2,1)S(1)}) custom-call(bf16[512,1152]{1,0:T(8,128)(2,1)} %patch_any.3, bf16[1152,3456]{1,0:T(8,128)(2,1)} %qkv_any.1, ...), custom_call_target="tpu_custom_call" | custom-call | flops 2717908992 | bytes 12582912 | tf_op jit(solution)/shard_map/fold/pallas_call | solution.py:266
  15.1 0.0 collective-permute-done.sibling_ref
  15.1 0.0 collective-permute-done.1.other_ref
  15.1 0.0 collective-permute-done.3.refs_2_
  15.2 2.1 %collective-permute-start.4 = (bf16[72,1152]{1,0:T(8,128)(2,1)S(1)}, bf16[72,1152]{1,0:T(8,128)(2,1)S(1)}, u32[]{:S(2)}, u32[]{:S(2)}) collective-permute-start(bf16[72,1152]{1,0:T(8,128)(2,1)S(1)} %collective-permute-done.2.refs_1_), channel_id=1, source_target_pairs={{0,4},{1,5},{4,8},{5,9},{8,12},{9,13},{12,14},{13,15},{14,10},{15,... | collective-permute-start | bytes 497672 | tf_op jit(solution)/shard_map/ppermute | solution.py:692
  17.3 0.0 copy-start.5
  17.3 3.9 %convolve.1 = (bf16[64,512]{1,0:T(8,128)(2,1)S(1)}, bf16[64,512]{1,0:T(8,128)(2,1)S(1)}) custom-call(s32[3]{0:T(128)S(1)} %copy-done.8, s32[1,3]{1,0:T(1,128)S(1)} %copy-done.4, bf16[8,2,32,128]{3,2,1,0:T(8,128)(2,1)S(1)} %copy-done.7, bf16[512,1152]{1,0:T(8,128)(2,1)S(1)} %copy-done.2, bf16[8,2,32,128]{3,2,1,0:T(8,128)(2,1)S(1)} %collective-permute-done.sibling_ref, ...), custom_call_target="tpu_custom_call" | custom-call | flops 2147483648 | bytes 4194304 | tf_op jit(solution)/shard_map/convolve/pallas_call | solution.py:420
  21.2 0.3 collective-permute-done.4.refs_3_
  21.5 1.3 %collective-permute-done.5.refs_4_ = bf16[72,1152]{1,0:T(8,128)(2,1)S(1)} collective-permute-done((bf16[72,1152]{1,0:T(8,128)(2,1)S(1)}, bf16[72,1152]{1,0:T(8,128)(2,1)S(1)}, u32[]{:S(2)}, u32[]{:S(2)}) %collective-permute-start.5) | collective-permute-done | bytes 165920 | tf_op jit(solution)/shard_map/ppermute | solution.py:692
  22.8 0.0 collective-permute-start.6
  22.8 1.2 %collective-permute-done.6 = bf16[64,512]{1,0:T(8,128)(2,1)S(1)} collective-permute-done((bf16[64,512]{1,0:T(8,128)(2,1)S(1)}, bf16[64,512]{1,0:T(8,128)(2,1)S(1)}, u32[]{:S(2)}, u32[]{:S(2)}) %collective-permute-start.6) | collective-permute-done | bytes 65568 | tf_op jit(solution)/shard_map/ppermute | solution.py:692
  24.1 0.5 collective-permute-start.8
  24.5 1.6 %collective-permute-start.7 = (bf16[128,512]{1,0:T(8,128)(2,1)S(1)}, bf16[128,512]{1,0:T(8,128)(2,1)S(1)}, u32[]{:S(2)}, u32[]{:S(2)}) collective-permute-start(bf16[128,512]{1,0:T(8,128)(2,1)S(1)} %constant_dynamic-update-slice_fusion.block_ref.refs_0_), channel_id=1, source_target_pairs={{0,4},{1,5},{4,8},{5,9},{8,12},{9,13},{12,14},{13,15},{14,10},{15,... | collective-permute-start | bytes 393224 | tf_op jit(solution)/shard_map/ppermute | solution.py:692
  26.1 1.6 %collective-permute-start.11 = (bf16[72,1152]{1,0:T(8,128)(2,1)S(1)}, bf16[72,1152]{1,0:T(8,128)(2,1)S(1)}, u32[]{:S(2)}, u32[]{:S(2)}) collective-permute-start(bf16[72,1152]{1,0:T(8,128)(2,1)S(1)} %collective-permute-done.4.refs_3_), channel_id=1, source_target_pairs={{0,4},{1,5},{4,8},{5,9},{8,12},{9,13},{12,14},{13,15},{14,10},{15,... | collective-permute-start | bytes 497672 | tf_op jit(solution)/shard_map/ppermute | solution.py:692
  27.7 0.4 collective-permute-start.12
  28.1 0.0 copy-start.9
  28.1 1.5 %queries.1.refs_4_.refs_5_ = bf16[16,128,80]{2,1,0:T(8,128)(2,1)S(1)} custom-call(s32[1,3]{1,0:T(1,128)S(1)} %copy-done.4, bf16[128,512]{1,0:T(8,128)(2,1)S(1)} %constant_dynamic-update-slice_fusion.block_ref.refs_0_, bf16[512,1152]{1,0:T(8,128)(2,1)S(1)} %copy-done.1, bf16[1152,1152]{1,0:T(8,128)(2,1)S(1)} %copy-done, f32[1,72]{1,0:T(1,128)S(1)} %bitcast.5), custom_call_target="tpu_custom_call" | custom-call | flops 1073741824 | bytes 4194304 | tf_op jit(solution)/shard_map/queries/pallas_call | solution.py:548
  29.7 1.2 %collective-permute-done.7.refs_0_ = bf16[128,512]{1,0:T(8,128)(2,1)S(1)} collective-permute-done((bf16[128,512]{1,0:T(8,128)(2,1)S(1)}, bf16[128,512]{1,0:T(8,128)(2,1)S(1)}, u32[]{:S(2)}, u32[]{:S(2)}) %collective-permute-start.7) | collective-permute-done | bytes 131104 | tf_op jit(solution)/shard_map/ppermute | solution.py:692
  30.9 1.6 %collective-permute-start.9 = (bf16[128,512]{1,0:T(8,128)(2,1)S(1)}, bf16[128,512]{1,0:T(8,128)(2,1)S(1)}, u32[]{:S(2)}, u32[]{:S(2)}) collective-permute-start(bf16[128,512]{1,0:T(8,128)(2,1)S(1)} %collective-permute-done.7.refs_0_), channel_id=1, source_target_pairs={{0,4},{1,5},{4,8},{5,9},{8,12},{9,13},{12,14},{13,15},{14,10},{15,... | collective-permute-start | bytes 393224 | tf_op jit(solution)/shard_map/ppermute | solution.py:692
  32.5 0.5 collective-permute-start.10
  32.9 2.5 %step_attention.4.refs_0_ = f32[16,80,128]{2,1,0:T(8,128)S(1)} custom-call(s32[1,3]{1,0:T(1,128)S(1)} %copy-done.4, bf16[128,512]{1,0:T(8,128)(2,1)S(1)} %collective-permute-done.7.refs_0_, bf16[128,512]{1,0:T(8,128)(2,1)S(1)} %collective-permute-done.8.refs_1_, bf16[2304,512]{1,0:T(8,128)(2,1)S(1)} %copy-done.6, f32[1,72]{1,0:T(1,128)S(1)} %bitcast.6, ...), custom_call_target="tpu_custom_call" | custom-call | flops 1744830464 | bytes 5242880 | tf_op jit(solution)/shard_map/step_attention/pallas_call | solution.py:576
  35.4 0.0 collective-permute-done.11.refs_5_
  35.5 1.6 %collective-permute-start.16 = (bf16[72,512]{1,0:T(8,128)(2,1)S(1)}, bf16[72,512]{1,0:T(8,128)(2,1)S(1)}, u32[]{:S(2)}, u32[]{:S(2)}) collective-permute-start(bf16[72,512]{1,0:T(8,128)(2,1)S(1)} %slice.13), channel_id=1, source_target_pairs={{4,0},{5,1},{8,4},{9,5},{12,8},{13,9},{14,12},{15,13},{10,14},{11,... | collective-permute-start | bytes 221192 | tf_op jit(solution)/shard_map/ppermute | solution.py:692
  37.1 0.0 copy-start.3
  37.1 0.6 %collective-permute-start.15 = (bf16[72,640]{1,0:T(8,128)(2,1)S(1)}, bf16[72,640]{1,0:T(8,128)(2,1)S(1)}, u32[]{:S(2)}, u32[]{:S(2)}) collective-permute-start(bf16[72,640]{1,0:T(8,128)(2,1)S(1)} %slice.12), channel_id=1, source_target_pairs={{0,4},{1,5},{4,8},{5,9},{8,12},{9,13},{12,14},{13,15},{14,10},{15,... | collective-permute-start | bytes 276488 | tf_op jit(solution)/shard_map/ppermute | solution.py:692
  37.6 0.2 collective-permute-done.10.refs_1_
  37.8 1.6 %collective-permute-start.13 = (bf16[128,512]{1,0:T(8,128)(2,1)S(1)}, bf16[128,512]{1,0:T(8,128)(2,1)S(1)}, u32[]{:S(2)}, u32[]{:S(2)}) collective-permute-start(bf16[128,512]{1,0:T(8,128)(2,1)S(1)} %collective-permute-done.9.refs_0_), channel_id=1, source_target_pairs={{0,4},{1,5},{4,8},{5,9},{8,12},{9,13},{12,14},{13,15},{14,10},{15,... | collective-permute-start | bytes 393224 | tf_op jit(solution)/shard_map/ppermute | solution.py:692
  39.4 0.4 collective-permute-start.14
  39.8 2.5 %step_attention.5.refs_1_ = f32[16,80,128]{2,1,0:T(8,128)S(1)} custom-call(s32[1,3]{1,0:T(1,128)S(1)} %copy-done.4, bf16[128,512]{1,0:T(8,128)(2,1)S(1)} %collective-permute-done.9.refs_0_, bf16[128,512]{1,0:T(8,128)(2,1)S(1)} %collective-permute-done.10.refs_1_, bf16[2304,512]{1,0:T(8,128)(2,1)S(1)} %copy-done.6, f32[1,72]{1,0:T(1,128)S(1)} %bitcast.7, ...), custom_call_target="tpu_custom_call" | custom-call | flops 1744830464 | bytes 5242880 | tf_op jit(solution)/shard_map/step_attention/pallas_call | solution.py:576
  42.3 0.0 collective-permute-done.16.refs_8_
  42.3 0.7 %collective-permute-done.13.refs_0_ = bf16[128,512]{1,0:T(8,128)(2,1)S(1)} collective-permute-done((bf16[128,512]{1,0:T(8,128)(2,1)S(1)}, bf16[128,512]{1,0:T(8,128)(2,1)S(1)}, u32[]{:S(2)}, u32[]{:S(2)}) %collective-permute-start.13) | collective-permute-done | bytes 131104 | tf_op jit(solution)/shard_map/ppermute | solution.py:692
  43.1 1.3 %collective-permute-done.14.refs_1_ = bf16[128,512]{1,0:T(8,128)(2,1)S(1)} collective-permute-done((bf16[128,512]{1,0:T(8,128)(2,1)S(1)}, bf16[128,512]{1,0:T(8,128)(2,1)S(1)}, u32[]{:S(2)}, u32[]{:S(2)}) %collective-permute-start.14) | collective-permute-done | bytes 131104 | tf_op jit(solution)/shard_map/ppermute | solution.py:692
  44.4 0.1 pack.1
  44.5 0.1 collective-permute-start.19
  44.6 0.5 collective-permute-start.18
  45.1 1.6 %collective-permute-start.17 = (bf16[64,512]{1,0:T(8,128)(2,1)S(1)}, bf16[64,512]{1,0:T(8,128)(2,1)S(1)}, u32[]{:S(2)}, u32[]{:S(2)}) collective-permute-start(bf16[64,512]{1,0:T(8,128)(2,1)S(1)} %slice.14), channel_id=1, source_target_pairs={{0,4},{1,5},{4,8},{5,9},{8,12},{9,13},{12,14},{13,15},{14,10},{15,... | collective-permute-start | bytes 196616 | tf_op jit(solution)/shard_map/ppermute | solution.py:692
  46.7 2.5 %step_attention.6.refs_2_ = f32[16,80,128]{2,1,0:T(8,128)S(1)} custom-call(s32[1,3]{1,0:T(1,128)S(1)} %copy-done.4, bf16[128,512]{1,0:T(8,128)(2,1)S(1)} %collective-permute-done.13.refs_0_, bf16[128,512]{1,0:T(8,128)(2,1)S(1)} %collective-permute-done.14.refs_1_, bf16[2304,512]{1,0:T(8,128)(2,1)S(1)} %copy-done.6, f32[1,72]{1,0:T(1,128)S(1)} %bitcast.8, ...), custom_call_target="tpu_custom_call" | custom-call | flops 1744830464 | bytes 5242880 | tf_op jit(solution)/shard_map/step_attention/pallas_call | solution.py:576
  49.2 0.0 collective-permute-done.18.refs_2_
  49.2 0.2 collective-permute-done.17.refs_1_
  49.3 2.5 %step_attention.7.refs_3_ = f32[16,80,128]{2,1,0:T(8,128)S(1)} custom-call(s32[1,3]{1,0:T(1,128)S(1)} %copy-done.4, bf16[128,512]{1,0:T(8,128)(2,1)S(1)} %constant_dynamic-update-slice_fusion.block_ref.refs_0_, bf16[64,512]{1,0:T(8,128)(2,1)S(1)} %collective-permute-done.17.refs_1_, bf16[64,512]{1,0:T(8,128)(2,1)S(1)} %collective-permute-done.18.refs_2_, ...), custom_call_target="tpu_custom_call" | custom-call | flops 1744830464 | bytes 5242880 | tf_op jit(solution)/shard_map/step_attention/pallas_call | solution.py:576
  51.8 0.0 collective-permute-done.19.refs_5_
  51.9 1.0 %project_out.1 = (bf16[64,1152]{1,0:T(8,128)(2,1)S(1)}, bf16[64,1152]{1,0:T(8,128)(2,1)S(1)}) custom-call(f32[16,80,128]{2,1,0:T(8,128)S(1)} %step_attention.4.refs_0_, f32[16,80,128]{2,1,0:T(8,128)S(1)} %step_attention.5.refs_1_, f32[16,80,128]{2,1,0:T(8,128)S(1)} %step_attention.6.refs_2_, f32[16,80,128]{2,1,0:T(8,128)S(1)} %step_attention.7.refs_3_, ...), custom_call_target="tpu_custom_call" | custom-call | flops 377487360 | bytes 4194304 | tf_op jit(solution)/shard_map/project_out/pallas_call | solution.py:621
  52.8 0.1 collective-permute-start.20
  52.9 1.4 %collective-permute-done.20.got_ref = bf16[64,1152]{1,0:T(8,128)(2,1)S(1)} collective-permute-done((bf16[64,1152]{1,0:T(8,128)(2,1)S(1)}, bf16[64,1152]{1,0:T(8,128)(2,1)S(1)}, u32[]{:S(2)}, u32[]{:S(2)}) %collective-permute-start.20) | collective-permute-done | bytes 147488 | tf_op jit(solution)/shard_map/ppermute | solution.py:692
  54.3 1.3 %merge.1 = bf16[128,1152]{1,0:T(8,128)(2,1)} custom-call(s32[1,3]{1,0:T(1,128)S(1)} %copy-done.4, bf16[64,1152]{1,0:T(8,128)(2,1)S(1)} %get-tuple-element.71.keep_ref, bf16[64,1152]{1,0:T(8,128)(2,1)S(1)} %collective-permute-done.20.got_ref), custom_call_target="tpu_custom_call" | custom-call | tf_op jit(solution)/shard_map/merge/pallas_call | solution.py:671
  (30 shorter events, 0.1 us)
Async XLA Ops:
  0.0 17.2 %copy-start.7 = (bf16[8,2,32,128]{3,2,1,0:T(8,128)(2,1)S(1)}, bf16[8,2,32,128]{3,2,1,0:T(8,128)(2,1)}, u32[]{:S(2)}) copy-start(bf16[8,2,32,128]{3,2,1,0:T(8,128)(2,1)} %own_any.1) | copy-start | bytes 393220
  0.0 17.2 %copy-start.2 = (bf16[512,1152]{1,0:T(8,128)(2,1)S(1)}, bf16[512,1152]{1,0:T(8,128)(2,1)}, u32[]{:S(2)}) copy-start(bf16[512,1152]{1,0:T(8,128)(2,1)} %patch_any.3) | copy-start | bytes 3538948
  0.0 17.2 %copy-start.4 = (s32[1,3]{1,0:T(1,128)S(1)}, s32[1,3]{1,0:T(1,128)}, u32[]{:S(2)}) copy-start(s32[1,3]{1,0:T(1,128)} %lengths_ref.11) | copy-start | bytes 40
  0.0 17.2 %copy-start.8 = (s32[3]{0:T(128)S(1)}, s32[3]{0:T(128)}, u32[]{:S(2)}) copy-start(s32[3]{0:T(128)} %counts_any.1) | copy-start | bytes 40
  0.0 15.1 %collective-permute-start = (bf16[8,2,32,128]{3,2,1,0:T(8,128)(2,1)}, bf16[8,2,32,128]{3,2,1,0:T(8,128)(2,1)S(1)}, u32[]{:S(2)}, u32[]{:S(2)}) collective-permute-start(bf16[8,2,32,128]{3,2,1,0:T(8,128)(2,1)} %own_any.1), channel_id=1, source_target_pairs={{0,1},{1,0},{2,3},{3,2},{4,5},{5,4},{6,7},{7,6},{8,9},{9,8},{10,11... | collective-permute-start | bytes 393224 | tf_op jit(solution)/shard_map/ppermute | solution.py:692
  0.5 14.6 %collective-permute-start.1 = (bf16[8,2,32,128]{3,2,1,0:T(8,128)(2,1)}, bf16[8,2,32,128]{3,2,1,0:T(8,128)(2,1)S(1)}, u32[]{:S(2)}, u32[]{:S(2)}) collective-permute-start(bf16[8,2,32,128]{3,2,1,0:T(8,128)(2,1)} %own_any.1), channel_id=1, source_target_pairs={{1,2},{2,1},{3,4},{4,3},{5,6},{6,5},{7,8},{8,7},{9,10},{10,9},{11,... | collective-permute-start | bytes 393224 | tf_op jit(solution)/shard_map/ppermute | solution.py:692
  1.2 13.9 %collective-permute-start.2 = (bf16[72,1152]{1,0:T(8,128)(2,1)}, bf16[72,1152]{1,0:T(8,128)(2,1)S(1)}, u32[]{:S(2)}, u32[]{:S(2)}) collective-permute-start(bf16[72,1152]{1,0:T(8,128)(2,1)} %refs_0_.1), channel_id=1, source_target_pairs={{0,4},{1,5},{4,8},{5,9},{8,12},{9,13},{12,14},{13,15},{14,10},{15,... | collective-permute-start | bytes 497672 | tf_op jit(solution)/shard_map/ppermute | solution.py:692
  6.6 8.6 %collective-permute-start.3 = (bf16[72,1152]{1,0:T(8,128)(2,1)}, bf16[72,1152]{1,0:T(8,128)(2,1)S(1)}, u32[]{:S(2)}, u32[]{:S(2)}) collective-permute-start(bf16[72,1152]{1,0:T(8,128)(2,1)} %refs_0_.1), channel_id=1, source_target_pairs={{4,0},{5,1},{8,4},{9,5},{12,8},{13,9},{14,12},{15,13},{10,14},{11,... | collective-permute-start | bytes 497672 | tf_op jit(solution)/shard_map/ppermute | solution.py:692
  15.2 6.4 %collective-permute-start.4 = (bf16[72,1152]{1,0:T(8,128)(2,1)S(1)}, bf16[72,1152]{1,0:T(8,128)(2,1)S(1)}, u32[]{:S(2)}, u32[]{:S(2)}) collective-permute-start(bf16[72,1152]{1,0:T(8,128)(2,1)S(1)} %collective-permute-done.2.refs_1_), channel_id=1, source_target_pairs={{0,4},{1,5},{4,8},{5,9},{8,12},{9,13},{12,14},{13,15},{14,10},{15,... | collective-permute-start | bytes 497672 | tf_op jit(solution)/shard_map/ppermute | solution.py:692
  17.2 5.6 %collective-permute-start.5 = (bf16[72,1152]{1,0:T(8,128)(2,1)S(1)}, bf16[72,1152]{1,0:T(8,128)(2,1)S(1)}, u32[]{:S(2)}, u32[]{:S(2)}) collective-permute-start(bf16[72,1152]{1,0:T(8,128)(2,1)S(1)} %collective-permute-done.3.refs_2_), channel_id=1, source_target_pairs={{4,0},{5,1},{8,4},{9,5},{12,8},{13,9},{14,12},{15,13},{10,14},{11,... | collective-permute-start | bytes 497672 | tf_op jit(solution)/shard_map/ppermute | solution.py:692
  17.3 10.9 %copy-start = (bf16[1152,1152]{1,0:T(8,128)(2,1)S(1)}, bf16[1152,1152]{1,0:T(8,128)(2,1)}, u32[]{:S(2)}) copy-start(bf16[1152,1152]{1,0:T(8,128)(2,1)} %get-tuple-element.50.query_ref) | copy-start | bytes 7962628
  17.3 10.9 %copy-start.1 = (bf16[512,1152]{1,0:T(8,128)(2,1)S(1)}, bf16[512,1152]{1,0:T(8,128)(2,1)}, u32[]{:S(2)}) copy-start(bf16[512,1152]{1,0:T(8,128)(2,1)} %get-tuple-element.49.centered_ref) | copy-start | bytes 3538948
  17.3 10.8 %copy-start.5 = (f32[72]{0:T(128)S(1)}, f32[72]{0:T(128)}, u32[]{:S(2)}) copy-start(f32[72]{0:T(128)} %param.16) | copy-start | bytes 868
  22.8 1.3 %collective-permute-start.6 = (bf16[64,512]{1,0:T(8,128)(2,1)S(1)}, bf16[64,512]{1,0:T(8,128)(2,1)S(1)}, u32[]{:S(2)}, u32[]{:S(2)}) collective-permute-start(bf16[64,512]{1,0:T(8,128)(2,1)S(1)} %get-tuple-element.48), channel_id=1, source_target_pairs={{0,1},{1,0},{2,3},{3,2},{4,5},{5,4},{6,7},{7,6},{8,9},{9,8},{10,11... | collective-permute-start | bytes 196616 | tf_op jit(solution)/shard_map/ppermute | solution.py:692
  24.1 5.6 %collective-permute-start.8 = (bf16[128,512]{1,0:T(8,128)(2,1)S(1)}, bf16[128,512]{1,0:T(8,128)(2,1)S(1)}, u32[]{:S(2)}, u32[]{:S(2)}) collective-permute-start(bf16[128,512]{1,0:T(8,128)(2,1)S(1)} %constant_dynamic-update-slice_fusion.block_ref.refs_0_), channel_id=1, source_target_pairs={{4,0},{5,1},{8,4},{9,5},{12,8},{13,9},{14,12},{15,13},{10,14},{11,... | collective-permute-start | bytes 393224 | tf_op jit(solution)/shard_map/ppermute | solution.py:692
  24.5 6.4 %collective-permute-start.7 = (bf16[128,512]{1,0:T(8,128)(2,1)S(1)}, bf16[128,512]{1,0:T(8,128)(2,1)S(1)}, u32[]{:S(2)}, u32[]{:S(2)}) collective-permute-start(bf16[128,512]{1,0:T(8,128)(2,1)S(1)} %constant_dynamic-update-slice_fusion.block_ref.refs_0_), channel_id=1, source_target_pairs={{0,4},{1,5},{4,8},{5,9},{8,12},{9,13},{12,14},{13,15},{14,10},{15,... | collective-permute-start | bytes 393224 | tf_op jit(solution)/shard_map/ppermute | solution.py:692
  26.1 9.4 %collective-permute-start.11 = (bf16[72,1152]{1,0:T(8,128)(2,1)S(1)}, bf16[72,1152]{1,0:T(8,128)(2,1)S(1)}, u32[]{:S(2)}, u32[]{:S(2)}) collective-permute-start(bf16[72,1152]{1,0:T(8,128)(2,1)S(1)} %collective-permute-done.4.refs_3_), channel_id=1, source_target_pairs={{0,4},{1,5},{4,8},{5,9},{8,12},{9,13},{12,14},{13,15},{14,10},{15,... | collective-permute-start | bytes 497672 | tf_op jit(solution)/shard_map/ppermute | solution.py:692
  27.7 7.8 %collective-permute-start.12 = (bf16[72,1152]{1,0:T(8,128)(2,1)S(1)}, bf16[72,1152]{1,0:T(8,128)(2,1)S(1)}, u32[]{:S(2)}, u32[]{:S(2)}) collective-permute-start(bf16[72,1152]{1,0:T(8,128)(2,1)S(1)} %collective-permute-done.5.refs_4_), channel_id=1, source_target_pairs={{4,0},{5,1},{8,4},{9,5},{12,8},{13,9},{14,12},{15,13},{10,14},{11,... | collective-permute-start | bytes 497672 | tf_op jit(solution)/shard_map/ppermute | solution.py:692
  28.1 4.8 %copy-start.6 = (bf16[2304,512]{1,0:T(8,128)(2,1)S(1)}, bf16[2304,512]{1,0:T(8,128)(2,1)}, u32[]{:S(2)}) copy-start(bf16[2304,512]{1,0:T(8,128)(2,1)} %get-tuple-element.55.refs_2_.refs_3_) | copy-start | bytes 7077892
  28.1 4.8 %copy-start.9 = (f32[72]{0:T(128)S(1)}, f32[72]{0:T(128)}, u32[]{:S(2)}) copy-start(f32[72]{0:T(128)} %param.17) | copy-start | bytes 868
  30.9 6.7 %collective-permute-start.9 = (bf16[128,512]{1,0:T(8,128)(2,1)S(1)}, bf16[128,512]{1,0:T(8,128)(2,1)S(1)}, u32[]{:S(2)}, u32[]{:S(2)}) collective-permute-start(bf16[128,512]{1,0:T(8,128)(2,1)S(1)} %collective-permute-done.7.refs_0_), channel_id=1, source_target_pairs={{0,4},{1,5},{4,8},{5,9},{8,12},{9,13},{12,14},{13,15},{14,10},{15,... | collective-permute-start | bytes 393224 | tf_op jit(solution)/shard_map/ppermute | solution.py:692
  32.5 5.3 %collective-permute-start.10 = (bf16[128,512]{1,0:T(8,128)(2,1)S(1)}, bf16[128,512]{1,0:T(8,128)(2,1)S(1)}, u32[]{:S(2)}, u32[]{:S(2)}) collective-permute-start(bf16[128,512]{1,0:T(8,128)(2,1)S(1)} %collective-permute-done.8.refs_1_), channel_id=1, source_target_pairs={{4,0},{5,1},{8,4},{9,5},{12,8},{13,9},{14,12},{15,13},{10,14},{11,... | collective-permute-start | bytes 393224 | tf_op jit(solution)/shard_map/ppermute | solution.py:692
  35.5 6.8 %collective-permute-start.16 = (bf16[72,512]{1,0:T(8,128)(2,1)S(1)}, bf16[72,512]{1,0:T(8,128)(2,1)S(1)}, u32[]{:S(2)}, u32[]{:S(2)}) collective-permute-start(bf16[72,512]{1,0:T(8,128)(2,1)S(1)} %slice.13), channel_id=1, source_target_pairs={{4,0},{5,1},{8,4},{9,5},{12,8},{13,9},{14,12},{15,13},{10,14},{11,... | collective-permute-start | bytes 221192 | tf_op jit(solution)/shard_map/ppermute | solution.py:692
  37.1 7.3 %copy-start.3 = (bf16[72,1152]{1,0:T(8,128)(2,1)S(1)}, bf16[72,1152]{1,0:T(8,128)(2,1)}, u32[]{:S(2)}) copy-start(bf16[72,1152]{1,0:T(8,128)(2,1)} %refs_0_.1) | copy-start | bytes 497668
  37.1 5.3 %collective-permute-start.15 = (bf16[72,640]{1,0:T(8,128)(2,1)S(1)}, bf16[72,640]{1,0:T(8,128)(2,1)S(1)}, u32[]{:S(2)}, u32[]{:S(2)}) collective-permute-start(bf16[72,640]{1,0:T(8,128)(2,1)S(1)} %slice.12), channel_id=1, source_target_pairs={{0,4},{1,5},{4,8},{5,9},{8,12},{9,13},{12,14},{13,15},{14,10},{15,... | collective-permute-start | bytes 276488 | tf_op jit(solution)/shard_map/ppermute | solution.py:692
  37.8 5.3 %collective-permute-start.13 = (bf16[128,512]{1,0:T(8,128)(2,1)S(1)}, bf16[128,512]{1,0:T(8,128)(2,1)S(1)}, u32[]{:S(2)}, u32[]{:S(2)}) collective-permute-start(bf16[128,512]{1,0:T(8,128)(2,1)S(1)} %collective-permute-done.9.refs_0_), channel_id=1, source_target_pairs={{0,4},{1,5},{4,8},{5,9},{8,12},{9,13},{12,14},{13,15},{14,10},{15,... | collective-permute-start | bytes 393224 | tf_op jit(solution)/shard_map/ppermute | solution.py:692
  39.4 5.0 %collective-permute-start.14 = (bf16[128,512]{1,0:T(8,128)(2,1)S(1)}, bf16[128,512]{1,0:T(8,128)(2,1)S(1)}, u32[]{:S(2)}, u32[]{:S(2)}) collective-permute-start(bf16[128,512]{1,0:T(8,128)(2,1)S(1)} %collective-permute-done.10.refs_1_), channel_id=1, source_target_pairs={{4,0},{5,1},{8,4},{9,5},{12,8},{13,9},{14,12},{15,13},{10,14},{11,... | collective-permute-start | bytes 393224 | tf_op jit(solution)/shard_map/ppermute | solution.py:692
  44.5 7.4 %collective-permute-start.19 = (bf16[576,1152]{1,0:T(8,128)(2,1)S(1)}, bf16[576,1152]{1,0:T(8,128)(2,1)S(1)}, u32[]{:S(2)}, u32[]{:S(2)}) collective-permute-start(bf16[576,1152]{1,0:T(8,128)(2,1)S(1)} %bitcast.3), channel_id=1, source_target_pairs={{0,1},{1,0},{2,3},{3,2},{4,5},{5,4},{6,7},{7,6},{8,9},{9,8},{10,11... | collective-permute-start | bytes 3981320 | tf_op jit(solution)/shard_map/ppermute | solution.py:692
  44.6 4.6 %collective-permute-start.18 = (bf16[64,512]{1,0:T(8,128)(2,1)S(1)}, bf16[64,512]{1,0:T(8,128)(2,1)S(1)}, u32[]{:S(2)}, u32[]{:S(2)}) collective-permute-start(bf16[64,512]{1,0:T(8,128)(2,1)S(1)} %slice.15), channel_id=1, source_target_pairs={{4,0},{5,1},{8,4},{9,5},{12,8},{13,9},{14,12},{15,13},{10,14},{11,... | collective-permute-start | bytes 196616 | tf_op jit(solution)/shard_map/ppermute | solution.py:692
  45.1 4.3 %collective-permute-start.17 = (bf16[64,512]{1,0:T(8,128)(2,1)S(1)}, bf16[64,512]{1,0:T(8,128)(2,1)S(1)}, u32[]{:S(2)}, u32[]{:S(2)}) collective-permute-start(bf16[64,512]{1,0:T(8,128)(2,1)S(1)} %slice.14), channel_id=1, source_target_pairs={{0,4},{1,5},{4,8},{5,9},{8,12},{9,13},{12,14},{13,15},{14,10},{15,... | collective-permute-start | bytes 196616 | tf_op jit(solution)/shard_map/ppermute | solution.py:692
  52.8 1.4 %collective-permute-start.20 = (bf16[64,1152]{1,0:T(8,128)(2,1)S(1)}, bf16[64,1152]{1,0:T(8,128)(2,1)S(1)}, u32[]{:S(2)}, u32[]{:S(2)}) collective-permute-start(bf16[64,1152]{1,0:T(8,128)(2,1)S(1)} %get-tuple-element.72), channel_id=1, source_target_pairs={{0,1},{1,0},{2,3},{3,2},{4,5},{5,4},{6,7},{7,6},{8,9},{9,8},{10,11... | collective-permute-start | bytes 442376 | tf_op jit(solution)/shard_map/ppermute | solution.py:692

commit v7 on v5

--- a/solution.py
+++ b/solution.py
@@ -284,13 +284,14 @@
 
 
 def conv_kernel(
-    counts_any, lengths_any, own_any, before_ref, after_ref, first_ref, second_ref, patch_ref,
-    keep_ref, send_ref, grid_one, grid_two, pixels, own_ref, counts_ref, lengths_ref, sems,
+    counts_any, lengths_any, own_any, patch_any, sibling_ref, other_ref, first_ref, second_ref,
+    keep_ref, send_ref, grid_one, grid_two, pixels, own_ref, patch_ref, counts_ref, lengths_ref, sems,
 ):
     copies = [
         pltpu.make_async_copy(own_any, own_ref, sems.at[0]),
         pltpu.make_async_copy(counts_any, counts_ref, sems.at[1]),
         pltpu.make_async_copy(lengths_any, lengths_ref, sems.at[2]),
+        pltpu.make_async_copy(patch_any, patch_ref, sems.at[3]),
     ]
     for copy in copies:
         copy.start()
@@ -310,11 +311,18 @@
         grid_one[g, frames + 1] = blank
     grid_two[0] = blank
     grid_two[frames + 1] = blank
-    sources = [before_ref, before_ref, own_ref, own_ref, after_ref, after_ref]
+    on_first = position % 2 == 0
+
+    def source_row(r):
+        if r in (2, 3):
+            return own_ref[:, r - 2].astype(F32)
+        sibling, other = sibling_ref[:, r % 2].astype(F32), other_ref[:, r % 2].astype(F32)
+        return jnp.where(on_first, other, sibling) if r < 2 else jnp.where(on_first, sibling, other)
+
     for r in (0, 1, 4, 5, 2, 3):
         if r == 2:
             copies[0].wait()
-        row = silu(sources[r][:, r % 2].astype(F32))
+        row = silu(source_row(r))
         parts = shifted(row)
         for g in range(2):
             four = r - 2 * g
@@ -370,6 +378,7 @@
     patches = jnp.concatenate(
         [pixels[a, pl.ds(b, tokens, 2), :] for a in range(2) for b in range(2)], axis=1
     )
+    copies[3].wait()
     embedded = jnp.dot(patches.astype(BF16), patch_ref[...], preferred_element_type=F32)
     centered = embedded - jnp.mean(embedded, axis=1, keepdims=True)
     variance = jnp.mean(centered * centered, axis=1, keepdims=True)
@@ -388,28 +397,29 @@
     send_ref[...] = send
 
 
-def convolve(counts, lengths, clip, before, after, conv_first, conv_second, patch_weight):
+def convolve(counts, lengths, clip, sibling_rows, other_rows, conv_first, conv_second, patch_weight):
     frames, _, cols, ch = clip.shape
     tokens = frames * cols // 2
     out = jax.ShapeDtypeStruct((tokens // 2, 4 * ch), BF16)
     return pl.pallas_call(
         conv_kernel,
         out_shape=(out, out),
-        in_specs=[ANY] * 3 + [VMEM] * 5,
+        in_specs=[ANY] * 4 + [VMEM] * 4,
         out_specs=(VMEM, VMEM),
         scratch_shapes=[
             pltpu.VMEM((2, frames + 2, cols, 12 * ch), BF16),
             pltpu.VMEM((frames + 2, cols, 12 * ch), BF16),
             pltpu.VMEM((2, frames * cols, ch), F32),
             pltpu.VMEM(clip.shape, BF16),
+            pltpu.VMEM(patch_weight.shape, BF16),
             pltpu.SMEM(counts.shape, jnp.int32),
             pltpu.SMEM(lengths.shape, jnp.int32),
-            pltpu.SemaphoreType.DMA((3,)),
+            pltpu.SemaphoreType.DMA((4,)),
         ],
         compiler_params=params(),
         name="convolve",
         cost_estimate=pl.CostEstimate(flops=2 << 30, bytes_accessed=4 << 20, transcendentals=1 << 18),
-    )(counts, lengths, clip, before, after, conv_first, conv_second, patch_weight)
+    )(counts, lengths, clip, patch_weight, sibling_rows, other_rows, conv_first, conv_second)
 
 
 def chip_at(place):
@@ -657,8 +667,7 @@
     out_weight, window_lengths,
 ):
     size = lax.axis_size("seq")
-    up = [(i, i + 1) for i in range(size - 1)]
-    down = [(j, i) for i, j in up]
+    facing = [(i, j) for i in range(1, size - 1, 2) for i, j in ((i, i + 1), (i + 1, i))]
     cores = [(i, i ^ 1) for i in range(size)]
     forward = ring_pairs()
     backward = [(j, i) for i, j in forward]
@@ -681,19 +690,19 @@
     def both_ways(ahead, behind):
         return send(ahead, forward), send(behind, backward)
 
-    before = send(clip, up)
-    after = send(clip, down)
+    sibling_rows = send(clip, cores)
+    other_rows = send(clip, facing)
     query_row, key_row = query_gain[None], key_gain[None]
     weight_one = both_ways(out_weight, out_weight)
     folded, query_weight, centered = fold(patch_weight, qkv_weight)
-    before, after, *weight_one, folded = tied(before, after, *weight_one, folded)
+    sibling_rows, other_rows, *weight_one, folded = tied(sibling_rows, other_rows, *weight_one, folded)
     weight_two = both_ways(*weight_one)
     keep, other = convolve(
-        frame_counts, window_lengths, clip, before, after, conv_first, conv_second, patch_weight
-    )
-    other, wu_a, wu_b = tied(other, *weight_two)
+        frame_counts, window_lengths, clip, sibling_rows, other_rows, conv_first, conv_second, patch_weight
+    )
+    got = send(other, cores)
+    got, wu_a, wu_b = tied(got, *weight_two)
     weight_two = (wu_a, wu_b)
-    got = send(other, cores)
     weight_three = both_ways(*weight_two)
     block = jnp.concatenate([keep, got], axis=0)
     one = both_ways(block, block)

time: 57.2 us -> 53.2 us (0.930)
  starting transfers between devices: 24.2 us -> 21.1 us
  waiting for transfers between devices: 7.98 us -> 6.84 us
    ppermute x21, starting transfers between devices: 24.2 us -> 21.1 us  [send(): return lax.ppermute(array, 'seq', pairs)]
    ppermute x21, waiting for transfers between devices: 7.98 us -> 6.84 us  [send(): return lax.ppermute(array, 'seq', pairs)]
  transfers between devices with their start and end apart: 21 -> 21, of which waited for: 8 -> 7; matrix products, arithmetic and copies ran while one was open for 0% -> 0% of each run, Pallas kernels for 36% -> 40%
where the time goes in v7:
time: 53.2 us; the launch traced here: 53 us
  Pallas kernels  23.5 us (44%)
  starting transfers between devices  21.1 us (40%)
  waiting for transfers between devices  6.84 us (13%)
  local copies, waits for them, and re-layouts  1.35 us (3%)
    ppermute x21, starting transfers between devices, send(): return lax.ppermute(array, 'seq', pairs)  21.1 us
    pallas_call x4, Pallas kernels, step_attention(): pl.pallas_call(functools.partial(step_kernel, offsets), out_shape=ACC, in...  9.98 us
    ppermute x21, waiting for transfers between devices, send(): return lax.ppermute(array, 'seq', pairs)  6.84 us
    pallas_call x1, Pallas kernels, fold(): pl.pallas_call(fold_kernel, out_shape=(jax.ShapeDtypeStruct((2 * D, inner...  5.67 us
    pallas_call x1, Pallas kernels, convolve(): pl.pallas_call(conv_kernel, out_shape=(out, out), in_specs=[ANY] * 4 + [V...  3.88 us
    pallas_call x1, Pallas kernels, make_queries(): pl.pallas_call(query_kernel, out_shape=jax.ShapeDtypeStruct((HEADS, 128,...  1.53 us
    pallas_call x1, Pallas kernels, merge(): pl.pallas_call(merge_kernel, out_shape=jax.ShapeDtypeStruct((128, D), BF1...  1.35 us
    unnamed x21, local copies, waits for them, and re-layouts  1.32 us
  transfers between devices with their start and end apart: 21, of which 7 were waited for; matrix products, arithmetic and copies ran while one was open for 0% of the time, Pallas kernels for 40%

profile of v7, /device:TPU:0, one launch (start us, length us, event | category | flops | bytes accessed | tf_op | source)
XLA Modules:
  0.0 53.0 jit_solution(2195604011369639521)
XLA Ops:
  0.0 0.5 collective-permute-start
  0.5 0.7 %collective-permute-start.1 = (bf16[8,2,32,128]{3,2,1,0:T(8,128)(2,1)}, bf16[8,2,32,128]{3,2,1,0:T(8,128)(2,1)S(1)}, u32[]{:S(2)}, u32[]{:S(2)}) collective-permute-start(bf16[8,2,32,128]{3,2,1,0:T(8,128)(2,1)} %own_any.1), channel_id=1, source_target_pairs={{1,2},{2,1},{3,4},{4,3},{5,6},{6,5},{7,8},{8,7},{9,10},{10,9},{11,... | collective-permute-start | bytes 393224 | tf_op jit(solution)/shard_map/ppermute | solution.py:676
  1.1 5.4 %collective-permute-start.2 = (bf16[72,1152]{1,0:T(8,128)(2,1)}, bf16[72,1152]{1,0:T(8,128)(2,1)S(1)}, u32[]{:S(2)}, u32[]{:S(2)}) collective-permute-start(bf16[72,1152]{1,0:T(8,128)(2,1)} %refs_0_.1), channel_id=1, source_target_pairs={{0,4},{1,5},{4,8},{5,9},{8,12},{9,13},{12,14},{13,15},{14,10},{15,... | collective-permute-start | bytes 497672 | tf_op jit(solution)/shard_map/ppermute | solution.py:676
  6.5 0.0 collective-permute-start.3
  6.5 1.3 %copy-done.3 = bf16[512,1152]{1,0:T(8,128)(2,1)S(1)} copy-done((bf16[512,1152]{1,0:T(8,128)(2,1)S(1)}, bf16[512,1152]{1,0:T(8,128)(2,1)}, u32[]{:S(2)}) %copy-start.3) | copy-done | bytes 1179672
  7.8 5.7 %fold.1 = (bf16[2304,512]{1,0:T(8,128)(2,1)S(1)}, bf16[1152,1152]{1,0:T(8,128)(2,1)S(1)}, bf16[512,1152]{1,0:T(8,128)(2,1)S(1)}) custom-call(bf16[512,1152]{1,0:T(8,128)(2,1)S(1)} %copy-done.3, bf16[1152,3456]{1,0:T(8,128)(2,1)} %qkv_any.1), custom_call_target="tpu_custom_call" | custom-call | flops 2717908992 | bytes 12582912 | tf_op jit(solution)/shard_map/fold/pallas_call | solution.py:252
  13.5 0.0 collective-permute-done.1.other_ref
  13.5 0.0 collective-permute-done.2.refs_1_
  13.5 0.0 copy-start.2
  13.5 2.1 %collective-permute-start.5 = (bf16[72,1152]{1,0:T(8,128)(2,1)S(1)}, bf16[72,1152]{1,0:T(8,128)(2,1)S(1)}, u32[]{:S(2)}, u32[]{:S(2)}) collective-permute-start(bf16[72,1152]{1,0:T(8,128)(2,1)S(1)} %collective-permute-done.2.refs_1_), channel_id=1, source_target_pairs={{0,4},{1,5},{4,8},{5,9},{8,12},{9,13},{12,14},{13,15},{14,10},{15,... | collective-permute-start | bytes 497672 | tf_op jit(solution)/shard_map/ppermute | solution.py:676
  15.6 0.0 collective-permute-start.6
  15.7 3.9 %convolve.1 = (bf16[64,512]{1,0:T(8,128)(2,1)S(1)}, bf16[64,512]{1,0:T(8,128)(2,1)S(1)}) custom-call(s32[3]{0:T(128)S(1)} %copy-done.8, s32[1,3]{1,0:T(1,128)S(1)} %copy-done.1, bf16[8,2,32,128]{3,2,1,0:T(8,128)(2,1)S(1)} %copy-done.7, bf16[512,1152]{1,0:T(8,128)(2,1)S(1)} %copy-done.4, bf16[8,2,32,128]{3,2,1,0:T(8,128)(2,1)S(1)} %collective-permute-done.sibling_ref, ...), custom_call_target="tpu_custom_call" | custom-call | flops 2147483648 | bytes 4194304 | tf_op jit(solution)/shard_map/convolve/pallas_call | solution.py:404
  19.5 0.1 collective-permute-start.4
  19.6 1.2 %collective-permute-done.4 = bf16[64,512]{1,0:T(8,128)(2,1)S(1)} collective-permute-done((bf16[64,512]{1,0:T(8,128)(2,1)S(1)}, bf16[64,512]{1,0:T(8,128)(2,1)S(1)}, u32[]{:S(2)}, u32[]{:S(2)}) %collective-permute-start.4) | collective-permute-done | bytes 65568 | tf_op jit(solution)/shard_map/ppermute | solution.py:676
  20.9 0.3 collective-permute-done.6.refs_4_
  21.2 0.8 %collective-permute-start.8 = (bf16[128,512]{1,0:T(8,128)(2,1)S(1)}, bf16[128,512]{1,0:T(8,128)(2,1)S(1)}, u32[]{:S(2)}, u32[]{:S(2)}) collective-permute-start(bf16[128,512]{1,0:T(8,128)(2,1)S(1)} %constant_dynamic-update-slice_fusion.block_ref.refs_0_), channel_id=1, source_target_pairs={{4,0},{5,1},{8,4},{9,5},{12,8},{13,9},{14,12},{15,13},{10,14},{11,... | collective-permute-start | bytes 393224 | tf_op jit(solution)/shard_map/ppermute | solution.py:676
  21.9 1.3 %collective-permute-start.7 = (bf16[128,512]{1,0:T(8,128)(2,1)S(1)}, bf16[128,512]{1,0:T(8,128)(2,1)S(1)}, u32[]{:S(2)}, u32[]{:S(2)}) collective-permute-start(bf16[128,512]{1,0:T(8,128)(2,1)S(1)} %constant_dynamic-update-slice_fusion.block_ref.refs_0_), channel_id=1, source_target_pairs={{0,4},{1,5},{4,8},{5,9},{8,12},{9,13},{12,14},{13,15},{14,10},{15,... | collective-permute-start | bytes 393224 | tf_op jit(solution)/shard_map/ppermute | solution.py:676
  23.2 1.8 %collective-permute-start.11 = (bf16[72,1152]{1,0:T(8,128)(2,1)S(1)}, bf16[72,1152]{1,0:T(8,128)(2,1)S(1)}, u32[]{:S(2)}, u32[]{:S(2)}) collective-permute-start(bf16[72,1152]{1,0:T(8,128)(2,1)S(1)} %collective-permute-done.5.refs_3_), channel_id=1, source_target_pairs={{0,4},{1,5},{4,8},{5,9},{8,12},{9,13},{12,14},{13,15},{14,10},{15,... | collective-permute-start | bytes 497672 | tf_op jit(solution)/shard_map/ppermute | solution.py:676
  25.0 0.3 collective-permute-start.12
  25.2 1.5 %queries.1.refs_4_.refs_5_ = bf16[16,128,80]{2,1,0:T(8,128)(2,1)S(1)} custom-call(s32[1,3]{1,0:T(1,128)S(1)} %copy-done.1, bf16[128,512]{1,0:T(8,128)(2,1)S(1)} %constant_dynamic-update-slice_fusion.block_ref.refs_0_, bf16[512,1152]{1,0:T(8,128)(2,1)S(1)} %get-tuple-element.45.centered_ref, bf16[1152,1152]{1,0:T(8,128)(2,1)S(1)} %get-tuple-element.46.query_ref, ...), custom_call_target="tpu_custom_call" | custom-call | flops 1073741824 | bytes 4194304 | tf_op jit(solution)/shard_map/queries/pallas_call | solution.py:532
  26.8 1.6 %collective-permute-done.7.refs_0_ = bf16[128,512]{1,0:T(8,128)(2,1)S(1)} collective-permute-done((bf16[128,512]{1,0:T(8,128)(2,1)S(1)}, bf16[128,512]{1,0:T(8,128)(2,1)S(1)}, u32[]{:S(2)}, u32[]{:S(2)}) %collective-permute-start.7) | collective-permute-done | bytes 131104 | tf_op jit(solution)/shard_map/ppermute | solution.py:676
  28.3 1.2 %collective-permute-start.9 = (bf16[128,512]{1,0:T(8,128)(2,1)S(1)}, bf16[128,512]{1,0:T(8,128)(2,1)S(1)}, u32[]{:S(2)}, u32[]{:S(2)}) collective-permute-start(bf16[128,512]{1,0:T(8,128)(2,1)S(1)} %collective-permute-done.7.refs_0_), channel_id=1, source_target_pairs={{0,4},{1,5},{4,8},{5,9},{8,12},{9,13},{12,14},{13,15},{14,10},{15,... | collective-permute-start | bytes 393224 | tf_op jit(solution)/shard_map/ppermute | solution.py:676
  29.6 0.8 %collective-permute-start.10 = (bf16[128,512]{1,0:T(8,128)(2,1)S(1)}, bf16[128,512]{1,0:T(8,128)(2,1)S(1)}, u32[]{:S(2)}, u32[]{:S(2)}) collective-permute-start(bf16[128,512]{1,0:T(8,128)(2,1)S(1)} %collective-permute-done.8.refs_1_), channel_id=1, source_target_pairs={{4,0},{5,1},{8,4},{9,5},{12,8},{13,9},{14,12},{15,13},{10,14},{11,... | collective-permute-start | bytes 393224 | tf_op jit(solution)/shard_map/ppermute | solution.py:676
  30.4 2.5 %step_attention.4.refs_0_ = f32[16,80,128]{2,1,0:T(8,128)S(1)} custom-call(s32[1,3]{1,0:T(1,128)S(1)} %copy-done.1, bf16[128,512]{1,0:T(8,128)(2,1)S(1)} %collective-permute-done.7.refs_0_, bf16[128,512]{1,0:T(8,128)(2,1)S(1)} %collective-permute-done.8.refs_1_, bf16[2304,512]{1,0:T(8,128)(2,1)S(1)} %get-tuple-element.51.refs_2_.refs_3_, ...), custom_call_target="tpu_custom_call" | custom-call | flops 1744830464 | bytes 5242880 | tf_op jit(solution)/shard_map/step_attention/pallas_call | solution.py:560
  32.9 0.0 collective-permute-done.11.refs_5_
  32.9 1.7 %collective-permute-start.16 = (bf16[72,512]{1,0:T(8,128)(2,1)S(1)}, bf16[72,512]{1,0:T(8,128)(2,1)S(1)}, u32[]{:S(2)}, u32[]{:S(2)}) collective-permute-start(bf16[72,512]{1,0:T(8,128)(2,1)S(1)} %slice.13), channel_id=1, source_target_pairs={{4,0},{5,1},{8,4},{9,5},{12,8},{13,9},{14,12},{15,13},{10,14},{11,... | collective-permute-start | bytes 221192 | tf_op jit(solution)/shard_map/ppermute | solution.py:676
  34.6 0.0 copy-start
  34.6 0.5 collective-permute-start.15
  35.1 0.0 collective-permute-done.10.refs_1_
  35.1 1.6 %collective-permute-start.13 = (bf16[128,512]{1,0:T(8,128)(2,1)S(1)}, bf16[128,512]{1,0:T(8,128)(2,1)S(1)}, u32[]{:S(2)}, u32[]{:S(2)}) collective-permute-start(bf16[128,512]{1,0:T(8,128)(2,1)S(1)} %collective-permute-done.9.refs_0_), channel_id=1, source_target_pairs={{0,4},{1,5},{4,8},{5,9},{8,12},{9,13},{12,14},{13,15},{14,10},{15,... | collective-permute-start | bytes 393224 | tf_op jit(solution)/shard_map/ppermute | solution.py:676
  36.7 0.4 collective-permute-start.14
  37.1 2.5 %step_attention.5.refs_1_ = f32[16,80,128]{2,1,0:T(8,128)S(1)} custom-call(s32[1,3]{1,0:T(1,128)S(1)} %copy-done.1, bf16[128,512]{1,0:T(8,128)(2,1)S(1)} %collective-permute-done.9.refs_0_, bf16[128,512]{1,0:T(8,128)(2,1)S(1)} %collective-permute-done.10.refs_1_, bf16[2304,512]{1,0:T(8,128)(2,1)S(1)} %get-tuple-element.51.refs_2_.refs_3_, ...), custom_call_target="tpu_custom_call" | custom-call | flops 1744830464 | bytes 5242880 | tf_op jit(solution)/shard_map/step_attention/pallas_call | solution.py:560
  39.6 0.0 collective-permute-done.16.refs_8_
  39.6 1.0 %collective-permute-done.13.refs_0_ = bf16[128,512]{1,0:T(8,128)(2,1)S(1)} collective-permute-done((bf16[128,512]{1,0:T(8,128)(2,1)S(1)}, bf16[128,512]{1,0:T(8,128)(2,1)S(1)}, u32[]{:S(2)}, u32[]{:S(2)}) %collective-permute-start.13) | collective-permute-done | bytes 131104 | tf_op jit(solution)/shard_map/ppermute | solution.py:676
  40.6 1.0 %collective-permute-done.14.refs_1_ = bf16[128,512]{1,0:T(8,128)(2,1)S(1)} collective-permute-done((bf16[128,512]{1,0:T(8,128)(2,1)S(1)}, bf16[128,512]{1,0:T(8,128)(2,1)S(1)}, u32[]{:S(2)}, u32[]{:S(2)}) %collective-permute-start.14) | collective-permute-done | bytes 131104 | tf_op jit(solution)/shard_map/ppermute | solution.py:676
  41.7 0.1 pack.1
  41.8 0.1 collective-permute-start.19
  41.9 0.6 %collective-permute-start.18 = (bf16[64,512]{1,0:T(8,128)(2,1)S(1)}, bf16[64,512]{1,0:T(8,128)(2,1)S(1)}, u32[]{:S(2)}, u32[]{:S(2)}) collective-permute-start(bf16[64,512]{1,0:T(8,128)(2,1)S(1)} %slice.15), channel_id=1, source_target_pairs={{4,0},{5,1},{8,4},{9,5},{12,8},{13,9},{14,12},{15,13},{10,14},{11,... | collective-permute-start | bytes 196616 | tf_op jit(solution)/shard_map/ppermute | solution.py:676
  42.5 1.5 %collective-permute-start.17 = (bf16[64,512]{1,0:T(8,128)(2,1)S(1)}, bf16[64,512]{1,0:T(8,128)(2,1)S(1)}, u32[]{:S(2)}, u32[]{:S(2)}) collective-permute-start(bf16[64,512]{1,0:T(8,128)(2,1)S(1)} %slice.14), channel_id=1, source_target_pairs={{0,4},{1,5},{4,8},{5,9},{8,12},{9,13},{12,14},{13,15},{14,10},{15,... | collective-permute-start | bytes 196616 | tf_op jit(solution)/shard_map/ppermute | solution.py:676
  44.0 2.5 %step_attention.6.refs_2_ = f32[16,80,128]{2,1,0:T(8,128)S(1)} custom-call(s32[1,3]{1,0:T(1,128)S(1)} %copy-done.1, bf16[128,512]{1,0:T(8,128)(2,1)S(1)} %collective-permute-done.13.refs_0_, bf16[128,512]{1,0:T(8,128)(2,1)S(1)} %collective-permute-done.14.refs_1_, bf16[2304,512]{1,0:T(8,128)(2,1)S(1)} %get-tuple-element.51.refs_2_.refs_3_, ...), custom_call_target="tpu_custom_call" | custom-call | flops 1744830464 | bytes 5242880 | tf_op jit(solution)/shard_map/step_attention/pallas_call | solution.py:560
  46.5 0.0 collective-permute-done.18.refs_2_
  46.5 0.3 collective-permute-done.17.refs_1_
  46.7 2.5 %step_attention.7.refs_3_ = f32[16,80,128]{2,1,0:T(8,128)S(1)} custom-call(s32[1,3]{1,0:T(1,128)S(1)} %copy-done.1, bf16[128,512]{1,0:T(8,128)(2,1)S(1)} %constant_dynamic-update-slice_fusion.block_ref.refs_0_, bf16[64,512]{1,0:T(8,128)(2,1)S(1)} %collective-permute-done.17.refs_1_, bf16[64,512]{1,0:T(8,128)(2,1)S(1)} %collective-permute-done.18.refs_2_, ...), custom_call_target="tpu_custom_call" | custom-call | flops 1744830464 | bytes 5242880 | tf_op jit(solution)/shard_map/step_attention/pallas_call | solution.py:560
  49.2 0.0 collective-permute-done.19.refs_5_
  49.3 1.0 %project_out.1 = (bf16[64,1152]{1,0:T(8,128)(2,1)S(1)}, bf16[64,1152]{1,0:T(8,128)(2,1)S(1)}) custom-call(f32[16,80,128]{2,1,0:T(8,128)S(1)} %step_attention.4.refs_0_, f32[16,80,128]{2,1,0:T(8,128)S(1)} %step_attention.5.refs_1_, f32[16,80,128]{2,1,0:T(8,128)S(1)} %step_attention.6.refs_2_, f32[16,80,128]{2,1,0:T(8,128)S(1)} %step_attention.7.refs_3_, ...), custom_call_target="tpu_custom_call" | custom-call | flops 377487360 | bytes 4194304 | tf_op jit(solution)/shard_map/project_out/pallas_call | solution.py:605
  50.2 0.1 collective-permute-start.20
  50.3 1.4 %collective-permute-done.20.got_ref = bf16[64,1152]{1,0:T(8,128)(2,1)S(1)} collective-permute-done((bf16[64,1152]{1,0:T(8,128)(2,1)S(1)}, bf16[64,1152]{1,0:T(8,128)(2,1)S(1)}, u32[]{:S(2)}, u32[]{:S(2)}) %collective-permute-start.20) | collective-permute-done | bytes 147488 | tf_op jit(solution)/shard_map/ppermute | solution.py:676
  51.7 1.3 %merge.1 = bf16[128,1152]{1,0:T(8,128)(2,1)} custom-call(s32[1,3]{1,0:T(1,128)S(1)} %copy-done.1, bf16[64,1152]{1,0:T(8,128)(2,1)S(1)} %get-tuple-element.67.keep_ref, bf16[64,1152]{1,0:T(8,128)(2,1)S(1)} %collective-permute-done.20.got_ref), custom_call_target="tpu_custom_call" | custom-call | tf_op jit(solution)/shard_map/merge/pallas_call | solution.py:655
  (30 shorter events, 0.1 us)
Async XLA Ops:
  0.0 15.6 %copy-start.1 = (s32[1,3]{1,0:T(1,128)S(1)}, s32[1,3]{1,0:T(1,128)}, u32[]{:S(2)}) copy-start(s32[1,3]{1,0:T(1,128)} %lengths_ref.11) | copy-start | bytes 40
  0.0 13.5 %collective-permute-start = (bf16[8,2,32,128]{3,2,1,0:T(8,128)(2,1)}, bf16[8,2,32,128]{3,2,1,0:T(8,128)(2,1)S(1)}, u32[]{:S(2)}, u32[]{:S(2)}) collective-permute-start(bf16[8,2,32,128]{3,2,1,0:T(8,128)(2,1)} %own_any.1), channel_id=1, source_target_pairs={{0,1},{1,0},{2,3},{3,2},{4,5},{5,4},{6,7},{7,6},{8,9},{9,8},{10,11... | collective-permute-start | bytes 393224 | tf_op jit(solution)/shard_map/ppermute | solution.py:676
  0.5 13.0 %collective-permute-start.1 = (bf16[8,2,32,128]{3,2,1,0:T(8,128)(2,1)}, bf16[8,2,32,128]{3,2,1,0:T(8,128)(2,1)S(1)}, u32[]{:S(2)}, u32[]{:S(2)}) collective-permute-start(bf16[8,2,32,128]{3,2,1,0:T(8,128)(2,1)} %own_any.1), channel_id=1, source_target_pairs={{1,2},{2,1},{3,4},{4,3},{5,6},{6,5},{7,8},{8,7},{9,10},{10,9},{11,... | collective-permute-start | bytes 393224 | tf_op jit(solution)/shard_map/ppermute | solution.py:676
  1.1 12.4 %collective-permute-start.2 = (bf16[72,1152]{1,0:T(8,128)(2,1)}, bf16[72,1152]{1,0:T(8,128)(2,1)S(1)}, u32[]{:S(2)}, u32[]{:S(2)}) collective-permute-start(bf16[72,1152]{1,0:T(8,128)(2,1)} %refs_0_.1), channel_id=1, source_target_pairs={{0,4},{1,5},{4,8},{5,9},{8,12},{9,13},{12,14},{13,15},{14,10},{15,... | collective-permute-start | bytes 497672 | tf_op jit(solution)/shard_map/ppermute | solution.py:676
  6.5 7.0 %collective-permute-start.3 = (bf16[72,1152]{1,0:T(8,128)(2,1)}, bf16[72,1152]{1,0:T(8,128)(2,1)S(1)}, u32[]{:S(2)}, u32[]{:S(2)}) collective-permute-start(bf16[72,1152]{1,0:T(8,128)(2,1)} %refs_0_.1), channel_id=1, source_target_pairs={{4,0},{5,1},{8,4},{9,5},{12,8},{13,9},{14,12},{15,13},{10,14},{11,... | collective-permute-start | bytes 497672 | tf_op jit(solution)/shard_map/ppermute | solution.py:676
  6.5 1.3 %copy-start.3 = (bf16[512,1152]{1,0:T(8,128)(2,1)S(1)}, bf16[512,1152]{1,0:T(8,128)(2,1)}, u32[]{:S(2)}) copy-start(bf16[512,1152]{1,0:T(8,128)(2,1)} %patch_any.3) | copy-start | bytes 3538948
  7.8 7.8 %copy-start.4 = (bf16[512,1152]{1,0:T(8,128)(2,1)S(1)}, bf16[512,1152]{1,0:T(8,128)(2,1)}, u32[]{:S(2)}) copy-start(bf16[512,1152]{1,0:T(8,128)(2,1)} %patch_any.3) | copy-start | bytes 3538948
  7.8 7.8 %copy-start.5 = (bf16[3,3,3,128,128]{4,3,2,1,0:T(8,128)(2,1)S(1)}, bf16[3,3,3,128,128]{4,3,2,1,0:T(8,128)(2,1)}, u32[]{:S(2)}) copy-start(bf16[3,3,3,128,128]{4,3,2,1,0:T(8,128)(2,1)} %first_ref.1) | copy-start | bytes 2654212
  7.8 7.8 %copy-start.6 = (bf16[3,3,3,128,128]{4,3,2,1,0:T(8,128)(2,1)S(1)}, bf16[3,3,3,128,128]{4,3,2,1,0:T(8,128)(2,1)}, u32[]{:S(2)}) copy-start(bf16[3,3,3,128,128]{4,3,2,1,0:T(8,128)(2,1)} %second_ref.1) | copy-start | bytes 2654212
  7.8 7.8 %copy-start.7 = (bf16[8,2,32,128]{3,2,1,0:T(8,128)(2,1)S(1)}, bf16[8,2,32,128]{3,2,1,0:T(8,128)(2,1)}, u32[]{:S(2)}) copy-start(bf16[8,2,32,128]{3,2,1,0:T(8,128)(2,1)} %own_any.1) | copy-start | bytes 393220
  7.8 7.9 %copy-start.8 = (s32[3]{0:T(128)S(1)}, s32[3]{0:T(128)}, u32[]{:S(2)}) copy-start(s32[3]{0:T(128)} %counts_any.1) | copy-start | bytes 40
  13.5 11.7 %copy-start.2 = (f32[72]{0:T(128)S(1)}, f32[72]{0:T(128)}, u32[]{:S(2)}) copy-start(f32[72]{0:T(128)} %param.16) | copy-start | bytes 868
  13.5 7.3 %collective-permute-start.5 = (bf16[72,1152]{1,0:T(8,128)(2,1)S(1)}, bf16[72,1152]{1,0:T(8,128)(2,1)S(1)}, u32[]{:S(2)}, u32[]{:S(2)}) collective-permute-start(bf16[72,1152]{1,0:T(8,128)(2,1)S(1)} %collective-permute-done.2.refs_1_), channel_id=1, source_target_pairs={{0,4},{1,5},{4,8},{5,9},{8,12},{9,13},{12,14},{13,15},{14,10},{15,... | collective-permute-start | bytes 497672 | tf_op jit(solution)/shard_map/ppermute | solution.py:676
  15.6 5.6 %collective-permute-start.6 = (bf16[72,1152]{1,0:T(8,128)(2,1)S(1)}, bf16[72,1152]{1,0:T(8,128)(2,1)S(1)}, u32[]{:S(2)}, u32[]{:S(2)}) collective-permute-start(bf16[72,1152]{1,0:T(8,128)(2,1)S(1)} %collective-permute-done.3.refs_2_), channel_id=1, source_target_pairs={{4,0},{5,1},{8,4},{9,5},{12,8},{13,9},{14,12},{15,13},{10,14},{11,... | collective-permute-start | bytes 497672 | tf_op jit(solution)/shard_map/ppermute | solution.py:676
  19.5 1.3 %collective-permute-start.4 = (bf16[64,512]{1,0:T(8,128)(2,1)S(1)}, bf16[64,512]{1,0:T(8,128)(2,1)S(1)}, u32[]{:S(2)}, u32[]{:S(2)}) collective-permute-start(bf16[64,512]{1,0:T(8,128)(2,1)S(1)} %get-tuple-element.41), channel_id=1, source_target_pairs={{0,1},{1,0},{2,3},{3,2},{4,5},{5,4},{6,7},{7,6},{8,9},{9,8},{10,11... | collective-permute-start | bytes 196616 | tf_op jit(solution)/shard_map/ppermute | solution.py:676
  21.2 5.6 %collective-permute-start.8 = (bf16[128,512]{1,0:T(8,128)(2,1)S(1)}, bf16[128,512]{1,0:T(8,128)(2,1)S(1)}, u32[]{:S(2)}, u32[]{:S(2)}) collective-permute-start(bf16[128,512]{1,0:T(8,128)(2,1)S(1)} %constant_dynamic-update-slice_fusion.block_ref.refs_0_), channel_id=1, source_target_pairs={{4,0},{5,1},{8,4},{9,5},{12,8},{13,9},{14,12},{15,13},{10,14},{11,... | collective-permute-start | bytes 393224 | tf_op jit(solution)/shard_map/ppermute | solution.py:676
  21.9 6.4 %collective-permute-start.7 = (bf16[128,512]{1,0:T(8,128)(2,1)S(1)}, bf16[128,512]{1,0:T(8,128)(2,1)S(1)}, u32[]{:S(2)}, u32[]{:S(2)}) collective-permute-start(bf16[128,512]{1,0:T(8,128)(2,1)S(1)} %constant_dynamic-update-slice_fusion.block_ref.refs_0_), channel_id=1, source_target_pairs={{0,4},{1,5},{4,8},{5,9},{8,12},{9,13},{12,14},{13,15},{14,10},{15,... | collective-permute-start | bytes 393224 | tf_op jit(solution)/shard_map/ppermute | solution.py:676
  23.2 9.7 %collective-permute-start.11 = (bf16[72,1152]{1,0:T(8,128)(2,1)S(1)}, bf16[72,1152]{1,0:T(8,128)(2,1)S(1)}, u32[]{:S(2)}, u32[]{:S(2)}) collective-permute-start(bf16[72,1152]{1,0:T(8,128)(2,1)S(1)} %collective-permute-done.5.refs_3_), channel_id=1, source_target_pairs={{0,4},{1,5},{4,8},{5,9},{8,12},{9,13},{12,14},{13,15},{14,10},{15,... | collective-permute-start | bytes 497672 | tf_op jit(solution)/shard_map/ppermute | solution.py:676
  25.0 7.9 %collective-permute-start.12 = (bf16[72,1152]{1,0:T(8,128)(2,1)S(1)}, bf16[72,1152]{1,0:T(8,128)(2,1)S(1)}, u32[]{:S(2)}, u32[]{:S(2)}) collective-permute-start(bf16[72,1152]{1,0:T(8,128)(2,1)S(1)} %collective-permute-done.6.refs_4_), channel_id=1, source_target_pairs={{4,0},{5,1},{8,4},{9,5},{12,8},{13,9},{14,12},{15,13},{10,14},{11,... | collective-permute-start | bytes 497672 | tf_op jit(solution)/shard_map/ppermute | solution.py:676
  25.2 5.1 %copy-start.9 = (f32[72]{0:T(128)S(1)}, f32[72]{0:T(128)}, u32[]{:S(2)}) copy-start(f32[72]{0:T(128)} %param.17) | copy-start | bytes 868
  28.3 6.8 %collective-permute-start.9 = (bf16[128,512]{1,0:T(8,128)(2,1)S(1)}, bf16[128,512]{1,0:T(8,128)(2,1)S(1)}, u32[]{:S(2)}, u32[]{:S(2)}) collective-permute-start(bf16[128,512]{1,0:T(8,128)(2,1)S(1)} %collective-permute-done.7.refs_0_), channel_id=1, source_target_pairs={{0,4},{1,5},{4,8},{5,9},{8,12},{9,13},{12,14},{13,15},{14,10},{15,... | collective-permute-start | bytes 393224 | tf_op jit(solution)/shard_map/ppermute | solution.py:676
  29.6 5.5 %collective-permute-start.10 = (bf16[128,512]{1,0:T(8,128)(2,1)S(1)}, bf16[128,512]{1,0:T(8,128)(2,1)S(1)}, u32[]{:S(2)}, u32[]{:S(2)}) collective-permute-start(bf16[128,512]{1,0:T(8,128)(2,1)S(1)} %collective-permute-done.8.refs_1_), channel_id=1, source_target_pairs={{4,0},{5,1},{8,4},{9,5},{12,8},{13,9},{14,12},{15,13},{10,14},{11,... | collective-permute-start | bytes 393224 | tf_op jit(solution)/shard_map/ppermute | solution.py:676
  32.9 6.7 %collective-permute-start.16 = (bf16[72,512]{1,0:T(8,128)(2,1)S(1)}, bf16[72,512]{1,0:T(8,128)(2,1)S(1)}, u32[]{:S(2)}, u32[]{:S(2)}) collective-permute-start(bf16[72,512]{1,0:T(8,128)(2,1)S(1)} %slice.13), channel_id=1, source_target_pairs={{4,0},{5,1},{8,4},{9,5},{12,8},{13,9},{14,12},{15,13},{10,14},{11,... | collective-permute-start | bytes 221192 | tf_op jit(solution)/shard_map/ppermute | solution.py:676
  34.6 7.1 %copy-start = (bf16[72,1152]{1,0:T(8,128)(2,1)S(1)}, bf16[72,1152]{1,0:T(8,128)(2,1)}, u32[]{:S(2)}) copy-start(bf16[72,1152]{1,0:T(8,128)(2,1)} %refs_0_.1) | copy-start | bytes 497668
  34.6 5.0 %collective-permute-start.15 = (bf16[72,640]{1,0:T(8,128)(2,1)S(1)}, bf16[72,640]{1,0:T(8,128)(2,1)S(1)}, u32[]{:S(2)}, u32[]{:S(2)}) collective-permute-start(bf16[72,640]{1,0:T(8,128)(2,1)S(1)} %slice.12), channel_id=1, source_target_pairs={{0,4},{1,5},{4,8},{5,9},{8,12},{9,13},{12,14},{13,15},{14,10},{15,... | collective-permute-start | bytes 276488 | tf_op jit(solution)/shard_map/ppermute | solution.py:676
  35.1 5.5 %collective-permute-start.13 = (bf16[128,512]{1,0:T(8,128)(2,1)S(1)}, bf16[128,512]{1,0:T(8,128)(2,1)S(1)}, u32[]{:S(2)}, u32[]{:S(2)}) collective-permute-start(bf16[128,512]{1,0:T(8,128)(2,1)S(1)} %collective-permute-done.9.refs_0_), channel_id=1, source_target_pairs={{0,4},{1,5},{4,8},{5,9},{8,12},{9,13},{12,14},{13,15},{14,10},{15,... | collective-permute-start | bytes 393224 | tf_op jit(solution)/shard_map/ppermute | solution.py:676
  36.7 5.0 %collective-permute-start.14 = (bf16[128,512]{1,0:T(8,128)(2,1)S(1)}, bf16[128,512]{1,0:T(8,128)(2,1)S(1)}, u32[]{:S(2)}, u32[]{:S(2)}) collective-permute-start(bf16[128,512]{1,0:T(8,128)(2,1)S(1)} %collective-permute-done.10.refs_1_), channel_id=1, source_target_pairs={{4,0},{5,1},{8,4},{9,5},{12,8},{13,9},{14,12},{15,13},{10,14},{11,... | collective-permute-start | bytes 393224 | tf_op jit(solution)/shard_map/ppermute | solution.py:676
  41.8 7.5 %collective-permute-start.19 = (bf16[576,1152]{1,0:T(8,128)(2,1)S(1)}, bf16[576,1152]{1,0:T(8,128)(2,1)S(1)}, u32[]{:S(2)}, u32[]{:S(2)}) collective-permute-start(bf16[576,1152]{1,0:T(8,128)(2,1)S(1)} %bitcast.3), channel_id=1, source_target_pairs={{0,1},{1,0},{2,3},{3,2},{4,5},{5,4},{6,7},{7,6},{8,9},{9,8},{10,11... | collective-permute-start | bytes 3981320 | tf_op jit(solution)/shard_map/ppermute | solution.py:676
  41.9 4.6 %collective-permute-start.18 = (bf16[64,512]{1,0:T(8,128)(2,1)S(1)}, bf16[64,512]{1,0:T(8,128)(2,1)S(1)}, u32[]{:S(2)}, u32[]{:S(2)}) collective-permute-start(bf16[64,512]{1,0:T(8,128)(2,1)S(1)} %slice.15), channel_id=1, source_target_pairs={{4,0},{5,1},{8,4},{9,5},{12,8},{13,9},{14,12},{15,13},{10,14},{11,... | collective-permute-start | bytes 196616 | tf_op jit(solution)/shard_map/ppermute | solution.py:676
  42.5 4.3 %collective-permute-start.17 = (bf16[64,512]{1,0:T(8,128)(2,1)S(1)}, bf16[64,512]{1,0:T(8,128)(2,1)S(1)}, u32[]{:S(2)}, u32[]{:S(2)}) collective-permute-start(bf16[64,512]{1,0:T(8,128)(2,1)S(1)} %slice.14), channel_id=1, source_target_pairs={{0,4},{1,5},{4,8},{5,9},{8,12},{9,13},{12,14},{13,15},{14,10},{15,... | collective-permute-start | bytes 196616 | tf_op jit(solution)/shard_map/ppermute | solution.py:676
  50.2 1.4 %collective-permute-start.20 = (bf16[64,1152]{1,0:T(8,128)(2,1)S(1)}, bf16[64,1152]{1,0:T(8,128)(2,1)S(1)}, u32[]{:S(2)}, u32[]{:S(2)}) collective-permute-start(bf16[64,1152]{1,0:T(8,128)(2,1)S(1)} %get-tuple-element.68), channel_id=1, source_target_pairs={{0,1},{1,0},{2,3},{3,2},{4,5},{5,4},{6,7},{7,6},{8,9},{9,8},{10,11... | collective-permute-start | bytes 442376 | tf_op jit(solution)/shard_map/ppermute | solution.py:676

commit v8 on v7

--- a/solution.py
+++ b/solution.py
@@ -485,13 +485,14 @@
         keys = normed_heads(part, key_gain)
         for h in range(heads_at_once):
             keys_ref[first + h] = jnp.concatenate([keys[h], key_tail], axis=0).astype(BF16)
-            scores_ref[first + h] = jnp.dot(queries[first + h], keys_ref[first + h], preferred_element_type=F32)
     for first in range(0, HEADS, heads_at_once):
         rows = slice(D + first * HD, D + (first + heads_at_once) * HD)
         part = lax.dot_general(folded[rows], tokens, NT, preferred_element_type=F32)
         values = part.reshape(heads_at_once, HD, count)
         for h in range(heads_at_once):
             values_ref[first + h] = jnp.concatenate([values[h], value_tail], axis=0).astype(BF16)
+    for h in range(HEADS):
+        scores_ref[h] = jnp.dot(queries[h], keys_ref[h], preferred_element_type=F32)
     lane = lax.broadcasted_iota(jnp.int32, (128, 128), 1)
     peaks = jnp.zeros((128, 128), F32)
     for h in range(HEADS):

time: 53.2 us -> 52.2 us (0.981)
  Pallas kernels: 23.5 us -> 21.6 us
  waiting for transfers between devices: 6.84 us -> 7.8 us
    pallas_call x4, Pallas kernels: 9.98 us -> 8.1 us  [step_attention(): pl.pallas_call(functools.partial(step_kernel, offsets), out_shape=ACC, in...]
    ppermute x21, waiting for transfers between devices: 6.84 us -> 7.8 us  [send(): return lax.ppermute(array, 'seq', pairs)]
  transfers between devices with their start and end apart: 21 -> 21, of which waited for: 7 -> 9; matrix products, arithmetic and copies ran while one was open for 0% -> 0% of each run, Pallas kernels for 40% -> 37%
where the time goes in v8:
time: 52.2 us; the launch traced here: 52.1 us
  Pallas kernels  21.6 us (41%)
  starting transfers between devices  21.1 us (40%)
  waiting for transfers between devices  7.8 us (15%)
  local copies, waits for them, and re-layouts  1.35 us (3%)
    ppermute x21, starting transfers between devices, send(): return lax.ppermute(array, 'seq', pairs)  21.1 us
    pallas_call x4, Pallas kernels, step_attention(): pl.pallas_call(functools.partial(step_kernel, offsets), out_shape=ACC, in...  8.1 us
    ppermute x21, waiting for transfers between devices, send(): return lax.ppermute(array, 'seq', pairs)  7.8 us
    pallas_call x1, Pallas kernels, fold(): pl.pallas_call(fold_kernel, out_shape=(jax.ShapeDtypeStruct((2 * D, inner...  5.67 us
    pallas_call x1, Pallas kernels, convolve(): pl.pallas_call(conv_kernel, out_shape=(out, out), in_specs=[ANY] * 4 + [V...  3.88 us
    pallas_call x1, Pallas kernels, make_queries(): pl.pallas_call(query_kernel, out_shape=jax.ShapeDtypeStruct((HEADS, 128,...  1.53 us
    pallas_call x1, Pallas kernels, merge(): pl.pallas_call(merge_kernel, out_shape=jax.ShapeDtypeStruct((128, D), BF1...  1.35 us
    unnamed x21, local copies, waits for them, and re-layouts  1.32 us
  transfers between devices with their start and end apart: 21, of which 9 were waited for; matrix products, arithmetic and copies ran while one was open for 0% of the time, Pallas kernels for 37%

profile of v8, /device:TPU:0, one launch (start us, length us, event | category | flops | bytes accessed | tf_op | source)
XLA Modules:
  0.0 52.1 jit_solution(8899663343967049117)
XLA Ops:
  0.0 0.5 collective-permute-start
  0.5 0.7 %collective-permute-start.1 = (bf16[8,2,32,128]{3,2,1,0:T(8,128)(2,1)}, bf16[8,2,32,128]{3,2,1,0:T(8,128)(2,1)S(1)}, u32[]{:S(2)}, u32[]{:S(2)}) collective-permute-start(bf16[8,2,32,128]{3,2,1,0:T(8,128)(2,1)} %own_any.1), channel_id=1, source_target_pairs={{1,2},{2,1},{3,4},{4,3},{5,6},{6,5},{7,8},{8,7},{9,10},{10,9},{11,... | collective-permute-start | bytes 393224 | tf_op jit(solution)/shard_map/ppermute | solution.py:677
  1.1 5.4 %collective-permute-start.2 = (bf16[72,1152]{1,0:T(8,128)(2,1)}, bf16[72,1152]{1,0:T(8,128)(2,1)S(1)}, u32[]{:S(2)}, u32[]{:S(2)}) collective-permute-start(bf16[72,1152]{1,0:T(8,128)(2,1)} %refs_0_.1), channel_id=1, source_target_pairs={{0,4},{1,5},{4,8},{5,9},{8,12},{9,13},{12,14},{13,15},{14,10},{15,... | collective-permute-start | bytes 497672 | tf_op jit(solution)/shard_map/ppermute | solution.py:677
  6.5 1.3 %copy-done.3 = bf16[512,1152]{1,0:T(8,128)(2,1)S(1)} copy-done((bf16[512,1152]{1,0:T(8,128)(2,1)S(1)}, bf16[512,1152]{1,0:T(8,128)(2,1)}, u32[]{:S(2)}) %copy-start.3) | copy-done | bytes 1179672
  7.8 5.7 %fold.1 = (bf16[2304,512]{1,0:T(8,128)(2,1)S(1)}, bf16[1152,1152]{1,0:T(8,128)(2,1)S(1)}, bf16[512,1152]{1,0:T(8,128)(2,1)S(1)}) custom-call(bf16[512,1152]{1,0:T(8,128)(2,1)S(1)} %copy-done.3, bf16[1152,3456]{1,0:T(8,128)(2,1)} %qkv_any.1), custom_call_target="tpu_custom_call" | custom-call | flops 2717908992 | bytes 12582912 | tf_op jit(solution)/shard_map/fold/pallas_call | solution.py:252
  13.5 0.0 collective-permute-done.2.refs_1_
  13.5 0.0 collective-permute-done.3.refs_2_
  13.5 0.0 copy-start.2
  13.5 2.1 %collective-permute-start.5 = (bf16[72,1152]{1,0:T(8,128)(2,1)S(1)}, bf16[72,1152]{1,0:T(8,128)(2,1)S(1)}, u32[]{:S(2)}, u32[]{:S(2)}) collective-permute-start(bf16[72,1152]{1,0:T(8,128)(2,1)S(1)} %collective-permute-done.2.refs_1_), channel_id=1, source_target_pairs={{0,4},{1,5},{4,8},{5,9},{8,12},{9,13},{12,14},{13,15},{14,10},{15,... | collective-permute-start | bytes 497672 | tf_op jit(solution)/shard_map/ppermute | solution.py:677
  15.6 0.0 collective-permute-start.6
  15.7 3.9 %convolve.1 = (bf16[64,512]{1,0:T(8,128)(2,1)S(1)}, bf16[64,512]{1,0:T(8,128)(2,1)S(1)}) custom-call(s32[3]{0:T(128)S(1)} %copy-done.8, s32[1,3]{1,0:T(1,128)S(1)} %copy-done.1, bf16[8,2,32,128]{3,2,1,0:T(8,128)(2,1)S(1)} %copy-done.7, bf16[512,1152]{1,0:T(8,128)(2,1)S(1)} %copy-done.4, bf16[8,2,32,128]{3,2,1,0:T(8,128)(2,1)S(1)} %collective-permute-done.sibling_ref, ...), custom_call_target="tpu_custom_call" | custom-call | flops 2147483648 | bytes 4194304 | tf_op jit(solution)/shard_map/convolve/pallas_call | solution.py:404
  19.5 0.1 collective-permute-start.4
  19.6 1.2 %collective-permute-done.4 = bf16[64,512]{1,0:T(8,128)(2,1)S(1)} collective-permute-done((bf16[64,512]{1,0:T(8,128)(2,1)S(1)}, bf16[64,512]{1,0:T(8,128)(2,1)S(1)}, u32[]{:S(2)}, u32[]{:S(2)}) %collective-permute-start.4) | collective-permute-done | bytes 65568 | tf_op jit(solution)/shard_map/ppermute | solution.py:677
  20.9 0.0 collective-permute-done.5.refs_3_
  20.9 0.3 collective-permute-done.6.refs_4_
  21.2 0.8 %collective-permute-start.8 = (bf16[128,512]{1,0:T(8,128)(2,1)S(1)}, bf16[128,512]{1,0:T(8,128)(2,1)S(1)}, u32[]{:S(2)}, u32[]{:S(2)}) collective-permute-start(bf16[128,512]{1,0:T(8,128)(2,1)S(1)} %constant_dynamic-update-slice_fusion.block_ref.refs_0_), channel_id=1, source_target_pairs={{4,0},{5,1},{8,4},{9,5},{12,8},{13,9},{14,12},{15,13},{10,14},{11,... | collective-permute-start | bytes 393224 | tf_op jit(solution)/shard_map/ppermute | solution.py:677
  21.9 1.3 %collective-permute-start.7 = (bf16[128,512]{1,0:T(8,128)(2,1)S(1)}, bf16[128,512]{1,0:T(8,128)(2,1)S(1)}, u32[]{:S(2)}, u32[]{:S(2)}) collective-permute-start(bf16[128,512]{1,0:T(8,128)(2,1)S(1)} %constant_dynamic-update-slice_fusion.block_ref.refs_0_), channel_id=1, source_target_pairs={{0,4},{1,5},{4,8},{5,9},{8,12},{9,13},{12,14},{13,15},{14,10},{15,... | collective-permute-start | bytes 393224 | tf_op jit(solution)/shard_map/ppermute | solution.py:677
  23.2 1.8 %collective-permute-start.11 = (bf16[72,1152]{1,0:T(8,128)(2,1)S(1)}, bf16[72,1152]{1,0:T(8,128)(2,1)S(1)}, u32[]{:S(2)}, u32[]{:S(2)}) collective-permute-start(bf16[72,1152]{1,0:T(8,128)(2,1)S(1)} %collective-permute-done.5.refs_3_), channel_id=1, source_target_pairs={{0,4},{1,5},{4,8},{5,9},{8,12},{9,13},{12,14},{13,15},{14,10},{15,... | collective-permute-start | bytes 497672 | tf_op jit(solution)/shard_map/ppermute | solution.py:677
  25.0 0.3 collective-permute-start.12
  25.2 1.5 %queries.1.refs_4_.refs_5_ = bf16[16,128,80]{2,1,0:T(8,128)(2,1)S(1)} custom-call(s32[1,3]{1,0:T(1,128)S(1)} %copy-done.1, bf16[128,512]{1,0:T(8,128)(2,1)S(1)} %constant_dynamic-update-slice_fusion.block_ref.refs_0_, bf16[512,1152]{1,0:T(8,128)(2,1)S(1)} %get-tuple-element.45.centered_ref, bf16[1152,1152]{1,0:T(8,128)(2,1)S(1)} %get-tuple-element.46.query_ref, ...), custom_call_target="tpu_custom_call" | custom-call | flops 1073741824 | bytes 4194304 | tf_op jit(solution)/shard_map/queries/pallas_call | solution.py:533
  26.8 0.0 collective-permute-done.8.refs_1_
  26.8 1.6 %collective-permute-done.7.refs_0_ = bf16[128,512]{1,0:T(8,128)(2,1)S(1)} collective-permute-done((bf16[128,512]{1,0:T(8,128)(2,1)S(1)}, bf16[128,512]{1,0:T(8,128)(2,1)S(1)}, u32[]{:S(2)}, u32[]{:S(2)}) %collective-permute-start.7) | collective-permute-done | bytes 131104 | tf_op jit(solution)/shard_map/ppermute | solution.py:677
  28.3 1.2 %collective-permute-start.9 = (bf16[128,512]{1,0:T(8,128)(2,1)S(1)}, bf16[128,512]{1,0:T(8,128)(2,1)S(1)}, u32[]{:S(2)}, u32[]{:S(2)}) collective-permute-start(bf16[128,512]{1,0:T(8,128)(2,1)S(1)} %collective-permute-done.7.refs_0_), channel_id=1, source_target_pairs={{0,4},{1,5},{4,8},{5,9},{8,12},{9,13},{12,14},{13,15},{14,10},{15,... | collective-permute-start | bytes 393224 | tf_op jit(solution)/shard_map/ppermute | solution.py:677
  29.6 0.8 %collective-permute-start.10 = (bf16[128,512]{1,0:T(8,128)(2,1)S(1)}, bf16[128,512]{1,0:T(8,128)(2,1)S(1)}, u32[]{:S(2)}, u32[]{:S(2)}) collective-permute-start(bf16[128,512]{1,0:T(8,128)(2,1)S(1)} %collective-permute-done.8.refs_1_), channel_id=1, source_target_pairs={{4,0},{5,1},{8,4},{9,5},{12,8},{13,9},{14,12},{15,13},{10,14},{11,... | collective-permute-start | bytes 393224 | tf_op jit(solution)/shard_map/ppermute | solution.py:677
  30.4 2.0 %step_attention.4.refs_0_ = f32[16,80,128]{2,1,0:T(8,128)S(1)} custom-call(s32[1,3]{1,0:T(1,128)S(1)} %copy-done.1, bf16[128,512]{1,0:T(8,128)(2,1)S(1)} %collective-permute-done.7.refs_0_, bf16[128,512]{1,0:T(8,128)(2,1)S(1)} %collective-permute-done.8.refs_1_, bf16[2304,512]{1,0:T(8,128)(2,1)S(1)} %get-tuple-element.51.refs_2_.refs_3_, ...), custom_call_target="tpu_custom_call" | custom-call | flops 1744830464 | bytes 5242880 | tf_op jit(solution)/shard_map/step_attention/pallas_call | solution.py:561
  32.4 0.0 collective-permute-done.11.refs_5_
  32.4 1.7 %collective-permute-start.16 = (bf16[72,512]{1,0:T(8,128)(2,1)S(1)}, bf16[72,512]{1,0:T(8,128)(2,1)S(1)}, u32[]{:S(2)}, u32[]{:S(2)}) collective-permute-start(bf16[72,512]{1,0:T(8,128)(2,1)S(1)} %slice.13), channel_id=1, source_target_pairs={{4,0},{5,1},{8,4},{9,5},{12,8},{13,9},{14,12},{15,13},{10,14},{11,... | collective-permute-start | bytes 221192 | tf_op jit(solution)/shard_map/ppermute | solution.py:677
  34.1 0.0 copy-start
  34.1 0.5 collective-permute-start.15
  34.6 0.1 collective-permute-done.10.refs_1_
  34.6 1.7 %collective-permute-start.13 = (bf16[128,512]{1,0:T(8,128)(2,1)S(1)}, bf16[128,512]{1,0:T(8,128)(2,1)S(1)}, u32[]{:S(2)}, u32[]{:S(2)}) collective-permute-start(bf16[128,512]{1,0:T(8,128)(2,1)S(1)} %collective-permute-done.9.refs_0_), channel_id=1, source_target_pairs={{0,4},{1,5},{4,8},{5,9},{8,12},{9,13},{12,14},{13,15},{14,10},{15,... | collective-permute-start | bytes 393224 | tf_op jit(solution)/shard_map/ppermute | solution.py:677
  36.3 0.4 collective-permute-start.14
  36.7 2.0 %step_attention.5.refs_1_ = f32[16,80,128]{2,1,0:T(8,128)S(1)} custom-call(s32[1,3]{1,0:T(1,128)S(1)} %copy-done.1, bf16[128,512]{1,0:T(8,128)(2,1)S(1)} %collective-permute-done.9.refs_0_, bf16[128,512]{1,0:T(8,128)(2,1)S(1)} %collective-permute-done.10.refs_1_, bf16[2304,512]{1,0:T(8,128)(2,1)S(1)} %get-tuple-element.51.refs_2_.refs_3_, ...), custom_call_target="tpu_custom_call" | custom-call | flops 1744830464 | bytes 5242880 | tf_op jit(solution)/shard_map/step_attention/pallas_call | solution.py:561
  38.7 0.0 collective-permute-done.15.refs_7_
  38.7 1.4 %collective-permute-done.13.refs_0_ = bf16[128,512]{1,0:T(8,128)(2,1)S(1)} collective-permute-done((bf16[128,512]{1,0:T(8,128)(2,1)S(1)}, bf16[128,512]{1,0:T(8,128)(2,1)S(1)}, u32[]{:S(2)}, u32[]{:S(2)}) %collective-permute-start.13) | collective-permute-done | bytes 131104 | tf_op jit(solution)/shard_map/ppermute | solution.py:677
  40.1 1.2 %collective-permute-done.14.refs_1_ = bf16[128,512]{1,0:T(8,128)(2,1)S(1)} collective-permute-done((bf16[128,512]{1,0:T(8,128)(2,1)S(1)}, bf16[128,512]{1,0:T(8,128)(2,1)S(1)}, u32[]{:S(2)}, u32[]{:S(2)}) %collective-permute-start.14) | collective-permute-done | bytes 131104 | tf_op jit(solution)/shard_map/ppermute | solution.py:677
  41.3 0.1 pack.1
  41.4 0.1 collective-permute-start.19
  41.5 0.5 collective-permute-start.18
  42.0 1.6 %collective-permute-start.17 = (bf16[64,512]{1,0:T(8,128)(2,1)S(1)}, bf16[64,512]{1,0:T(8,128)(2,1)S(1)}, u32[]{:S(2)}, u32[]{:S(2)}) collective-permute-start(bf16[64,512]{1,0:T(8,128)(2,1)S(1)} %slice.14), channel_id=1, source_target_pairs={{0,4},{1,5},{4,8},{5,9},{8,12},{9,13},{12,14},{13,15},{14,10},{15,... | collective-permute-start | bytes 196616 | tf_op jit(solution)/shard_map/ppermute | solution.py:677
  43.6 2.0 %step_attention.6.refs_2_ = f32[16,80,128]{2,1,0:T(8,128)S(1)} custom-call(s32[1,3]{1,0:T(1,128)S(1)} %copy-done.1, bf16[128,512]{1,0:T(8,128)(2,1)S(1)} %collective-permute-done.13.refs_0_, bf16[128,512]{1,0:T(8,128)(2,1)S(1)} %collective-permute-done.14.refs_1_, bf16[2304,512]{1,0:T(8,128)(2,1)S(1)} %get-tuple-element.51.refs_2_.refs_3_, ...), custom_call_target="tpu_custom_call" | custom-call | flops 1744830464 | bytes 5242880 | tf_op jit(solution)/shard_map/step_attention/pallas_call | solution.py:561
  45.6 0.4 collective-permute-done.18.refs_2_
  46.0 0.2 collective-permute-done.17.refs_1_
  46.3 2.0 %step_attention.7.refs_3_ = f32[16,80,128]{2,1,0:T(8,128)S(1)} custom-call(s32[1,3]{1,0:T(1,128)S(1)} %copy-done.1, bf16[128,512]{1,0:T(8,128)(2,1)S(1)} %constant_dynamic-update-slice_fusion.block_ref.refs_0_, bf16[64,512]{1,0:T(8,128)(2,1)S(1)} %collective-permute-done.17.refs_1_, bf16[64,512]{1,0:T(8,128)(2,1)S(1)} %collective-permute-done.18.refs_2_, ...), custom_call_target="tpu_custom_call" | custom-call | flops 1744830464 | bytes 5242880 | tf_op jit(solution)/shard_map/step_attention/pallas_call | solution.py:561
  48.3 1.0 %project_out.1 = (bf16[64,1152]{1,0:T(8,128)(2,1)S(1)}, bf16[64,1152]{1,0:T(8,128)(2,1)S(1)}) custom-call(f32[16,80,128]{2,1,0:T(8,128)S(1)} %step_attention.4.refs_0_, f32[16,80,128]{2,1,0:T(8,128)S(1)} %step_attention.5.refs_1_, f32[16,80,128]{2,1,0:T(8,128)S(1)} %step_attention.6.refs_2_, f32[16,80,128]{2,1,0:T(8,128)S(1)} %step_attention.7.refs_3_, ...), custom_call_target="tpu_custom_call" | custom-call | flops 377487360 | bytes 4194304 | tf_op jit(solution)/shard_map/project_out/pallas_call | solution.py:606
  49.3 0.1 collective-permute-start.20
  49.4 1.4 %collective-permute-done.20.got_ref = bf16[64,1152]{1,0:T(8,128)(2,1)S(1)} collective-permute-done((bf16[64,1152]{1,0:T(8,128)(2,1)S(1)}, bf16[64,1152]{1,0:T(8,128)(2,1)S(1)}, u32[]{:S(2)}, u32[]{:S(2)}) %collective-permute-start.20) | collective-permute-done | bytes 147488 | tf_op jit(solution)/shard_map/ppermute | solution.py:677
  50.7 1.3 %merge.1 = bf16[128,1152]{1,0:T(8,128)(2,1)} custom-call(s32[1,3]{1,0:T(1,128)S(1)} %copy-done.1, bf16[64,1152]{1,0:T(8,128)(2,1)S(1)} %get-tuple-element.67.keep_ref, bf16[64,1152]{1,0:T(8,128)(2,1)S(1)} %collective-permute-done.20.got_ref), custom_call_target="tpu_custom_call" | custom-call | tf_op jit(solution)/shard_map/merge/pallas_call | solution.py:656
  (30 shorter events, 0.1 us)
Async XLA Ops:
  0.0 15.6 %copy-start.1 = (s32[1,3]{1,0:T(1,128)S(1)}, s32[1,3]{1,0:T(1,128)}, u32[]{:S(2)}) copy-start(s32[1,3]{1,0:T(1,128)} %lengths_ref.11) | copy-start | bytes 40
  0.0 13.5 %collective-permute-start = (bf16[8,2,32,128]{3,2,1,0:T(8,128)(2,1)}, bf16[8,2,32,128]{3,2,1,0:T(8,128)(2,1)S(1)}, u32[]{:S(2)}, u32[]{:S(2)}) collective-permute-start(bf16[8,2,32,128]{3,2,1,0:T(8,128)(2,1)} %own_any.1), channel_id=1, source_target_pairs={{0,1},{1,0},{2,3},{3,2},{4,5},{5,4},{6,7},{7,6},{8,9},{9,8},{10,11... | collective-permute-start | bytes 393224 | tf_op jit(solution)/shard_map/ppermute | solution.py:677
  0.5 13.0 %collective-permute-start.1 = (bf16[8,2,32,128]{3,2,1,0:T(8,128)(2,1)}, bf16[8,2,32,128]{3,2,1,0:T(8,128)(2,1)S(1)}, u32[]{:S(2)}, u32[]{:S(2)}) collective-permute-start(bf16[8,2,32,128]{3,2,1,0:T(8,128)(2,1)} %own_any.1), channel_id=1, source_target_pairs={{1,2},{2,1},{3,4},{4,3},{5,6},{6,5},{7,8},{8,7},{9,10},{10,9},{11,... | collective-permute-start | bytes 393224 | tf_op jit(solution)/shard_map/ppermute | solution.py:677
  1.1 12.4 %collective-permute-start.2 = (bf16[72,1152]{1,0:T(8,128)(2,1)}, bf16[72,1152]{1,0:T(8,128)(2,1)S(1)}, u32[]{:S(2)}, u32[]{:S(2)}) collective-permute-start(bf16[72,1152]{1,0:T(8,128)(2,1)} %refs_0_.1), channel_id=1, source_target_pairs={{0,4},{1,5},{4,8},{5,9},{8,12},{9,13},{12,14},{13,15},{14,10},{15,... | collective-permute-start | bytes 497672 | tf_op jit(solution)/shard_map/ppermute | solution.py:677
  6.5 7.0 %collective-permute-start.3 = (bf16[72,1152]{1,0:T(8,128)(2,1)}, bf16[72,1152]{1,0:T(8,128)(2,1)S(1)}, u32[]{:S(2)}, u32[]{:S(2)}) collective-permute-start(bf16[72,1152]{1,0:T(8,128)(2,1)} %refs_0_.1), channel_id=1, source_target_pairs={{4,0},{5,1},{8,4},{9,5},{12,8},{13,9},{14,12},{15,13},{10,14},{11,... | collective-permute-start | bytes 497672 | tf_op jit(solution)/shard_map/ppermute | solution.py:677
  6.5 1.3 %copy-start.3 = (bf16[512,1152]{1,0:T(8,128)(2,1)S(1)}, bf16[512,1152]{1,0:T(8,128)(2,1)}, u32[]{:S(2)}) copy-start(bf16[512,1152]{1,0:T(8,128)(2,1)} %patch_any.3) | copy-start | bytes 3538948
  7.8 7.8 %copy-start.4 = (bf16[512,1152]{1,0:T(8,128)(2,1)S(1)}, bf16[512,1152]{1,0:T(8,128)(2,1)}, u32[]{:S(2)}) copy-start(bf16[512,1152]{1,0:T(8,128)(2,1)} %patch_any.3) | copy-start | bytes 3538948
  7.8 7.8 %copy-start.5 = (bf16[3,3,3,128,128]{4,3,2,1,0:T(8,128)(2,1)S(1)}, bf16[3,3,3,128,128]{4,3,2,1,0:T(8,128)(2,1)}, u32[]{:S(2)}) copy-start(bf16[3,3,3,128,128]{4,3,2,1,0:T(8,128)(2,1)} %first_ref.1) | copy-start | bytes 2654212
  7.8 7.8 %copy-start.6 = (bf16[3,3,3,128,128]{4,3,2,1,0:T(8,128)(2,1)S(1)}, bf16[3,3,3,128,128]{4,3,2,1,0:T(8,128)(2,1)}, u32[]{:S(2)}) copy-start(bf16[3,3,3,128,128]{4,3,2,1,0:T(8,128)(2,1)} %second_ref.1) | copy-start | bytes 2654212
  7.8 7.8 %copy-start.7 = (bf16[8,2,32,128]{3,2,1,0:T(8,128)(2,1)S(1)}, bf16[8,2,32,128]{3,2,1,0:T(8,128)(2,1)}, u32[]{:S(2)}) copy-start(bf16[8,2,32,128]{3,2,1,0:T(8,128)(2,1)} %own_any.1) | copy-start | bytes 393220
  7.8 7.9 %copy-start.8 = (s32[3]{0:T(128)S(1)}, s32[3]{0:T(128)}, u32[]{:S(2)}) copy-start(s32[3]{0:T(128)} %counts_any.1) | copy-start | bytes 40
  13.5 11.7 %copy-start.2 = (f32[72]{0:T(128)S(1)}, f32[72]{0:T(128)}, u32[]{:S(2)}) copy-start(f32[72]{0:T(128)} %param.16) | copy-start | bytes 868
  13.5 7.3 %collective-permute-start.5 = (bf16[72,1152]{1,0:T(8,128)(2,1)S(1)}, bf16[72,1152]{1,0:T(8,128)(2,1)S(1)}, u32[]{:S(2)}, u32[]{:S(2)}) collective-permute-start(bf16[72,1152]{1,0:T(8,128)(2,1)S(1)} %collective-permute-done.2.refs_1_), channel_id=1, source_target_pairs={{0,4},{1,5},{4,8},{5,9},{8,12},{9,13},{12,14},{13,15},{14,10},{15,... | collective-permute-start | bytes 497672 | tf_op jit(solution)/shard_map/ppermute | solution.py:677
  15.6 5.6 %collective-permute-start.6 = (bf16[72,1152]{1,0:T(8,128)(2,1)S(1)}, bf16[72,1152]{1,0:T(8,128)(2,1)S(1)}, u32[]{:S(2)}, u32[]{:S(2)}) collective-permute-start(bf16[72,1152]{1,0:T(8,128)(2,1)S(1)} %collective-permute-done.3.refs_2_), channel_id=1, source_target_pairs={{4,0},{5,1},{8,4},{9,5},{12,8},{13,9},{14,12},{15,13},{10,14},{11,... | collective-permute-start | bytes 497672 | tf_op jit(solution)/shard_map/ppermute | solution.py:677
  19.5 1.3 %collective-permute-start.4 = (bf16[64,512]{1,0:T(8,128)(2,1)S(1)}, bf16[64,512]{1,0:T(8,128)(2,1)S(1)}, u32[]{:S(2)}, u32[]{:S(2)}) collective-permute-start(bf16[64,512]{1,0:T(8,128)(2,1)S(1)} %get-tuple-element.41), channel_id=1, source_target_pairs={{0,1},{1,0},{2,3},{3,2},{4,5},{5,4},{6,7},{7,6},{8,9},{9,8},{10,11... | collective-permute-start | bytes 196616 | tf_op jit(solution)/shard_map/ppermute | solution.py:677
  21.2 5.6 %collective-permute-start.8 = (bf16[128,512]{1,0:T(8,128)(2,1)S(1)}, bf16[128,512]{1,0:T(8,128)(2,1)S(1)}, u32[]{:S(2)}, u32[]{:S(2)}) collective-permute-start(bf16[128,512]{1,0:T(8,128)(2,1)S(1)} %constant_dynamic-update-slice_fusion.block_ref.refs_0_), channel_id=1, source_target_pairs={{4,0},{5,1},{8,4},{9,5},{12,8},{13,9},{14,12},{15,13},{10,14},{11,... | collective-permute-start | bytes 393224 | tf_op jit(solution)/shard_map/ppermute | solution.py:677
  21.9 6.4 %collective-permute-start.7 = (bf16[128,512]{1,0:T(8,128)(2,1)S(1)}, bf16[128,512]{1,0:T(8,128)(2,1)S(1)}, u32[]{:S(2)}, u32[]{:S(2)}) collective-permute-start(bf16[128,512]{1,0:T(8,128)(2,1)S(1)} %constant_dynamic-update-slice_fusion.block_ref.refs_0_), channel_id=1, source_target_pairs={{0,4},{1,5},{4,8},{5,9},{8,12},{9,13},{12,14},{13,15},{14,10},{15,... | collective-permute-start | bytes 393224 | tf_op jit(solution)/shard_map/ppermute | solution.py:677
  23.2 9.2 %collective-permute-start.11 = (bf16[72,1152]{1,0:T(8,128)(2,1)S(1)}, bf16[72,1152]{1,0:T(8,128)(2,1)S(1)}, u32[]{:S(2)}, u32[]{:S(2)}) collective-permute-start(bf16[72,1152]{1,0:T(8,128)(2,1)S(1)} %collective-permute-done.5.refs_3_), channel_id=1, source_target_pairs={{0,4},{1,5},{4,8},{5,9},{8,12},{9,13},{12,14},{13,15},{14,10},{15,... | collective-permute-start | bytes 497672 | tf_op jit(solution)/shard_map/ppermute | solution.py:677
  25.0 7.4 %collective-permute-start.12 = (bf16[72,1152]{1,0:T(8,128)(2,1)S(1)}, bf16[72,1152]{1,0:T(8,128)(2,1)S(1)}, u32[]{:S(2)}, u32[]{:S(2)}) collective-permute-start(bf16[72,1152]{1,0:T(8,128)(2,1)S(1)} %collective-permute-done.6.refs_4_), channel_id=1, source_target_pairs={{4,0},{5,1},{8,4},{9,5},{12,8},{13,9},{14,12},{15,13},{10,14},{11,... | collective-permute-start | bytes 497672 | tf_op jit(solution)/shard_map/ppermute | solution.py:677
  25.2 5.1 %copy-start.9 = (f32[72]{0:T(128)S(1)}, f32[72]{0:T(128)}, u32[]{:S(2)}) copy-start(f32[72]{0:T(128)} %param.17) | copy-start | bytes 868
  28.3 6.2 %collective-permute-start.9 = (bf16[128,512]{1,0:T(8,128)(2,1)S(1)}, bf16[128,512]{1,0:T(8,128)(2,1)S(1)}, u32[]{:S(2)}, u32[]{:S(2)}) collective-permute-start(bf16[128,512]{1,0:T(8,128)(2,1)S(1)} %collective-permute-done.7.refs_0_), channel_id=1, source_target_pairs={{0,4},{1,5},{4,8},{5,9},{8,12},{9,13},{12,14},{13,15},{14,10},{15,... | collective-permute-start | bytes 393224 | tf_op jit(solution)/shard_map/ppermute | solution.py:677
  29.6 5.1 %collective-permute-start.10 = (bf16[128,512]{1,0:T(8,128)(2,1)S(1)}, bf16[128,512]{1,0:T(8,128)(2,1)S(1)}, u32[]{:S(2)}, u32[]{:S(2)}) collective-permute-start(bf16[128,512]{1,0:T(8,128)(2,1)S(1)} %collective-permute-done.8.refs_1_), channel_id=1, source_target_pairs={{4,0},{5,1},{8,4},{9,5},{12,8},{13,9},{14,12},{15,13},{10,14},{11,... | collective-permute-start | bytes 393224 | tf_op jit(solution)/shard_map/ppermute | solution.py:677
  32.4 6.3 %collective-permute-start.16 = (bf16[72,512]{1,0:T(8,128)(2,1)S(1)}, bf16[72,512]{1,0:T(8,128)(2,1)S(1)}, u32[]{:S(2)}, u32[]{:S(2)}) collective-permute-start(bf16[72,512]{1,0:T(8,128)(2,1)S(1)} %slice.13), channel_id=1, source_target_pairs={{4,0},{5,1},{8,4},{9,5},{12,8},{13,9},{14,12},{15,13},{10,14},{11,... | collective-permute-start | bytes 221192 | tf_op jit(solution)/shard_map/ppermute | solution.py:677
  34.1 7.2 %copy-start = (bf16[72,1152]{1,0:T(8,128)(2,1)S(1)}, bf16[72,1152]{1,0:T(8,128)(2,1)}, u32[]{:S(2)}) copy-start(bf16[72,1152]{1,0:T(8,128)(2,1)} %refs_0_.1) | copy-start | bytes 497668
  34.1 4.6 %collective-permute-start.15 = (bf16[72,640]{1,0:T(8,128)(2,1)S(1)}, bf16[72,640]{1,0:T(8,128)(2,1)S(1)}, u32[]{:S(2)}, u32[]{:S(2)}) collective-permute-start(bf16[72,640]{1,0:T(8,128)(2,1)S(1)} %slice.12), channel_id=1, source_target_pairs={{0,4},{1,5},{4,8},{5,9},{8,12},{9,13},{12,14},{13,15},{14,10},{15,... | collective-permute-start | bytes 276488 | tf_op jit(solution)/shard_map/ppermute | solution.py:677
  34.6 5.5 %collective-permute-start.13 = (bf16[128,512]{1,0:T(8,128)(2,1)S(1)}, bf16[128,512]{1,0:T(8,128)(2,1)S(1)}, u32[]{:S(2)}, u32[]{:S(2)}) collective-permute-start(bf16[128,512]{1,0:T(8,128)(2,1)S(1)} %collective-permute-done.9.refs_0_), channel_id=1, source_target_pairs={{0,4},{1,5},{4,8},{5,9},{8,12},{9,13},{12,14},{13,15},{14,10},{15,... | collective-permute-start | bytes 393224 | tf_op jit(solution)/shard_map/ppermute | solution.py:677
  36.3 5.0 %collective-permute-start.14 = (bf16[128,512]{1,0:T(8,128)(2,1)S(1)}, bf16[128,512]{1,0:T(8,128)(2,1)S(1)}, u32[]{:S(2)}, u32[]{:S(2)}) collective-permute-start(bf16[128,512]{1,0:T(8,128)(2,1)S(1)} %collective-permute-done.10.refs_1_), channel_id=1, source_target_pairs={{4,0},{5,1},{8,4},{9,5},{12,8},{13,9},{14,12},{15,13},{10,14},{11,... | collective-permute-start | bytes 393224 | tf_op jit(solution)/shard_map/ppermute | solution.py:677
  41.4 6.9 %collective-permute-start.19 = (bf16[576,1152]{1,0:T(8,128)(2,1)S(1)}, bf16[576,1152]{1,0:T(8,128)(2,1)S(1)}, u32[]{:S(2)}, u32[]{:S(2)}) collective-permute-start(bf16[576,1152]{1,0:T(8,128)(2,1)S(1)} %bitcast.3), channel_id=1, source_target_pairs={{0,1},{1,0},{2,3},{3,2},{4,5},{5,4},{6,7},{7,6},{8,9},{9,8},{10,11... | collective-permute-start | bytes 3981320 | tf_op jit(solution)/shard_map/ppermute | solution.py:677
  41.5 4.5 %collective-permute-start.18 = (bf16[64,512]{1,0:T(8,128)(2,1)S(1)}, bf16[64,512]{1,0:T(8,128)(2,1)S(1)}, u32[]{:S(2)}, u32[]{:S(2)}) collective-permute-start(bf16[64,512]{1,0:T(8,128)(2,1)S(1)} %slice.15), channel_id=1, source_target_pairs={{4,0},{5,1},{8,4},{9,5},{12,8},{13,9},{14,12},{15,13},{10,14},{11,... | collective-permute-start | bytes 196616 | tf_op jit(solution)/shard_map/ppermute | solution.py:677
  42.0 4.3 %collective-permute-start.17 = (bf16[64,512]{1,0:T(8,128)(2,1)S(1)}, bf16[64,512]{1,0:T(8,128)(2,1)S(1)}, u32[]{:S(2)}, u32[]{:S(2)}) collective-permute-start(bf16[64,512]{1,0:T(8,128)(2,1)S(1)} %slice.14), channel_id=1, source_target_pairs={{0,4},{1,5},{4,8},{5,9},{8,12},{9,13},{12,14},{13,15},{14,10},{15,... | collective-permute-start | bytes 196616 | tf_op jit(solution)/shard_map/ppermute | solution.py:677
  49.3 1.4 %collective-permute-start.20 = (bf16[64,1152]{1,0:T(8,128)(2,1)S(1)}, bf16[64,1152]{1,0:T(8,128)(2,1)S(1)}, u32[]{:S(2)}, u32[]{:S(2)}) collective-permute-start(bf16[64,1152]{1,0:T(8,128)(2,1)S(1)} %get-tuple-element.68), channel_id=1, source_target_pairs={{0,1},{1,0},{2,3},{3,2},{4,5},{5,4},{6,7},{7,6},{8,9},{9,8},{10,11... | collective-permute-start | bytes 442376 | tf_op jit(solution)/shard_map/ppermute | solution.py:677

commit v9 on v8

--- a/solution.py
+++ b/solution.py
@@ -707,19 +707,19 @@
     weight_three = both_ways(*weight_two)
     block = jnp.concatenate([keep, got], axis=0)
     one = both_ways(block, block)
-    queries = make_queries(window_lengths, block, centered, query_weight, query_row)
+    wt_a, wt_b, query_block = tied(*weight_three, block)
+    cut = 640
+    weight_four = both_ways(wt_a[:, :cut], wt_b[:, cut:])
+    queries = make_queries(window_lengths, query_block, centered, query_weight, query_row)
     *one, queries = tied(*one, queries)
     two = both_ways(*one)
     acc_one = step_attention((-1, 1), window_lengths, one, folded, key_row, queries)
-    wt_a, wt_b, acc_one = tied(*weight_three, acc_one)
-    cut = 640
-    weight_four = both_ways(wt_a[:, :cut], wt_b[:, cut:])
-    *two, acc_one = tied(*two, acc_one)
+    wf_a, wf_b, *two, acc_one = tied(*weight_four, *two, acc_one)
     three = both_ways(*two)
+    weights = pack([out_weight, *weight_one, *weight_two, wt_a, wt_b, wf_a, wf_b])
     acc_two = step_attention((-2, 2), window_lengths, two, folded, key_row, queries)
-    *three, acc_two, wf_a, wf_b = tied(*three, acc_two, *weight_four)
+    *three, acc_two, weights = tied(*three, acc_two, weights)
     four = both_ways(three[0][:64], three[1][64:])
-    weights = pack([out_weight, *weight_one, *weight_two, wt_a, wt_b, wf_a, wf_b])
     sibling = send(weights, cores)
     acc_three = step_attention((-3, 3), window_lengths, three, folded, key_row, queries)
     *four, acc_three = tied(*four, acc_three)

time: 52.2 us -> 57.2 us (1.096)
  waiting for transfers between devices: 7.8 us -> 12.8 us
    ppermute x21, waiting for transfers between devices: 7.8 us -> 12.8 us  [send(): return lax.ppermute(array, 'seq', pairs)]
  transfers between devices with their start and end apart: 21 -> 21, of which waited for: 9 -> 10; matrix products, arithmetic and copies ran while one was open for 0% -> 0% of each run, Pallas kernels for 37% -> 34%
where the time goes in v9:
time: 57.2 us; the launch traced here: 57.1 us
  Pallas kernels  21.6 us (38%)
  starting transfers between devices  21.1 us (37%)
  waiting for transfers between devices  12.8 us (22%)
  local copies, waits for them, and re-layouts  1.34 us (2%)
    ppermute x21, starting transfers between devices, send(): return lax.ppermute(array, 'seq', pairs)  21.1 us
    ppermute x21, waiting for transfers between devices, send(): return lax.ppermute(array, 'seq', pairs)  12.8 us
    pallas_call x4, Pallas kernels, step_attention(): pl.pallas_call(functools.partial(step_kernel, offsets), out_shape=ACC, in...  8.11 us
    pallas_call x1, Pallas kernels, fold(): pl.pallas_call(fold_kernel, out_shape=(jax.ShapeDtypeStruct((2 * D, inner...  5.68 us
    pallas_call x1, Pallas kernels, convolve(): pl.pallas_call(conv_kernel, out_shape=(out, out), in_specs=[ANY] * 4 + [V...  3.88 us
    pallas_call x1, Pallas kernels, make_queries(): pl.pallas_call(query_kernel, out_shape=jax.ShapeDtypeStruct((HEADS, 128,...  1.53 us
    pallas_call x1, Pallas kernels, merge(): pl.pallas_call(merge_kernel, out_shape=jax.ShapeDtypeStruct((128, D), BF1...  1.35 us
    unnamed x21, local copies, waits for them, and re-layouts  1.31 us
  transfers between devices with their start and end apart: 21, of which 10 were waited for; matrix products, arithmetic and copies ran while one was open for 0% of the time, Pallas kernels for 34%

profile of v9, /device:TPU:0, one launch (start us, length us, event | category | flops | bytes accessed | tf_op | source)
XLA Modules:
  0.0 57.1 jit_solution(10050271627587605360)
XLA Ops:
  0.0 3.0 %collective-permute-start.2 = (bf16[72,1152]{1,0:T(8,128)(2,1)}, bf16[72,1152]{1,0:T(8,128)(2,1)S(1)}, u32[]{:S(2)}, u32[]{:S(2)}) collective-permute-start(bf16[72,1152]{1,0:T(8,128)(2,1)} %refs_0_.1), channel_id=1, source_target_pairs={{0,4},{1,5},{4,8},{5,9},{8,12},{9,13},{12,14},{13,15},{14,10},{15,... | collective-permute-start | bytes 497672 | tf_op jit(solution)/shard_map/ppermute | solution.py:677
  3.0 0.7 %collective-permute-start.1 = (bf16[8,2,32,128]{3,2,1,0:T(8,128)(2,1)}, bf16[8,2,32,128]{3,2,1,0:T(8,128)(2,1)S(1)}, u32[]{:S(2)}, u32[]{:S(2)}) collective-permute-start(bf16[8,2,32,128]{3,2,1,0:T(8,128)(2,1)} %own_any.1), channel_id=1, source_target_pairs={{1,2},{2,1},{3,4},{4,3},{5,6},{6,5},{7,8},{8,7},{9,10},{10,9},{11,... | collective-permute-start | bytes 393224 | tf_op jit(solution)/shard_map/ppermute | solution.py:677
  3.7 1.3 %copy-done.3 = bf16[512,1152]{1,0:T(8,128)(2,1)S(1)} copy-done((bf16[512,1152]{1,0:T(8,128)(2,1)S(1)}, bf16[512,1152]{1,0:T(8,128)(2,1)}, u32[]{:S(2)}) %copy-start.3) | copy-done | bytes 1179672
  5.0 5.7 %fold.1 = (bf16[2304,512]{1,0:T(8,128)(2,1)S(1)}, bf16[1152,1152]{1,0:T(8,128)(2,1)S(1)}, bf16[512,1152]{1,0:T(8,128)(2,1)S(1)}) custom-call(bf16[512,1152]{1,0:T(8,128)(2,1)S(1)} %copy-done.3, bf16[1152,3456]{1,0:T(8,128)(2,1)} %qkv_any.1), custom_call_target="tpu_custom_call" | custom-call | flops 2717908992 | bytes 12582912 | tf_op jit(solution)/shard_map/fold/pallas_call | solution.py:252
  10.7 0.0 collective-permute-done.1.other_ref
  10.7 0.0 collective-permute-done.2.refs_1_
  10.7 0.0 copy-start.2
  10.7 4.8 %collective-permute-start.5 = (bf16[72,1152]{1,0:T(8,128)(2,1)S(1)}, bf16[72,1152]{1,0:T(8,128)(2,1)S(1)}, u32[]{:S(2)}, u32[]{:S(2)}) collective-permute-start(bf16[72,1152]{1,0:T(8,128)(2,1)S(1)} %collective-permute-done.2.refs_1_), channel_id=1, source_target_pairs={{0,4},{1,5},{4,8},{5,9},{8,12},{9,13},{12,14},{13,15},{14,10},{15,... | collective-permute-start | bytes 497672 | tf_op jit(solution)/shard_map/ppermute | solution.py:677
  15.6 0.0 collective-permute-start.6
  15.6 3.9 %convolve.1 = (bf16[64,512]{1,0:T(8,128)(2,1)S(1)}, bf16[64,512]{1,0:T(8,128)(2,1)S(1)}) custom-call(s32[3]{0:T(128)S(1)} %copy-done.8, s32[1,3]{1,0:T(1,128)S(1)} %copy-done.1, bf16[8,2,32,128]{3,2,1,0:T(8,128)(2,1)S(1)} %copy-done.7, bf16[512,1152]{1,0:T(8,128)(2,1)S(1)} %copy-done.4, bf16[8,2,32,128]{3,2,1,0:T(8,128)(2,1)S(1)} %collective-permute-done.sibling_ref, ...), custom_call_target="tpu_custom_call" | custom-call | flops 2147483648 | bytes 4194304 | tf_op jit(solution)/shard_map/convolve/pallas_call | solution.py:404
  19.5 0.1 collective-permute-start.4
  19.6 1.2 %collective-permute-done.4 = bf16[64,512]{1,0:T(8,128)(2,1)S(1)} collective-permute-done((bf16[64,512]{1,0:T(8,128)(2,1)S(1)}, bf16[64,512]{1,0:T(8,128)(2,1)S(1)}, u32[]{:S(2)}, u32[]{:S(2)}) %collective-permute-start.4) | collective-permute-done | bytes 65568 | tf_op jit(solution)/shard_map/ppermute | solution.py:677
  20.8 0.7 %collective-permute-done.6.refs_4_ = bf16[72,1152]{1,0:T(8,128)(2,1)S(1)} collective-permute-done((bf16[72,1152]{1,0:T(8,128)(2,1)S(1)}, bf16[72,1152]{1,0:T(8,128)(2,1)S(1)}, u32[]{:S(2)}, u32[]{:S(2)}) %collective-permute-start.6) | collective-permute-done | bytes 165920 | tf_op jit(solution)/shard_map/ppermute | solution.py:677
  21.5 1.6 %collective-permute-start.7 = (bf16[72,1152]{1,0:T(8,128)(2,1)S(1)}, bf16[72,1152]{1,0:T(8,128)(2,1)S(1)}, u32[]{:S(2)}, u32[]{:S(2)}) collective-permute-start(bf16[72,1152]{1,0:T(8,128)(2,1)S(1)} %collective-permute-done.5.refs_3_), channel_id=1, source_target_pairs={{0,4},{1,5},{4,8},{5,9},{8,12},{9,13},{12,14},{13,15},{14,10},{15,... | collective-permute-start | bytes 497672 | tf_op jit(solution)/shard_map/ppermute | solution.py:677
  23.1 0.4 collective-permute-start.8
  23.6 1.6 %collective-permute-start.11 = (bf16[128,512]{1,0:T(8,128)(2,1)S(1)}, bf16[128,512]{1,0:T(8,128)(2,1)S(1)}, u32[]{:S(2)}, u32[]{:S(2)}) collective-permute-start(bf16[128,512]{1,0:T(8,128)(2,1)S(1)} %constant_dynamic-update-slice_fusion.block_ref.refs_0_), channel_id=1, source_target_pairs={{0,4},{1,5},{4,8},{5,9},{8,12},{9,13},{12,14},{13,15},{14,10},{15,... | collective-permute-start | bytes 393224 | tf_op jit(solution)/shard_map/ppermute | solution.py:677
  25.2 0.4 collective-permute-start.12
  25.7 2.9 %collective-permute-done.7.refs_5_ = bf16[72,1152]{1,0:T(8,128)(2,1)S(1)} collective-permute-done((bf16[72,1152]{1,0:T(8,128)(2,1)S(1)}, bf16[72,1152]{1,0:T(8,128)(2,1)S(1)}, u32[]{:S(2)}, u32[]{:S(2)}) %collective-permute-start.7) | collective-permute-done | bytes 165920 | tf_op jit(solution)/shard_map/ppermute | solution.py:677
  28.5 1.7 %collective-permute-done.8.refs_6_ = bf16[72,1152]{1,0:T(8,128)(2,1)S(1)} collective-permute-done((bf16[72,1152]{1,0:T(8,128)(2,1)S(1)}, bf16[72,1152]{1,0:T(8,128)(2,1)S(1)}, u32[]{:S(2)}, u32[]{:S(2)}) %collective-permute-start.8) | collective-permute-done | bytes 165920 | tf_op jit(solution)/shard_map/ppermute | solution.py:677
  30.3 1.5 %queries.1.refs_4_.refs_5_ = bf16[16,128,80]{2,1,0:T(8,128)(2,1)S(1)} custom-call(s32[1,3]{1,0:T(1,128)S(1)} %copy-done.1, bf16[128,512]{1,0:T(8,128)(2,1)S(1)} %constant_dynamic-update-slice_fusion.block_ref.refs_0_, bf16[512,1152]{1,0:T(8,128)(2,1)S(1)} %get-tuple-element.51.centered_ref, bf16[1152,1152]{1,0:T(8,128)(2,1)S(1)} %get-tuple-element.52.query_ref, ...), custom_call_target="tpu_custom_call" | custom-call | flops 1073741824 | bytes 4194304 | tf_op jit(solution)/shard_map/queries/pallas_call | solution.py:533
  31.8 0.0 collective-permute-done.11.refs_0_
  31.8 0.0 collective-permute-done.12.refs_1_
  31.8 1.6 %collective-permute-start.13 = (bf16[128,512]{1,0:T(8,128)(2,1)S(1)}, bf16[128,512]{1,0:T(8,128)(2,1)S(1)}, u32[]{:S(2)}, u32[]{:S(2)}) collective-permute-start(bf16[128,512]{1,0:T(8,128)(2,1)S(1)} %collective-permute-done.11.refs_0_), channel_id=1, source_target_pairs={{0,4},{1,5},{4,8},{5,9},{8,12},{9,13},{12,14},{13,15},{14,10},{15,... | collective-permute-start | bytes 393224 | tf_op jit(solution)/shard_map/ppermute | solution.py:677
  33.4 0.4 collective-permute-start.14
  33.9 1.6 %collective-permute-start.9 = (bf16[72,640]{1,0:T(8,128)(2,1)S(1)}, bf16[72,640]{1,0:T(8,128)(2,1)S(1)}, u32[]{:S(2)}, u32[]{:S(2)}) collective-permute-start(bf16[72,640]{1,0:T(8,128)(2,1)S(1)} %slice.12), channel_id=1, source_target_pairs={{0,4},{1,5},{4,8},{5,9},{8,12},{9,13},{12,14},{13,15},{14,10},{15,... | collective-permute-start | bytes 276488 | tf_op jit(solution)/shard_map/ppermute | solution.py:677
  35.5 0.4 collective-permute-start.10
  36.0 2.0 %step_attention.4.refs_0_ = f32[16,80,128]{2,1,0:T(8,128)S(1)} custom-call(s32[1,3]{1,0:T(1,128)S(1)} %copy-done.1, bf16[128,512]{1,0:T(8,128)(2,1)S(1)} %collective-permute-done.11.refs_0_, bf16[128,512]{1,0:T(8,128)(2,1)S(1)} %collective-permute-done.12.refs_1_, bf16[2304,512]{1,0:T(8,128)(2,1)S(1)} %get-tuple-element.55.refs_2_.refs_3_, ...), custom_call_target="tpu_custom_call" | custom-call | flops 1744830464 | bytes 5242880 | tf_op jit(solution)/shard_map/step_attention/pallas_call | solution.py:561
  38.0 1.9 %collective-permute-done.10.refs_8_ = bf16[72,512]{1,0:T(8,128)(2,1)S(1)} collective-permute-done((bf16[72,512]{1,0:T(8,128)(2,1)S(1)}, bf16[72,512]{1,0:T(8,128)(2,1)S(1)}, u32[]{:S(2)}, u32[]{:S(2)}) %collective-permute-start.10) | collective-permute-done | bytes 73760 | tf_op jit(solution)/shard_map/ppermute | solution.py:677
  39.9 0.0 collective-permute-done.9.refs_7_
  39.9 0.0 collective-permute-done.13.refs_0_
  39.9 0.0 collective-permute-done.14.refs_1_
  39.9 1.4 %collective-permute-start.15 = (bf16[128,512]{1,0:T(8,128)(2,1)S(1)}, bf16[128,512]{1,0:T(8,128)(2,1)S(1)}, u32[]{:S(2)}, u32[]{:S(2)}) collective-permute-start(bf16[128,512]{1,0:T(8,128)(2,1)S(1)} %collective-permute-done.13.refs_0_), channel_id=1, source_target_pairs={{0,4},{1,5},{4,8},{5,9},{8,12},{9,13},{12,14},{13,15},{14,10},{15,... | collective-permute-start | bytes 393224 | tf_op jit(solution)/shard_map/ppermute | solution.py:677
  41.3 0.7 %collective-permute-start.16 = (bf16[128,512]{1,0:T(8,128)(2,1)S(1)}, bf16[128,512]{1,0:T(8,128)(2,1)S(1)}, u32[]{:S(2)}, u32[]{:S(2)}) collective-permute-start(bf16[128,512]{1,0:T(8,128)(2,1)S(1)} %collective-permute-done.14.refs_1_), channel_id=1, source_target_pairs={{4,0},{5,1},{8,4},{9,5},{12,8},{13,9},{14,12},{15,13},{10,14},{11,... | collective-permute-start | bytes 393224 | tf_op jit(solution)/shard_map/ppermute | solution.py:677
  42.0 0.1 pack.1
  42.1 2.0 %step_attention.5.refs_1_ = f32[16,80,128]{2,1,0:T(8,128)S(1)} custom-call(s32[1,3]{1,0:T(1,128)S(1)} %copy-done.1, bf16[128,512]{1,0:T(8,128)(2,1)S(1)} %collective-permute-done.13.refs_0_, bf16[128,512]{1,0:T(8,128)(2,1)S(1)} %collective-permute-done.14.refs_1_, bf16[2304,512]{1,0:T(8,128)(2,1)S(1)} %get-tuple-element.55.refs_2_.refs_3_, ...), custom_call_target="tpu_custom_call" | custom-call | flops 1744830464 | bytes 5242880 | tf_op jit(solution)/shard_map/step_attention/pallas_call | solution.py:561
  44.1 0.8 %collective-permute-done.15.refs_0_ = bf16[128,512]{1,0:T(8,128)(2,1)S(1)} collective-permute-done((bf16[128,512]{1,0:T(8,128)(2,1)S(1)}, bf16[128,512]{1,0:T(8,128)(2,1)S(1)}, u32[]{:S(2)}, u32[]{:S(2)}) %collective-permute-start.15) | collective-permute-done | bytes 131104 | tf_op jit(solution)/shard_map/ppermute | solution.py:677
  44.9 1.4 %collective-permute-done.16.refs_1_ = bf16[128,512]{1,0:T(8,128)(2,1)S(1)} collective-permute-done((bf16[128,512]{1,0:T(8,128)(2,1)S(1)}, bf16[128,512]{1,0:T(8,128)(2,1)S(1)}, u32[]{:S(2)}, u32[]{:S(2)}) %collective-permute-start.16) | collective-permute-done | bytes 131104 | tf_op jit(solution)/shard_map/ppermute | solution.py:677
  46.3 0.7 %collective-permute-start.17 = (bf16[64,512]{1,0:T(8,128)(2,1)S(1)}, bf16[64,512]{1,0:T(8,128)(2,1)S(1)}, u32[]{:S(2)}, u32[]{:S(2)}) collective-permute-start(bf16[64,512]{1,0:T(8,128)(2,1)S(1)} %slice.14), channel_id=1, source_target_pairs={{0,4},{1,5},{4,8},{5,9},{8,12},{9,13},{12,14},{13,15},{14,10},{15,... | collective-permute-start | bytes 196616 | tf_op jit(solution)/shard_map/ppermute | solution.py:677
  47.0 1.4 %collective-permute-start.18 = (bf16[64,512]{1,0:T(8,128)(2,1)S(1)}, bf16[64,512]{1,0:T(8,128)(2,1)S(1)}, u32[]{:S(2)}, u32[]{:S(2)}) collective-permute-start(bf16[64,512]{1,0:T(8,128)(2,1)S(1)} %slice.15), channel_id=1, source_target_pairs={{4,0},{5,1},{8,4},{9,5},{12,8},{13,9},{14,12},{15,13},{10,14},{11,... | collective-permute-start | bytes 196616 | tf_op jit(solution)/shard_map/ppermute | solution.py:677
  48.4 2.0 %step_attention.6.refs_2_ = f32[16,80,128]{2,1,0:T(8,128)S(1)} custom-call(s32[1,3]{1,0:T(1,128)S(1)} %copy-done.1, bf16[128,512]{1,0:T(8,128)(2,1)S(1)} %collective-permute-done.15.refs_0_, bf16[128,512]{1,0:T(8,128)(2,1)S(1)} %collective-permute-done.16.refs_1_, bf16[2304,512]{1,0:T(8,128)(2,1)S(1)} %get-tuple-element.55.refs_2_.refs_3_, ...), custom_call_target="tpu_custom_call" | custom-call | flops 1744830464 | bytes 5242880 | tf_op jit(solution)/shard_map/step_attention/pallas_call | solution.py:561
  50.4 0.4 collective-permute-done.17.refs_1_
  50.8 0.4 collective-permute-done.18.refs_2_
  51.3 2.0 %step_attention.7.refs_3_ = f32[16,80,128]{2,1,0:T(8,128)S(1)} custom-call(s32[1,3]{1,0:T(1,128)S(1)} %copy-done.1, bf16[128,512]{1,0:T(8,128)(2,1)S(1)} %constant_dynamic-update-slice_fusion.block_ref.refs_0_, bf16[64,512]{1,0:T(8,128)(2,1)S(1)} %collective-permute-done.17.refs_1_, bf16[64,512]{1,0:T(8,128)(2,1)S(1)} %collective-permute-done.18.refs_2_, ...), custom_call_target="tpu_custom_call" | custom-call | flops 1744830464 | bytes 5242880 | tf_op jit(solution)/shard_map/step_attention/pallas_call | solution.py:561
  53.3 0.0 collective-permute-done.19.refs_5_
  53.3 1.0 %project_out.1 = (bf16[64,1152]{1,0:T(8,128)(2,1)S(1)}, bf16[64,1152]{1,0:T(8,128)(2,1)S(1)}) custom-call(f32[16,80,128]{2,1,0:T(8,128)S(1)} %step_attention.4.refs_0_, f32[16,80,128]{2,1,0:T(8,128)S(1)} %step_attention.5.refs_1_, f32[16,80,128]{2,1,0:T(8,128)S(1)} %step_attention.6.refs_2_, f32[16,80,128]{2,1,0:T(8,128)S(1)} %step_attention.7.refs_3_, ...), custom_call_target="tpu_custom_call" | custom-call | flops 377487360 | bytes 4194304 | tf_op jit(solution)/shard_map/project_out/pallas_call | solution.py:606
  54.3 0.1 collective-permute-start.20
  54.4 1.4 %collective-permute-done.20.got_ref = bf16[64,1152]{1,0:T(8,128)(2,1)S(1)} collective-permute-done((bf16[64,1152]{1,0:T(8,128)(2,1)S(1)}, bf16[64,1152]{1,0:T(8,128)(2,1)S(1)}, u32[]{:S(2)}, u32[]{:S(2)}) %collective-permute-start.20) | collective-permute-done | bytes 147488 | tf_op jit(solution)/shard_map/ppermute | solution.py:677
  55.7 1.3 %merge.1 = bf16[128,1152]{1,0:T(8,128)(2,1)} custom-call(s32[1,3]{1,0:T(1,128)S(1)} %copy-done.1, bf16[64,1152]{1,0:T(8,128)(2,1)S(1)} %get-tuple-element.69.keep_ref, bf16[64,1152]{1,0:T(8,128)(2,1)S(1)} %collective-permute-done.20.got_ref), custom_call_target="tpu_custom_call" | custom-call | tf_op jit(solution)/shard_map/merge/pallas_call | solution.py:656
  (30 shorter events, 0.1 us)
Async XLA Ops:
  0.0 15.6 %copy-start.1 = (s32[1,3]{1,0:T(1,128)S(1)}, s32[1,3]{1,0:T(1,128)}, u32[]{:S(2)}) copy-start(s32[1,3]{1,0:T(1,128)} %lengths_ref.11) | copy-start | bytes 40
  0.0 10.7 %collective-permute-start.2 = (bf16[72,1152]{1,0:T(8,128)(2,1)}, bf16[72,1152]{1,0:T(8,128)(2,1)S(1)}, u32[]{:S(2)}, u32[]{:S(2)}) collective-permute-start(bf16[72,1152]{1,0:T(8,128)(2,1)} %refs_0_.1), channel_id=1, source_target_pairs={{0,4},{1,5},{4,8},{5,9},{8,12},{9,13},{12,14},{13,15},{14,10},{15,... | collective-permute-start | bytes 497672 | tf_op jit(solution)/shard_map/ppermute | solution.py:677
  3.0 7.7 %collective-permute-start.3 = (bf16[72,1152]{1,0:T(8,128)(2,1)}, bf16[72,1152]{1,0:T(8,128)(2,1)S(1)}, u32[]{:S(2)}, u32[]{:S(2)}) collective-permute-start(bf16[72,1152]{1,0:T(8,128)(2,1)} %refs_0_.1), channel_id=1, source_target_pairs={{4,0},{5,1},{8,4},{9,5},{12,8},{13,9},{14,12},{15,13},{10,14},{11,... | collective-permute-start | bytes 497672 | tf_op jit(solution)/shard_map/ppermute | solution.py:677
  3.0 7.6 %collective-permute-start = (bf16[8,2,32,128]{3,2,1,0:T(8,128)(2,1)}, bf16[8,2,32,128]{3,2,1,0:T(8,128)(2,1)S(1)}, u32[]{:S(2)}, u32[]{:S(2)}) collective-permute-start(bf16[8,2,32,128]{3,2,1,0:T(8,128)(2,1)} %own_any.1), channel_id=1, source_target_pairs={{0,1},{1,0},{2,3},{3,2},{4,5},{5,4},{6,7},{7,6},{8,9},{9,8},{10,11... | collective-permute-start | bytes 393224 | tf_op jit(solution)/shard_map/ppermute | solution.py:677
  3.0 7.7 %collective-permute-start.1 = (bf16[8,2,32,128]{3,2,1,0:T(8,128)(2,1)}, bf16[8,2,32,128]{3,2,1,0:T(8,128)(2,1)S(1)}, u32[]{:S(2)}, u32[]{:S(2)}) collective-permute-start(bf16[8,2,32,128]{3,2,1,0:T(8,128)(2,1)} %own_any.1), channel_id=1, source_target_pairs={{1,2},{2,1},{3,4},{4,3},{5,6},{6,5},{7,8},{8,7},{9,10},{10,9},{11,... | collective-permute-start | bytes 393224 | tf_op jit(solution)/shard_map/ppermute | solution.py:677
  3.7 1.3 %copy-start.3 = (bf16[512,1152]{1,0:T(8,128)(2,1)S(1)}, bf16[512,1152]{1,0:T(8,128)(2,1)}, u32[]{:S(2)}) copy-start(bf16[512,1152]{1,0:T(8,128)(2,1)} %patch_any.3) | copy-start | bytes 3538948
  5.0 10.6 %copy-start.4 = (bf16[512,1152]{1,0:T(8,128)(2,1)S(1)}, bf16[512,1152]{1,0:T(8,128)(2,1)}, u32[]{:S(2)}) copy-start(bf16[512,1152]{1,0:T(8,128)(2,1)} %patch_any.3) | copy-start | bytes 3538948
  5.0 10.6 %copy-start.5 = (bf16[3,3,3,128,128]{4,3,2,1,0:T(8,128)(2,1)S(1)}, bf16[3,3,3,128,128]{4,3,2,1,0:T(8,128)(2,1)}, u32[]{:S(2)}) copy-start(bf16[3,3,3,128,128]{4,3,2,1,0:T(8,128)(2,1)} %first_ref.1) | copy-start | bytes 2654212
  5.0 10.6 %copy-start.6 = (bf16[3,3,3,128,128]{4,3,2,1,0:T(8,128)(2,1)S(1)}, bf16[3,3,3,128,128]{4,3,2,1,0:T(8,128)(2,1)}, u32[]{:S(2)}) copy-start(bf16[3,3,3,128,128]{4,3,2,1,0:T(8,128)(2,1)} %second_ref.1) | copy-start | bytes 2654212
  5.0 10.6 %copy-start.7 = (bf16[8,2,32,128]{3,2,1,0:T(8,128)(2,1)S(1)}, bf16[8,2,32,128]{3,2,1,0:T(8,128)(2,1)}, u32[]{:S(2)}) copy-start(bf16[8,2,32,128]{3,2,1,0:T(8,128)(2,1)} %own_any.1) | copy-start | bytes 393220
  5.0 10.6 %copy-start.8 = (s32[3]{0:T(128)S(1)}, s32[3]{0:T(128)}, u32[]{:S(2)}) copy-start(s32[3]{0:T(128)} %counts_any.1) | copy-start | bytes 40
  10.7 19.5 %copy-start.2 = (f32[72]{0:T(128)S(1)}, f32[72]{0:T(128)}, u32[]{:S(2)}) copy-start(f32[72]{0:T(128)} %param.16) | copy-start | bytes 868
  10.7 10.1 %collective-permute-start.5 = (bf16[72,1152]{1,0:T(8,128)(2,1)S(1)}, bf16[72,1152]{1,0:T(8,128)(2,1)S(1)}, u32[]{:S(2)}, u32[]{:S(2)}) collective-permute-start(bf16[72,1152]{1,0:T(8,128)(2,1)S(1)} %collective-permute-done.2.refs_1_), channel_id=1, source_target_pairs={{0,4},{1,5},{4,8},{5,9},{8,12},{9,13},{12,14},{13,15},{14,10},{15,... | collective-permute-start | bytes 497672 | tf_op jit(solution)/shard_map/ppermute | solution.py:677
  15.6 6.0 %collective-permute-start.6 = (bf16[72,1152]{1,0:T(8,128)(2,1)S(1)}, bf16[72,1152]{1,0:T(8,128)(2,1)S(1)}, u32[]{:S(2)}, u32[]{:S(2)}) collective-permute-start(bf16[72,1152]{1,0:T(8,128)(2,1)S(1)} %collective-permute-done.3.refs_2_), channel_id=1, source_target_pairs={{4,0},{5,1},{8,4},{9,5},{12,8},{13,9},{14,12},{15,13},{10,14},{11,... | collective-permute-start | bytes 497672 | tf_op jit(solution)/shard_map/ppermute | solution.py:677
  19.5 1.3 %collective-permute-start.4 = (bf16[64,512]{1,0:T(8,128)(2,1)S(1)}, bf16[64,512]{1,0:T(8,128)(2,1)S(1)}, u32[]{:S(2)}, u32[]{:S(2)}) collective-permute-start(bf16[64,512]{1,0:T(8,128)(2,1)S(1)} %get-tuple-element.41), channel_id=1, source_target_pairs={{0,1},{1,0},{2,3},{3,2},{4,5},{5,4},{6,7},{7,6},{8,9},{9,8},{10,11... | collective-permute-start | bytes 196616 | tf_op jit(solution)/shard_map/ppermute | solution.py:677
  21.5 7.0 %collective-permute-start.7 = (bf16[72,1152]{1,0:T(8,128)(2,1)S(1)}, bf16[72,1152]{1,0:T(8,128)(2,1)S(1)}, u32[]{:S(2)}, u32[]{:S(2)}) collective-permute-start(bf16[72,1152]{1,0:T(8,128)(2,1)S(1)} %collective-permute-done.5.refs_3_), channel_id=1, source_target_pairs={{0,4},{1,5},{4,8},{5,9},{8,12},{9,13},{12,14},{13,15},{14,10},{15,... | collective-permute-start | bytes 497672 | tf_op jit(solution)/shard_map/ppermute | solution.py:677
  23.1 7.1 %collective-permute-start.8 = (bf16[72,1152]{1,0:T(8,128)(2,1)S(1)}, bf16[72,1152]{1,0:T(8,128)(2,1)S(1)}, u32[]{:S(2)}, u32[]{:S(2)}) collective-permute-start(bf16[72,1152]{1,0:T(8,128)(2,1)S(1)} %collective-permute-done.6.refs_4_), channel_id=1, source_target_pairs={{4,0},{5,1},{8,4},{9,5},{12,8},{13,9},{14,12},{15,13},{10,14},{11,... | collective-permute-start | bytes 497672 | tf_op jit(solution)/shard_map/ppermute | solution.py:677
  23.6 8.2 %collective-permute-start.11 = (bf16[128,512]{1,0:T(8,128)(2,1)S(1)}, bf16[128,512]{1,0:T(8,128)(2,1)S(1)}, u32[]{:S(2)}, u32[]{:S(2)}) collective-permute-start(bf16[128,512]{1,0:T(8,128)(2,1)S(1)} %constant_dynamic-update-slice_fusion.block_ref.refs_0_), channel_id=1, source_target_pairs={{0,4},{1,5},{4,8},{5,9},{8,12},{9,13},{12,14},{13,15},{14,10},{15,... | collective-permute-start | bytes 393224 | tf_op jit(solution)/shard_map/ppermute | solution.py:677
  25.2 6.6 %collective-permute-start.12 = (bf16[128,512]{1,0:T(8,128)(2,1)S(1)}, bf16[128,512]{1,0:T(8,128)(2,1)S(1)}, u32[]{:S(2)}, u32[]{:S(2)}) collective-permute-start(bf16[128,512]{1,0:T(8,128)(2,1)S(1)} %constant_dynamic-update-slice_fusion.block_ref.refs_0_), channel_id=1, source_target_pairs={{4,0},{5,1},{8,4},{9,5},{12,8},{13,9},{14,12},{15,13},{10,14},{11,... | collective-permute-start | bytes 393224 | tf_op jit(solution)/shard_map/ppermute | solution.py:677
  30.3 5.7 %copy-start.9 = (f32[72]{0:T(128)S(1)}, f32[72]{0:T(128)}, u32[]{:S(2)}) copy-start(f32[72]{0:T(128)} %param.17) | copy-start | bytes 868
  31.8 8.1 %collective-permute-start.13 = (bf16[128,512]{1,0:T(8,128)(2,1)S(1)}, bf16[128,512]{1,0:T(8,128)(2,1)S(1)}, u32[]{:S(2)}, u32[]{:S(2)}) collective-permute-start(bf16[128,512]{1,0:T(8,128)(2,1)S(1)} %collective-permute-done.11.refs_0_), channel_id=1, source_target_pairs={{0,4},{1,5},{4,8},{5,9},{8,12},{9,13},{12,14},{13,15},{14,10},{15,... | collective-permute-start | bytes 393224 | tf_op jit(solution)/shard_map/ppermute | solution.py:677
  33.4 6.5 %collective-permute-start.14 = (bf16[128,512]{1,0:T(8,128)(2,1)S(1)}, bf16[128,512]{1,0:T(8,128)(2,1)S(1)}, u32[]{:S(2)}, u32[]{:S(2)}) collective-permute-start(bf16[128,512]{1,0:T(8,128)(2,1)S(1)} %collective-permute-done.12.refs_1_), channel_id=1, source_target_pairs={{4,0},{5,1},{8,4},{9,5},{12,8},{13,9},{14,12},{15,13},{10,14},{11,... | collective-permute-start | bytes 393224 | tf_op jit(solution)/shard_map/ppermute | solution.py:677
  33.9 6.0 %collective-permute-start.9 = (bf16[72,640]{1,0:T(8,128)(2,1)S(1)}, bf16[72,640]{1,0:T(8,128)(2,1)S(1)}, u32[]{:S(2)}, u32[]{:S(2)}) collective-permute-start(bf16[72,640]{1,0:T(8,128)(2,1)S(1)} %slice.12), channel_id=1, source_target_pairs={{0,4},{1,5},{4,8},{5,9},{8,12},{9,13},{12,14},{13,15},{14,10},{15,... | collective-permute-start | bytes 276488 | tf_op jit(solution)/shard_map/ppermute | solution.py:677
  35.5 4.4 %collective-permute-start.10 = (bf16[72,512]{1,0:T(8,128)(2,1)S(1)}, bf16[72,512]{1,0:T(8,128)(2,1)S(1)}, u32[]{:S(2)}, u32[]{:S(2)}) collective-permute-start(bf16[72,512]{1,0:T(8,128)(2,1)S(1)} %slice.13), channel_id=1, source_target_pairs={{4,0},{5,1},{8,4},{9,5},{12,8},{13,9},{14,12},{15,13},{10,14},{11,... | collective-permute-start | bytes 221192 | tf_op jit(solution)/shard_map/ppermute | solution.py:677
  36.0 6.0 %copy-start = (bf16[72,1152]{1,0:T(8,128)(2,1)S(1)}, bf16[72,1152]{1,0:T(8,128)(2,1)}, u32[]{:S(2)}) copy-start(bf16[72,1152]{1,0:T(8,128)(2,1)} %refs_0_.1) | copy-start | bytes 497668
  39.9 5.0 %collective-permute-start.15 = (bf16[128,512]{1,0:T(8,128)(2,1)S(1)}, bf16[128,512]{1,0:T(8,128)(2,1)S(1)}, u32[]{:S(2)}, u32[]{:S(2)}) collective-permute-start(bf16[128,512]{1,0:T(8,128)(2,1)S(1)} %collective-permute-done.13.refs_0_), channel_id=1, source_target_pairs={{0,4},{1,5},{4,8},{5,9},{8,12},{9,13},{12,14},{13,15},{14,10},{15,... | collective-permute-start | bytes 393224 | tf_op jit(solution)/shard_map/ppermute | solution.py:677
  41.3 5.0 %collective-permute-start.16 = (bf16[128,512]{1,0:T(8,128)(2,1)S(1)}, bf16[128,512]{1,0:T(8,128)(2,1)S(1)}, u32[]{:S(2)}, u32[]{:S(2)}) collective-permute-start(bf16[128,512]{1,0:T(8,128)(2,1)S(1)} %collective-permute-done.14.refs_1_), channel_id=1, source_target_pairs={{4,0},{5,1},{8,4},{9,5},{12,8},{13,9},{14,12},{15,13},{10,14},{11,... | collective-permute-start | bytes 393224 | tf_op jit(solution)/shard_map/ppermute | solution.py:677
  46.3 7.0 %collective-permute-start.19 = (bf16[576,1152]{1,0:T(8,128)(2,1)S(1)}, bf16[576,1152]{1,0:T(8,128)(2,1)S(1)}, u32[]{:S(2)}, u32[]{:S(2)}) collective-permute-start(bf16[576,1152]{1,0:T(8,128)(2,1)S(1)} %bitcast.3), channel_id=1, source_target_pairs={{0,1},{1,0},{2,3},{3,2},{4,5},{5,4},{6,7},{7,6},{8,9},{9,8},{10,11... | collective-permute-start | bytes 3981320 | tf_op jit(solution)/shard_map/ppermute | solution.py:677
  46.3 4.5 %collective-permute-start.17 = (bf16[64,512]{1,0:T(8,128)(2,1)S(1)}, bf16[64,512]{1,0:T(8,128)(2,1)S(1)}, u32[]{:S(2)}, u32[]{:S(2)}) collective-permute-start(bf16[64,512]{1,0:T(8,128)(2,1)S(1)} %slice.14), channel_id=1, source_target_pairs={{0,4},{1,5},{4,8},{5,9},{8,12},{9,13},{12,14},{13,15},{14,10},{15,... | collective-permute-start | bytes 196616 | tf_op jit(solution)/shard_map/ppermute | solution.py:677
  47.0 4.3 %collective-permute-start.18 = (bf16[64,512]{1,0:T(8,128)(2,1)S(1)}, bf16[64,512]{1,0:T(8,128)(2,1)S(1)}, u32[]{:S(2)}, u32[]{:S(2)}) collective-permute-start(bf16[64,512]{1,0:T(8,128)(2,1)S(1)} %slice.15), channel_id=1, source_target_pairs={{4,0},{5,1},{8,4},{9,5},{12,8},{13,9},{14,12},{15,13},{10,14},{11,... | collective-permute-start | bytes 196616 | tf_op jit(solution)/shard_map/ppermute | solution.py:677
  54.3 1.4 %collective-permute-start.20 = (bf16[64,1152]{1,0:T(8,128)(2,1)S(1)}, bf16[64,1152]{1,0:T(8,128)(2,1)S(1)}, u32[]{:S(2)}, u32[]{:S(2)}) collective-permute-start(bf16[64,1152]{1,0:T(8,128)(2,1)S(1)} %get-tuple-element.70), channel_id=1, source_target_pairs={{0,1},{1,0},{2,3},{3,2},{4,5},{5,4},{6,7},{7,6},{8,9},{9,8},{10,11... | collective-permute-start | bytes 442376 | tf_op jit(solution)/shard_map/ppermute | solution.py:677

commit v10 on v8

--- a/solution.py
+++ b/solution.py
@@ -203,7 +203,7 @@
 
 
 def silu(v):
-    return v / (1.0 + jnp.exp(-v))
+    return 0.5 * v * (1.0 + jnp.tanh(0.5 * v))
 
 
 def long_window(lengths):
@@ -637,30 +637,14 @@
     return out.reshape(8 * rows, columns)
 
 
-def merge_kernel(lengths_ref, keep_ref, got_ref, out_ref):
+def merge(lengths, keep, got):
+    start, _ = long_window(lengths)
     position = lax.axis_index("seq")
-    keep = keep_ref[...].astype(F32)
-    got = got_ref[...].astype(F32)
-    start, _ = long_window(lengths_ref)
     q_cols = 16
-    slot = lax.broadcasted_iota(jnp.int32, keep.shape, 0)
+    slot = jnp.arange(keep.shape[0], dtype=jnp.int32)
     token = (slot // q_cols) * (lax.axis_size("seq") * q_cols) + position * q_cols + slot % q_cols
-    inside = jnp.where(token >= start, 1, 0)
-    mine = inside == jnp.where(position % 2 == 0, 1, 0)
-    half = keep.shape[0]
-    out_ref[:half] = jnp.where(mine, keep, got).astype(BF16)
-    out_ref[half:] = jnp.where(mine, got, keep).astype(BF16)
-
-
-def merge(lengths, keep, got):
-    return pl.pallas_call(
-        merge_kernel,
-        out_shape=jax.ShapeDtypeStruct((128, D), BF16),
-        in_specs=[SMEM, VMEM, VMEM],
-        out_specs=VMEM,
-        compiler_params=params(),
-        name="merge",
-    )(lengths, keep, got)
+    mine = ((token >= start) == (position % 2 == 0))[:, None]
+    return jnp.concatenate([jnp.where(mine, keep, got), jnp.where(mine, got, keep)], axis=0)
 
 
 def shards(

time: 52.2 us -> 53.9 us (1.033)
  between operations: 0.22 us -> 3.22 us
  Pallas kernels: 21.6 us -> 20.2 us
  waiting for transfers between devices: 7.8 us -> 6.44 us
  other arithmetic: 0 us -> 0.85 us
  local copies, waits for them, and re-layouts: 1.35 us -> 1.93 us
    ppermute x21, waiting for transfers between devices: 7.8 us -> 6.44 us  [send(): return lax.ppermute(array, 'seq', pairs)]
    pallas_call x1 -> x0, Pallas kernels: 1.35 us -> none  [merge(): pl.pallas_call(merge_kernel, out_shape=jax.ShapeDtypeStruct((128, D), BF1...]
    concatenate x0 -> x1, other arithmetic: none -> 0.74 us  [merge(): jnp.concatenate([jnp.where(mine, keep, got), jnp.where(mine, got, keep)],...]
    slice x0 -> x1, local copies, waits for them, and re-layouts: none -> 0.58 us  [long_window(): first, second = (lengths[0, 0], lengths[0, 1])]
  transfers between devices with their start and end apart: 21 -> 21, of which waited for: 9 -> 8; matrix products, arithmetic and copies ran while one was open for 0% -> 1% of each run, Pallas kernels for 37% -> 36%
where the time goes in v10:
time: 53.9 us; the launch traced here: 53.7 us
  starting transfers between devices  21.1 us (39%)
  Pallas kernels  20.2 us (37%)
  waiting for transfers between devices  6.44 us (12%)
  between operations  3.22 us (6%)
  local copies, waits for them, and re-layouts  1.93 us (4%)
  other arithmetic  0.85 us (2%)
    ppermute x21, starting transfers between devices, send(): return lax.ppermute(array, 'seq', pairs)  21.1 us
    pallas_call x4, Pallas kernels, step_attention(): pl.pallas_call(functools.partial(step_kernel, offsets), out_shape=ACC, in...  8.11 us
    ppermute x21, waiting for transfers between devices, send(): return lax.ppermute(array, 'seq', pairs)  6.44 us
    pallas_call x1, Pallas kernels, fold(): pl.pallas_call(fold_kernel, out_shape=(jax.ShapeDtypeStruct((2 * D, inner...  5.67 us
    pallas_call x1, Pallas kernels, convolve(): pl.pallas_call(conv_kernel, out_shape=(out, out), in_specs=[ANY] * 4 + [V...  3.78 us
    pallas_call x1, Pallas kernels, make_queries(): pl.pallas_call(query_kernel, out_shape=jax.ShapeDtypeStruct((HEADS, 128,...  1.53 us
    unnamed x21, local copies, waits for them, and re-layouts  1.32 us
  transfers between devices with their start and end apart: 21, of which 8 were waited for; matrix products, arithmetic and copies ran while one was open for 1% of the time, Pallas kernels for 36%

profile of v10, /device:TPU:0, one launch (start us, length us, event | category | flops | bytes accessed | tf_op | source)
XLA Modules:
  0.0 53.7 jit_solution(2898080810560281464)
XLA Ops:
  0.0 0.5 collective-permute-start
  0.5 0.7 %collective-permute-start.1 = (bf16[8,2,32,128]{3,2,1,0:T(8,128)(2,1)}, bf16[8,2,32,128]{3,2,1,0:T(8,128)(2,1)S(1)}, u32[]{:S(2)}, u32[]{:S(2)}) collective-permute-start(bf16[8,2,32,128]{3,2,1,0:T(8,128)(2,1)} %own_any.1), channel_id=1, source_target_pairs={{1,2},{2,1},{3,4},{4,3},{5,6},{6,5},{7,8},{8,7},{9,10},{10,9},{11,... | collective-permute-start | bytes 393224 | tf_op jit(solution)/shard_map/ppermute | solution.py:661
  1.1 5.4 %collective-permute-start.2 = (bf16[72,1152]{1,0:T(8,128)(2,1)}, bf16[72,1152]{1,0:T(8,128)(2,1)S(1)}, u32[]{:S(2)}, u32[]{:S(2)}) collective-permute-start(bf16[72,1152]{1,0:T(8,128)(2,1)} %refs_0_.1), channel_id=1, source_target_pairs={{0,4},{1,5},{4,8},{5,9},{8,12},{9,13},{12,14},{13,15},{14,10},{15,... | collective-permute-start | bytes 497672 | tf_op jit(solution)/shard_map/ppermute | solution.py:661
  6.5 0.0 collective-permute-start.3
  6.5 1.3 %copy-done.3 = bf16[512,1152]{1,0:T(8,128)(2,1)S(1)} copy-done((bf16[512,1152]{1,0:T(8,128)(2,1)S(1)}, bf16[512,1152]{1,0:T(8,128)(2,1)}, u32[]{:S(2)}) %copy-start.3) | copy-done | bytes 1179672
  7.8 5.7 %fold.1 = (bf16[2304,512]{1,0:T(8,128)(2,1)S(1)}, bf16[1152,1152]{1,0:T(8,128)(2,1)S(1)}, bf16[512,1152]{1,0:T(8,128)(2,1)S(1)}) custom-call(bf16[512,1152]{1,0:T(8,128)(2,1)S(1)} %copy-done.3, bf16[1152,3456]{1,0:T(8,128)(2,1)} %qkv_any.1), custom_call_target="tpu_custom_call" | custom-call | flops 2717908992 | bytes 12582912 | tf_op jit(solution)/shard_map/fold/pallas_call | solution.py:252
  13.5 0.0 collective-permute-done.1.other_ref
  13.5 0.0 copy-start.2
  13.5 2.1 %collective-permute-start.5 = (bf16[72,1152]{1,0:T(8,128)(2,1)S(1)}, bf16[72,1152]{1,0:T(8,128)(2,1)S(1)}, u32[]{:S(2)}, u32[]{:S(2)}) collective-permute-start(bf16[72,1152]{1,0:T(8,128)(2,1)S(1)} %collective-permute-done.2.refs_1_), channel_id=1, source_target_pairs={{0,4},{1,5},{4,8},{5,9},{8,12},{9,13},{12,14},{13,15},{14,10},{15,... | collective-permute-start | bytes 497672 | tf_op jit(solution)/shard_map/ppermute | solution.py:661
  15.6 0.0 collective-permute-start.6
  15.7 3.8 %convolve.1 = (bf16[64,512]{1,0:T(8,128)(2,1)S(1)}, bf16[64,512]{1,0:T(8,128)(2,1)S(1)}) custom-call(s32[3]{0:T(128)S(1)} %copy-done.8, s32[1,3]{1,0:T(1,128)S(1)} %copy-done.1, bf16[8,2,32,128]{3,2,1,0:T(8,128)(2,1)S(1)} %copy-done.7, bf16[512,1152]{1,0:T(8,128)(2,1)S(1)} %copy-done.4, bf16[8,2,32,128]{3,2,1,0:T(8,128)(2,1)S(1)} %collective-permute-done.sibling_ref, ...), custom_call_target="tpu_custom_call" | custom-call | flops 2147483648 | bytes 4194304 | tf_op jit(solution)/shard_map/convolve/pallas_call | solution.py:404
  19.4 0.1 collective-permute-start.4
  19.5 1.2 %collective-permute-done.4 = bf16[64,512]{1,0:T(8,128)(2,1)S(1)} collective-permute-done((bf16[64,512]{1,0:T(8,128)(2,1)S(1)}, bf16[64,512]{1,0:T(8,128)(2,1)S(1)}, u32[]{:S(2)}, u32[]{:S(2)}) %collective-permute-start.4) | collective-permute-done | bytes 65568 | tf_op jit(solution)/shard_map/ppermute | solution.py:661
  20.8 0.0 collective-permute-done.5.refs_3_
  20.8 0.4 collective-permute-done.6.refs_4_
  21.2 0.7 %collective-permute-start.8 = (bf16[128,512]{1,0:T(8,128)(2,1)S(1)}, bf16[128,512]{1,0:T(8,128)(2,1)S(1)}, u32[]{:S(2)}, u32[]{:S(2)}) collective-permute-start(bf16[128,512]{1,0:T(8,128)(2,1)S(1)} %constant_dynamic-update-slice_fusion.block_ref.refs_0_), channel_id=1, source_target_pairs={{4,0},{5,1},{8,4},{9,5},{12,8},{13,9},{14,12},{15,13},{10,14},{11,... | collective-permute-start | bytes 393224 | tf_op jit(solution)/shard_map/ppermute | solution.py:661
  21.8 1.4 %collective-permute-start.7 = (bf16[128,512]{1,0:T(8,128)(2,1)S(1)}, bf16[128,512]{1,0:T(8,128)(2,1)S(1)}, u32[]{:S(2)}, u32[]{:S(2)}) collective-permute-start(bf16[128,512]{1,0:T(8,128)(2,1)S(1)} %constant_dynamic-update-slice_fusion.block_ref.refs_0_), channel_id=1, source_target_pairs={{0,4},{1,5},{4,8},{5,9},{8,12},{9,13},{12,14},{13,15},{14,10},{15,... | collective-permute-start | bytes 393224 | tf_op jit(solution)/shard_map/ppermute | solution.py:661
  23.2 1.7 %collective-permute-start.11 = (bf16[72,1152]{1,0:T(8,128)(2,1)S(1)}, bf16[72,1152]{1,0:T(8,128)(2,1)S(1)}, u32[]{:S(2)}, u32[]{:S(2)}) collective-permute-start(bf16[72,1152]{1,0:T(8,128)(2,1)S(1)} %collective-permute-done.5.refs_3_), channel_id=1, source_target_pairs={{0,4},{1,5},{4,8},{5,9},{8,12},{9,13},{12,14},{13,15},{14,10},{15,... | collective-permute-start | bytes 497672 | tf_op jit(solution)/shard_map/ppermute | solution.py:661
  24.9 0.4 collective-permute-start.12
  25.2 1.5 %queries.1.refs_4_.refs_5_ = bf16[16,128,80]{2,1,0:T(8,128)(2,1)S(1)} custom-call(s32[1,3]{1,0:T(1,128)S(1)} %copy-done.1, bf16[128,512]{1,0:T(8,128)(2,1)S(1)} %constant_dynamic-update-slice_fusion.block_ref.refs_0_, bf16[512,1152]{1,0:T(8,128)(2,1)S(1)} %get-tuple-element.45.centered_ref, bf16[1152,1152]{1,0:T(8,128)(2,1)S(1)} %get-tuple-element.46.query_ref, ...), custom_call_target="tpu_custom_call" | custom-call | flops 1073741824 | bytes 4194304 | tf_op jit(solution)/shard_map/queries/pallas_call | solution.py:533
  26.8 0.0 collective-permute-done.8.refs_1_
  26.8 1.5 %collective-permute-done.7.refs_0_ = bf16[128,512]{1,0:T(8,128)(2,1)S(1)} collective-permute-done((bf16[128,512]{1,0:T(8,128)(2,1)S(1)}, bf16[128,512]{1,0:T(8,128)(2,1)S(1)}, u32[]{:S(2)}, u32[]{:S(2)}) %collective-permute-start.7) | collective-permute-done | bytes 131104 | tf_op jit(solution)/shard_map/ppermute | solution.py:661
  28.2 1.4 %collective-permute-start.9 = (bf16[128,512]{1,0:T(8,128)(2,1)S(1)}, bf16[128,512]{1,0:T(8,128)(2,1)S(1)}, u32[]{:S(2)}, u32[]{:S(2)}) collective-permute-start(bf16[128,512]{1,0:T(8,128)(2,1)S(1)} %collective-permute-done.7.refs_0_), channel_id=1, source_target_pairs={{0,4},{1,5},{4,8},{5,9},{8,12},{9,13},{12,14},{13,15},{14,10},{15,... | collective-permute-start | bytes 393224 | tf_op jit(solution)/shard_map/ppermute | solution.py:661
  29.6 0.7 %collective-permute-start.10 = (bf16[128,512]{1,0:T(8,128)(2,1)S(1)}, bf16[128,512]{1,0:T(8,128)(2,1)S(1)}, u32[]{:S(2)}, u32[]{:S(2)}) collective-permute-start(bf16[128,512]{1,0:T(8,128)(2,1)S(1)} %collective-permute-done.8.refs_1_), channel_id=1, source_target_pairs={{4,0},{5,1},{8,4},{9,5},{12,8},{13,9},{14,12},{15,13},{10,14},{11,... | collective-permute-start | bytes 393224 | tf_op jit(solution)/shard_map/ppermute | solution.py:661
  30.3 2.0 %step_attention.4.refs_0_ = f32[16,80,128]{2,1,0:T(8,128)S(1)} custom-call(s32[1,3]{1,0:T(1,128)S(1)} %copy-done.1, bf16[128,512]{1,0:T(8,128)(2,1)S(1)} %collective-permute-done.7.refs_0_, bf16[128,512]{1,0:T(8,128)(2,1)S(1)} %collective-permute-done.8.refs_1_, bf16[2304,512]{1,0:T(8,128)(2,1)S(1)} %get-tuple-element.51.refs_2_.refs_3_, ...), custom_call_target="tpu_custom_call" | custom-call | flops 1744830464 | bytes 5242880 | tf_op jit(solution)/shard_map/step_attention/pallas_call | solution.py:561
  32.3 1.7 %collective-permute-start.16 = (bf16[72,512]{1,0:T(8,128)(2,1)S(1)}, bf16[72,512]{1,0:T(8,128)(2,1)S(1)}, u32[]{:S(2)}, u32[]{:S(2)}) collective-permute-start(bf16[72,512]{1,0:T(8,128)(2,1)S(1)} %slice.21), channel_id=1, source_target_pairs={{4,0},{5,1},{8,4},{9,5},{12,8},{13,9},{14,12},{15,13},{10,14},{11,... | collective-permute-start | bytes 221192 | tf_op jit(solution)/shard_map/ppermute | solution.py:661
  34.0 0.0 copy-start
  34.0 0.5 collective-permute-start.15
  34.5 0.1 collective-permute-done.10.refs_1_
  34.6 1.7 %collective-permute-start.13 = (bf16[128,512]{1,0:T(8,128)(2,1)S(1)}, bf16[128,512]{1,0:T(8,128)(2,1)S(1)}, u32[]{:S(2)}, u32[]{:S(2)}) collective-permute-start(bf16[128,512]{1,0:T(8,128)(2,1)S(1)} %collective-permute-done.9.refs_0_), channel_id=1, source_target_pairs={{0,4},{1,5},{4,8},{5,9},{8,12},{9,13},{12,14},{13,15},{14,10},{15,... | collective-permute-start | bytes 393224 | tf_op jit(solution)/shard_map/ppermute | solution.py:661
  36.2 0.4 collective-permute-start.14
  36.6 2.0 %step_attention.5.refs_1_ = f32[16,80,128]{2,1,0:T(8,128)S(1)} custom-call(s32[1,3]{1,0:T(1,128)S(1)} %copy-done.1, bf16[128,512]{1,0:T(8,128)(2,1)S(1)} %collective-permute-done.9.refs_0_, bf16[128,512]{1,0:T(8,128)(2,1)S(1)} %collective-permute-done.10.refs_1_, bf16[2304,512]{1,0:T(8,128)(2,1)S(1)} %get-tuple-element.51.refs_2_.refs_3_, ...), custom_call_target="tpu_custom_call" | custom-call | flops 1744830464 | bytes 5242880 | tf_op jit(solution)/shard_map/step_attention/pallas_call | solution.py:561
  38.6 0.0 collective-permute-done.15.refs_7_
  38.6 1.4 %collective-permute-done.13.refs_0_ = bf16[128,512]{1,0:T(8,128)(2,1)S(1)} collective-permute-done((bf16[128,512]{1,0:T(8,128)(2,1)S(1)}, bf16[128,512]{1,0:T(8,128)(2,1)S(1)}, u32[]{:S(2)}, u32[]{:S(2)}) %collective-permute-start.13) | collective-permute-done | bytes 131104 | tf_op jit(solution)/shard_map/ppermute | solution.py:661
  40.0 1.2 %collective-permute-done.14.refs_1_ = bf16[128,512]{1,0:T(8,128)(2,1)S(1)} collective-permute-done((bf16[128,512]{1,0:T(8,128)(2,1)S(1)}, bf16[128,512]{1,0:T(8,128)(2,1)S(1)}, u32[]{:S(2)}, u32[]{:S(2)}) %collective-permute-start.14) | collective-permute-done | bytes 131104 | tf_op jit(solution)/shard_map/ppermute | solution.py:661
  41.2 0.1 pack.1
  41.3 0.1 collective-permute-start.19
  41.4 0.5 collective-permute-start.18
  41.9 1.6 %collective-permute-start.17 = (bf16[64,512]{1,0:T(8,128)(2,1)S(1)}, bf16[64,512]{1,0:T(8,128)(2,1)S(1)}, u32[]{:S(2)}, u32[]{:S(2)}) collective-permute-start(bf16[64,512]{1,0:T(8,128)(2,1)S(1)} %slice.22), channel_id=1, source_target_pairs={{0,4},{1,5},{4,8},{5,9},{8,12},{9,13},{12,14},{13,15},{14,10},{15,... | collective-permute-start | bytes 196616 | tf_op jit(solution)/shard_map/ppermute | solution.py:661
  43.5 2.0 %step_attention.6.refs_2_ = f32[16,80,128]{2,1,0:T(8,128)S(1)} custom-call(s32[1,3]{1,0:T(1,128)S(1)} %copy-done.1, bf16[128,512]{1,0:T(8,128)(2,1)S(1)} %collective-permute-done.13.refs_0_, bf16[128,512]{1,0:T(8,128)(2,1)S(1)} %collective-permute-done.14.refs_1_, bf16[2304,512]{1,0:T(8,128)(2,1)S(1)} %get-tuple-element.51.refs_2_.refs_3_, ...), custom_call_target="tpu_custom_call" | custom-call | flops 1744830464 | bytes 5242880 | tf_op jit(solution)/shard_map/step_attention/pallas_call | solution.py:561
  45.5 0.4 collective-permute-done.18.refs_2_
  45.9 0.2 collective-permute-done.17.refs_1_
  46.2 2.0 %step_attention.7.refs_3_ = f32[16,80,128]{2,1,0:T(8,128)S(1)} custom-call(s32[1,3]{1,0:T(1,128)S(1)} %copy-done.1, bf16[128,512]{1,0:T(8,128)(2,1)S(1)} %constant_dynamic-update-slice_fusion.block_ref.refs_0_, bf16[64,512]{1,0:T(8,128)(2,1)S(1)} %collective-permute-done.17.refs_1_, bf16[64,512]{1,0:T(8,128)(2,1)S(1)} %collective-permute-done.18.refs_2_, ...), custom_call_target="tpu_custom_call" | custom-call | flops 1744830464 | bytes 5242880 | tf_op jit(solution)/shard_map/step_attention/pallas_call | solution.py:561
  48.2 1.0 %project_out.1 = (bf16[64,1152]{1,0:T(8,128)(2,1)S(1)}, bf16[64,1152]{1,0:T(8,128)(2,1)S(1)}) custom-call(f32[16,80,128]{2,1,0:T(8,128)S(1)} %step_attention.4.refs_0_, f32[16,80,128]{2,1,0:T(8,128)S(1)} %step_attention.5.refs_1_, f32[16,80,128]{2,1,0:T(8,128)S(1)} %step_attention.6.refs_2_, f32[16,80,128]{2,1,0:T(8,128)S(1)} %step_attention.7.refs_3_, ...), custom_call_target="tpu_custom_call" | custom-call | flops 377487360 | bytes 4194304 | tf_op jit(solution)/shard_map/project_out/pallas_call | solution.py:606
  49.2 0.1 collective-permute-start.20
  49.3 0.6 %fusion.3 = (s32[1,1]{1,0:T(1,128)}, s32[1,1]{1,0:T(1,128)}) fusion(s32[1,3]{1,0:T(1,128)S(1)} %copy-done.1), kind=kLoop, calls=%fused_computation.14 | loop fusion | bytes 16 | tf_op jit(solution)/shard_map/slice | solution.py:210
  52.9 0.1 broadcast_select_fusion.1
  53.0 0.7 %pad_maximum_fusion = bf16[128,1152]{1,0:T(8,128)(2,1)} fusion(bf16[64,1152]{1,0:T(8,128)(2,1)S(1)} %get-tuple-element.70, bf16[64,1152]{1,0:T(8,128)(2,1)S(1)} %get-tuple-element.69), kind=kLoop, calls=%fused_computation | loop fusion | flops 589824 | bytes 589824 | tf_op jit(solution)/shard_map/concatenate | solution.py:647
  (33 shorter events, 0.1 us)
Async XLA Ops:
  0.0 15.6 %copy-start.1 = (s32[1,3]{1,0:T(1,128)S(1)}, s32[1,3]{1,0:T(1,128)}, u32[]{:S(2)}) copy-start(s32[1,3]{1,0:T(1,128)} %lengths_ref.9) | copy-start | bytes 40
  0.0 13.5 %collective-permute-start = (bf16[8,2,32,128]{3,2,1,0:T(8,128)(2,1)}, bf16[8,2,32,128]{3,2,1,0:T(8,128)(2,1)S(1)}, u32[]{:S(2)}, u32[]{:S(2)}) collective-permute-start(bf16[8,2,32,128]{3,2,1,0:T(8,128)(2,1)} %own_any.1), channel_id=1, source_target_pairs={{0,1},{1,0},{2,3},{3,2},{4,5},{5,4},{6,7},{7,6},{8,9},{9,8},{10,11... | collective-permute-start | bytes 393224 | tf_op jit(solution)/shard_map/ppermute | solution.py:661
  0.5 13.0 %collective-permute-start.1 = (bf16[8,2,32,128]{3,2,1,0:T(8,128)(2,1)}, bf16[8,2,32,128]{3,2,1,0:T(8,128)(2,1)S(1)}, u32[]{:S(2)}, u32[]{:S(2)}) collective-permute-start(bf16[8,2,32,128]{3,2,1,0:T(8,128)(2,1)} %own_any.1), channel_id=1, source_target_pairs={{1,2},{2,1},{3,4},{4,3},{5,6},{6,5},{7,8},{8,7},{9,10},{10,9},{11,... | collective-permute-start | bytes 393224 | tf_op jit(solution)/shard_map/ppermute | solution.py:661
  1.1 12.4 %collective-permute-start.2 = (bf16[72,1152]{1,0:T(8,128)(2,1)}, bf16[72,1152]{1,0:T(8,128)(2,1)S(1)}, u32[]{:S(2)}, u32[]{:S(2)}) collective-permute-start(bf16[72,1152]{1,0:T(8,128)(2,1)} %refs_0_.1), channel_id=1, source_target_pairs={{0,4},{1,5},{4,8},{5,9},{8,12},{9,13},{12,14},{13,15},{14,10},{15,... | collective-permute-start | bytes 497672 | tf_op jit(solution)/shard_map/ppermute | solution.py:661
  6.5 7.0 %collective-permute-start.3 = (bf16[72,1152]{1,0:T(8,128)(2,1)}, bf16[72,1152]{1,0:T(8,128)(2,1)S(1)}, u32[]{:S(2)}, u32[]{:S(2)}) collective-permute-start(bf16[72,1152]{1,0:T(8,128)(2,1)} %refs_0_.1), channel_id=1, source_target_pairs={{4,0},{5,1},{8,4},{9,5},{12,8},{13,9},{14,12},{15,13},{10,14},{11,... | collective-permute-start | bytes 497672 | tf_op jit(solution)/shard_map/ppermute | solution.py:661
  6.5 1.3 %copy-start.3 = (bf16[512,1152]{1,0:T(8,128)(2,1)S(1)}, bf16[512,1152]{1,0:T(8,128)(2,1)}, u32[]{:S(2)}) copy-start(bf16[512,1152]{1,0:T(8,128)(2,1)} %patch_any.3) | copy-start | bytes 3538948
  7.8 7.8 %copy-start.4 = (bf16[512,1152]{1,0:T(8,128)(2,1)S(1)}, bf16[512,1152]{1,0:T(8,128)(2,1)}, u32[]{:S(2)}) copy-start(bf16[512,1152]{1,0:T(8,128)(2,1)} %patch_any.3) | copy-start | bytes 3538948
  7.8 7.8 %copy-start.5 = (bf16[3,3,3,128,128]{4,3,2,1,0:T(8,128)(2,1)S(1)}, bf16[3,3,3,128,128]{4,3,2,1,0:T(8,128)(2,1)}, u32[]{:S(2)}) copy-start(bf16[3,3,3,128,128]{4,3,2,1,0:T(8,128)(2,1)} %first_ref.1) | copy-start | bytes 2654212
  7.8 7.8 %copy-start.6 = (bf16[3,3,3,128,128]{4,3,2,1,0:T(8,128)(2,1)S(1)}, bf16[3,3,3,128,128]{4,3,2,1,0:T(8,128)(2,1)}, u32[]{:S(2)}) copy-start(bf16[3,3,3,128,128]{4,3,2,1,0:T(8,128)(2,1)} %second_ref.1) | copy-start | bytes 2654212
  7.8 7.8 %copy-start.7 = (bf16[8,2,32,128]{3,2,1,0:T(8,128)(2,1)S(1)}, bf16[8,2,32,128]{3,2,1,0:T(8,128)(2,1)}, u32[]{:S(2)}) copy-start(bf16[8,2,32,128]{3,2,1,0:T(8,128)(2,1)} %own_any.1) | copy-start | bytes 393220
  7.8 7.9 %copy-start.8 = (s32[3]{0:T(128)S(1)}, s32[3]{0:T(128)}, u32[]{:S(2)}) copy-start(s32[3]{0:T(128)} %counts_any.1) | copy-start | bytes 40
  13.5 11.7 %copy-start.2 = (f32[72]{0:T(128)S(1)}, f32[72]{0:T(128)}, u32[]{:S(2)}) copy-start(f32[72]{0:T(128)} %param.16) | copy-start | bytes 868
  13.5 7.2 %collective-permute-start.5 = (bf16[72,1152]{1,0:T(8,128)(2,1)S(1)}, bf16[72,1152]{1,0:T(8,128)(2,1)S(1)}, u32[]{:S(2)}, u32[]{:S(2)}) collective-permute-start(bf16[72,1152]{1,0:T(8,128)(2,1)S(1)} %collective-permute-done.2.refs_1_), channel_id=1, source_target_pairs={{0,4},{1,5},{4,8},{5,9},{8,12},{9,13},{12,14},{13,15},{14,10},{15,... | collective-permute-start | bytes 497672 | tf_op jit(solution)/shard_map/ppermute | solution.py:661
  15.6 5.6 %collective-permute-start.6 = (bf16[72,1152]{1,0:T(8,128)(2,1)S(1)}, bf16[72,1152]{1,0:T(8,128)(2,1)S(1)}, u32[]{:S(2)}, u32[]{:S(2)}) collective-permute-start(bf16[72,1152]{1,0:T(8,128)(2,1)S(1)} %collective-permute-done.3.refs_2_), channel_id=1, source_target_pairs={{4,0},{5,1},{8,4},{9,5},{12,8},{13,9},{14,12},{15,13},{10,14},{11,... | collective-permute-start | bytes 497672 | tf_op jit(solution)/shard_map/ppermute | solution.py:661
  19.4 1.3 %collective-permute-start.4 = (bf16[64,512]{1,0:T(8,128)(2,1)S(1)}, bf16[64,512]{1,0:T(8,128)(2,1)S(1)}, u32[]{:S(2)}, u32[]{:S(2)}) collective-permute-start(bf16[64,512]{1,0:T(8,128)(2,1)S(1)} %get-tuple-element.41), channel_id=1, source_target_pairs={{0,1},{1,0},{2,3},{3,2},{4,5},{5,4},{6,7},{7,6},{8,9},{9,8},{10,11... | collective-permute-start | bytes 196616 | tf_op jit(solution)/shard_map/ppermute | solution.py:661
  21.2 5.6 %collective-permute-start.8 = (bf16[128,512]{1,0:T(8,128)(2,1)S(1)}, bf16[128,512]{1,0:T(8,128)(2,1)S(1)}, u32[]{:S(2)}, u32[]{:S(2)}) collective-permute-start(bf16[128,512]{1,0:T(8,128)(2,1)S(1)} %constant_dynamic-update-slice_fusion.block_ref.refs_0_), channel_id=1, source_target_pairs={{4,0},{5,1},{8,4},{9,5},{12,8},{13,9},{14,12},{15,13},{10,14},{11,... | collective-permute-start | bytes 393224 | tf_op jit(solution)/shard_map/ppermute | solution.py:661
  21.8 6.4 %collective-permute-start.7 = (bf16[128,512]{1,0:T(8,128)(2,1)S(1)}, bf16[128,512]{1,0:T(8,128)(2,1)S(1)}, u32[]{:S(2)}, u32[]{:S(2)}) collective-permute-start(bf16[128,512]{1,0:T(8,128)(2,1)S(1)} %constant_dynamic-update-slice_fusion.block_ref.refs_0_), channel_id=1, source_target_pairs={{0,4},{1,5},{4,8},{5,9},{8,12},{9,13},{12,14},{13,15},{14,10},{15,... | collective-permute-start | bytes 393224 | tf_op jit(solution)/shard_map/ppermute | solution.py:661
  23.2 9.1 %collective-permute-start.11 = (bf16[72,1152]{1,0:T(8,128)(2,1)S(1)}, bf16[72,1152]{1,0:T(8,128)(2,1)S(1)}, u32[]{:S(2)}, u32[]{:S(2)}) collective-permute-start(bf16[72,1152]{1,0:T(8,128)(2,1)S(1)} %collective-permute-done.5.refs_3_), channel_id=1, source_target_pairs={{0,4},{1,5},{4,8},{5,9},{8,12},{9,13},{12,14},{13,15},{14,10},{15,... | collective-permute-start | bytes 497672 | tf_op jit(solution)/shard_map/ppermute | solution.py:661
  24.9 7.4 %collective-permute-start.12 = (bf16[72,1152]{1,0:T(8,128)(2,1)S(1)}, bf16[72,1152]{1,0:T(8,128)(2,1)S(1)}, u32[]{:S(2)}, u32[]{:S(2)}) collective-permute-start(bf16[72,1152]{1,0:T(8,128)(2,1)S(1)} %collective-permute-done.6.refs_4_), channel_id=1, source_target_pairs={{4,0},{5,1},{8,4},{9,5},{12,8},{13,9},{14,12},{15,13},{10,14},{11,... | collective-permute-start | bytes 497672 | tf_op jit(solution)/shard_map/ppermute | solution.py:661
  25.2 5.0 %copy-start.9 = (f32[72]{0:T(128)S(1)}, f32[72]{0:T(128)}, u32[]{:S(2)}) copy-start(f32[72]{0:T(128)} %param.17) | copy-start | bytes 868
  28.2 6.3 %collective-permute-start.9 = (bf16[128,512]{1,0:T(8,128)(2,1)S(1)}, bf16[128,512]{1,0:T(8,128)(2,1)S(1)}, u32[]{:S(2)}, u32[]{:S(2)}) collective-permute-start(bf16[128,512]{1,0:T(8,128)(2,1)S(1)} %collective-permute-done.7.refs_0_), channel_id=1, source_target_pairs={{0,4},{1,5},{4,8},{5,9},{8,12},{9,13},{12,14},{13,15},{14,10},{15,... | collective-permute-start | bytes 393224 | tf_op jit(solution)/shard_map/ppermute | solution.py:661
  29.6 5.0 %collective-permute-start.10 = (bf16[128,512]{1,0:T(8,128)(2,1)S(1)}, bf16[128,512]{1,0:T(8,128)(2,1)S(1)}, u32[]{:S(2)}, u32[]{:S(2)}) collective-permute-start(bf16[128,512]{1,0:T(8,128)(2,1)S(1)} %collective-permute-done.8.refs_1_), channel_id=1, source_target_pairs={{4,0},{5,1},{8,4},{9,5},{12,8},{13,9},{14,12},{15,13},{10,14},{11,... | collective-permute-start | bytes 393224 | tf_op jit(solution)/shard_map/ppermute | solution.py:661
  32.3 6.3 %collective-permute-start.16 = (bf16[72,512]{1,0:T(8,128)(2,1)S(1)}, bf16[72,512]{1,0:T(8,128)(2,1)S(1)}, u32[]{:S(2)}, u32[]{:S(2)}) collective-permute-start(bf16[72,512]{1,0:T(8,128)(2,1)S(1)} %slice.21), channel_id=1, source_target_pairs={{4,0},{5,1},{8,4},{9,5},{12,8},{13,9},{14,12},{15,13},{10,14},{11,... | collective-permute-start | bytes 221192 | tf_op jit(solution)/shard_map/ppermute | solution.py:661
  34.0 7.2 %copy-start = (bf16[72,1152]{1,0:T(8,128)(2,1)S(1)}, bf16[72,1152]{1,0:T(8,128)(2,1)}, u32[]{:S(2)}) copy-start(bf16[72,1152]{1,0:T(8,128)(2,1)} %refs_0_.1) | copy-start | bytes 497668
  34.0 4.6 %collective-permute-start.15 = (bf16[72,640]{1,0:T(8,128)(2,1)S(1)}, bf16[72,640]{1,0:T(8,128)(2,1)S(1)}, u32[]{:S(2)}, u32[]{:S(2)}) collective-permute-start(bf16[72,640]{1,0:T(8,128)(2,1)S(1)} %slice.20), channel_id=1, source_target_pairs={{0,4},{1,5},{4,8},{5,9},{8,12},{9,13},{12,14},{13,15},{14,10},{15,... | collective-permute-start | bytes 276488 | tf_op jit(solution)/shard_map/ppermute | solution.py:661
  34.6 5.5 %collective-permute-start.13 = (bf16[128,512]{1,0:T(8,128)(2,1)S(1)}, bf16[128,512]{1,0:T(8,128)(2,1)S(1)}, u32[]{:S(2)}, u32[]{:S(2)}) collective-permute-start(bf16[128,512]{1,0:T(8,128)(2,1)S(1)} %collective-permute-done.9.refs_0_), channel_id=1, source_target_pairs={{0,4},{1,5},{4,8},{5,9},{8,12},{9,13},{12,14},{13,15},{14,10},{15,... | collective-permute-start | bytes 393224 | tf_op jit(solution)/shard_map/ppermute | solution.py:661
  36.2 5.0 %collective-permute-start.14 = (bf16[128,512]{1,0:T(8,128)(2,1)S(1)}, bf16[128,512]{1,0:T(8,128)(2,1)S(1)}, u32[]{:S(2)}, u32[]{:S(2)}) collective-permute-start(bf16[128,512]{1,0:T(8,128)(2,1)S(1)} %collective-permute-done.10.refs_1_), channel_id=1, source_target_pairs={{4,0},{5,1},{8,4},{9,5},{12,8},{13,9},{14,12},{15,13},{10,14},{11,... | collective-permute-start | bytes 393224 | tf_op jit(solution)/shard_map/ppermute | solution.py:661
  41.3 6.9 %collective-permute-start.19 = (bf16[576,1152]{1,0:T(8,128)(2,1)S(1)}, bf16[576,1152]{1,0:T(8,128)(2,1)S(1)}, u32[]{:S(2)}, u32[]{:S(2)}) collective-permute-start(bf16[576,1152]{1,0:T(8,128)(2,1)S(1)} %bitcast.5), channel_id=1, source_target_pairs={{0,1},{1,0},{2,3},{3,2},{4,5},{5,4},{6,7},{7,6},{8,9},{9,8},{10,11... | collective-permute-start | bytes 3981320 | tf_op jit(solution)/shard_map/ppermute | solution.py:661
  41.4 4.5 %collective-permute-start.18 = (bf16[64,512]{1,0:T(8,128)(2,1)S(1)}, bf16[64,512]{1,0:T(8,128)(2,1)S(1)}, u32[]{:S(2)}, u32[]{:S(2)}) collective-permute-start(bf16[64,512]{1,0:T(8,128)(2,1)S(1)} %slice.23), channel_id=1, source_target_pairs={{4,0},{5,1},{8,4},{9,5},{12,8},{13,9},{14,12},{15,13},{10,14},{11,... | collective-permute-start | bytes 196616 | tf_op jit(solution)/shard_map/ppermute | solution.py:661
  41.9 4.3 %collective-permute-start.17 = (bf16[64,512]{1,0:T(8,128)(2,1)S(1)}, bf16[64,512]{1,0:T(8,128)(2,1)S(1)}, u32[]{:S(2)}, u32[]{:S(2)}) collective-permute-start(bf16[64,512]{1,0:T(8,128)(2,1)S(1)} %slice.22), channel_id=1, source_target_pairs={{0,4},{1,5},{4,8},{5,9},{8,12},{9,13},{12,14},{13,15},{14,10},{15,... | collective-permute-start | bytes 196616 | tf_op jit(solution)/shard_map/ppermute | solution.py:661
  49.2 3.7 %collective-permute-start.20 = (bf16[64,1152]{1,0:T(8,128)(2,1)S(1)}, bf16[64,1152]{1,0:T(8,128)(2,1)S(1)}, u32[]{:S(2)}, u32[]{:S(2)}) collective-permute-start(bf16[64,1152]{1,0:T(8,128)(2,1)S(1)} %get-tuple-element.68), channel_id=1, source_target_pairs={{0,1},{1,0},{2,3},{3,2},{4,5},{5,4},{6,7},{7,6},{8,9},{9,8},{10,11... | collective-permute-start | bytes 442376 | tf_op jit(solution)/shard_map/ppermute | solution.py:661

commit v11 on v8

--- a/solution.py
+++ b/solution.py
@@ -711,14 +711,15 @@
     *one, queries = tied(*one, queries)
     two = both_ways(*one)
     acc_one = step_attention((-1, 1), window_lengths, one, folded, key_row, queries)
-    wt_a, wt_b, acc_one = tied(*weight_three, acc_one)
-    cut = 640
-    weight_four = both_ways(wt_a[:, :cut], wt_b[:, cut:])
     *two, acc_one = tied(*two, acc_one)
     three = both_ways(*two)
     acc_two = step_attention((-2, 2), window_lengths, two, folded, key_row, queries)
-    *three, acc_two, wf_a, wf_b = tied(*three, acc_two, *weight_four)
+    wt_a, wt_b, acc_two = tied(*weight_three, acc_two)
+    cut = 640
+    weight_four = both_ways(wt_a[:, :cut], wt_b[:, cut:])
+    *three, acc_two = tied(*three, acc_two)
     four = both_ways(three[0][:64], three[1][64:])
+    *three, wf_a, wf_b = tied(*three, *weight_four)
     weights = pack([out_weight, *weight_one, *weight_two, wt_a, wt_b, wf_a, wf_b])
     sibling = send(weights, cores)
     acc_three = step_attention((-3, 3), window_lengths, three, folded, key_row, queries)

time: 52.2 us -> 55.7 us (1.067)
  waiting for transfers between devices: 7.8 us -> 11.4 us
    ppermute x21, waiting for transfers between devices: 7.8 us -> 11.4 us  [send(): return lax.ppermute(array, 'seq', pairs)]
  transfers between devices with their start and end apart: 21 -> 21, of which waited for: 9 -> 10; matrix products, arithmetic and copies ran while one was open for 0% -> 0% of each run, Pallas kernels for 37% -> 34%
where the time goes in v11:
time: 55.7 us; the launch traced here: 55.6 us
  Pallas kernels  21.6 us (39%)
  starting transfers between devices  21 us (38%)
  waiting for transfers between devices  11.4 us (20%)
  local copies, waits for them, and re-layouts  1.35 us (2%)
    ppermute x21, starting transfers between devices, send(): return lax.ppermute(array, 'seq', pairs)  21 us
    ppermute x21, waiting for transfers between devices, send(): return lax.ppermute(array, 'seq', pairs)  11.4 us
    pallas_call x4, Pallas kernels, step_attention(): pl.pallas_call(functools.partial(step_kernel, offsets), out_shape=ACC, in...  8.09 us
    pallas_call x1, Pallas kernels, fold(): pl.pallas_call(fold_kernel, out_shape=(jax.ShapeDtypeStruct((2 * D, inner...  5.67 us
    pallas_call x1, Pallas kernels, convolve(): pl.pallas_call(conv_kernel, out_shape=(out, out), in_specs=[ANY] * 4 + [V...  3.88 us
    pallas_call x1, Pallas kernels, make_queries(): pl.pallas_call(query_kernel, out_shape=jax.ShapeDtypeStruct((HEADS, 128,...  1.53 us
    pallas_call x1, Pallas kernels, merge(): pl.pallas_call(merge_kernel, out_shape=jax.ShapeDtypeStruct((128, D), BF1...  1.35 us
    unnamed x21, local copies, waits for them, and re-layouts  1.31 us
  transfers between devices with their start and end apart: 21, of which 10 were waited for; matrix products, arithmetic and copies ran while one was open for 0% of the time, Pallas kernels for 34%

profile of v11, /device:TPU:0, one launch (start us, length us, event | category | flops | bytes accessed | tf_op | source)
XLA Modules:
  0.0 55.6 jit_solution(2134902446056951574)
XLA Ops:
  0.0 0.5 collective-permute-start
  0.5 0.7 %collective-permute-start.1 = (bf16[8,2,32,128]{3,2,1,0:T(8,128)(2,1)}, bf16[8,2,32,128]{3,2,1,0:T(8,128)(2,1)S(1)}, u32[]{:S(2)}, u32[]{:S(2)}) collective-permute-start(bf16[8,2,32,128]{3,2,1,0:T(8,128)(2,1)} %own_any.1), channel_id=1, source_target_pairs={{1,2},{2,1},{3,4},{4,3},{5,6},{6,5},{7,8},{8,7},{9,10},{10,9},{11,... | collective-permute-start | bytes 393224 | tf_op jit(solution)/shard_map/ppermute | solution.py:677
  1.1 5.4 %collective-permute-start.2 = (bf16[72,1152]{1,0:T(8,128)(2,1)}, bf16[72,1152]{1,0:T(8,128)(2,1)S(1)}, u32[]{:S(2)}, u32[]{:S(2)}) collective-permute-start(bf16[72,1152]{1,0:T(8,128)(2,1)} %refs_0_.1), channel_id=1, source_target_pairs={{0,4},{1,5},{4,8},{5,9},{8,12},{9,13},{12,14},{13,15},{14,10},{15,... | collective-permute-start | bytes 497672 | tf_op jit(solution)/shard_map/ppermute | solution.py:677
  6.5 1.3 %copy-done.3 = bf16[512,1152]{1,0:T(8,128)(2,1)S(1)} copy-done((bf16[512,1152]{1,0:T(8,128)(2,1)S(1)}, bf16[512,1152]{1,0:T(8,128)(2,1)}, u32[]{:S(2)}) %copy-start.3) | copy-done | bytes 1179672
  7.8 5.7 %fold.1 = (bf16[2304,512]{1,0:T(8,128)(2,1)S(1)}, bf16[1152,1152]{1,0:T(8,128)(2,1)S(1)}, bf16[512,1152]{1,0:T(8,128)(2,1)S(1)}) custom-call(bf16[512,1152]{1,0:T(8,128)(2,1)S(1)} %copy-done.3, bf16[1152,3456]{1,0:T(8,128)(2,1)} %qkv_any.1), custom_call_target="tpu_custom_call" | custom-call | flops 2717908992 | bytes 12582912 | tf_op jit(solution)/shard_map/fold/pallas_call | solution.py:252
  13.5 0.0 collective-permute-done.1.other_ref
  13.5 0.0 collective-permute-done.2.refs_1_
  13.5 0.0 copy-start.2
  13.5 2.1 %collective-permute-start.5 = (bf16[72,1152]{1,0:T(8,128)(2,1)S(1)}, bf16[72,1152]{1,0:T(8,128)(2,1)S(1)}, u32[]{:S(2)}, u32[]{:S(2)}) collective-permute-start(bf16[72,1152]{1,0:T(8,128)(2,1)S(1)} %collective-permute-done.2.refs_1_), channel_id=1, source_target_pairs={{0,4},{1,5},{4,8},{5,9},{8,12},{9,13},{12,14},{13,15},{14,10},{15,... | collective-permute-start | bytes 497672 | tf_op jit(solution)/shard_map/ppermute | solution.py:677
  15.6 0.0 collective-permute-start.6
  15.7 3.9 %convolve.1 = (bf16[64,512]{1,0:T(8,128)(2,1)S(1)}, bf16[64,512]{1,0:T(8,128)(2,1)S(1)}) custom-call(s32[3]{0:T(128)S(1)} %copy-done.8, s32[1,3]{1,0:T(1,128)S(1)} %copy-done.1, bf16[8,2,32,128]{3,2,1,0:T(8,128)(2,1)S(1)} %copy-done.7, bf16[512,1152]{1,0:T(8,128)(2,1)S(1)} %copy-done.4, bf16[8,2,32,128]{3,2,1,0:T(8,128)(2,1)S(1)} %collective-permute-done.sibling_ref, ...), custom_call_target="tpu_custom_call" | custom-call | flops 2147483648 | bytes 4194304 | tf_op jit(solution)/shard_map/convolve/pallas_call | solution.py:404
  19.5 0.1 collective-permute-start.4
  19.6 1.2 %collective-permute-done.4 = bf16[64,512]{1,0:T(8,128)(2,1)S(1)} collective-permute-done((bf16[64,512]{1,0:T(8,128)(2,1)S(1)}, bf16[64,512]{1,0:T(8,128)(2,1)S(1)}, u32[]{:S(2)}, u32[]{:S(2)}) %collective-permute-start.4) | collective-permute-done | bytes 65568 | tf_op jit(solution)/shard_map/ppermute | solution.py:677
  20.9 0.0 collective-permute-done.5.refs_3_
  20.9 0.3 collective-permute-done.6.refs_4_
  21.2 0.8 %collective-permute-start.8 = (bf16[128,512]{1,0:T(8,128)(2,1)S(1)}, bf16[128,512]{1,0:T(8,128)(2,1)S(1)}, u32[]{:S(2)}, u32[]{:S(2)}) collective-permute-start(bf16[128,512]{1,0:T(8,128)(2,1)S(1)} %constant_dynamic-update-slice_fusion.block_ref.refs_0_), channel_id=1, source_target_pairs={{4,0},{5,1},{8,4},{9,5},{12,8},{13,9},{14,12},{15,13},{10,14},{11,... | collective-permute-start | bytes 393224 | tf_op jit(solution)/shard_map/ppermute | solution.py:677
  21.9 1.3 %collective-permute-start.7 = (bf16[128,512]{1,0:T(8,128)(2,1)S(1)}, bf16[128,512]{1,0:T(8,128)(2,1)S(1)}, u32[]{:S(2)}, u32[]{:S(2)}) collective-permute-start(bf16[128,512]{1,0:T(8,128)(2,1)S(1)} %constant_dynamic-update-slice_fusion.block_ref.refs_0_), channel_id=1, source_target_pairs={{0,4},{1,5},{4,8},{5,9},{8,12},{9,13},{12,14},{13,15},{14,10},{15,... | collective-permute-start | bytes 393224 | tf_op jit(solution)/shard_map/ppermute | solution.py:677
  23.2 1.8 %collective-permute-start.13 = (bf16[72,1152]{1,0:T(8,128)(2,1)S(1)}, bf16[72,1152]{1,0:T(8,128)(2,1)S(1)}, u32[]{:S(2)}, u32[]{:S(2)}) collective-permute-start(bf16[72,1152]{1,0:T(8,128)(2,1)S(1)} %collective-permute-done.5.refs_3_), channel_id=1, source_target_pairs={{0,4},{1,5},{4,8},{5,9},{8,12},{9,13},{12,14},{13,15},{14,10},{15,... | collective-permute-start | bytes 497672 | tf_op jit(solution)/shard_map/ppermute | solution.py:677
  25.0 0.3 collective-permute-start.14
  25.2 1.5 %queries.1.refs_4_.refs_5_ = bf16[16,128,80]{2,1,0:T(8,128)(2,1)S(1)} custom-call(s32[1,3]{1,0:T(1,128)S(1)} %copy-done.1, bf16[128,512]{1,0:T(8,128)(2,1)S(1)} %constant_dynamic-update-slice_fusion.block_ref.refs_0_, bf16[512,1152]{1,0:T(8,128)(2,1)S(1)} %get-tuple-element.47.centered_ref, bf16[1152,1152]{1,0:T(8,128)(2,1)S(1)} %get-tuple-element.48.query_ref, ...), custom_call_target="tpu_custom_call" | custom-call | flops 1073741824 | bytes 4194304 | tf_op jit(solution)/shard_map/queries/pallas_call | solution.py:533
  26.8 0.0 collective-permute-done.8.refs_1_
  26.8 1.6 %collective-permute-done.7.refs_0_ = bf16[128,512]{1,0:T(8,128)(2,1)S(1)} collective-permute-done((bf16[128,512]{1,0:T(8,128)(2,1)S(1)}, bf16[128,512]{1,0:T(8,128)(2,1)S(1)}, u32[]{:S(2)}, u32[]{:S(2)}) %collective-permute-start.7) | collective-permute-done | bytes 131104 | tf_op jit(solution)/shard_map/ppermute | solution.py:677
  28.3 1.2 %collective-permute-start.9 = (bf16[128,512]{1,0:T(8,128)(2,1)S(1)}, bf16[128,512]{1,0:T(8,128)(2,1)S(1)}, u32[]{:S(2)}, u32[]{:S(2)}) collective-permute-start(bf16[128,512]{1,0:T(8,128)(2,1)S(1)} %collective-permute-done.7.refs_0_), channel_id=1, source_target_pairs={{0,4},{1,5},{4,8},{5,9},{8,12},{9,13},{12,14},{13,15},{14,10},{15,... | collective-permute-start | bytes 393224 | tf_op jit(solution)/shard_map/ppermute | solution.py:677
  29.6 0.8 %collective-permute-start.10 = (bf16[128,512]{1,0:T(8,128)(2,1)S(1)}, bf16[128,512]{1,0:T(8,128)(2,1)S(1)}, u32[]{:S(2)}, u32[]{:S(2)}) collective-permute-start(bf16[128,512]{1,0:T(8,128)(2,1)S(1)} %collective-permute-done.8.refs_1_), channel_id=1, source_target_pairs={{4,0},{5,1},{8,4},{9,5},{12,8},{13,9},{14,12},{15,13},{10,14},{11,... | collective-permute-start | bytes 393224 | tf_op jit(solution)/shard_map/ppermute | solution.py:677
  30.4 2.0 %step_attention.4.refs_0_ = f32[16,80,128]{2,1,0:T(8,128)S(1)} custom-call(s32[1,3]{1,0:T(1,128)S(1)} %copy-done.1, bf16[128,512]{1,0:T(8,128)(2,1)S(1)} %collective-permute-done.7.refs_0_, bf16[128,512]{1,0:T(8,128)(2,1)S(1)} %collective-permute-done.8.refs_1_, bf16[2304,512]{1,0:T(8,128)(2,1)S(1)} %get-tuple-element.51.refs_2_.refs_3_, ...), custom_call_target="tpu_custom_call" | custom-call | flops 1744830464 | bytes 5242880 | tf_op jit(solution)/shard_map/step_attention/pallas_call | solution.py:561
  32.4 1.2 %collective-permute-done.9.refs_0_ = bf16[128,512]{1,0:T(8,128)(2,1)S(1)} collective-permute-done((bf16[128,512]{1,0:T(8,128)(2,1)S(1)}, bf16[128,512]{1,0:T(8,128)(2,1)S(1)}, u32[]{:S(2)}, u32[]{:S(2)}) %collective-permute-start.9) | collective-permute-done | bytes 131104 | tf_op jit(solution)/shard_map/ppermute | solution.py:677
  33.6 0.9 %collective-permute-done.10.refs_1_ = bf16[128,512]{1,0:T(8,128)(2,1)S(1)} collective-permute-done((bf16[128,512]{1,0:T(8,128)(2,1)S(1)}, bf16[128,512]{1,0:T(8,128)(2,1)S(1)}, u32[]{:S(2)}, u32[]{:S(2)}) %collective-permute-start.10) | collective-permute-done | bytes 131104 | tf_op jit(solution)/shard_map/ppermute | solution.py:677
  34.5 1.8 %collective-permute-start.11 = (bf16[128,512]{1,0:T(8,128)(2,1)S(1)}, bf16[128,512]{1,0:T(8,128)(2,1)S(1)}, u32[]{:S(2)}, u32[]{:S(2)}) collective-permute-start(bf16[128,512]{1,0:T(8,128)(2,1)S(1)} %collective-permute-done.9.refs_0_), channel_id=1, source_target_pairs={{0,4},{1,5},{4,8},{5,9},{8,12},{9,13},{12,14},{13,15},{14,10},{15,... | collective-permute-start | bytes 393224 | tf_op jit(solution)/shard_map/ppermute | solution.py:677
  36.3 0.3 collective-permute-start.12
  36.6 2.0 %step_attention.5.refs_1_ = f32[16,80,128]{2,1,0:T(8,128)S(1)} custom-call(s32[1,3]{1,0:T(1,128)S(1)} %copy-done.1, bf16[128,512]{1,0:T(8,128)(2,1)S(1)} %collective-permute-done.9.refs_0_, bf16[128,512]{1,0:T(8,128)(2,1)S(1)} %collective-permute-done.10.refs_1_, bf16[2304,512]{1,0:T(8,128)(2,1)S(1)} %get-tuple-element.51.refs_2_.refs_3_, ...), custom_call_target="tpu_custom_call" | custom-call | flops 1744830464 | bytes 5242880 | tf_op jit(solution)/shard_map/step_attention/pallas_call | solution.py:561
  38.6 1.8 %collective-permute-start.17 = (bf16[72,640]{1,0:T(8,128)(2,1)S(1)}, bf16[72,640]{1,0:T(8,128)(2,1)S(1)}, u32[]{:S(2)}, u32[]{:S(2)}) collective-permute-start(bf16[72,640]{1,0:T(8,128)(2,1)S(1)} %slice.14), channel_id=1, source_target_pairs={{0,4},{1,5},{4,8},{5,9},{8,12},{9,13},{12,14},{13,15},{14,10},{15,... | collective-permute-start | bytes 276488 | tf_op jit(solution)/shard_map/ppermute | solution.py:677
  40.4 0.2 collective-permute-start.18
  40.7 1.3 %collective-permute-done.12.refs_1_ = bf16[128,512]{1,0:T(8,128)(2,1)S(1)} collective-permute-done((bf16[128,512]{1,0:T(8,128)(2,1)S(1)}, bf16[128,512]{1,0:T(8,128)(2,1)S(1)}, u32[]{:S(2)}, u32[]{:S(2)}) %collective-permute-start.12) | collective-permute-done | bytes 131104 | tf_op jit(solution)/shard_map/ppermute | solution.py:677
  42.0 2.8 %collective-permute-done.18.refs_8_ = bf16[72,512]{1,0:T(8,128)(2,1)S(1)} collective-permute-done((bf16[72,512]{1,0:T(8,128)(2,1)S(1)}, bf16[72,512]{1,0:T(8,128)(2,1)S(1)}, u32[]{:S(2)}, u32[]{:S(2)}) %collective-permute-start.18) | collective-permute-done | bytes 73760 | tf_op jit(solution)/shard_map/ppermute | solution.py:677
  44.8 0.0 collective-permute-done.17.refs_7_
  44.8 0.1 pack.1
  44.9 0.1 collective-permute-start.19
  45.0 0.3 collective-permute-start.16
  45.3 1.8 %collective-permute-start.15 = (bf16[64,512]{1,0:T(8,128)(2,1)S(1)}, bf16[64,512]{1,0:T(8,128)(2,1)S(1)}, u32[]{:S(2)}, u32[]{:S(2)}) collective-permute-start(bf16[64,512]{1,0:T(8,128)(2,1)S(1)} %slice.12), channel_id=1, source_target_pairs={{0,4},{1,5},{4,8},{5,9},{8,12},{9,13},{12,14},{13,15},{14,10},{15,... | collective-permute-start | bytes 196616 | tf_op jit(solution)/shard_map/ppermute | solution.py:677
  47.1 2.0 %step_attention.6.refs_2_ = f32[16,80,128]{2,1,0:T(8,128)S(1)} custom-call(s32[1,3]{1,0:T(1,128)S(1)} %copy-done.1, bf16[128,512]{1,0:T(8,128)(2,1)S(1)} %collective-permute-done.11.refs_0_, bf16[128,512]{1,0:T(8,128)(2,1)S(1)} %collective-permute-done.12.refs_1_, bf16[2304,512]{1,0:T(8,128)(2,1)S(1)} %get-tuple-element.51.refs_2_.refs_3_, ...), custom_call_target="tpu_custom_call" | custom-call | flops 1744830464 | bytes 5242880 | tf_op jit(solution)/shard_map/step_attention/pallas_call | solution.py:561
  49.1 0.4 collective-permute-done.16.refs_2_
  49.5 0.2 collective-permute-done.15.refs_1_
  49.8 2.0 %step_attention.7.refs_3_ = f32[16,80,128]{2,1,0:T(8,128)S(1)} custom-call(s32[1,3]{1,0:T(1,128)S(1)} %copy-done.1, bf16[128,512]{1,0:T(8,128)(2,1)S(1)} %constant_dynamic-update-slice_fusion.block_ref.refs_0_, bf16[64,512]{1,0:T(8,128)(2,1)S(1)} %collective-permute-done.15.refs_1_, bf16[64,512]{1,0:T(8,128)(2,1)S(1)} %collective-permute-done.16.refs_2_, ...), custom_call_target="tpu_custom_call" | custom-call | flops 1744830464 | bytes 5242880 | tf_op jit(solution)/shard_map/step_attention/pallas_call | solution.py:561
  51.8 0.0 collective-permute-done.19.refs_5_
  51.8 1.0 %project_out.1 = (bf16[64,1152]{1,0:T(8,128)(2,1)S(1)}, bf16[64,1152]{1,0:T(8,128)(2,1)S(1)}) custom-call(f32[16,80,128]{2,1,0:T(8,128)S(1)} %step_attention.4.refs_0_, f32[16,80,128]{2,1,0:T(8,128)S(1)} %step_attention.5.refs_1_, f32[16,80,128]{2,1,0:T(8,128)S(1)} %step_attention.6.refs_2_, f32[16,80,128]{2,1,0:T(8,128)S(1)} %step_attention.7.refs_3_, ...), custom_call_target="tpu_custom_call" | custom-call | flops 377487360 | bytes 4194304 | tf_op jit(solution)/shard_map/project_out/pallas_call | solution.py:606
  52.8 0.1 collective-permute-start.20
  52.9 1.4 %collective-permute-done.20.got_ref = bf16[64,1152]{1,0:T(8,128)(2,1)S(1)} collective-permute-done((bf16[64,1152]{1,0:T(8,128)(2,1)S(1)}, bf16[64,1152]{1,0:T(8,128)(2,1)S(1)}, u32[]{:S(2)}, u32[]{:S(2)}) %collective-permute-start.20) | collective-permute-done | bytes 147488 | tf_op jit(solution)/shard_map/ppermute | solution.py:677
  54.2 1.3 %merge.1 = bf16[128,1152]{1,0:T(8,128)(2,1)} custom-call(s32[1,3]{1,0:T(1,128)S(1)} %copy-done.1, bf16[64,1152]{1,0:T(8,128)(2,1)S(1)} %get-tuple-element.71.keep_ref, bf16[64,1152]{1,0:T(8,128)(2,1)S(1)} %collective-permute-done.20.got_ref), custom_call_target="tpu_custom_call" | custom-call | tf_op jit(solution)/shard_map/merge/pallas_call | solution.py:656
  (30 shorter events, 0.1 us)
Async XLA Ops:
  0.0 15.6 %copy-start.1 = (s32[1,3]{1,0:T(1,128)S(1)}, s32[1,3]{1,0:T(1,128)}, u32[]{:S(2)}) copy-start(s32[1,3]{1,0:T(1,128)} %lengths_ref.11) | copy-start | bytes 40
  0.0 13.5 %collective-permute-start = (bf16[8,2,32,128]{3,2,1,0:T(8,128)(2,1)}, bf16[8,2,32,128]{3,2,1,0:T(8,128)(2,1)S(1)}, u32[]{:S(2)}, u32[]{:S(2)}) collective-permute-start(bf16[8,2,32,128]{3,2,1,0:T(8,128)(2,1)} %own_any.1), channel_id=1, source_target_pairs={{0,1},{1,0},{2,3},{3,2},{4,5},{5,4},{6,7},{7,6},{8,9},{9,8},{10,11... | collective-permute-start | bytes 393224 | tf_op jit(solution)/shard_map/ppermute | solution.py:677
  0.5 13.0 %collective-permute-start.1 = (bf16[8,2,32,128]{3,2,1,0:T(8,128)(2,1)}, bf16[8,2,32,128]{3,2,1,0:T(8,128)(2,1)S(1)}, u32[]{:S(2)}, u32[]{:S(2)}) collective-permute-start(bf16[8,2,32,128]{3,2,1,0:T(8,128)(2,1)} %own_any.1), channel_id=1, source_target_pairs={{1,2},{2,1},{3,4},{4,3},{5,6},{6,5},{7,8},{8,7},{9,10},{10,9},{11,... | collective-permute-start | bytes 393224 | tf_op jit(solution)/shard_map/ppermute | solution.py:677
  1.1 12.4 %collective-permute-start.2 = (bf16[72,1152]{1,0:T(8,128)(2,1)}, bf16[72,1152]{1,0:T(8,128)(2,1)S(1)}, u32[]{:S(2)}, u32[]{:S(2)}) collective-permute-start(bf16[72,1152]{1,0:T(8,128)(2,1)} %refs_0_.1), channel_id=1, source_target_pairs={{0,4},{1,5},{4,8},{5,9},{8,12},{9,13},{12,14},{13,15},{14,10},{15,... | collective-permute-start | bytes 497672 | tf_op jit(solution)/shard_map/ppermute | solution.py:677
  6.5 7.0 %collective-permute-start.3 = (bf16[72,1152]{1,0:T(8,128)(2,1)}, bf16[72,1152]{1,0:T(8,128)(2,1)S(1)}, u32[]{:S(2)}, u32[]{:S(2)}) collective-permute-start(bf16[72,1152]{1,0:T(8,128)(2,1)} %refs_0_.1), channel_id=1, source_target_pairs={{4,0},{5,1},{8,4},{9,5},{12,8},{13,9},{14,12},{15,13},{10,14},{11,... | collective-permute-start | bytes 497672 | tf_op jit(solution)/shard_map/ppermute | solution.py:677
  6.5 1.3 %copy-start.3 = (bf16[512,1152]{1,0:T(8,128)(2,1)S(1)}, bf16[512,1152]{1,0:T(8,128)(2,1)}, u32[]{:S(2)}) copy-start(bf16[512,1152]{1,0:T(8,128)(2,1)} %patch_any.3) | copy-start | bytes 3538948
  7.8 7.8 %copy-start.4 = (bf16[512,1152]{1,0:T(8,128)(2,1)S(1)}, bf16[512,1152]{1,0:T(8,128)(2,1)}, u32[]{:S(2)}) copy-start(bf16[512,1152]{1,0:T(8,128)(2,1)} %patch_any.3) | copy-start | bytes 3538948
  7.8 7.8 %copy-start.5 = (bf16[3,3,3,128,128]{4,3,2,1,0:T(8,128)(2,1)S(1)}, bf16[3,3,3,128,128]{4,3,2,1,0:T(8,128)(2,1)}, u32[]{:S(2)}) copy-start(bf16[3,3,3,128,128]{4,3,2,1,0:T(8,128)(2,1)} %first_ref.1) | copy-start | bytes 2654212
  7.8 7.8 %copy-start.6 = (bf16[3,3,3,128,128]{4,3,2,1,0:T(8,128)(2,1)S(1)}, bf16[3,3,3,128,128]{4,3,2,1,0:T(8,128)(2,1)}, u32[]{:S(2)}) copy-start(bf16[3,3,3,128,128]{4,3,2,1,0:T(8,128)(2,1)} %second_ref.1) | copy-start | bytes 2654212
  7.8 7.8 %copy-start.7 = (bf16[8,2,32,128]{3,2,1,0:T(8,128)(2,1)S(1)}, bf16[8,2,32,128]{3,2,1,0:T(8,128)(2,1)}, u32[]{:S(2)}) copy-start(bf16[8,2,32,128]{3,2,1,0:T(8,128)(2,1)} %own_any.1) | copy-start | bytes 393220
  7.8 7.9 %copy-start.8 = (s32[3]{0:T(128)S(1)}, s32[3]{0:T(128)}, u32[]{:S(2)}) copy-start(s32[3]{0:T(128)} %counts_any.1) | copy-start | bytes 40
  13.5 11.7 %copy-start.2 = (f32[72]{0:T(128)S(1)}, f32[72]{0:T(128)}, u32[]{:S(2)}) copy-start(f32[72]{0:T(128)} %param.16) | copy-start | bytes 868
  13.5 7.3 %collective-permute-start.5 = (bf16[72,1152]{1,0:T(8,128)(2,1)S(1)}, bf16[72,1152]{1,0:T(8,128)(2,1)S(1)}, u32[]{:S(2)}, u32[]{:S(2)}) collective-permute-start(bf16[72,1152]{1,0:T(8,128)(2,1)S(1)} %collective-permute-done.2.refs_1_), channel_id=1, source_target_pairs={{0,4},{1,5},{4,8},{5,9},{8,12},{9,13},{12,14},{13,15},{14,10},{15,... | collective-permute-start | bytes 497672 | tf_op jit(solution)/shard_map/ppermute | solution.py:677
  15.6 5.6 %collective-permute-start.6 = (bf16[72,1152]{1,0:T(8,128)(2,1)S(1)}, bf16[72,1152]{1,0:T(8,128)(2,1)S(1)}, u32[]{:S(2)}, u32[]{:S(2)}) collective-permute-start(bf16[72,1152]{1,0:T(8,128)(2,1)S(1)} %collective-permute-done.3.refs_2_), channel_id=1, source_target_pairs={{4,0},{5,1},{8,4},{9,5},{12,8},{13,9},{14,12},{15,13},{10,14},{11,... | collective-permute-start | bytes 497672 | tf_op jit(solution)/shard_map/ppermute | solution.py:677
  19.5 1.3 %collective-permute-start.4 = (bf16[64,512]{1,0:T(8,128)(2,1)S(1)}, bf16[64,512]{1,0:T(8,128)(2,1)S(1)}, u32[]{:S(2)}, u32[]{:S(2)}) collective-permute-start(bf16[64,512]{1,0:T(8,128)(2,1)S(1)} %get-tuple-element.43), channel_id=1, source_target_pairs={{0,1},{1,0},{2,3},{3,2},{4,5},{5,4},{6,7},{7,6},{8,9},{9,8},{10,11... | collective-permute-start | bytes 196616 | tf_op jit(solution)/shard_map/ppermute | solution.py:677
  21.2 5.6 %collective-permute-start.8 = (bf16[128,512]{1,0:T(8,128)(2,1)S(1)}, bf16[128,512]{1,0:T(8,128)(2,1)S(1)}, u32[]{:S(2)}, u32[]{:S(2)}) collective-permute-start(bf16[128,512]{1,0:T(8,128)(2,1)S(1)} %constant_dynamic-update-slice_fusion.block_ref.refs_0_), channel_id=1, source_target_pairs={{4,0},{5,1},{8,4},{9,5},{12,8},{13,9},{14,12},{15,13},{10,14},{11,... | collective-permute-start | bytes 393224 | tf_op jit(solution)/shard_map/ppermute | solution.py:677
  21.9 6.4 %collective-permute-start.7 = (bf16[128,512]{1,0:T(8,128)(2,1)S(1)}, bf16[128,512]{1,0:T(8,128)(2,1)S(1)}, u32[]{:S(2)}, u32[]{:S(2)}) collective-permute-start(bf16[128,512]{1,0:T(8,128)(2,1)S(1)} %constant_dynamic-update-slice_fusion.block_ref.refs_0_), channel_id=1, source_target_pairs={{0,4},{1,5},{4,8},{5,9},{8,12},{9,13},{12,14},{13,15},{14,10},{15,... | collective-permute-start | bytes 393224 | tf_op jit(solution)/shard_map/ppermute | solution.py:677
  23.2 15.4 %collective-permute-start.13 = (bf16[72,1152]{1,0:T(8,128)(2,1)S(1)}, bf16[72,1152]{1,0:T(8,128)(2,1)S(1)}, u32[]{:S(2)}, u32[]{:S(2)}) collective-permute-start(bf16[72,1152]{1,0:T(8,128)(2,1)S(1)} %collective-permute-done.5.refs_3_), channel_id=1, source_target_pairs={{0,4},{1,5},{4,8},{5,9},{8,12},{9,13},{12,14},{13,15},{14,10},{15,... | collective-permute-start | bytes 497672 | tf_op jit(solution)/shard_map/ppermute | solution.py:677
  25.0 13.6 %collective-permute-start.14 = (bf16[72,1152]{1,0:T(8,128)(2,1)S(1)}, bf16[72,1152]{1,0:T(8,128)(2,1)S(1)}, u32[]{:S(2)}, u32[]{:S(2)}) collective-permute-start(bf16[72,1152]{1,0:T(8,128)(2,1)S(1)} %collective-permute-done.6.refs_4_), channel_id=1, source_target_pairs={{4,0},{5,1},{8,4},{9,5},{12,8},{13,9},{14,12},{15,13},{10,14},{11,... | collective-permute-start | bytes 497672 | tf_op jit(solution)/shard_map/ppermute | solution.py:677
  25.2 5.1 %copy-start.9 = (f32[72]{0:T(128)S(1)}, f32[72]{0:T(128)}, u32[]{:S(2)}) copy-start(f32[72]{0:T(128)} %param.17) | copy-start | bytes 868
  28.3 5.3 %collective-permute-start.9 = (bf16[128,512]{1,0:T(8,128)(2,1)S(1)}, bf16[128,512]{1,0:T(8,128)(2,1)S(1)}, u32[]{:S(2)}, u32[]{:S(2)}) collective-permute-start(bf16[128,512]{1,0:T(8,128)(2,1)S(1)} %collective-permute-done.7.refs_0_), channel_id=1, source_target_pairs={{0,4},{1,5},{4,8},{5,9},{8,12},{9,13},{12,14},{13,15},{14,10},{15,... | collective-permute-start | bytes 393224 | tf_op jit(solution)/shard_map/ppermute | solution.py:677
  29.6 5.0 %collective-permute-start.10 = (bf16[128,512]{1,0:T(8,128)(2,1)S(1)}, bf16[128,512]{1,0:T(8,128)(2,1)S(1)}, u32[]{:S(2)}, u32[]{:S(2)}) collective-permute-start(bf16[128,512]{1,0:T(8,128)(2,1)S(1)} %collective-permute-done.8.refs_1_), channel_id=1, source_target_pairs={{4,0},{5,1},{8,4},{9,5},{12,8},{13,9},{14,12},{15,13},{10,14},{11,... | collective-permute-start | bytes 393224 | tf_op jit(solution)/shard_map/ppermute | solution.py:677
  32.4 12.4 %copy-start = (bf16[72,1152]{1,0:T(8,128)(2,1)S(1)}, bf16[72,1152]{1,0:T(8,128)(2,1)}, u32[]{:S(2)}) copy-start(bf16[72,1152]{1,0:T(8,128)(2,1)} %refs_0_.1) | copy-start | bytes 497668
  34.5 6.2 %collective-permute-start.11 = (bf16[128,512]{1,0:T(8,128)(2,1)S(1)}, bf16[128,512]{1,0:T(8,128)(2,1)S(1)}, u32[]{:S(2)}, u32[]{:S(2)}) collective-permute-start(bf16[128,512]{1,0:T(8,128)(2,1)S(1)} %collective-permute-done.9.refs_0_), channel_id=1, source_target_pairs={{0,4},{1,5},{4,8},{5,9},{8,12},{9,13},{12,14},{13,15},{14,10},{15,... | collective-permute-start | bytes 393224 | tf_op jit(solution)/shard_map/ppermute | solution.py:677
  36.3 5.7 %collective-permute-start.12 = (bf16[128,512]{1,0:T(8,128)(2,1)S(1)}, bf16[128,512]{1,0:T(8,128)(2,1)S(1)}, u32[]{:S(2)}, u32[]{:S(2)}) collective-permute-start(bf16[128,512]{1,0:T(8,128)(2,1)S(1)} %collective-permute-done.10.refs_1_), channel_id=1, source_target_pairs={{4,0},{5,1},{8,4},{9,5},{12,8},{13,9},{14,12},{15,13},{10,14},{11,... | collective-permute-start | bytes 393224 | tf_op jit(solution)/shard_map/ppermute | solution.py:677
  38.6 6.2 %collective-permute-start.17 = (bf16[72,640]{1,0:T(8,128)(2,1)S(1)}, bf16[72,640]{1,0:T(8,128)(2,1)S(1)}, u32[]{:S(2)}, u32[]{:S(2)}) collective-permute-start(bf16[72,640]{1,0:T(8,128)(2,1)S(1)} %slice.14), channel_id=1, source_target_pairs={{0,4},{1,5},{4,8},{5,9},{8,12},{9,13},{12,14},{13,15},{14,10},{15,... | collective-permute-start | bytes 276488 | tf_op jit(solution)/shard_map/ppermute | solution.py:677
  40.4 4.4 %collective-permute-start.18 = (bf16[72,512]{1,0:T(8,128)(2,1)S(1)}, bf16[72,512]{1,0:T(8,128)(2,1)S(1)}, u32[]{:S(2)}, u32[]{:S(2)}) collective-permute-start(bf16[72,512]{1,0:T(8,128)(2,1)S(1)} %slice.15), channel_id=1, source_target_pairs={{4,0},{5,1},{8,4},{9,5},{12,8},{13,9},{14,12},{15,13},{10,14},{11,... | collective-permute-start | bytes 221192 | tf_op jit(solution)/shard_map/ppermute | solution.py:677
  44.9 6.9 %collective-permute-start.19 = (bf16[576,1152]{1,0:T(8,128)(2,1)S(1)}, bf16[576,1152]{1,0:T(8,128)(2,1)S(1)}, u32[]{:S(2)}, u32[]{:S(2)}) collective-permute-start(bf16[576,1152]{1,0:T(8,128)(2,1)S(1)} %bitcast.3), channel_id=1, source_target_pairs={{0,1},{1,0},{2,3},{3,2},{4,5},{5,4},{6,7},{7,6},{8,9},{9,8},{10,11... | collective-permute-start | bytes 3981320 | tf_op jit(solution)/shard_map/ppermute | solution.py:677
  45.0 4.5 %collective-permute-start.16 = (bf16[64,512]{1,0:T(8,128)(2,1)S(1)}, bf16[64,512]{1,0:T(8,128)(2,1)S(1)}, u32[]{:S(2)}, u32[]{:S(2)}) collective-permute-start(bf16[64,512]{1,0:T(8,128)(2,1)S(1)} %slice.13), channel_id=1, source_target_pairs={{4,0},{5,1},{8,4},{9,5},{12,8},{13,9},{14,12},{15,13},{10,14},{11,... | collective-permute-start | bytes 196616 | tf_op jit(solution)/shard_map/ppermute | solution.py:677
  45.3 4.5 %collective-permute-start.15 = (bf16[64,512]{1,0:T(8,128)(2,1)S(1)}, bf16[64,512]{1,0:T(8,128)(2,1)S(1)}, u32[]{:S(2)}, u32[]{:S(2)}) collective-permute-start(bf16[64,512]{1,0:T(8,128)(2,1)S(1)} %slice.12), channel_id=1, source_target_pairs={{0,4},{1,5},{4,8},{5,9},{8,12},{9,13},{12,14},{13,15},{14,10},{15,... | collective-permute-start | bytes 196616 | tf_op jit(solution)/shard_map/ppermute | solution.py:677
  52.8 1.4 %collective-permute-start.20 = (bf16[64,1152]{1,0:T(8,128)(2,1)S(1)}, bf16[64,1152]{1,0:T(8,128)(2,1)S(1)}, u32[]{:S(2)}, u32[]{:S(2)}) collective-permute-start(bf16[64,1152]{1,0:T(8,128)(2,1)S(1)} %get-tuple-element.72), channel_id=1, source_target_pairs={{0,1},{1,0},{2,3},{3,2},{4,5},{5,4},{6,7},{7,6},{8,9},{9,8},{10,11... | collective-permute-start | bytes 442376 | tf_op jit(solution)/shard_map/ppermute | solution.py:677

commit v12 on v8

--- a/solution.py
+++ b/solution.py
@@ -617,11 +617,8 @@
 
 def pack_kernel(*refs):
     out_ref = refs[-1]
-    for i in range(7):
+    for i in range(8):
         out_ref[i] = refs[i][...]
-    cut = refs[7].shape[1]
-    out_ref[7, :, :cut] = refs[7][...]
-    out_ref[7, :, cut:] = refs[8][...]
 
 
 def pack(pieces):
@@ -629,7 +626,7 @@
     out = pl.pallas_call(
         pack_kernel,
         out_shape=jax.ShapeDtypeStruct((8, rows, columns), BF16),
-        in_specs=[VMEM] * 9,
+        in_specs=[VMEM] * 8,
         out_specs=VMEM,
         compiler_params=params(),
         name="pack",
@@ -712,14 +709,13 @@
     two = both_ways(*one)
     acc_one = step_attention((-1, 1), window_lengths, one, folded, key_row, queries)
     wt_a, wt_b, acc_one = tied(*weight_three, acc_one)
-    cut = 640
-    weight_four = both_ways(wt_a[:, :cut], wt_b[:, cut:])
+    weight_four = send(wt_a, forward)
     *two, acc_one = tied(*two, acc_one)
     three = both_ways(*two)
     acc_two = step_attention((-2, 2), window_lengths, two, folded, key_row, queries)
-    *three, acc_two, wf_a, wf_b = tied(*three, acc_two, *weight_four)
+    *three, acc_two, weight_four = tied(*three, acc_two, weight_four)
     four = both_ways(three[0][:64], three[1][64:])
-    weights = pack([out_weight, *weight_one, *weight_two, wt_a, wt_b, wf_a, wf_b])
+    weights = pack([out_weight, *weight_one, *weight_two, wt_a, wt_b, weight_four])
     sibling = send(weights, cores)
     acc_three = step_attention((-3, 3), window_lengths, three, folded, key_row, queries)
     *four, acc_three = tied(*four, acc_three)

time: 52.2 us -> 52.3 us (level)
  starting transfers between devices: 21.1 us -> 20.2 us
  waiting for transfers between devices: 7.8 us -> 8.68 us
    ppermute x21 -> x20, waiting for transfers between devices: 7.8 us -> 8.68 us  [send(): return lax.ppermute(array, 'seq', pairs)]
    ppermute x21 -> x20, starting transfers between devices: 21.1 us -> 20.2 us  [send(): return lax.ppermute(array, 'seq', pairs)]
  transfers between devices with their start and end apart: 21 -> 20, of which waited for: 9 -> 9; matrix products, arithmetic and copies ran while one was open for 0% -> 0% of each run, Pallas kernels for 37% -> 37%
where the time goes in v12:
time: 52.3 us; the launch traced here: 52.1 us
  Pallas kernels  21.6 us (41%)
  starting transfers between devices  20.2 us (39%)
  waiting for transfers between devices  8.68 us (17%)
  local copies, waits for them, and re-layouts  1.33 us (3%)
    ppermute x20, starting transfers between devices, send(): return lax.ppermute(array, 'seq', pairs)  20.2 us
    ppermute x20, waiting for transfers between devices, send(): return lax.ppermute(array, 'seq', pairs)  8.68 us
    pallas_call x4, Pallas kernels, step_attention(): pl.pallas_call(functools.partial(step_kernel, offsets), out_shape=ACC, in...  8.12 us
    pallas_call x1, Pallas kernels, fold(): pl.pallas_call(fold_kernel, out_shape=(jax.ShapeDtypeStruct((2 * D, inner...  5.67 us
    pallas_call x1, Pallas kernels, convolve(): pl.pallas_call(conv_kernel, out_shape=(out, out), in_specs=[ANY] * 4 + [V...  3.89 us
    pallas_call x1, Pallas kernels, make_queries(): pl.pallas_call(query_kernel, out_shape=jax.ShapeDtypeStruct((HEADS, 128,...  1.53 us
    pallas_call x1, Pallas kernels, merge(): pl.pallas_call(merge_kernel, out_shape=jax.ShapeDtypeStruct((128, D), BF1...  1.35 us
    unnamed x21, local copies, waits for them, and re-layouts  1.31 us
  transfers between devices with their start and end apart: 20, of which 9 were waited for; matrix products, arithmetic and copies ran while one was open for 0% of the time, Pallas kernels for 37%

profile of v12, /device:TPU:0, one launch (start us, length us, event | category | flops | bytes accessed | tf_op | source)
XLA Modules:
  0.0 52.1 jit_solution(12295336184814825634)
XLA Ops:
  0.0 0.5 collective-permute-start
  0.5 0.7 %collective-permute-start.1 = (bf16[8,2,32,128]{3,2,1,0:T(8,128)(2,1)}, bf16[8,2,32,128]{3,2,1,0:T(8,128)(2,1)S(1)}, u32[]{:S(2)}, u32[]{:S(2)}) collective-permute-start(bf16[8,2,32,128]{3,2,1,0:T(8,128)(2,1)} %own_any.1), channel_id=1, source_target_pairs={{1,2},{2,1},{3,4},{4,3},{5,6},{6,5},{7,8},{8,7},{9,10},{10,9},{11,... | collective-permute-start | bytes 393224 | tf_op jit(solution)/shard_map/ppermute | solution.py:674
  1.1 5.4 %collective-permute-start.2 = (bf16[72,1152]{1,0:T(8,128)(2,1)}, bf16[72,1152]{1,0:T(8,128)(2,1)S(1)}, u32[]{:S(2)}, u32[]{:S(2)}) collective-permute-start(bf16[72,1152]{1,0:T(8,128)(2,1)} %refs_0_.1), channel_id=1, source_target_pairs={{0,4},{1,5},{4,8},{5,9},{8,12},{9,13},{12,14},{13,15},{14,10},{15,... | collective-permute-start | bytes 497672 | tf_op jit(solution)/shard_map/ppermute | solution.py:674
  6.5 0.0 collective-permute-start.3
  6.5 1.3 %copy-done.3 = bf16[512,1152]{1,0:T(8,128)(2,1)S(1)} copy-done((bf16[512,1152]{1,0:T(8,128)(2,1)S(1)}, bf16[512,1152]{1,0:T(8,128)(2,1)}, u32[]{:S(2)}) %copy-start.3) | copy-done | bytes 1179672
  7.8 5.7 %fold.1 = (bf16[2304,512]{1,0:T(8,128)(2,1)S(1)}, bf16[1152,1152]{1,0:T(8,128)(2,1)S(1)}, bf16[512,1152]{1,0:T(8,128)(2,1)S(1)}) custom-call(bf16[512,1152]{1,0:T(8,128)(2,1)S(1)} %copy-done.3, bf16[1152,3456]{1,0:T(8,128)(2,1)} %qkv_any.1), custom_call_target="tpu_custom_call" | custom-call | flops 2717908992 | bytes 12582912 | tf_op jit(solution)/shard_map/fold/pallas_call | solution.py:252
  13.5 0.0 collective-permute-done.sibling_ref
  13.5 0.0 collective-permute-done.1.other_ref
  13.5 0.0 collective-permute-done.2.refs_1_
  13.5 0.0 copy-start.2
  13.5 2.1 %collective-permute-start.5 = (bf16[72,1152]{1,0:T(8,128)(2,1)S(1)}, bf16[72,1152]{1,0:T(8,128)(2,1)S(1)}, u32[]{:S(2)}, u32[]{:S(2)}) collective-permute-start(bf16[72,1152]{1,0:T(8,128)(2,1)S(1)} %collective-permute-done.2.refs_1_), channel_id=1, source_target_pairs={{0,4},{1,5},{4,8},{5,9},{8,12},{9,13},{12,14},{13,15},{14,10},{15,... | collective-permute-start | bytes 497672 | tf_op jit(solution)/shard_map/ppermute | solution.py:674
  15.6 0.0 collective-permute-start.6
  15.7 3.9 %convolve.1 = (bf16[64,512]{1,0:T(8,128)(2,1)S(1)}, bf16[64,512]{1,0:T(8,128)(2,1)S(1)}) custom-call(s32[3]{0:T(128)S(1)} %copy-done.8, s32[1,3]{1,0:T(1,128)S(1)} %copy-done.1, bf16[8,2,32,128]{3,2,1,0:T(8,128)(2,1)S(1)} %copy-done.7, bf16[512,1152]{1,0:T(8,128)(2,1)S(1)} %copy-done.4, bf16[8,2,32,128]{3,2,1,0:T(8,128)(2,1)S(1)} %collective-permute-done.sibling_ref, ...), custom_call_target="tpu_custom_call" | custom-call | flops 2147483648 | bytes 4194304 | tf_op jit(solution)/shard_map/convolve/pallas_call | solution.py:404
  19.6 0.1 collective-permute-start.4
  19.6 1.2 %collective-permute-done.4 = bf16[64,512]{1,0:T(8,128)(2,1)S(1)} collective-permute-done((bf16[64,512]{1,0:T(8,128)(2,1)S(1)}, bf16[64,512]{1,0:T(8,128)(2,1)S(1)}, u32[]{:S(2)}, u32[]{:S(2)}) %collective-permute-start.4) | collective-permute-done | bytes 65568 | tf_op jit(solution)/shard_map/ppermute | solution.py:674
  20.9 0.3 collective-permute-done.6.refs_4_
  21.2 0.8 %collective-permute-start.8 = (bf16[128,512]{1,0:T(8,128)(2,1)S(1)}, bf16[128,512]{1,0:T(8,128)(2,1)S(1)}, u32[]{:S(2)}, u32[]{:S(2)}) collective-permute-start(bf16[128,512]{1,0:T(8,128)(2,1)S(1)} %constant_dynamic-update-slice_fusion.block_ref.refs_0_), channel_id=1, source_target_pairs={{4,0},{5,1},{8,4},{9,5},{12,8},{13,9},{14,12},{15,13},{10,14},{11,... | collective-permute-start | bytes 393224 | tf_op jit(solution)/shard_map/ppermute | solution.py:674
  22.0 1.2 %collective-permute-start.7 = (bf16[128,512]{1,0:T(8,128)(2,1)S(1)}, bf16[128,512]{1,0:T(8,128)(2,1)S(1)}, u32[]{:S(2)}, u32[]{:S(2)}) collective-permute-start(bf16[128,512]{1,0:T(8,128)(2,1)S(1)} %constant_dynamic-update-slice_fusion.block_ref.refs_0_), channel_id=1, source_target_pairs={{0,4},{1,5},{4,8},{5,9},{8,12},{9,13},{12,14},{13,15},{14,10},{15,... | collective-permute-start | bytes 393224 | tf_op jit(solution)/shard_map/ppermute | solution.py:674
  23.2 1.8 %collective-permute-start.11 = (bf16[72,1152]{1,0:T(8,128)(2,1)S(1)}, bf16[72,1152]{1,0:T(8,128)(2,1)S(1)}, u32[]{:S(2)}, u32[]{:S(2)}) collective-permute-start(bf16[72,1152]{1,0:T(8,128)(2,1)S(1)} %collective-permute-done.5.refs_3_), channel_id=1, source_target_pairs={{0,4},{1,5},{4,8},{5,9},{8,12},{9,13},{12,14},{13,15},{14,10},{15,... | collective-permute-start | bytes 497672 | tf_op jit(solution)/shard_map/ppermute | solution.py:674
  25.0 0.3 collective-permute-start.12
  25.2 1.5 %queries.1.refs_4_.refs_5_ = bf16[16,128,80]{2,1,0:T(8,128)(2,1)S(1)} custom-call(s32[1,3]{1,0:T(1,128)S(1)} %copy-done.1, bf16[128,512]{1,0:T(8,128)(2,1)S(1)} %constant_dynamic-update-slice_fusion.block_ref.refs_0_, bf16[512,1152]{1,0:T(8,128)(2,1)S(1)} %get-tuple-element.44.centered_ref, bf16[1152,1152]{1,0:T(8,128)(2,1)S(1)} %get-tuple-element.45.query_ref, ...), custom_call_target="tpu_custom_call" | custom-call | flops 1073741824 | bytes 4194304 | tf_op jit(solution)/shard_map/queries/pallas_call | solution.py:533
  26.8 0.0 collective-permute-done.8.refs_1_
  26.8 1.6 %collective-permute-done.7.refs_0_ = bf16[128,512]{1,0:T(8,128)(2,1)S(1)} collective-permute-done((bf16[128,512]{1,0:T(8,128)(2,1)S(1)}, bf16[128,512]{1,0:T(8,128)(2,1)S(1)}, u32[]{:S(2)}, u32[]{:S(2)}) %collective-permute-start.7) | collective-permute-done | bytes 131104 | tf_op jit(solution)/shard_map/ppermute | solution.py:674
  28.3 1.2 %collective-permute-start.9 = (bf16[128,512]{1,0:T(8,128)(2,1)S(1)}, bf16[128,512]{1,0:T(8,128)(2,1)S(1)}, u32[]{:S(2)}, u32[]{:S(2)}) collective-permute-start(bf16[128,512]{1,0:T(8,128)(2,1)S(1)} %collective-permute-done.7.refs_0_), channel_id=1, source_target_pairs={{0,4},{1,5},{4,8},{5,9},{8,12},{9,13},{12,14},{13,15},{14,10},{15,... | collective-permute-start | bytes 393224 | tf_op jit(solution)/shard_map/ppermute | solution.py:674
  29.6 0.8 %collective-permute-start.10 = (bf16[128,512]{1,0:T(8,128)(2,1)S(1)}, bf16[128,512]{1,0:T(8,128)(2,1)S(1)}, u32[]{:S(2)}, u32[]{:S(2)}) collective-permute-start(bf16[128,512]{1,0:T(8,128)(2,1)S(1)} %collective-permute-done.8.refs_1_), channel_id=1, source_target_pairs={{4,0},{5,1},{8,4},{9,5},{12,8},{13,9},{14,12},{15,13},{10,14},{11,... | collective-permute-start | bytes 393224 | tf_op jit(solution)/shard_map/ppermute | solution.py:674
  30.4 2.0 %step_attention.4.refs_0_ = f32[16,80,128]{2,1,0:T(8,128)S(1)} custom-call(s32[1,3]{1,0:T(1,128)S(1)} %copy-done.1, bf16[128,512]{1,0:T(8,128)(2,1)S(1)} %collective-permute-done.7.refs_0_, bf16[128,512]{1,0:T(8,128)(2,1)S(1)} %collective-permute-done.8.refs_1_, bf16[2304,512]{1,0:T(8,128)(2,1)S(1)} %get-tuple-element.50.refs_2_.refs_3_, ...), custom_call_target="tpu_custom_call" | custom-call | flops 1744830464 | bytes 5242880 | tf_op jit(solution)/shard_map/step_attention/pallas_call | solution.py:561
  32.4 0.0 collective-permute-done.12.refs_6_
  32.4 1.3 %collective-permute-start.15 = (bf16[72,1152]{1,0:T(8,128)(2,1)S(1)}, bf16[72,1152]{1,0:T(8,128)(2,1)S(1)}, u32[]{:S(2)}, u32[]{:S(2)}) collective-permute-start(bf16[72,1152]{1,0:T(8,128)(2,1)S(1)} %collective-permute-done.11.refs_5_), channel_id=1, source_target_pairs={{0,4},{1,5},{4,8},{5,9},{8,12},{9,13},{12,14},{13,15},{14,10},{15,... | collective-permute-start | bytes 497672 | tf_op jit(solution)/shard_map/ppermute | solution.py:674
  33.7 1.1 %collective-permute-done.9.refs_0_ = bf16[128,512]{1,0:T(8,128)(2,1)S(1)} collective-permute-done((bf16[128,512]{1,0:T(8,128)(2,1)S(1)}, bf16[128,512]{1,0:T(8,128)(2,1)S(1)}, u32[]{:S(2)}, u32[]{:S(2)}) %collective-permute-start.9) | collective-permute-done | bytes 131104 | tf_op jit(solution)/shard_map/ppermute | solution.py:674
  34.8 1.5 %collective-permute-start.13 = (bf16[128,512]{1,0:T(8,128)(2,1)S(1)}, bf16[128,512]{1,0:T(8,128)(2,1)S(1)}, u32[]{:S(2)}, u32[]{:S(2)}) collective-permute-start(bf16[128,512]{1,0:T(8,128)(2,1)S(1)} %collective-permute-done.9.refs_0_), channel_id=1, source_target_pairs={{0,4},{1,5},{4,8},{5,9},{8,12},{9,13},{12,14},{13,15},{14,10},{15,... | collective-permute-start | bytes 393224 | tf_op jit(solution)/shard_map/ppermute | solution.py:674
  36.3 0.5 collective-permute-start.14
  36.8 2.0 %step_attention.5.refs_1_ = f32[16,80,128]{2,1,0:T(8,128)S(1)} custom-call(s32[1,3]{1,0:T(1,128)S(1)} %copy-done.1, bf16[128,512]{1,0:T(8,128)(2,1)S(1)} %collective-permute-done.9.refs_0_, bf16[128,512]{1,0:T(8,128)(2,1)S(1)} %collective-permute-done.10.refs_1_, bf16[2304,512]{1,0:T(8,128)(2,1)S(1)} %get-tuple-element.50.refs_2_.refs_3_, ...), custom_call_target="tpu_custom_call" | custom-call | flops 1744830464 | bytes 5242880 | tf_op jit(solution)/shard_map/step_attention/pallas_call | solution.py:561
  38.8 0.0 collective-permute-done.15.refs_7_
  38.9 1.1 %collective-permute-done.13.refs_0_ = bf16[128,512]{1,0:T(8,128)(2,1)S(1)} collective-permute-done((bf16[128,512]{1,0:T(8,128)(2,1)S(1)}, bf16[128,512]{1,0:T(8,128)(2,1)S(1)}, u32[]{:S(2)}, u32[]{:S(2)}) %collective-permute-start.13) | collective-permute-done | bytes 131104 | tf_op jit(solution)/shard_map/ppermute | solution.py:674
  40.0 1.3 %collective-permute-done.14.refs_1_ = bf16[128,512]{1,0:T(8,128)(2,1)S(1)} collective-permute-done((bf16[128,512]{1,0:T(8,128)(2,1)S(1)}, bf16[128,512]{1,0:T(8,128)(2,1)S(1)}, u32[]{:S(2)}, u32[]{:S(2)}) %collective-permute-start.14) | collective-permute-done | bytes 131104 | tf_op jit(solution)/shard_map/ppermute | solution.py:674
  41.3 0.1 pack.1
  41.4 0.1 collective-permute-start.18
  41.5 0.5 %collective-permute-start.17 = (bf16[64,512]{1,0:T(8,128)(2,1)S(1)}, bf16[64,512]{1,0:T(8,128)(2,1)S(1)}, u32[]{:S(2)}, u32[]{:S(2)}) collective-permute-start(bf16[64,512]{1,0:T(8,128)(2,1)S(1)} %slice.7), channel_id=1, source_target_pairs={{4,0},{5,1},{8,4},{9,5},{12,8},{13,9},{14,12},{15,13},{10,14},{11,... | collective-permute-start | bytes 196616 | tf_op jit(solution)/shard_map/ppermute | solution.py:674
  42.0 1.5 %collective-permute-start.16 = (bf16[64,512]{1,0:T(8,128)(2,1)S(1)}, bf16[64,512]{1,0:T(8,128)(2,1)S(1)}, u32[]{:S(2)}, u32[]{:S(2)}) collective-permute-start(bf16[64,512]{1,0:T(8,128)(2,1)S(1)} %slice.6), channel_id=1, source_target_pairs={{0,4},{1,5},{4,8},{5,9},{8,12},{9,13},{12,14},{13,15},{14,10},{15,... | collective-permute-start | bytes 196616 | tf_op jit(solution)/shard_map/ppermute | solution.py:674
  43.6 2.0 %step_attention.6.refs_2_ = f32[16,80,128]{2,1,0:T(8,128)S(1)} custom-call(s32[1,3]{1,0:T(1,128)S(1)} %copy-done.1, bf16[128,512]{1,0:T(8,128)(2,1)S(1)} %collective-permute-done.13.refs_0_, bf16[128,512]{1,0:T(8,128)(2,1)S(1)} %collective-permute-done.14.refs_1_, bf16[2304,512]{1,0:T(8,128)(2,1)S(1)} %get-tuple-element.50.refs_2_.refs_3_, ...), custom_call_target="tpu_custom_call" | custom-call | flops 1744830464 | bytes 5242880 | tf_op jit(solution)/shard_map/step_attention/pallas_call | solution.py:561
  45.6 0.4 collective-permute-done.17.refs_2_
  46.0 0.3 collective-permute-done.16.refs_1_
  46.3 2.0 %step_attention.7.refs_3_ = f32[16,80,128]{2,1,0:T(8,128)S(1)} custom-call(s32[1,3]{1,0:T(1,128)S(1)} %copy-done.1, bf16[128,512]{1,0:T(8,128)(2,1)S(1)} %constant_dynamic-update-slice_fusion.block_ref.refs_0_, bf16[64,512]{1,0:T(8,128)(2,1)S(1)} %collective-permute-done.16.refs_1_, bf16[64,512]{1,0:T(8,128)(2,1)S(1)} %collective-permute-done.17.refs_2_, ...), custom_call_target="tpu_custom_call" | custom-call | flops 1744830464 | bytes 5242880 | tf_op jit(solution)/shard_map/step_attention/pallas_call | solution.py:561
  48.3 0.0 collective-permute-done.18.refs_5_
  48.3 1.0 %project_out.1 = (bf16[64,1152]{1,0:T(8,128)(2,1)S(1)}, bf16[64,1152]{1,0:T(8,128)(2,1)S(1)}) custom-call(f32[16,80,128]{2,1,0:T(8,128)S(1)} %step_attention.4.refs_0_, f32[16,80,128]{2,1,0:T(8,128)S(1)} %step_attention.5.refs_1_, f32[16,80,128]{2,1,0:T(8,128)S(1)} %step_attention.6.refs_2_, f32[16,80,128]{2,1,0:T(8,128)S(1)} %step_attention.7.refs_3_, ...), custom_call_target="tpu_custom_call" | custom-call | flops 377487360 | bytes 4194304 | tf_op jit(solution)/shard_map/project_out/pallas_call | solution.py:606
  49.3 0.1 collective-permute-start.19
  49.4 1.4 %collective-permute-done.19.got_ref = bf16[64,1152]{1,0:T(8,128)(2,1)S(1)} collective-permute-done((bf16[64,1152]{1,0:T(8,128)(2,1)S(1)}, bf16[64,1152]{1,0:T(8,128)(2,1)S(1)}, u32[]{:S(2)}, u32[]{:S(2)}) %collective-permute-start.19) | collective-permute-done | bytes 147488 | tf_op jit(solution)/shard_map/ppermute | solution.py:674
  50.8 1.3 %merge.1 = bf16[128,1152]{1,0:T(8,128)(2,1)} custom-call(s32[1,3]{1,0:T(1,128)S(1)} %copy-done.1, bf16[64,1152]{1,0:T(8,128)(2,1)S(1)} %get-tuple-element.65.keep_ref, bf16[64,1152]{1,0:T(8,128)(2,1)S(1)} %collective-permute-done.19.got_ref), custom_call_target="tpu_custom_call" | custom-call | tf_op jit(solution)/shard_map/merge/pallas_call | solution.py:653
  (26 shorter events, 0.1 us)
Async XLA Ops:
  0.0 15.6 %copy-start.1 = (s32[1,3]{1,0:T(1,128)S(1)}, s32[1,3]{1,0:T(1,128)}, u32[]{:S(2)}) copy-start(s32[1,3]{1,0:T(1,128)} %lengths_ref.11) | copy-start | bytes 40
  0.0 13.5 %collective-permute-start = (bf16[8,2,32,128]{3,2,1,0:T(8,128)(2,1)}, bf16[8,2,32,128]{3,2,1,0:T(8,128)(2,1)S(1)}, u32[]{:S(2)}, u32[]{:S(2)}) collective-permute-start(bf16[8,2,32,128]{3,2,1,0:T(8,128)(2,1)} %own_any.1), channel_id=1, source_target_pairs={{0,1},{1,0},{2,3},{3,2},{4,5},{5,4},{6,7},{7,6},{8,9},{9,8},{10,11... | collective-permute-start | bytes 393224 | tf_op jit(solution)/shard_map/ppermute | solution.py:674
  0.5 13.0 %collective-permute-start.1 = (bf16[8,2,32,128]{3,2,1,0:T(8,128)(2,1)}, bf16[8,2,32,128]{3,2,1,0:T(8,128)(2,1)S(1)}, u32[]{:S(2)}, u32[]{:S(2)}) collective-permute-start(bf16[8,2,32,128]{3,2,1,0:T(8,128)(2,1)} %own_any.1), channel_id=1, source_target_pairs={{1,2},{2,1},{3,4},{4,3},{5,6},{6,5},{7,8},{8,7},{9,10},{10,9},{11,... | collective-permute-start | bytes 393224 | tf_op jit(solution)/shard_map/ppermute | solution.py:674
  1.1 12.4 %collective-permute-start.2 = (bf16[72,1152]{1,0:T(8,128)(2,1)}, bf16[72,1152]{1,0:T(8,128)(2,1)S(1)}, u32[]{:S(2)}, u32[]{:S(2)}) collective-permute-start(bf16[72,1152]{1,0:T(8,128)(2,1)} %refs_0_.1), channel_id=1, source_target_pairs={{0,4},{1,5},{4,8},{5,9},{8,12},{9,13},{12,14},{13,15},{14,10},{15,... | collective-permute-start | bytes 497672 | tf_op jit(solution)/shard_map/ppermute | solution.py:674
  6.5 7.0 %collective-permute-start.3 = (bf16[72,1152]{1,0:T(8,128)(2,1)}, bf16[72,1152]{1,0:T(8,128)(2,1)S(1)}, u32[]{:S(2)}, u32[]{:S(2)}) collective-permute-start(bf16[72,1152]{1,0:T(8,128)(2,1)} %refs_0_.1), channel_id=1, source_target_pairs={{4,0},{5,1},{8,4},{9,5},{12,8},{13,9},{14,12},{15,13},{10,14},{11,... | collective-permute-start | bytes 497672 | tf_op jit(solution)/shard_map/ppermute | solution.py:674
  6.5 1.3 %copy-start.3 = (bf16[512,1152]{1,0:T(8,128)(2,1)S(1)}, bf16[512,1152]{1,0:T(8,128)(2,1)}, u32[]{:S(2)}) copy-start(bf16[512,1152]{1,0:T(8,128)(2,1)} %patch_any.3) | copy-start | bytes 3538948
  7.8 7.8 %copy-start.4 = (bf16[512,1152]{1,0:T(8,128)(2,1)S(1)}, bf16[512,1152]{1,0:T(8,128)(2,1)}, u32[]{:S(2)}) copy-start(bf16[512,1152]{1,0:T(8,128)(2,1)} %patch_any.3) | copy-start | bytes 3538948
  7.8 7.8 %copy-start.5 = (bf16[3,3,3,128,128]{4,3,2,1,0:T(8,128)(2,1)S(1)}, bf16[3,3,3,128,128]{4,3,2,1,0:T(8,128)(2,1)}, u32[]{:S(2)}) copy-start(bf16[3,3,3,128,128]{4,3,2,1,0:T(8,128)(2,1)} %first_ref.1) | copy-start | bytes 2654212
  7.8 7.8 %copy-start.6 = (bf16[3,3,3,128,128]{4,3,2,1,0:T(8,128)(2,1)S(1)}, bf16[3,3,3,128,128]{4,3,2,1,0:T(8,128)(2,1)}, u32[]{:S(2)}) copy-start(bf16[3,3,3,128,128]{4,3,2,1,0:T(8,128)(2,1)} %second_ref.1) | copy-start | bytes 2654212
  7.8 7.8 %copy-start.7 = (bf16[8,2,32,128]{3,2,1,0:T(8,128)(2,1)S(1)}, bf16[8,2,32,128]{3,2,1,0:T(8,128)(2,1)}, u32[]{:S(2)}) copy-start(bf16[8,2,32,128]{3,2,1,0:T(8,128)(2,1)} %own_any.1) | copy-start | bytes 393220
  7.8 7.9 %copy-start.8 = (s32[3]{0:T(128)S(1)}, s32[3]{0:T(128)}, u32[]{:S(2)}) copy-start(s32[3]{0:T(128)} %counts_any.1) | copy-start | bytes 40
  13.5 11.7 %copy-start.2 = (f32[72]{0:T(128)S(1)}, f32[72]{0:T(128)}, u32[]{:S(2)}) copy-start(f32[72]{0:T(128)} %param.16) | copy-start | bytes 868
  13.5 7.3 %collective-permute-start.5 = (bf16[72,1152]{1,0:T(8,128)(2,1)S(1)}, bf16[72,1152]{1,0:T(8,128)(2,1)S(1)}, u32[]{:S(2)}, u32[]{:S(2)}) collective-permute-start(bf16[72,1152]{1,0:T(8,128)(2,1)S(1)} %collective-permute-done.2.refs_1_), channel_id=1, source_target_pairs={{0,4},{1,5},{4,8},{5,9},{8,12},{9,13},{12,14},{13,15},{14,10},{15,... | collective-permute-start | bytes 497672 | tf_op jit(solution)/shard_map/ppermute | solution.py:674
  15.6 5.6 %collective-permute-start.6 = (bf16[72,1152]{1,0:T(8,128)(2,1)S(1)}, bf16[72,1152]{1,0:T(8,128)(2,1)S(1)}, u32[]{:S(2)}, u32[]{:S(2)}) collective-permute-start(bf16[72,1152]{1,0:T(8,128)(2,1)S(1)} %collective-permute-done.3.refs_2_), channel_id=1, source_target_pairs={{4,0},{5,1},{8,4},{9,5},{12,8},{13,9},{14,12},{15,13},{10,14},{11,... | collective-permute-start | bytes 497672 | tf_op jit(solution)/shard_map/ppermute | solution.py:674
  19.6 1.3 %collective-permute-start.4 = (bf16[64,512]{1,0:T(8,128)(2,1)S(1)}, bf16[64,512]{1,0:T(8,128)(2,1)S(1)}, u32[]{:S(2)}, u32[]{:S(2)}) collective-permute-start(bf16[64,512]{1,0:T(8,128)(2,1)S(1)} %get-tuple-element.40), channel_id=1, source_target_pairs={{0,1},{1,0},{2,3},{3,2},{4,5},{5,4},{6,7},{7,6},{8,9},{9,8},{10,11... | collective-permute-start | bytes 196616 | tf_op jit(solution)/shard_map/ppermute | solution.py:674
  21.2 5.6 %collective-permute-start.8 = (bf16[128,512]{1,0:T(8,128)(2,1)S(1)}, bf16[128,512]{1,0:T(8,128)(2,1)S(1)}, u32[]{:S(2)}, u32[]{:S(2)}) collective-permute-start(bf16[128,512]{1,0:T(8,128)(2,1)S(1)} %constant_dynamic-update-slice_fusion.block_ref.refs_0_), channel_id=1, source_target_pairs={{4,0},{5,1},{8,4},{9,5},{12,8},{13,9},{14,12},{15,13},{10,14},{11,... | collective-permute-start | bytes 393224 | tf_op jit(solution)/shard_map/ppermute | solution.py:674
  22.0 6.4 %collective-permute-start.7 = (bf16[128,512]{1,0:T(8,128)(2,1)S(1)}, bf16[128,512]{1,0:T(8,128)(2,1)S(1)}, u32[]{:S(2)}, u32[]{:S(2)}) collective-permute-start(bf16[128,512]{1,0:T(8,128)(2,1)S(1)} %constant_dynamic-update-slice_fusion.block_ref.refs_0_), channel_id=1, source_target_pairs={{0,4},{1,5},{4,8},{5,9},{8,12},{9,13},{12,14},{13,15},{14,10},{15,... | collective-permute-start | bytes 393224 | tf_op jit(solution)/shard_map/ppermute | solution.py:674
  23.2 9.2 %collective-permute-start.11 = (bf16[72,1152]{1,0:T(8,128)(2,1)S(1)}, bf16[72,1152]{1,0:T(8,128)(2,1)S(1)}, u32[]{:S(2)}, u32[]{:S(2)}) collective-permute-start(bf16[72,1152]{1,0:T(8,128)(2,1)S(1)} %collective-permute-done.5.refs_3_), channel_id=1, source_target_pairs={{0,4},{1,5},{4,8},{5,9},{8,12},{9,13},{12,14},{13,15},{14,10},{15,... | collective-permute-start | bytes 497672 | tf_op jit(solution)/shard_map/ppermute | solution.py:674
  25.0 7.5 %collective-permute-start.12 = (bf16[72,1152]{1,0:T(8,128)(2,1)S(1)}, bf16[72,1152]{1,0:T(8,128)(2,1)S(1)}, u32[]{:S(2)}, u32[]{:S(2)}) collective-permute-start(bf16[72,1152]{1,0:T(8,128)(2,1)S(1)} %collective-permute-done.6.refs_4_), channel_id=1, source_target_pairs={{4,0},{5,1},{8,4},{9,5},{12,8},{13,9},{14,12},{15,13},{10,14},{11,... | collective-permute-start | bytes 497672 | tf_op jit(solution)/shard_map/ppermute | solution.py:674
  25.2 5.1 %copy-start.9 = (f32[72]{0:T(128)S(1)}, f32[72]{0:T(128)}, u32[]{:S(2)}) copy-start(f32[72]{0:T(128)} %param.17) | copy-start | bytes 868
  28.3 6.4 %collective-permute-start.9 = (bf16[128,512]{1,0:T(8,128)(2,1)S(1)}, bf16[128,512]{1,0:T(8,128)(2,1)S(1)}, u32[]{:S(2)}, u32[]{:S(2)}) collective-permute-start(bf16[128,512]{1,0:T(8,128)(2,1)S(1)} %collective-permute-done.7.refs_0_), channel_id=1, source_target_pairs={{0,4},{1,5},{4,8},{5,9},{8,12},{9,13},{12,14},{13,15},{14,10},{15,... | collective-permute-start | bytes 393224 | tf_op jit(solution)/shard_map/ppermute | solution.py:674
  29.6 5.2 %collective-permute-start.10 = (bf16[128,512]{1,0:T(8,128)(2,1)S(1)}, bf16[128,512]{1,0:T(8,128)(2,1)S(1)}, u32[]{:S(2)}, u32[]{:S(2)}) collective-permute-start(bf16[128,512]{1,0:T(8,128)(2,1)S(1)} %collective-permute-done.8.refs_1_), channel_id=1, source_target_pairs={{4,0},{5,1},{8,4},{9,5},{12,8},{13,9},{14,12},{15,13},{10,14},{11,... | collective-permute-start | bytes 393224 | tf_op jit(solution)/shard_map/ppermute | solution.py:674
  32.4 8.9 %copy-start = (bf16[72,1152]{1,0:T(8,128)(2,1)S(1)}, bf16[72,1152]{1,0:T(8,128)(2,1)}, u32[]{:S(2)}) copy-start(bf16[72,1152]{1,0:T(8,128)(2,1)} %refs_0_.1) | copy-start | bytes 497668
  32.4 6.4 %collective-permute-start.15 = (bf16[72,1152]{1,0:T(8,128)(2,1)S(1)}, bf16[72,1152]{1,0:T(8,128)(2,1)S(1)}, u32[]{:S(2)}, u32[]{:S(2)}) collective-permute-start(bf16[72,1152]{1,0:T(8,128)(2,1)S(1)} %collective-permute-done.11.refs_5_), channel_id=1, source_target_pairs={{0,4},{1,5},{4,8},{5,9},{8,12},{9,13},{12,14},{13,15},{14,10},{15,... | collective-permute-start | bytes 497672 | tf_op jit(solution)/shard_map/ppermute | solution.py:674
  34.8 5.2 %collective-permute-start.13 = (bf16[128,512]{1,0:T(8,128)(2,1)S(1)}, bf16[128,512]{1,0:T(8,128)(2,1)S(1)}, u32[]{:S(2)}, u32[]{:S(2)}) collective-permute-start(bf16[128,512]{1,0:T(8,128)(2,1)S(1)} %collective-permute-done.9.refs_0_), channel_id=1, source_target_pairs={{0,4},{1,5},{4,8},{5,9},{8,12},{9,13},{12,14},{13,15},{14,10},{15,... | collective-permute-start | bytes 393224 | tf_op jit(solution)/shard_map/ppermute | solution.py:674
  36.3 5.0 %collective-permute-start.14 = (bf16[128,512]{1,0:T(8,128)(2,1)S(1)}, bf16[128,512]{1,0:T(8,128)(2,1)S(1)}, u32[]{:S(2)}, u32[]{:S(2)}) collective-permute-start(bf16[128,512]{1,0:T(8,128)(2,1)S(1)} %collective-permute-done.10.refs_1_), channel_id=1, source_target_pairs={{4,0},{5,1},{8,4},{9,5},{12,8},{13,9},{14,12},{15,13},{10,14},{11,... | collective-permute-start | bytes 393224 | tf_op jit(solution)/shard_map/ppermute | solution.py:674
  41.4 6.9 %collective-permute-start.18 = (bf16[576,1152]{1,0:T(8,128)(2,1)S(1)}, bf16[576,1152]{1,0:T(8,128)(2,1)S(1)}, u32[]{:S(2)}, u32[]{:S(2)}) collective-permute-start(bf16[576,1152]{1,0:T(8,128)(2,1)S(1)} %bitcast.3), channel_id=1, source_target_pairs={{0,1},{1,0},{2,3},{3,2},{4,5},{5,4},{6,7},{7,6},{8,9},{9,8},{10,11... | collective-permute-start | bytes 3981320 | tf_op jit(solution)/shard_map/ppermute | solution.py:674
  41.5 4.5 %collective-permute-start.17 = (bf16[64,512]{1,0:T(8,128)(2,1)S(1)}, bf16[64,512]{1,0:T(8,128)(2,1)S(1)}, u32[]{:S(2)}, u32[]{:S(2)}) collective-permute-start(bf16[64,512]{1,0:T(8,128)(2,1)S(1)} %slice.7), channel_id=1, source_target_pairs={{4,0},{5,1},{8,4},{9,5},{12,8},{13,9},{14,12},{15,13},{10,14},{11,... | collective-permute-start | bytes 196616 | tf_op jit(solution)/shard_map/ppermute | solution.py:674
  42.0 4.3 %collective-permute-start.16 = (bf16[64,512]{1,0:T(8,128)(2,1)S(1)}, bf16[64,512]{1,0:T(8,128)(2,1)S(1)}, u32[]{:S(2)}, u32[]{:S(2)}) collective-permute-start(bf16[64,512]{1,0:T(8,128)(2,1)S(1)} %slice.6), channel_id=1, source_target_pairs={{0,4},{1,5},{4,8},{5,9},{8,12},{9,13},{12,14},{13,15},{14,10},{15,... | collective-permute-start | bytes 196616 | tf_op jit(solution)/shard_map/ppermute | solution.py:674
  49.3 1.4 %collective-permute-start.19 = (bf16[64,1152]{1,0:T(8,128)(2,1)S(1)}, bf16[64,1152]{1,0:T(8,128)(2,1)S(1)}, u32[]{:S(2)}, u32[]{:S(2)}) collective-permute-start(bf16[64,1152]{1,0:T(8,128)(2,1)S(1)} %get-tuple-element.66), channel_id=1, source_target_pairs={{0,1},{1,0},{2,3},{3,2},{4,5},{5,4},{6,7},{7,6},{8,9},{9,8},{10,11... | collective-permute-start | bytes 442376 | tf_op jit(solution)/shard_map/ppermute | solution.py:674
